TPU v7x, 32 devices: a whole 2x2x4 slice. The times are simulated.
32 devices in a mesh: img: 4 (over z), hid: 8 (over y, x, core).
Axes of the slice: x: 2, y: 2, z: 4, core: 2. Of those that a mesh axis runs over, the one named last changes fastest.
Arguments:
- images: bfloat16 [64, 36, 36, 128], P(('img', 'hid')), may hold values from -6 to 6
- valid_sizes: int32 [64, 2], P(('img', 'hid')), may hold values from 12 to 36, as said below
- cotangent: bfloat16 [64, 18, 5760], P(('img', 'hid')), may hold values from -6 to 6
- mix_weight: bfloat16 [2, 3, 128, 128], replicated, may hold values from -0.5 to 0.5
- mix_bias: float32 [2, 2, 128], replicated, may hold values from -3 to 3
- squeeze_weight: float32 [2, 128, 32], replicated, may hold values from -1 to 1
- squeeze_bias: float32 [2, 32], replicated, may hold values from -3 to 3
- expand_weight: float32 [2, 32, 384], replicated, may hold values from -2 to 2
- expand_bias: float32 [2, 384], replicated, may hold values from -4 to 4
- project_weight: bfloat16 [2, 128, 128], replicated, may hold values from -0.75 to 0.75
- project_bias: float32 [2, 128], replicated, may hold values from -2 to 2
- norm_gain: float32 [2, 2, 128], replicated, may hold values from 0.5 to 1.5
- norm_bias: float32 [2, 2, 128], replicated, may hold values from -2 to 2
- inner_weight: bfloat16 [2, 128, 512], P(None, None, 'hid'), may hold values from -0.5 to 0.5
- inner_bias: bfloat16 [2, 512], P(None, 'hid'), may hold values from -3 to 3
- outer_weight: bfloat16 [2, 512, 128], P(None, 'hid'), may hold values from -0.5 to 0.5
- outer_bias: float32 [2, 128], replicated, may hold values from -2 to 2
- merge_weight: bfloat16 [1152, 320], replicated, may hold values from -0.1875 to 0.1875
- merge_bias: float32 [320], replicated, may hold values from -2 to 2
Outputs:
- features: bfloat16 [64, 18, 5760], P(('img', 'hid'))
- images_grad: float32 [64, 36, 36, 128], P(('img', 'hid'))
- grad_mix_weight: float32 [2, 3, 128, 128], replicated
- grad_mix_bias: float32 [2, 2, 128], replicated
- grad_squeeze_weight: float32 [2, 128, 32], replicated
- grad_squeeze_bias: float32 [2, 32], replicated
- grad_expand_weight: float32 [2, 32, 384], replicated
- grad_expand_bias: float32 [2, 384], replicated
- grad_project_weight: float32 [2, 128, 128], replicated
- grad_project_bias: float32 [2, 128], replicated
- grad_norm_gain: float32 [2, 2, 128], replicated
- grad_norm_bias: float32 [2, 2, 128], replicated
- grad_inner_weight: float32 [2, 128, 512], P(None, None, 'hid')
- grad_inner_bias: float32 [2, 512], P(None, 'hid')
- grad_outer_weight: float32 [2, 512, 128], P(None, 'hid')
- grad_outer_bias: float32 [2, 128], replicated
- grad_merge_weight: float32 [1152, 320], replicated
- grad_merge_bias: float32 [320], replicated
Inputs may be any that keep to these rules, and one draw needn't show every extreme that they name: `valid_sizes`: each map's valid region holds its first rows and columns; some map is wholly valid and some map has 12 valid rows and columns.
All inputs are finite; a program needn't handle non-finite values.
Results may differ from a plain program's by a relative error of at most 0.025.
Values may be sent and summed in bfloat16 or wider, within the bound.
No kernel may reach another device: no remote copies, remote signals or barrier semaphores. Data moves between devices by JAX's collectives and lax.ppermute only.
A program may use at most 320 MiB of HBM per device.

v0:
```python
from functools import partial

import jax
import jax.numpy as jnp
from jax import lax
from jax.sharding import PartitionSpec as P

PRECISE = lax.Precision.HIGHEST


def layer_norm(values, gain_vec, bias_vec):
    average = jnp.mean(values, axis=-1, keepdims=True)
    centered = values - average
    variance = jnp.mean(centered * centered, axis=-1, keepdims=True)
    return centered * lax.rsqrt(variance + 1e-05) * gain_vec + bias_vec


def cycle_shift(grid_in, axis_dim, direction):
    channels = grid_in.shape[-1]
    offset = ((jnp.arange(channels) + 1) % 3 - 1) * direction
    widths = [(0, 0)] * grid_in.ndim
    widths[axis_dim] = (1, 1)
    padded = jnp.pad(grid_in, widths)
    length = grid_in.shape[axis_dim]
    lower_rows = lax.slice_in_dim(padded, 0, length, axis=axis_dim)
    middle = lax.slice_in_dim(padded, 1, length + 1, axis=axis_dim)
    upper_rows = lax.slice_in_dim(padded, 2, length + 2, axis=axis_dim)
    return jnp.where(offset == -1, lower_rows, jnp.where(offset == 0, middle, upper_rows))


def pixel_mask(valid_sizes, side_len):
    places = jnp.arange(side_len, dtype=jnp.int32)
    rows_ok = (places[None, :] < valid_sizes[:, 0:1]).astype(jnp.float32)
    cols_ok = (places[None, :] < valid_sizes[:, 1:2]).astype(jnp.float32)
    return rows_ok[:, :, None, None] * cols_ok[:, None, :, None]


def reweight_mix(
    h_branch, w_branch, c_branch, squeeze_w, squeeze_b, expand_w, expand_b, valid_mask, counts
):
    branch_sum = h_branch + w_branch + c_branch
    pooled = jnp.sum(branch_sum * valid_mask, axis=(1, 2)) / counts[:, None]
    hidden = jax.nn.gelu(
        jnp.dot(pooled, squeeze_w, precision=PRECISE) + squeeze_b, approximate=False
    )
    logits = jnp.dot(hidden, expand_w, precision=PRECISE) + expand_b
    logits = logits.reshape(logits.shape[0], -1, 3)
    weights = jax.nn.softmax(logits, axis=-1)
    return (
        h_branch * weights[:, None, None, :, 0]
        + w_branch * weights[:, None, None, :, 1]
        + c_branch * weights[:, None, None, :, 2]
    )


def patches(grid_in):
    side_len = grid_in.shape[1]
    padded = jnp.pad(grid_in, ((0, 0), (1, 1), (1, 1), (0, 0)))
    pieces = []
    for row_off in range(3):
        for col_off in range(3):
            pieces.append(
                padded[:, row_off : row_off + side_len : 2, col_off : col_off + side_len : 2, :]
            )
    return jnp.concatenate(pieces, axis=-1)


def matmul(left_op, right_op):
    return lax.dot_general(
        left_op,
        right_op,
        (((left_op.ndim - 1,), (0,)), ((), ())),
        preferred_element_type=jnp.float32,
    )


def matmul_back(left_op, right_op):
    return lax.dot_general(
        left_op,
        right_op,
        (((left_op.ndim - 1,), (1,)), ((), ())),
        preferred_element_type=jnp.float32,
    )


def contract_rows(left_op, right_op):
    left_flat = left_op.reshape(-1, left_op.shape[-1])
    right_flat = right_op.reshape(-1, right_op.shape[-1])
    return lax.dot_general(
        left_flat, right_flat, (((0,), (0,)), ((), ())), preferred_element_type=jnp.float32
    )


def gelu_exact(values):
    return jax.nn.gelu(values, approximate=False)


def per_device(
    images,
    valid_sizes,
    cotangent,
    mix_weight,
    mix_bias,
    squeeze_weight,
    squeeze_bias,
    expand_weight,
    expand_bias,
    project_weight,
    project_bias,
    norm_gain,
    norm_bias,
    inner_weight,
    inner_bias,
    outer_weight,
    outer_bias,
    merge_weight,
    merge_bias,
):
    image_count = images.shape[0]
    side_len = images.shape[1]
    channels = images.shape[3]
    layer_total = mix_weight.shape[0]
    local_rows = image_count * side_len * side_len
    valid_mask = pixel_mask(valid_sizes, side_len)
    counts = (valid_sizes[:, 0] * valid_sizes[:, 1]).astype(jnp.float32)
    mixer = partial(reweight_mix, valid_mask=valid_mask, counts=counts)
    inner_used, inner_bias_used, outer_used = (inner_weight, inner_bias, outer_weight)

    def mlp_backward(out_grad, kept_rows, layer_at):
        rows_in, pre_act, hidden = kept_rows
        grad_in = lax.all_gather(out_grad, "hid", axis=0, tiled=True)
        hidden_grad = matmul_back(grad_in, outer_used[layer_at])
        _, gelu_pull = jax.vjp(gelu_exact, pre_act)
        pre_grad = gelu_pull(hidden_grad)[0].astype(jnp.bfloat16)
        outer_grad = contract_rows(hidden, grad_in)
        inner_grad = contract_rows(rows_in, pre_grad)
        inner_bias_grad = jnp.sum(pre_grad.astype(jnp.float32), axis=0)
        outer_bias_grad = jnp.sum(out_grad.astype(jnp.float32), axis=0)
        normed_grad = lax.psum_scatter(
            matmul_back(pre_grad, inner_used[layer_at]).astype(jnp.bfloat16),
            "hid",
            scatter_dimension=0,
            tiled=True,
        ).astype(jnp.float32)
        return (normed_grad, inner_grad, inner_bias_grad, outer_grad, outer_bias_grad)

    state = images.astype(jnp.float32) * valid_mask
    saved = []
    for layer_at in range(layer_total):
        normed = layer_norm(state, norm_gain[layer_at, 0], norm_bias[layer_at, 0]).astype(
            jnp.bfloat16
        )
        rows_shift = cycle_shift(normed, 1, 1)
        cols_shift = cycle_shift(normed, 2, 1)
        h_branch = matmul(rows_shift, mix_weight[layer_at, 0]) + mix_bias[layer_at, 0]
        w_branch = matmul(cols_shift, mix_weight[layer_at, 1]) + mix_bias[layer_at, 1]
        c_branch = matmul(normed, mix_weight[layer_at, 2])
        mixed_out, mix_pull = jax.vjp(
            mixer,
            h_branch,
            w_branch,
            c_branch,
            squeeze_weight[layer_at],
            squeeze_bias[layer_at],
            expand_weight[layer_at],
            expand_bias[layer_at],
        )
        mixed_low = mixed_out.astype(jnp.bfloat16)
        token_out = matmul(mixed_low, project_weight[layer_at]) + project_bias[layer_at]
        halfway = state + valid_mask * token_out
        normed2 = layer_norm(halfway, norm_gain[layer_at, 1], norm_bias[layer_at, 1]).astype(
            jnp.bfloat16
        )
        mlp_rows_in = lax.all_gather(
            normed2.reshape(local_rows, channels), "hid", axis=0, tiled=True
        )
        mlp_pre_act = jnp.dot(
            mlp_rows_in, inner_used[layer_at], preferred_element_type=jnp.float32
        ) + inner_bias_used[layer_at].astype(jnp.float32)
        mlp_hidden = gelu_exact(mlp_pre_act).astype(jnp.bfloat16)
        summed = lax.psum_scatter(
            jnp.dot(mlp_hidden, outer_used[layer_at], preferred_element_type=jnp.float32).astype(
                jnp.bfloat16
            ),
            "hid",
            scatter_dimension=0,
            tiled=True,
        ).astype(jnp.float32)
        channel_out = summed + outer_bias[layer_at]
        kept_rows = (mlp_rows_in, mlp_pre_act, mlp_hidden)
        saved.append(
            (state, normed, rows_shift, cols_shift, mix_pull, mixed_low, halfway, kept_rows)
        )
        state = halfway + valid_mask * channel_out.reshape(state.shape)
    final_low = state.astype(jnp.bfloat16)
    merge_in = patches(final_low)
    merged = matmul(merge_in, merge_weight) + merge_bias
    features = merged.reshape(image_count, side_len // 2, -1).astype(jnp.bfloat16)
    out_grad = cotangent.reshape(image_count, side_len // 2, side_len // 2, -1)
    merge_weight_grad = contract_rows(merge_in, out_grad)
    merge_bias_grad = jnp.sum(out_grad.astype(jnp.float32), axis=(0, 1, 2))
    patch_grad = matmul_back(out_grad, merge_weight)
    _, patch_pull = jax.vjp(patches, jnp.zeros(final_low.shape, jnp.float32))
    state_grad = patch_pull(patch_grad)[0]
    grad_store = [None] * layer_total
    for layer_at in reversed(range(layer_total)):
        before, normed, rows_shift, cols_shift, mix_pull, mixed_low, halfway, kept_rows = saved[
            layer_at
        ]
        channel_grad = (state_grad * valid_mask).astype(jnp.bfloat16).reshape(local_rows, channels)
        normed2_grad, inner_grad, inner_bias_grad, outer_grad, outer_bias_grad = mlp_backward(
            channel_grad, kept_rows, layer_at
        )
        _, norm_pull2 = jax.vjp(layer_norm, halfway, norm_gain[layer_at, 1], norm_bias[layer_at, 1])
        ln_grad, gain2_grad, shift2_grad = norm_pull2(normed2_grad.reshape(halfway.shape))
        halfway_grad = state_grad + ln_grad
        token_grad = (halfway_grad * valid_mask).astype(jnp.bfloat16)
        project_w_grad = contract_rows(mixed_low, token_grad)
        project_b_grad = jnp.sum(token_grad.astype(jnp.float32), axis=(0, 1, 2))
        mixed_grad = matmul_back(token_grad, project_weight[layer_at])
        h_grad, w_grad, c_grad, squeeze_w_grad, squeeze_b_grad, expand_w_grad, expand_b_grad = (
            mix_pull(mixed_grad)
        )
        h_low = h_grad.astype(jnp.bfloat16)
        w_low = w_grad.astype(jnp.bfloat16)
        c_low = c_grad.astype(jnp.bfloat16)
        mix_w_grad = jnp.stack(
            [
                contract_rows(rows_shift, h_low),
                contract_rows(cols_shift, w_low),
                contract_rows(normed, c_low),
            ]
        )
        mix_b_grad = jnp.stack(
            [
                jnp.sum(h_low.astype(jnp.float32), axis=(0, 1, 2)),
                jnp.sum(w_low.astype(jnp.float32), axis=(0, 1, 2)),
            ]
        )
        normed_grad = (
            cycle_shift(matmul_back(h_low, mix_weight[layer_at, 0]), 1, -1)
            + cycle_shift(matmul_back(w_low, mix_weight[layer_at, 1]), 2, -1)
            + matmul_back(c_low, mix_weight[layer_at, 2])
        )
        _, norm_pull1 = jax.vjp(layer_norm, before, norm_gain[layer_at, 0], norm_bias[layer_at, 0])
        first_grad, gain1_grad, shift1_grad = norm_pull1(normed_grad)
        state_grad = halfway_grad + first_grad
        grad_store[layer_at] = (
            mix_w_grad,
            mix_b_grad,
            squeeze_w_grad,
            squeeze_b_grad,
            expand_w_grad,
            expand_b_grad,
            project_w_grad,
            project_b_grad,
            jnp.stack([gain1_grad, gain2_grad]),
            jnp.stack([shift1_grad, shift2_grad]),
            inner_grad,
            inner_bias_grad,
            outer_grad,
            outer_bias_grad,
        )
    images_grad = state_grad * valid_mask
    stacked = [
        jnp.stack([grad_store[layer_at][member] for layer_at in range(layer_total)])
        for member in range(14)
    ]
    inner_total, inner_bias_total, outer_total = (stacked[10], stacked[11], stacked[12])
    inner_total, inner_bias_total, outer_total = (
        lax.psum(inner_total.astype(jnp.bfloat16), "img").astype(jnp.float32),
        lax.psum(inner_bias_total.astype(jnp.bfloat16), "img").astype(jnp.float32),
        lax.psum(outer_total.astype(jnp.bfloat16), "img").astype(jnp.float32),
    )
    shared = lax.psum(
        (
            stacked[0],
            stacked[1],
            stacked[2],
            stacked[3],
            stacked[4],
            stacked[5],
            stacked[6],
            stacked[7],
            stacked[8],
            stacked[9],
            stacked[13],
            merge_weight_grad,
            merge_bias_grad,
        ),
        ("img", "hid"),
    )
    return (
        features,
        images_grad,
        shared[0],
        shared[1],
        shared[2],
        shared[3],
        shared[4],
        shared[5],
        shared[6],
        shared[7],
        shared[8],
        shared[9],
        inner_total,
        inner_bias_total,
        outer_total,
        shared[10],
        shared[11],
        shared[12],
    )


def solution(mesh):
    in_specs = (
        P(("img", "hid"), None, None, None),
        P(("img", "hid"), None),
        P(("img", "hid"), None, None),
        P(),
        P(),
        P(),
        P(),
        P(),
        P(),
        P(),
        P(),
        P(),
        P(),
        P(None, None, "hid"),
        P(None, "hid"),
        P(None, "hid", None),
        P(),
        P(),
        P(),
    )
    out_specs = (
        P(("img", "hid"), None, None),
        P(("img", "hid"), None, None, None),
        P(),
        P(),
        P(),
        P(),
        P(),
        P(),
        P(),
        P(),
        P(),
        P(),
        P(None, None, "hid"),
        P(None, "hid"),
        P(None, "hid", None),
        P(),
        P(),
        P(),
    )
    return jax.shard_map(
        per_device, mesh=mesh, in_specs=in_specs, out_specs=out_specs, check_vma=False
    )
```

profile of v0, /device:TPU:0, one launch (start us, length us, event | category | flops | bytes accessed | tf_op | source)
XLA Modules:
  0.0 906.5 jit_solution(48933299161098231)
XLA Ops:
  18.6 17.6 %pad.87 = f32[2,38,38,128]{3,2,1,0:T(8,128)} pad(f32[2,18,18,128]{3,2,1,0:T(8,128)} %get-tuple-element.174, f32[]{:T(128)} %constant.51.clone.1), padding=0_0_0x2_1_1x2_1_1x0_0_0 | pad | bytes 1810436 | tf_op jit(solution)/shard_map/transpose(jvp())/pad | solution.py:63
  36.2 17.6 %pad.88 = f32[2,38,38,128]{3,2,1,0:T(8,128)} pad(f32[2,18,18,128]{3,2,1,0:T(8,128)} %get-tuple-element.166, f32[]{:T(128)} %constant.51.clone.1), padding=0_0_0x2_1_1x1_2_1x0_0_0 | pad | bytes 1810436 | tf_op jit(solution)/shard_map/transpose(jvp())/pad | solution.py:63
  53.8 17.6 %pad.89 = f32[2,38,38,128]{3,2,1,0:T(8,128)} pad(f32[2,18,18,128]{3,2,1,0:T(8,128)} %get-tuple-element.173, f32[]{:T(128)} %constant.51.clone.1), padding=0_0_0x2_1_1x0_3_1x0_0_0 | pad | bytes 1810436 | tf_op jit(solution)/shard_map/transpose(jvp())/pad | solution.py:63
  71.4 17.7 %pad.277 = f32[2,37,37,128]{3,2,1,0:T(8,128)} pad(f32[2,18,18,128]{3,2,1,0:T(8,128)} %get-tuple-element.167, f32[]{:T(128)} %constant.51.clone.1), padding=0_0_0x0_2_1x0_2_1x0_0_0 | pad | bytes 1733636
  89.1 12.1 %pad.278 = f32[2,37,36,128]{3,2,1,0:T(8,128)} pad(f32[2,18,18,128]{3,2,1,0:T(8,128)S(1)} %get-tuple-element.168, f32[]{:T(128)} %constant.51.clone.1), padding=0_0_0x0_2_1x0_1_1x0_0_0 | pad | bytes 1695748
  101.1 12.1 %pad.279 = f32[2,37,36,128]{3,2,1,0:T(8,128)} pad(f32[2,18,18,128]{3,2,1,0:T(8,128)S(1)} %get-tuple-element.169, f32[]{:T(128)} %constant.51.clone.1), padding=0_0_0x0_2_1x1_0_1x0_0_0 | pad | bytes 1695748
  113.2 12.0 %pad.154 = f32[2,36,36,128]{3,2,1,0:T(8,128)} pad(f32[2,18,18,128]{3,2,1,0:T(8,128)S(1)} %get-tuple-element.172, f32[]{:T(128)} %constant.51.clone.1), padding=0_0_0x0_1_1x1_0_1x0_0_0 | pad | bytes 1658884 | tf_op jit(solution)/shard_map/transpose(jvp(jit(_pad)))/pad | solution.py:58
  125.2 12.0 %pad.155 = f32[2,36,36,128]{3,2,1,0:T(8,128)} pad(f32[2,18,18,128]{3,2,1,0:T(8,128)S(1)} %get-tuple-element.171, f32[]{:T(128)} %constant.51.clone.1), padding=0_0_0x0_1_1x0_1_1x0_0_0 | pad | bytes 1658884 | tf_op jit(solution)/shard_map/transpose(jvp(jit(_pad)))/pad | solution.py:58
  137.2 12.1 %pad.280 = f32[2,36,37,128]{3,2,1,0:T(8,128)} pad(f32[2,18,18,128]{3,2,1,0:T(8,128)S(1)} %get-tuple-element.170, f32[]{:T(128)} %constant.51.clone.1), padding=0_0_0x0_1_1x0_2_1x0_0_0 | pad | bytes 1695748
  171.8 43.5 %all-gather.5.cloned.1.call-done = bf16[20736,128]{1,0:T(8,128)(2,1)} async-done(((bf16[2592,128]{1,0:T(8,128)(2,1)}), bf16[20736,128]{1,0:T(8,128)(2,1)}) %all-gather.5.cloned.1.call-update) | async-done | bytes 5308432 | tf_op jit(solution)/shard_map/all_gather | solution.py:174
  215.3 15.7 %multiply_convert_fusion.1 = (bf16[20736,64]{0,1:T(8,128)(2,1)S(1)}, f32[20736,64]{0,1:T(8,128)}, f32[20736,64]{0,1:T(8,128)}) fusion(f32[64]{0:T(128)S(1)} %get-tuple-element.204, bf16[20736,128]{1,0:T(8,128)(2,1)} %all-gather.5.cloned.1.call-done, bf16[2,128,64]{1,2,0:T(8,128)(2,1)S(1)} %copy-done.96), kind=kOutput, calls=%fused_computation.27 | convolution fusion | flops 427327488 | bytes 18596352 | tf_op jit(solution)/shard_map/dot_general | solution.py:177
  236.6 56.4 %reduce-scatter.5.cloned.1.call-done = bf16[2592,128]{1,0:T(8,128)(2,1)} async-done(((bf16[20736,128]{1,0:T(8,128)(2,1)}), bf16[2592,128]{1,0:T(8,128)(2,1)}) %reduce-scatter.5.cloned.1.call-update) | async-done | bytes 663568 | tf_op jit(solution)/shard_map/reduce_scatter | solution.py:181
  316.3 40.0 %all-gather.7.cloned.1.call-done = bf16[20736,128]{1,0:T(8,128)(2,1)} async-done(((bf16[2592,128]{1,0:T(8,128)(2,1)}), bf16[20736,128]{1,0:T(8,128)(2,1)}) %all-gather.7.cloned.1.call-update) | async-done | bytes 5308432 | tf_op jit(solution)/shard_map/all_gather | solution.py:174
  356.3 15.9 %multiply_convert_fusion = (bf16[20736,64]{0,1:T(8,128)(2,1)}, f32[20736,64]{0,1:T(8,128)}, f32[20736,64]{0,1:T(8,128)}) fusion(f32[64]{0:T(128)S(1)} %copy-done.167, bf16[20736,128]{1,0:T(8,128)(2,1)} %all-gather.7.cloned.1.call-done, bf16[2,128,64]{1,2,0:T(8,128)(2,1)S(1)} %copy-done.97), kind=kOutput, calls=%fused_computation.14 | convolution fusion | flops 427327488 | bytes 18596352 | tf_op jit(solution)/shard_map/dot_general | solution.py:177
  372.2 28.0 %all-gather.9.cloned.1.call-done = bf16[20736,128]{1,0:T(8,128)(2,1)} async-done(((bf16[2592,128]{1,0:T(8,128)(2,1)}), bf16[20736,128]{1,0:T(8,128)(2,1)}) %all-gather.9.cloned.1.call-update) | async-done | bytes 5308432 | tf_op jit(solution)/shard_map/all_gather | solution.py:131
  400.2 8.6 fusion.175
  413.8 5.7 convolution_convert_fusion.2
  421.0 49.9 %reduce-scatter.9.cloned.1.call-done = bf16[2592,128]{1,0:T(8,128)(2,1)} async-done(((bf16[20736,128]{1,0:T(8,128)(2,1)}), bf16[2592,128]{1,0:T(8,128)(2,1)}) %reduce-scatter.9.cloned.1.call-update) | async-done | bytes 663568 | tf_op jit(solution)/shard_map/reduce_scatter | solution.py:139
  476.4 54.7 %reduce-scatter.7.cloned.1.call-done = bf16[2592,128]{1,0:T(8,128)(2,1)} async-done(((bf16[20736,128]{1,0:T(8,128)(2,1)}), bf16[2592,128]{1,0:T(8,128)(2,1)}) %reduce-scatter.7.cloned.1.call-update) | async-done | bytes 663568 | tf_op jit(solution)/shard_map/reduce_scatter | solution.py:181
  535.7 5.1 fusion.164
  564.3 4.6 fusion.42
  568.9 4.1 fusion.44
  573.0 32.6 %all-gather.11.cloned.1.call-done = bf16[20736,128]{1,0:T(8,128)(2,1)} async-done(((bf16[2592,128]{1,0:T(8,128)(2,1)}), bf16[20736,128]{1,0:T(8,128)(2,1)}) %all-gather.11.cloned.1.call-update) | async-done | bytes 5308432 | tf_op jit(solution)/shard_map/all_gather | solution.py:131
  610.0 8.2 fusion.176
  627.2 11.0 %slice.297 = bf16[2,18,18,128]{3,2,1,0:T(8,128)(2,1)} slice(bf16[2,38,38,128]{3,2,1,0:T(8,128)(2,1)S(1)} %pad.86), slice={[0:2:1], [0:36:2], [0:36:2], [0:128:1]} | slice | bytes 331776 | tf_op jit(solution)/shard_map/slice | solution.py:63
  638.2 11.0 %slice.298 = bf16[2,18,18,128]{3,2,1,0:T(8,128)(2,1)} slice(bf16[2,38,38,128]{3,2,1,0:T(8,128)(2,1)S(1)} %pad.86), slice={[0:2:1], [0:36:2], [1:37:2], [0:128:1]} | slice | bytes 331776 | tf_op jit(solution)/shard_map/slice | solution.py:63
  649.2 11.0 %slice.299 = bf16[2,18,18,128]{3,2,1,0:T(8,128)(2,1)} slice(bf16[2,38,38,128]{3,2,1,0:T(8,128)(2,1)S(1)} %pad.86), slice={[0:2:1], [0:36:2], [2:38:2], [0:128:1]} | slice | bytes 331776 | tf_op jit(solution)/shard_map/slice | solution.py:63
  660.2 11.0 %slice.300 = bf16[2,18,18,128]{3,2,1,0:T(8,128)(2,1)} slice(bf16[2,38,38,128]{3,2,1,0:T(8,128)(2,1)S(1)} %pad.86), slice={[0:2:1], [1:37:2], [0:36:2], [0:128:1]} | slice | bytes 331776 | tf_op jit(solution)/shard_map/slice | solution.py:63
  671.1 11.0 %slice.301 = bf16[2,18,18,128]{3,2,1,0:T(8,128)(2,1)} slice(bf16[2,38,38,128]{3,2,1,0:T(8,128)(2,1)S(1)} %pad.86), slice={[0:2:1], [1:37:2], [1:37:2], [0:128:1]} | slice | bytes 331776 | tf_op jit(solution)/shard_map/slice | solution.py:63
  682.1 11.0 %slice.302 = bf16[2,18,18,128]{3,2,1,0:T(8,128)(2,1)} slice(bf16[2,38,38,128]{3,2,1,0:T(8,128)(2,1)S(1)} %pad.86), slice={[0:2:1], [1:37:2], [2:38:2], [0:128:1]} | slice | bytes 331776 | tf_op jit(solution)/shard_map/slice | solution.py:63
  759.0 40.8 %all-reduce.24 = (f32[2,2,128]{2,1,0:T(2,128)}, f32[2,128,32]{1,2,0:T(8,128)}, f32[2,32]{1,0:T(2,128)}, f32[2,384]{1,0:T(2,128)}, f32[2,128]{1,0:T(2,128)}, /*in...) all-reduce(f32[2,2,128]{2,1,0:T(2,128)S(1)} %pad_maximum_fusion.7, ...), channel_id=1, replica_groups=mesh['img'=4,'hid'=8] {'img','hid'}, use_global_device_ids=true, to_apply=%region_39.40 | all-reduce | flops 11392 | bytes 91136 | tf_op jit(solution)/shard_map/psum | solution.py:275
  799.9 91.9 %all-reduce.30.cloned.1.call-done = (f32[2,3,128,128]{3,2,1,0:T(8,128)}, f32[2,32,384]{2,1,0:T(8,128)}, f32[2,128,128]{2,1,0:T(8,128)}, f32[1152,320]{0,1:T(8,128)}) async-done(((f32[2,3,128,128]{3,2,1,0:T(8,128)}, f32[2,32,384]{2,1,0:T(8,128)}, f32[2,128,128]{2,1,0:T(8,128)}, f32[1152,320]{0,1:T(8,128)}), (f32[2,3,128,128]{3,2,1,0:T(8,128)}, f32[2,32,384]{2,1,0:T(8,128)}, f32[2,128,128]{2,1,0:T(8,128)}, ...) | async-done | bytes 2097168 | tf_op jit(solution)/shard_map/psum | solution.py:275
  (601 shorter events, 187.1 us)
Async XLA Ops:
  7.2 208.1 %all-gather.5.cloned.1.call-start = ((), (), s32[]{:S(2)}) async-start(), calls=%async_computation.4 | async-start | bytes 5971968 | tf_op jit(solution)/shard_map/all_gather | solution.py:174
  7.3 145.1 %copy-start.143 = (pred[128]{0:T(512)(128)(4,1)}, pred[128]{0:T(512)(128)(4,1)S(1)}, u32[]{:S(2)}) copy-start(pred[128]{0:T(512)(128)(4,1)S(1)} %get-tuple-element.236) | copy-start | bytes 388
  7.3 145.1 %copy-start.145 = (pred[128]{0:T(512)(128)(4,1)}, pred[128]{0:T(512)(128)(4,1)S(1)}, u32[]{:S(2)}) copy-start(pred[128]{0:T(512)(128)(4,1)S(1)} %get-tuple-element.237) | copy-start | bytes 388
  9.3 154.1 %copy-start.158 = (f32[2]{0:T(128)}, f32[2]{0:T(128)S(1)}, u32[]{:S(2)}) copy-start(f32[2]{0:T(128)S(1)} %convert_reduce_fusion.11) | copy-start | bytes 28
  11.4 139.5 %copy-start.68 = (f32[2,36,36]{2,1,0:T(8,128)}, f32[2,36,36]{2,1,0:T(8,128)S(1)}, u32[]{:S(2)}) copy-start(f32[2,36,36]{2,1,0:T(8,128)S(1)} %broadcast_multiply_fusion.3) | copy-start | bytes 31108
  14.4 136.6 %copy-start.75 = (f32[2,36,36]{2,1,0:T(8,128)}, f32[2,36,36]{2,1,0:T(8,128)S(1)}, u32[]{:S(2)}) copy-start(f32[2,36,36]{2,1,0:T(8,128)S(1)} %fusion.65) | copy-start | bytes 31108
  125.2 24.1 %copy-start.153 = (f32[2,32]{1,0:T(2,128)S(1)}, f32[2,32]{1,0:T(2,128)}, u32[]{:S(2)}) copy-start(f32[2,32]{1,0:T(2,128)} %param.25) | copy-start | bytes 772
  125.2 24.6 %copy-start.123 = (f32[2,384]{1,0:T(2,128)S(1)}, f32[2,384]{1,0:T(2,128)}, u32[]{:S(2)}) copy-start(f32[2,384]{1,0:T(2,128)} %param.27) | copy-start | bytes 9220
  125.2 25.2 %copy-start.136 = (f32[2,2,128]{2,1,0:T(2,128)S(1)}, f32[2,2,128]{2,1,0:T(2,128)}, u32[]{:S(2)}) copy-start(f32[2,2,128]{2,1,0:T(2,128)} %param.31) | copy-start | bytes 6148
  125.2 25.2 %copy-start.137 = (f32[2,2,128]{2,1,0:T(2,128)S(1)}, f32[2,2,128]{2,1,0:T(2,128)}, u32[]{:S(2)}) copy-start(f32[2,2,128]{2,1,0:T(2,128)} %param.30) | copy-start | bytes 6148
  125.2 25.8 %copy-start.12 = (bf16[2,36,36,128]{3,0,2,1:T(2,128)(2,1)S(1)}, bf16[2,36,36,128]{3,0,2,1:T(2,128)(2,1)}, u32[]{:S(2)}) copy-start(bf16[2,36,36,128]{3,0,2,1:T(2,128)(2,1)} %param.19) | copy-start | bytes 1990660
  150.9 18.0 %copy-start.109 = (f32[128]{0:T(128)}, f32[128]{0:T(128)S(1)}, u32[]{:S(2)}) copy-start(f32[128]{0:T(128)S(1)} %get-tuple-element.234) | copy-start | bytes 1540
  150.9 148.1 %copy-start.111 = (f32[128]{0:T(128)}, f32[128]{0:T(128)S(1)}, u32[]{:S(2)}) copy-start(f32[128]{0:T(128)S(1)} %get-tuple-element.232) | copy-start | bytes 1540
  154.7 10.1 %copy-start.4 = (f32[2,36,36,128]{3,2,1,0:T(8,128)}, f32[2,36,36,128]{3,2,1,0:T(8,128)S(1)}, u32[]{:S(2)}) copy-start(f32[2,36,36,128]{3,2,1,0:T(8,128)S(1)} %convolution_add_fusion.4) | copy-start | bytes 3981316
  170.1 45.3 %copy-start.96 = (bf16[2,128,64]{1,2,0:T(8,128)(2,1)S(1)}, bf16[2,128,64]{1,2,0:T(8,128)(2,1)}, u32[]{:S(2)}) copy-start(bf16[2,128,64]{1,2,0:T(8,128)(2,1)} %param.32) | copy-start | bytes 98308
  171.1 121.9 %reduce-scatter.5.cloned.1.call-start = ((), (), s32[]{:S(2)}) async-start(), calls=%async_computation.5 | async-start | bytes 5971968 | tf_op jit(solution)/shard_map/reduce_scatter | solution.py:181
  215.3 17.2 %copy-start.94 = (bf16[2,64,128]{2,1,0:T(8,128)(2,1)S(1)}, bf16[2,64,128]{2,1,0:T(8,128)(2,1)}, u32[]{:S(2)}) copy-start(bf16[2,64,128]{2,1,0:T(8,128)(2,1)} %param.34) | copy-start | bytes 98308
  235.9 120.4 %all-gather.7.cloned.1.call-start = ((), (), s32[]{:S(2)}) async-start(), calls=%async_computation.6 | async-start | bytes 5971968 | tf_op jit(solution)/shard_map/all_gather | solution.py:174
  314.8 41.6 %copy-start.97 = (bf16[2,128,64]{1,2,0:T(8,128)(2,1)S(1)}, bf16[2,128,64]{1,2,0:T(8,128)(2,1)}, u32[]{:S(2)}) copy-start(bf16[2,128,64]{1,2,0:T(8,128)(2,1)} %param.32) | copy-start | bytes 98308
  314.8 41.6 %copy-start.167 = (f32[64]{0:T(128)S(1)}, f32[64]{0:T(128)}, u32[]{:S(2)}) copy-start(f32[64]{0:T(128)} %get-tuple-element.203) | copy-start | bytes 772
  314.8 85.4 %all-gather.9.cloned.1.call-start = ((), (), s32[]{:S(2)}) async-start(), calls=%async_computation.8 | async-start | bytes 5971968 | tf_op jit(solution)/shard_map/all_gather | solution.py:131
  315.9 155.0 %reduce-scatter.9.cloned.1.call-start = ((), (), s32[]{:S(2)}) async-start(), calls=%async_computation.9 | async-start | bytes 5971968 | tf_op jit(solution)/shard_map/reduce_scatter | solution.py:139
  413.8 117.3 %reduce-scatter.7.cloned.1.call-start = ((), (), s32[]{:S(2)}) async-start(), calls=%async_computation.7 | async-start | bytes 5971968 | tf_op jit(solution)/shard_map/reduce_scatter | solution.py:181
  419.6 186.0 %all-gather.11.cloned.1.call-start = ((), (), s32[]{:S(2)}) async-start(), calls=%async_computation.10 | async-start | bytes 5971968 | tf_op jit(solution)/shard_map/all_gather | solution.py:131
  564.1 157.4 %all-reduce.32.cloned.1.call-start = ((), (), s32[]{:S(2)}) async-start(), calls=%async_computation.13 | async-start | bytes 132096 | tf_op jit(solution)/shard_map/psum | solution.py:271
  568.9 36.7 %copy-start.15 = (bf16[20736,64]{0,1:T(8,128)(2,1)S(1)}, bf16[20736,64]{0,1:T(8,128)(2,1)}, u32[]{:S(2)}) copy-start(bf16[20736,64]{0,1:T(8,128)(2,1)} %copy-done.14) | copy-start | bytes 7962628
  573.0 37.0 %copy-start.95 = (bf16[2,64,128]{2,1,0:T(8,128)(2,1)S(1)}, bf16[2,64,128]{2,1,0:T(8,128)(2,1)}, u32[]{:S(2)}) copy-start(bf16[2,64,128]{2,1,0:T(8,128)(2,1)} %param.34) | copy-start | bytes 98308
  605.6 13.2 %slice-start = ((s8[5308416]{0:T(1024)(128)(4,1)}), s8[4194304]{0:T(1024)(128)(4,1)S(1)}, s32[]{:S(2)}) async-start(s8[5308416]{0:T(1024)(128)(4,1)} %bitcast.362), calls=%async_computation.14 | async-start | bytes 8388608
  610.0 8.8 slice-start.1
  620.5 105.1 %reduce-scatter.11.cloned.1.call-start = ((), (), s32[]{:S(2)}) async-start(), calls=%async_computation.11 | async-start | bytes 5971968 | tf_op jit(solution)/shard_map/reduce_scatter | solution.py:139
  624.0 267.7 %all-reduce.30.cloned.1.call-start = ((), (), s32[]{:S(2)}) async-start(), calls=%async_computation.12 | async-start | bytes 4194304 | tf_op jit(solution)/shard_map/psum | solution.py:275
  649.2 47.1 %copy-start.87 = (f32[128,3]{1,0:T(8,128)S(1)}, f32[128,3]{1,0:T(8,128)}, u32[]{:S(2)}) copy-start(f32[128,3]{1,0:T(8,128)} %get-tuple-element.146) | copy-start | bytes 4612
  (172 other events, 477.5 us)
Sparse Core Ops, SparseCore 0:
  171.2 44.0 all-gather.4
  236.0 56.9 reduce-scatter.4
  314.9 41.3 all-gather.6
  358.8 41.3 all-gather.8
  413.9 56.9 reduce-scatter.8
  474.1 56.8 reduce-scatter.6
  564.2 41.3 all-gather.10
  620.6 34.1 all-reduce.31
  658.3 56.9 reduce-scatter.10
  756.2 135.4 all-reduce.29
where the time goes:
time: 922 us; the launch traced here: 907 us
  waiting for transfers between devices  397 us (43%)
  local copies, waits for them, and re-layouts  263 us (29%)
  matrix products  110 us (12%)
  other arithmetic  76.5 us (8%)
  blocking collectives  40.8 us (4%)
  between operations  17.2 us (2%)
    reduce_scatter x2, waiting for transfers between devices, per_device(): lax.psum_scatter(jnp.dot(mlp_hidden, outer_used[layer_at], preferred_elem...  111 us
    psum x1, waiting for transfers between devices, per_device(): lax.psum((stacked[0], stacked[1], stacked[2], stacked[3], stacked[4], sta...  91.9 us
    unnamed x406, local copies, waits for them, and re-layouts  87.4 us
    all_gather x2, waiting for transfers between devices, per_device(): lax.all_gather(normed2.reshape(local_rows, channels), 'hid', axis=0, tile...  83.5 us
    slice x9, local copies, waits for them, and re-layouts, patches(): padded[:, row_off:row_off + side_len:2, col_off:col_off + side_len:2, :]  69 us
    all_gather x2, waiting for transfers between devices, mlp_backward(): grad_in = lax.all_gather(out_grad, 'hid', axis=0, tiled=True)  60.6 us
    pad x3, local copies, waits for them, and re-layouts, patches(): padded[:, row_off:row_off + side_len:2, col_off:col_off + side_len:2, :]  52.8 us
    reduce_scatter x2, waiting for transfers between devices, mlp_backward(): lax.psum_scatter(matmul_back(pre_grad, inner_used[layer_at]).astype(jnp.b...  49.9 us
  transfers between devices with their start and end apart: 10, of which 8 were waited for; matrix products, arithmetic and copies ran while one was open for 16% of the time, Pallas kernels for 0%

commit v1 on v0

v1 whole, which is shorter than its diff:
```python
from functools import partial

import jax
import jax.numpy as jnp
from jax import lax
from jax.experimental import pallas as pl
from jax.experimental.pallas import tpu as pltpu
from jax.sharding import PartitionSpec as P

F32 = jnp.float32
BF16 = jnp.bfloat16
PRECISE = lax.Precision.HIGHEST
GROUP = 8


def dot(a, b, dims=(1, 0), precision=None):
    return lax.dot_general(
        a, b, (((dims[0],), (dims[1],)), ((), ())), precision=precision, preferred_element_type=F32
    )


def fine(a, b, dims=(1, 0)):
    return dot(a, b, dims, PRECISE)


def rows8(v):
    return v.reshape(-1, 8, v.shape[-1]).sum(axis=0)


def gelu_pair(x):
    d = 1.0 + jnp.abs(x) * (0.3275911 * 0.7071067811865476)
    t = pl.reciprocal(d, approx=True)
    t = t * (2.0 - d * t)
    bell = jnp.exp(x * x * -0.5)
    poly = 0.5 * 1.061405429
    for coef in (-1.453152027, 1.421413741, -0.284496736, 0.254829592):
        poly = poly * t + 0.5 * coef
    tail = poly * t * bell
    cdf = jnp.where(x >= 0.0, 1.0 - tail, tail)
    return x * cdf, cdf + x * bell * 0.3989422804014327


def norm_parts(v):
    mean = jnp.mean(v, axis=-1, keepdims=True)
    centred = v - mean
    rstd = lax.rsqrt(jnp.mean(centred * centred, axis=-1, keepdims=True) + 1e-05)
    return centred * rstd, rstd


def norm_back(grad, unit, rstd, gain):
    scaled = grad * gain
    first = jnp.mean(scaled, axis=-1, keepdims=True)
    second = jnp.mean(scaled * unit, axis=-1, keepdims=True)
    return rstd * (scaled - first - unit * second)


class Sizes:
    def __init__(self, images, side, channels, hidden, red, out, layers):
        self.I, self.side, self.C, self.H, self.R, self.O, self.L = images, side, channels, hidden, red, out, layers
        self.pitch = -(-(side + 1) // 8) * 8
        self.N = side * self.pitch
        self.per = 6 if side % 6 == 0 else 2
        self.CH = self.per * self.pitch
        self.chunks = side // self.per
        self.half = side // 2
        self.hp = -(-self.half // 8) * 8
        self.base = 8 + self.pitch
        self.tall = 8 + self.pitch * (2 * self.hp + 2)


def pick(z, low, mid, high):
    kind = lax.broadcasted_iota(jnp.int32, (8, z.C), 1) % 3
    kind = jnp.broadcast_to(kind[None], (mid.shape[0] // 8, 8, z.C)).reshape(mid.shape)
    return jnp.where(kind == 2, low, jnp.where(kind == 0, mid, high))


def over(z, body):
    def step(c, carry):
        body(pl.multiple_of(c * z.CH, 16), c)
        return carry
    lax.fori_loop(0, z.chunks, step, 0)


def setup_phase(z, r):
    r.nrm[...] = jnp.zeros_like(r.nrm)
    r.sg[...] = jnp.zeros_like(r.sg)
    r.gw[...] = jnp.zeros_like(r.gw)
    cols = lax.broadcasted_iota(jnp.int32, (z.per, z.pitch, z.C), 1)
    r.colmask[...] = jnp.where(cols < z.side, 1.0, 0.0).reshape(z.CH, z.C)
    for i in range(z.I):
        high, wide = r.sizes[i, 0], r.sizes[i, 1]
        r.state[i, :, 32:, :] = jnp.zeros((z.side, z.pitch - 32, z.C), F32)

        def body(at, c, i=i, high=high, wide=wide):
            cols = lax.broadcasted_iota(jnp.int32, (z.per, z.pitch, z.C), 1)
            rows = lax.broadcasted_iota(jnp.int32, (z.per, z.pitch, z.C), 0) + c * z.per
            mask = jnp.where((cols < wide) & (rows < high), 1.0, 0.0)
            r.mask[i, pl.ds(at, z.CH), :] = mask.reshape(z.CH, z.C)
            take = r.images[i, pl.ds(c * z.per, z.per)].astype(F32)
            r.state[i, pl.ds(c * z.per, z.per), : z.side, :] = take * mask[:, : z.side]

        over(z, body)
    spots = lax.broadcasted_iota(jnp.int32, (3 * z.C, 3 * z.C), 0)
    ends = lax.broadcasted_iota(jnp.int32, (3 * z.C, 3 * z.C), 1)
    kind = ends // z.C
    r.perm[...] = jnp.where(spots == 3 * (ends - kind * z.C) + kind, 1.0, 0.0)
    for l in range(z.L):
        r.ewp[l] = fine(r.expand_weight[l], r.perm[...])
    r.ebp[...] = fine(r.expand_bias[...], r.perm[...])


def counts_of(z, r):
    rows = []
    for i in range(GROUP):
        if i < z.I:
            count = (r.sizes[i, 0] * r.sizes[i, 1]).astype(F32)
            rows.append(jnp.full((1, z.C), 1.0, F32) * count)
        else:
            rows.append(jnp.ones((1, z.C), F32))
    return jnp.concatenate(rows, axis=0)


def state_chunk(z, r, i, c):
    return r.state[i, pl.ds(c * z.per, z.per)].reshape(z.CH, z.C)


def norm_phase(z, r, l, i):
    gain, bias = r.norm_gain[l, 0:1], r.norm_bias[l, 0:1]

    def body(at, c):
        unit, rstd = norm_parts(state_chunk(z, r, i, c))
        r.xh1[l, i, pl.ds(at, z.CH), :] = unit
        r.rs1[l, i, pl.ds(at, z.CH), :] = jnp.broadcast_to(rstd, unit.shape)
        normed = (unit * gain + bias) * r.colmask[...]
        r.nrm[i, pl.ds(z.base + at, z.CH), :] = normed

    over(z, body)


def shift_phase(z, r, l, i):
    r.sums[...] = jnp.zeros_like(r.sums)

    def body(at, c):
        def view(off):
            return r.nrm[i, pl.ds(z.base + at + off, z.CH), :]
        mid = view(0)
        high = pick(z, view(-z.pitch), mid, view(z.pitch)).astype(BF16)
        wide = pick(z, view(-1), mid, view(1)).astype(BF16)
        mid = mid.astype(BF16)
        mask = r.mask[i, pl.ds(at, z.CH), :]
        for j, part in enumerate((high, wide, mid)):
            r.cat[l, i, pl.ds(at, z.CH), j * z.C : (j + 1) * z.C] = part
            r.sums[j] += rows8(part.astype(F32) * mask)

    over(z, body)
    for j in range(3):
        r.pool[l, j, i : i + 1] = r.sums[j].sum(axis=0, keepdims=True)


def weigh_phase(z, r, l):
    counts = counts_of(z, r)
    total = fine(r.pool[l, 0], r.mix_weight[l, 0].astype(F32))
    for j in (1, 2):
        total += fine(r.pool[l, j], r.mix_weight[l, j].astype(F32))
    pooled = total / counts + r.mix_bias[l, 0:1] + r.mix_bias[l, 1:2]
    r.pooled[l] = pooled
    act, slope = gelu_pair(fine(pooled, r.squeeze_weight[l]) + r.squeeze_bias[l : l + 1])
    r.act[l] = act
    r.slope[l] = slope
    logits = fine(act, r.ewp[l]) + r.ebp[l : l + 1]
    parts = [logits[:, j * z.C : (j + 1) * z.C] for j in range(3)]
    top = jnp.maximum(jnp.maximum(parts[0], parts[1]), parts[2])
    parts = [jnp.exp(part - top) for part in parts]
    whole = parts[0] + parts[1] + parts[2]
    for j in range(3):
        r.share[l, j] = parts[j] / whole
    for i in range(z.I):
        for j in range(3):
            scaled = r.mix_weight[l, j].astype(F32) * r.share[l, j, i : i + 1]
            r.wp[l, i, j * z.C : (j + 1) * z.C, :] = scaled.astype(BF16)


def mix_phase(z, r, l, i):
    bias = r.mix_bias[l, 0:1] * r.share[l, 0, i : i + 1] + r.mix_bias[l, 1:2] * r.share[l, 1, i : i + 1]
    gain2, bias2 = r.norm_gain[l, 1:2], r.norm_bias[l, 1:2]

    def body(at, c):
        rows = pl.ds(at, z.CH)
        mixed = (dot(r.cat[l, i, rows, :], r.wp[l, i]) + bias).astype(BF16)
        r.mixed[l, i, rows, :] = mixed
        token = dot(mixed, r.project_weight[l]) + r.project_bias[l : l + 1]
        halfway = state_chunk(z, r, i, c) + r.mask[i, rows, :] * token
        unit, rstd = norm_parts(halfway)
        r.xh2[l, i, rows, :] = unit
        r.rs2[l, i, rows, :] = jnp.broadcast_to(rstd, unit.shape)
        r.n2[l, i, rows, :] = (unit * gain2 + bias2).astype(BF16)
        r.state[i, pl.ds(c * z.per, z.per)] = halfway.reshape(z.per, z.pitch, z.C)

    over(z, body)


def feed_phase(z, r, l, i):
    def body(at, c):
        rows = pl.ds(at, z.CH)
        pre = dot(r.n2[l, i, rows, :], r.inner_weight[l]) + r.inner_bias[l : l + 1].astype(F32)
        act, slope = gelu_pair(pre)
        act = act.astype(BF16)
        r.hid[l, i, rows, :] = act
        r.gp[l, i, rows, :] = slope.astype(BF16)
        out = dot(act, r.outer_weight[l]) + r.outer_bias[l : l + 1]
        after = state_chunk(z, r, i, c) + r.mask[i, rows, :] * out
        r.state[i, pl.ds(c * z.per, z.per)] = after.reshape(z.per, z.pitch, z.C)

    over(z, body)


def merge_forward(z, r, i):
    def body(at, c):
        low = state_chunk(z, r, i, c)
        r.nrm[i, pl.ds(z.base + at, z.CH), :] = low

    over(z, body)
    for pair in range(z.half // 2):
        for k in range(9):
            dr, ds = divmod(k, 3)
            two = [
                r.nrm[i, pl.ds(8 + dr * z.pitch + 2 * b + ds - 1, z.hp, stride=2 * z.pitch), :]
                for b in (2 * pair, 2 * pair + 1)
            ]
            r.patch[i, 2 * pair * z.hp : (2 * pair + 2) * z.hp, k * z.C : (k + 1) * z.C] = jnp.concatenate(
                two, axis=0
            ).astype(BF16)
    for pair in range(z.half // 2):
        rows = slice(2 * pair * z.hp, (2 * pair + 2) * z.hp)
        merged = dot(r.patch[i, rows, :], r.merge_weight[...]) + r.merge_bias[...]
        wide = jnp.concatenate([merged[: z.half], merged[z.hp : z.hp + z.half]], axis=1)
        r.features[i, :, 2 * pair * z.O : (2 * pair + 2) * z.O] = wide.astype(BF16)


def merge_backward(z, r, i):
    pad = jnp.zeros((z.hp - z.half, z.O), F32)
    for pair in range(z.half // 2):
        wide = r.cotangent[i, :, 2 * pair * z.O : (2 * pair + 2) * z.O].astype(F32)
        both = jnp.concatenate([wide[:, : z.O], pad, wide[:, z.O :], pad], axis=0)
        r.cot[i, 2 * pair * z.hp : (2 * pair + 2) * z.hp, :] = both.astype(BF16)
        r.gmb[...] += rows8(both)
    for pair in range(z.half // 2):
        rows = slice(2 * pair * z.hp, (2 * pair + 2) * z.hp)
        r.pgrad[rows, :] = dot(r.cot[i, rows, :], r.merge_weight[...], (1, 1))

    def part(dr, ds, b, down=0):
        k = 3 * dr + ds
        return r.pgrad[pl.ds(b * z.hp + down, z.hp), k * z.C : (k + 1) * z.C]

    for b in range(z.half):
        last = b == z.half - 1
        planes = [
            part(1, 1, b),
            part(2, 1, b) + part(0, 1, b, 1),
            part(1, 2, b),
            part(2, 2, b) + part(0, 2, b, 1),
        ]
        if not last:
            planes[2] += part(1, 0, b + 1)
            planes[3] += part(2, 0, b + 1) + part(0, 0, b + 1, 1)
        for plane, start in zip(planes, (2 * b, z.pitch + 2 * b, 2 * b + 1, z.pitch + 2 * b + 1)):
            r.sg[i, pl.ds(start, z.hp, stride=2 * z.pitch), :] = plane


def merge_weights(z, r):
    total = dot(r.patch[0], r.cot[0], (0, 0))
    for i in range(1, z.I):
        total += dot(r.patch[i], r.cot[i], (0, 0))
    r.gmw[...] = total


def feed_back(z, r, l, i):
    gain2 = r.norm_gain[l, 1:2]

    def body(at, c):
        rows = pl.ds(at, z.CH)
        mask = r.mask[i, rows, :]
        grad = r.sg[i, rows, :]
        cg = (grad * mask).astype(BF16)
        r.vec[0] += rows8(cg.astype(F32))
        slope = r.gp[l, i, rows, :]
        pg = (dot(cg, r.outer_weight[l], (1, 1)) * slope.astype(F32)).astype(BF16)
        r.gib[...] += rows8(pg.astype(F32))
        r.gwo[...] += dot(cg, r.hid[l, i, rows, :], (0, 0))
        r.gwi[...] += dot(r.n2[l, i, rows, :], pg, (0, 0))
        ng = dot(pg, r.inner_weight[l], (1, 1))
        unit = r.xh2[l, i, rows, :]
        r.vec[1] += rows8(ng * unit)
        r.vec[2] += rows8(ng)
        grad = grad + norm_back(ng, unit, r.rs2[l, i, rows, :], gain2)
        r.sg[i, rows, :] = grad
        tg = (grad * mask).astype(BF16)
        r.vec[3] += rows8(tg.astype(F32))
        r.gpw[...] += dot(r.mixed[l, i, rows, :], tg, (0, 0))
        mg = dot(tg, r.project_weight[l], (1, 1)).astype(BF16)
        r.mg[i, rows, :] = mg
        r.smg[i] += rows8(mg.astype(F32))
        r.gt[i] += dot(mg, r.cat[l, i, rows, :], (0, 0))

    over(z, body)


def clear_layer(z, r):
    for ref in (r.vec, r.gib, r.gwo, r.gwi, r.gpw, r.smg, r.gt):
        ref[...] = jnp.zeros_like(ref)


def weigh_back(z, r, l):
    counts = counts_of(z, r)
    zeros = jnp.zeros((GROUP - z.I, z.C), F32)
    smg = jnp.concatenate([r.smg[i].sum(axis=0, keepdims=True) for i in range(z.I)] + [zeros], axis=0)
    share = [r.share[l, j] for j in range(3)]
    dp = []
    for j in range(3):
        weight = r.mix_weight[l, j].astype(F32)
        rows = []
        for i in range(z.I):
            tile = r.gt[i, :, j * z.C : (j + 1) * z.C].T
            rows.append((weight * tile).sum(axis=0, keepdims=True))
            if i == 0:
                r.g_mix_weight[l, j] = tile * share[j][i : i + 1]
            else:
                r.g_mix_weight[l, j] += tile * share[j][i : i + 1]
        dp.append(jnp.concatenate(rows + [zeros], axis=0))
    for j in range(2):
        dp[j] += smg * r.mix_bias[l, j : j + 1]
    even = dp[0] * share[0] + dp[1] * share[1] + dp[2] * share[2]
    dz = jnp.concatenate([share[j] * (dp[j] - even) for j in range(3)], axis=1)
    act, slope, pooled = r.act[l], r.slope[l], r.pooled[l]
    r.g_expand_weight[l] = fine(fine(act, dz, (0, 0)), r.perm[...], (1, 1))
    r.g_expand_bias[l : l + 1] = fine(dz, r.perm[...], (1, 1)).sum(axis=0, keepdims=True)
    dact = fine(dz, r.ewp[l], (1, 1)) * slope
    r.g_squeeze_weight[l] = fine(pooled, dact, (0, 0))
    r.g_squeeze_bias[l : l + 1] = dact.sum(axis=0, keepdims=True)
    dpool = fine(dact, r.squeeze_weight[l], (1, 1))
    push = dpool / counts
    for j in range(3):
        r.g_mix_weight[l, j] += fine(r.pool[l, j], push, (0, 0))
        r.push[j] = fine(push, r.mix_weight[l, j].astype(F32), (1, 1))
    for j in range(2):
        r.g_mix_bias[l, j : j + 1] = (share[j] * smg + dpool).sum(axis=0, keepdims=True)
    r.g_project_weight[l] = r.gpw[...]
    r.g_project_bias[l : l + 1] = r.vec[3].sum(axis=0, keepdims=True)
    r.g_outer_bias[l : l + 1] = r.vec[0].sum(axis=0, keepdims=True)
    r.g_norm_gain[l, 1:2] = r.vec[1].sum(axis=0, keepdims=True)
    r.g_norm_bias[l, 1:2] = r.vec[2].sum(axis=0, keepdims=True)
    r.g_inner_bias[l : l + 1] = r.gib[...].sum(axis=0, keepdims=True)
    r.g_feed[l, 0] = r.gwi[...].T
    r.g_feed[l, 1] = r.gwo[...].T


def mix_back(z, r, l, i):
    def body(at, c):
        rows = pl.ds(at, z.CH)
        mask = r.mask[i, rows, :]
        parts = dot(r.mg[i, rows, :], r.wp[l, i], (1, 1))
        for j, ref in enumerate((r.nrm, r.gw, r.gc)):
            ref[i, pl.ds(z.base + at, z.CH), :] = (
                parts[:, j * z.C : (j + 1) * z.C] + mask * r.push[j, i : i + 1]
            )

    over(z, body)


def norm_back_phase(z, r, l, i, images_grad=None):
    gain = r.norm_gain[l, 0:1]

    def body(at, c):
        rows = pl.ds(at, z.CH)

        def view(ref, off):
            return ref[i, pl.ds(z.base + at + off, z.CH), :]

        ng = (
            pick(z, view(r.nrm, z.pitch), view(r.nrm, 0), view(r.nrm, -z.pitch))
            + pick(z, view(r.gw, 1), view(r.gw, 0), view(r.gw, -1))
            + view(r.gc, 0)
        )
        unit = r.xh1[l, i, rows, :]
        r.vec[4] += rows8(ng * unit)
        r.vec[5] += rows8(ng * r.colmask[...])
        grad = r.sg[i, rows, :] + norm_back(ng, unit, r.rs1[l, i, rows, :], gain)
        if images_grad is None:
            r.sg[i, rows, :] = grad
        else:
            grad = (grad * r.mask[i, rows, :]).reshape(z.per, z.pitch, z.C)
            images_grad[i, pl.ds(c * z.per, z.per)] = grad[:, : z.side]

    over(z, body)


class Refs:
    pass


ARGS = (
    "images", "sizes", "cotangent", "mix_weight", "mix_bias", "squeeze_weight", "squeeze_bias", "expand_weight",
    "expand_bias", "project_weight", "project_bias", "norm_gain", "norm_bias", "inner_parts", "bias_parts",
    "outer_parts", "outer_bias", "merge_weight", "merge_bias",
)


def outputs_of(z):
    return {
        "features": ((z.I, z.half, z.half * z.O), BF16),
        "images_grad": ((z.I, z.side, z.side, z.C), F32),
        "feed": ((z.parts, 2 * z.L * z.units, z.C), BF16),
        "shared": ((z.total, z.C), BF16),
    }


def layout(z):
    at, where = 0, {}
    for name, rows in (
        ("mix", 3 * z.L * z.C), ("project", z.L * z.C), ("merge", 9 * z.C * 5 // 2), ("squeeze", z.C),
        ("expand", 3 * z.L * z.R), ("small", 64),
    ):
        where[name] = at
        at += rows
    return where, at


SMALL = ("mix_bias", "project_bias", "norm_gain", "norm_bias", "outer_bias", "inner_bias", "expand_bias", "merge_bias", "squeeze_bias")


def pack_phase(z, r):
    where, _ = layout(z)

    def put(at, value):
        r.shared[at : at + value.shape[0], :] = value.astype(BF16)

    for l in range(z.L):
        for j in range(3):
            put(where["mix"] + (3 * l + j) * z.C, r.g_mix_weight[l, j])
            put(where["expand"] + (3 * l + j) * z.R, r.g_expand_weight[l, :, j * z.C : (j + 1) * z.C])
        put(where["project"] + l * z.C, r.g_project_weight[l])
        for k in range(2):
            for h in range(z.parts):
                r.feed[h, (2 * l + k) * z.units : (2 * l + k + 1) * z.units, :] = r.g_feed[l, k, h * z.units : (h + 1) * z.units].astype(BF16)
    wide = 9 * z.C
    put(where["merge"], r.gmw[:, : z.C])
    put(where["merge"] + wide, r.gmw[:, z.C : 2 * z.C])
    put(where["merge"] + 2 * wide, jnp.concatenate([r.gmw[: wide // 2, 2 * z.C :], r.gmw[wide // 2 :, 2 * z.C :]], axis=1))
    put(where["squeeze"], jnp.concatenate([r.g_squeeze_weight[l] for l in range(z.L)] + [jnp.zeros((z.C, z.C - z.L * z.R), F32)], axis=1))
    rows = []
    for l in range(z.L):
        rows += [r.g_mix_bias[l], r.g_project_bias[l : l + 1], r.g_norm_gain[l], r.g_norm_bias[l], r.g_outer_bias[l : l + 1]]
        rows += [r.g_inner_bias[l : l + 1, k * z.C : (k + 1) * z.C] for k in range(z.H // z.C)]
        rows += [r.g_expand_bias[l : l + 1, k * z.C : (k + 1) * z.C] for k in range(3)]
    bias = r.gmb[...].sum(axis=0, keepdims=True)
    rows += [bias[:, : z.C], bias[:, z.C : 2 * z.C]]
    rows += [jnp.concatenate([bias[:, 2 * z.C :], r.g_squeeze_bias[0:1], r.g_squeeze_bias[1:2]], axis=1)]
    rows += [jnp.zeros((64 - sum(row.shape[0] for row in rows), z.C), F32)]
    put(where["small"], jnp.concatenate(rows, axis=0))


def final_outputs(z):
    return {
        "mix_weight": (z.L, 3, z.C, z.C),
        "mix_bias": (z.L, 2, z.C),
        "squeeze_weight": (z.L, z.C, z.R),
        "squeeze_bias": (z.L, z.R),
        "expand_weight": (z.L, z.R, 3 * z.C),
        "expand_bias": (z.L, 3 * z.C),
        "project_weight": (z.L, z.C, z.C),
        "project_bias": (z.L, z.C),
        "norm_gain": (z.L, 2, z.C),
        "norm_bias": (z.L, 2, z.C),
        "inner_weight": (z.L, z.C, z.units),
        "inner_bias": (z.L, z.H),
        "outer_weight": (z.L, z.units, z.C),
        "outer_bias": (z.L, z.C),
        "merge_weight": (9 * z.C, z.O),
        "merge_bias": (1, z.O),
    }


def unpack_kernel(z, shared, feed, *outs):
    where, _ = layout(z)
    o = Refs()
    for name, ref in zip(final_outputs(z), outs):
        setattr(o, name, ref)

    def get(at, rows):
        return shared[at : at + rows, :].astype(F32)

    small = get(where["small"], 64)
    at = 0
    squeeze = get(where["squeeze"], z.C)

    def take(rows):
        nonlocal at
        at += rows
        return small[at - rows : at]

    for l in range(z.L):
        for j in range(3):
            o.mix_weight[l, j] = get(where["mix"] + (3 * l + j) * z.C, z.C)
            o.expand_weight[l, :, j * z.C : (j + 1) * z.C] = get(where["expand"] + (3 * l + j) * z.R, z.R)
        o.project_weight[l] = get(where["project"] + l * z.C, z.C)
        o.squeeze_weight[l] = squeeze[:, l * z.R : (l + 1) * z.R]
        o.inner_weight[l] = feed[2 * l * z.units : (2 * l + 1) * z.units, :].astype(F32).T
        o.outer_weight[l] = feed[(2 * l + 1) * z.units : (2 * l + 2) * z.units, :].astype(F32)
        o.mix_bias[l] = take(2)
        o.project_bias[l : l + 1] = take(1)
        o.norm_gain[l] = take(2)
        o.norm_bias[l] = take(2)
        o.outer_bias[l : l + 1] = take(1)
        for k in range(z.H // z.C):
            o.inner_bias[l : l + 1, k * z.C : (k + 1) * z.C] = take(1)
        for k in range(3):
            o.expand_bias[l : l + 1, k * z.C : (k + 1) * z.C] = take(1)
    wide = 9 * z.C
    o.merge_weight[:, : z.C] = get(where["merge"], wide)
    o.merge_weight[:, z.C : 2 * z.C] = get(where["merge"] + wide, wide)
    pair = get(where["merge"] + 2 * wide, wide // 2)
    o.merge_weight[: wide // 2, 2 * z.C :] = pair[:, : z.O - 2 * z.C]
    o.merge_weight[wide // 2 :, 2 * z.C :] = pair[:, z.O - 2 * z.C :]
    o.merge_bias[:, : z.C] = take(1)
    o.merge_bias[:, z.C : 2 * z.C] = take(1)
    last = take(1)
    o.merge_bias[:, 2 * z.C :] = last[:, : z.O - 2 * z.C]
    for l in range(z.L):
        o.squeeze_bias[l : l + 1] = last[:, z.O - 2 * z.C + l * z.R : z.O - 2 * z.C + (l + 1) * z.R]


def scratch_of(z):
    return {
        "g_mix_weight": ((z.L, 3, z.C, z.C), F32),
        "g_mix_bias": ((z.L, 2, z.C), F32),
        "g_squeeze_weight": ((z.L, z.C, z.R), F32),
        "g_squeeze_bias": ((z.L, z.R), F32),
        "g_expand_weight": ((z.L, z.R, 3 * z.C), F32),
        "g_expand_bias": ((z.L, 3 * z.C), F32),
        "g_project_weight": ((z.L, z.C, z.C), F32),
        "g_project_bias": ((z.L, z.C), F32),
        "g_norm_gain": ((z.L, 2, z.C), F32),
        "g_norm_bias": ((z.L, 2, z.C), F32),
        "g_feed": ((z.L, 2, z.H, z.C), F32),
        "g_inner_bias": ((z.L, z.H), F32),
        "g_outer_bias": ((z.L, z.C), F32),
        "gmw": ((9 * z.C, z.O), F32),
        "gmb": ((8, z.O), F32),
        "inner_weight": ((z.L, z.C, z.H), BF16),
        "inner_bias": ((z.L, z.H), F32),
        "outer_weight": ((z.L, z.H, z.C), BF16),
        "nrm": ((z.I, z.tall, z.C), F32),
        "state": ((z.I, z.side, z.pitch, z.C), F32),
        "mask": ((z.I, z.N, z.C), F32),
        "colmask": ((z.CH, z.C), F32),
        "sg": ((z.I, 2 * z.hp * z.pitch, z.C), F32),
        "xh1": ((z.L, z.I, z.N, z.C), F32),
        "rs1": ((z.L, z.I, z.N, z.C), F32),
        "xh2": ((z.L, z.I, z.N, z.C), F32),
        "rs2": ((z.L, z.I, z.N, z.C), F32),
        "cat": ((z.L, z.I, z.N, 3 * z.C), BF16),
        "mixed": ((z.L, z.I, z.N, z.C), BF16),
        "n2": ((z.L, z.I, z.N, z.C), BF16),
        "hid": ((z.L, z.I, z.N, z.H), BF16),
        "gp": ((z.L, z.I, z.N, z.H), BF16),
        "sums": ((3, 8, z.C), F32),
        "pool": ((z.L, 3, GROUP, z.C), F32),
        "pooled": ((z.L, GROUP, z.C), F32),
        "act": ((z.L, GROUP, z.R), F32),
        "slope": ((z.L, GROUP, z.R), F32),
        "share": ((z.L, 3, GROUP, z.C), F32),
        "wp": ((z.L, z.I, 3 * z.C, z.C), BF16),
        "perm": ((3 * z.C, 3 * z.C), F32),
        "ewp": ((z.L, z.R, 3 * z.C), F32),
        "ebp": ((z.L, 3 * z.C), F32),
        "patch": ((z.I, z.half * z.hp, 9 * z.C), BF16),
        "cot": ((z.I, z.half * z.hp, z.O), BF16),
        "pgrad": ((z.half * z.hp + 8, 9 * z.C), F32),
        "vec": ((6, 8, z.C), F32),
        "gib": ((8, z.H), F32),
        "gwo": ((z.C, z.H), F32),
        "gwi": ((z.C, z.H), F32),
        "gpw": ((z.C, z.C), F32),
        "smg": ((z.I, 8, z.C), F32),
        "gt": ((z.I, z.C, 3 * z.C), F32),
        "mg": ((z.I, z.N, z.C), BF16),
        "push": ((3, GROUP, z.C), F32),
        "gw": ((z.I, z.base + z.N + z.pitch, z.C), F32),
        "gc": ((z.I, z.base + z.N, z.C), F32),
    }


def kernel(z, outs, scratch, *refs):
    r = Refs()
    for name, ref in zip(list(ARGS) + list(outs) + list(scratch), refs):
        setattr(r, name, ref)
    images = range(z.I)
    todo = []
    todo.append(("setup", lambda: setup_phase(z, r)))
    todo.append(("gather", lambda: gather_phase(z, r)))
    for l in range(z.L):
        todo.append((f"norm{l}", lambda l=l: [norm_phase(z, r, l, i) for i in images]))
        todo.append((f"shift{l}", lambda l=l: [shift_phase(z, r, l, i) for i in images]))
        todo.append((f"weigh{l}", lambda l=l: weigh_phase(z, r, l)))
        todo.append((f"mix{l}", lambda l=l: [mix_phase(z, r, l, i) for i in images]))
        todo.append((f"feed{l}", lambda l=l: [feed_phase(z, r, l, i) for i in images]))
    todo.append(("mergef", lambda: [merge_forward(z, r, i) for i in images]))

    def clear():
        r.gmb[...] = jnp.zeros_like(r.gmb)
        r.pgrad[...] = jnp.zeros_like(r.pgrad)
    todo.append(("clear", clear))
    todo.append(("mergeb", lambda: [merge_backward(z, r, i) for i in images]))
    todo.append(("mergew", lambda: merge_weights(z, r)))
    for l in reversed(range(z.L)):
        todo.append((f"clear{l}", lambda l=l: clear_layer(z, r)))
        todo.append((f"feedb{l}", lambda l=l: [feed_back(z, r, l, i) for i in images]))
        todo.append((f"weighb{l}", lambda l=l: weigh_back(z, r, l)))
        todo.append((f"mixb{l}", lambda l=l: [mix_back(z, r, l, i) for i in images]))

        def normb(l=l):
            for i in images:
                norm_back_phase(z, r, l, i, r.images_grad if l == 0 else None)
            r.g_norm_gain[l, 0:1] = r.vec[4].sum(axis=0, keepdims=True)
            r.g_norm_bias[l, 0:1] = r.vec[5].sum(axis=0, keepdims=True)
        todo.append((f"normb{l}", normb))
    todo.append(("pack", lambda: pack_phase(z, r)))
    for name, phase in todo:
        phase()


def gather_phase(z, r):
    for l in range(z.L):
        r.inner_weight[l] = jnp.concatenate([r.inner_parts[h, l] for h in range(z.parts)], axis=1)
        r.inner_bias[l : l + 1] = jnp.concatenate([r.bias_parts[h, l : l + 1].astype(F32) for h in range(z.parts)], axis=1)
        for h in range(z.parts):
            r.outer_weight[l, h * z.units : (h + 1) * z.units, :] = r.outer_parts[h, l]


def run_kernel(args, z):
    outs, scratch = outputs_of(z), scratch_of(z)
    vmem = pl.BlockSpec(memory_space=pltpu.VMEM)
    smem = pl.BlockSpec(memory_space=pltpu.SMEM)
    found = pl.pallas_call(
        partial(kernel, z, outs, scratch),
        out_shape=[jax.ShapeDtypeStruct(s, d) for s, d in outs.values()],
        in_specs=[smem if name == "sizes" else vmem for name in ARGS],
        out_specs=[vmem] * len(outs),
        scratch_shapes=[pltpu.VMEM(s, d) for s, d in scratch.values()],
        compiler_params=pltpu.CompilerParams(vmem_limit_bytes=62 * 2**20),
    )(*args)
    return dict(zip(outs, found))


def run_unpack(shared, feed, z):
    outs = final_outputs(z)
    vmem = pl.BlockSpec(memory_space=pltpu.VMEM)
    found = pl.pallas_call(
        partial(unpack_kernel, z),
        out_shape=[jax.ShapeDtypeStruct(s, F32) for s in outs.values()],
        in_specs=[vmem] * 2,
        out_specs=[vmem] * len(outs),
        compiler_params=pltpu.CompilerParams(vmem_limit_bytes=32 * 2**20),
    )(shared, feed)
    return dict(zip(outs, found))


def scatter_sum(x, axis, n):
    got = lax.all_to_all(x, axis, 0, 0, tiled=True)
    return got.reshape(n, -1, x.shape[-1]).astype(F32).sum(axis=0).astype(BF16)


def share_sum(x, axis, n):
    total = x.astype(F32)
    for step in range(1, n):
        total += lax.ppermute(x, axis, [(a, (a + step) % n) for a in range(n)]).astype(F32)
    return total.astype(BF16)


def per_device(
    img, hid, images, sizes, cotangent, mix_weight, mix_bias, squeeze_weight, squeeze_bias, expand_weight, expand_bias,
    project_weight, project_bias, norm_gain, norm_bias, inner_weight, inner_bias, outer_weight, outer_bias,
    merge_weight, merge_bias,
):
    z = Sizes(
        images.shape[0], images.shape[1], images.shape[3], inner_weight.shape[2] * hid, squeeze_weight.shape[2],
        merge_weight.shape[1], mix_weight.shape[0],
    )
    z.parts, z.units = hid, inner_weight.shape[2]
    step = hid * 16
    z.total = -(-layout(z)[1] // step) * step
    inner_parts, bias_parts, outer_parts = (
        lax.all_gather(part, "hid", axis=0) for part in (inner_weight, inner_bias, outer_weight)
    )
    found = run_kernel(
        (
            images, sizes, cotangent, mix_weight, mix_bias, squeeze_weight, squeeze_bias, expand_weight, expand_bias,
            project_weight, project_bias, norm_gain, norm_bias, inner_parts, bias_parts, outer_parts, outer_bias,
            merge_weight, merge_bias.reshape(1, -1),
        ),
        z,
    )
    feed = share_sum(scatter_sum(found["feed"].reshape(-1, z.C), "hid", hid), "img", img)
    shared = share_sum(scatter_sum(found["shared"], "hid", hid), "img", img)
    shared = lax.all_gather(shared, "hid", axis=0, tiled=True)
    g = run_unpack(shared, feed, z)
    inner_bias_grad = lax.dynamic_slice_in_dim(g["inner_bias"], lax.axis_index("hid") * z.units, z.units, axis=1)
    return (
        found["features"], found["images_grad"], g["mix_weight"], g["mix_bias"], g["squeeze_weight"], g["squeeze_bias"],
        g["expand_weight"], g["expand_bias"], g["project_weight"], g["project_bias"], g["norm_gain"], g["norm_bias"],
        g["inner_weight"], inner_bias_grad, g["outer_weight"], g["outer_bias"], g["merge_weight"],
        g["merge_bias"].reshape(-1),
    )


def solution(mesh):
    maps = ("img", "hid")
    in_specs = (
        P(maps, None, None, None), P(maps, None), P(maps, None, None), P(), P(), P(), P(), P(), P(), P(), P(), P(), P(),
        P(None, None, "hid"), P(None, "hid"), P(None, "hid", None), P(), P(), P(),
    )
    out_specs = (
        P(maps, None, None), P(maps, None, None, None), P(), P(), P(), P(), P(), P(), P(), P(), P(), P(),
        P(None, None, "hid"), P(None, "hid"), P(None, "hid", None), P(), P(), P(),
    )
    return jax.shard_map(
        partial(per_device, mesh.shape["img"], mesh.shape["hid"]),
        mesh=mesh, in_specs=in_specs, out_specs=out_specs, check_vma=False,
    )
```

time: 922 us -> 213 us (0.23); the launches traced: 907 us -> 213 us
  waiting for transfers between devices: 397 us -> 11 us
  local copies, waits for them, and re-layouts: 263 us -> 14.7 us
  matrix products: 110 us -> 0 us
  Pallas kernels: 0 us -> 97 us
  other arithmetic: 76.5 us -> 1.61 us
  blocking collectives: 40.8 us -> 62.3 us
  starting transfers between devices: 1.67 us -> 12.1 us
    reduce_scatter x4 -> x0, waiting for transfers between devices: 161 us -> none  [the longest x2 111 us: per_device(): lax.psum_scatter(jnp.dot(mlp_hidden, outer_used[layer_at], preferred_elem...]
    all_gather x4 -> x1, waiting for transfers between devices: 144 us -> 2.37 us  [per_device(): shared = lax.all_gather(shared, 'hid', axis=0, tiled=True)]
    dot_general x51 -> x0, matrix products: 110 us -> none  [the longest x13 33.8 us: matmul_back(): lax.dot_general(left_op, right_op, (((left_op.ndim - 1,), (1,)), ((), ())...]
    pallas_call x0 -> x2, Pallas kernels: none -> 97 us  [the longest x1 96 us: run_kernel(): pl.pallas_call(partial(kernel, z, outs, scratch), out_shape=[jax.ShapeDty...]
    psum x2 -> x0, waiting for transfers between devices: 91.9 us -> none  [the longest x1 91.9 us: per_device(): lax.psum((stacked[0], stacked[1], stacked[2], stacked[3], stacked[4], sta...]
    pad x6 -> x0, local copies, waits for them, and re-layouts: 77.1 us -> none  [the longest x3 52.8 us: patches(): padded[:, row_off:row_off + side_len:2, col_off:col_off + side_len:2, :]]
    unnamed x406 -> x31, local copies, waits for them, and re-layouts: 87.4 us -> 12.5 us
    slice x13 -> x0, local copies, waits for them, and re-layouts: 71.2 us -> none  [the longest x9 69 us: patches(): padded[:, row_off:row_off + side_len:2, col_off:col_off + side_len:2, :]]
  transfers between devices with their start and end apart: 10 -> 7, of which waited for: 8 -> 5; matrix products, arithmetic and copies ran while one was open for 16% -> 2% of each run, Pallas kernels for 0% -> 0%
where the time goes in v1:
time: 213 us
  Pallas kernels  97 us (46%)
  blocking collectives  62.3 us (29%)
  local copies, waits for them, and re-layouts  14.7 us (7%)
  between operations  14.1 us (7%)
  starting transfers between devices  12.1 us (6%)
  waiting for transfers between devices  11 us (5%)
    pallas_call x1, Pallas kernels, run_kernel(): pl.pallas_call(partial(kernel, z, outs, scratch), out_shape=[jax.ShapeDty...  96 us
    all_to_all x2, blocking collectives, scatter_sum(): got = lax.all_to_all(x, axis, 0, 0, tiled=True)  32.7 us
    all_gather x3, blocking collectives, per_device(): lax.all_gather(part, 'hid', axis=0)  29.6 us
    unnamed x31, local copies, waits for them, and re-layouts  12.5 us
    ppermute x6, starting transfers between devices, share_sum(): lax.ppermute(x, axis, [(a, (a + step) % n) for a in range(n)]).astype(F32)  12 us
    ppermute x6, waiting for transfers between devices, share_sum(): lax.ppermute(x, axis, [(a, (a + step) % n) for a in range(n)]).astype(F32)  8.62 us
  transfers between devices with their start and end apart: 7, of which 5 were waited for; matrix products, arithmetic and copies ran while one was open for 2% of the time, Pallas kernels for 0%

profile of v1, /device:TPU:0, one launch (start us, length us, event | category | flops | bytes accessed | tf_op | source)
XLA Modules:
  0.0 212.8 jit_solution(17629350877875119003)
XLA Ops:
  7.3 2.2 %copy.51.refs_17_ = bf16[1152,320]{1,0:T(8,128)(2,1)} copy(bf16[1152,320]{0,1:T(8,128)(2,1)} %param.36) | data formatting | bytes 1474560 | tf_op args[17]
  9.5 10.9 %all-gather = bf16[16,128,64]{1,2,0:T(8,128)(2,1)S(1)} all-gather(bf16[2,128,64]{1,2,0:T(8,128)(2,1)S(1)} %copy-done.6), channel_id=2, replica_groups=mesh['img'=4,'hid'=8] {'hid'}, dimensions={0}, use_global_device_ids=true | all-gather | bytes 294912 | tf_op jit(solution)/shard_map/all_gather | solution.py:693
  20.4 1.0 copy.47
  21.4 1.0 copy.48.refs_0_
  22.4 0.9 copy.49.refs_2_
  23.3 10.2 %all-gather.2 = bf16[16,64,128]{2,1,0:T(8,128)(2,1)} all-gather(bf16[2,64,128]{2,1,0:T(8,128)(2,1)S(1)} %copy-done.7), channel_id=4, replica_groups=mesh['img'=4,'hid'=8] {'hid'}, dimensions={0}, use_global_device_ids=true | all-gather | bytes 294912 | tf_op jit(solution)/shard_map/all_gather | solution.py:693
  33.5 0.8 copy.50.refs_5_
  34.3 8.5 %all-gather.3.refs_14_ = bf16[8,2,64]{2,1,0:T(2,128)(2,1)} all-gather(bf16[1,2,64]{2,1,0:T(2,128)(2,1)S(1)} %bitcast.7), channel_id=3, replica_groups=mesh['img'=4,'hid'=8] {'hid'}, dimensions={0}, use_global_device_ids=true | all-gather | bytes 2304 | tf_op jit(solution)/shard_map/all_gather | solution.py:693
  42.8 0.6 reshape.52.refs_18_
  43.4 96.0 %shard_map.322 = (bf16[2,18,5760]{2,1,0:T(8,128)(2,1)}, f32[2,36,36,128]{3,2,1,0:T(8,128)}, bf16[8,256,128]{2,1,0:T(8,128)(2,1)}, bf16[4352,128]{1,0:T(8,128)(2,1)}) custom-call(bf16[2,36,36,128]{3,2,1,0:T(8,128)(2,1)} %copy.48.refs_0_, s32[2,2]{1,0:T(2,128)} %refs_1_.1, bf16[2,18,5760]{2,1,0:T(8,128)(2,1)} %copy.49.refs_2_, ...), custom_call_target="tpu_custom_call" | custom-call | tf_op jit(solution)/shard_map/pallas_call | solution.py:644
  139.4 19.5 %all_to_all.15 = bf16[8,544,128]{2,1,0:T(8,128)(2,1)S(1)} all-to-all(bf16[8,544,128]{2,1,0:T(8,128)(2,1)} %bitcast.5), channel_id=1, replica_groups=mesh['img'=4,'hid'=8] {'hid'}, dimensions={0} | all-to-all | bytes 2228224 | tf_op jit(solution)/shard_map/all_to_all | solution.py:669
  159.1 1.6 collective-permute-start
  160.7 2.6 %collective-permute-start.1 = (bf16[544,128]{1,0:T(8,128)(2,1)S(1)}, bf16[544,128]{1,0:T(8,128)(2,1)S(1)}, u32[]{:S(2)}, u32[]{:S(2)}) collective-permute-start(bf16[544,128]{1,0:T(8,128)(2,1)S(1)} %reduce_sum.24), channel_id=1, source_target_pairs={{0,16},{8,24},{16,0},{24,8},{1,17},{9,25},{17,1},{25,9},{2,18},{10... | collective-permute-start | bytes 417800 | tf_op jit(solution)/shard_map/ppermute | solution.py:676
  163.3 1.3 collective-permute-start.2
  164.7 2.9 %collective-permute-done = bf16[544,128]{1,0:T(8,128)(2,1)S(1)} collective-permute-done((bf16[544,128]{1,0:T(8,128)(2,1)S(1)}, bf16[544,128]{1,0:T(8,128)(2,1)S(1)}, u32[]{:S(2)}, u32[]{:S(2)}) %collective-permute-start) | collective-permute-done | bytes 139296 | tf_op jit(solution)/shard_map/ppermute | solution.py:676
  167.6 4.8 %collective-permute-done.1 = bf16[544,128]{1,0:T(8,128)(2,1)S(1)} collective-permute-done((bf16[544,128]{1,0:T(8,128)(2,1)S(1)}, bf16[544,128]{1,0:T(8,128)(2,1)S(1)}, u32[]{:S(2)}, u32[]{:S(2)}) %collective-permute-start.1) | collective-permute-done | bytes 139296 | tf_op jit(solution)/shard_map/ppermute | solution.py:676
  172.4 0.7 add_convert_fusion
  173.2 13.1 %all_to_all.16 = bf16[8,256,128]{2,1,0:T(8,128)(2,1)S(1)} all-to-all(bf16[8,256,128]{2,1,0:T(8,128)(2,1)S(1)} %copy-done.4), channel_id=1, replica_groups=mesh['img'=4,'hid'=8] {'hid'}, dimensions={0} | all-to-all | bytes 1048576 | tf_op jit(solution)/shard_map/all_to_all | solution.py:669
  186.4 4.0 %collective-permute-start.3 = (bf16[256,128]{1,0:T(8,128)(2,1)S(1)}, bf16[256,128]{1,0:T(8,128)(2,1)S(1)}, u32[]{:S(2)}, u32[]{:S(2)}) collective-permute-start(bf16[256,128]{1,0:T(8,128)(2,1)S(1)} %reduce_sum.25), channel_id=1, source_target_pairs={{0,8},{8,16},{16,24},{24,0},{1,9},{9,17},{17,25},{25,1},{2,10},{10... | collective-permute-start | bytes 196616 | tf_op jit(solution)/shard_map/ppermute | solution.py:676
  190.4 1.6 collective-permute-start.4
  192.1 0.8 collective-permute-start.5
  192.9 2.1 copy.53
  195.0 1.1 copy.52
  196.0 0.7 collective-permute-done.4
  196.9 2.4 %all-gather.6.cloned.1.call-done.shared = bf16[4352,128]{1,0:T(8,128)(2,1)} async-done(((bf16[544,128]{1,0:T(8,128)(2,1)}), bf16[4352,128]{1,0:T(8,128)(2,1)}) %all-gather.6.cloned.1.call-update) | async-done | bytes 1114128 | tf_op jit(solution)/shard_map/all_gather | solution.py:705
  199.3 1.2 copy-done
  200.6 0.9 shard_map.323
  201.5 1.8 copy.56
  203.3 0.7 copy.55
  204.0 0.7 copy.54
  204.7 0.6 constant_dynamic-slice_fusion
  205.3 0.6 reduce.4
  (29 shorter events, 0.5 us)
Async XLA Ops:
  7.2 2.3 %copy-start.6 = (bf16[2,128,64]{1,2,0:T(8,128)(2,1)S(1)}, bf16[2,128,64]{1,2,0:T(8,128)(2,1)}, u32[]{:S(2)}) copy-start(bf16[2,128,64]{1,2,0:T(8,128)(2,1)} %param.32) | copy-start | bytes 98308
  7.2 14.2 %copy-start.2 = (bf16[2,36,36,128]{3,0,2,1:T(2,128)(2,1)S(1)}, bf16[2,36,36,128]{3,0,2,1:T(2,128)(2,1)}, u32[]{:S(2)}) copy-start(bf16[2,36,36,128]{3,0,2,1:T(2,128)(2,1)} %param.19) | copy-start | bytes 1990660
  7.2 192.1 %all-gather.6.cloned.1.call-start = ((), (), s32[]{:S(2)}) async-start(), calls=%async_computation.2 | async-start | bytes 1253376 | tf_op jit(solution)/shard_map/all_gather | solution.py:705
  9.5 12.9 %copy-start.5 = (bf16[2,18,5760]{2,0,1:T(2,128)(2,1)S(1)}, bf16[2,18,5760]{2,0,1:T(2,128)(2,1)}, u32[]{:S(2)}) copy-start(bf16[2,18,5760]{2,0,1:T(2,128)(2,1)} %param.21) | copy-start | bytes 1244164
  21.4 1.9 copy-start.7
  21.4 12.1 %copy-start.8 = (f32[2,128,32]{1,2,0:T(8,128)S(1)}, f32[2,128,32]{1,2,0:T(8,128)}, u32[]{:S(2)}) copy-start(f32[2,128,32]{1,2,0:T(8,128)} %param.24) | copy-start | bytes 98308
  21.4 12.9 %copy-start.10 = (bf16[2,64]{1,0:T(2,128)(2,1)S(1)}, bf16[2,64]{1,0:T(2,128)(2,1)}, u32[]{:S(2)}) copy-start(bf16[2,64]{1,0:T(2,128)(2,1)} %param.33) | copy-start | bytes 772
  21.4 21.4 %copy-start.9 = (f32[320]{0:T(512)S(1)}, f32[320]{0:T(512)}, u32[]{:S(2)}) copy-start(f32[320]{0:T(512)} %param.37) | copy-start | bytes 3844
  158.9 14.3 %copy-start.4 = (bf16[8,256,128]{2,1,0:T(8,128)(2,1)S(1)}, bf16[8,256,128]{2,1,0:T(8,128)(2,1)}, u32[]{:S(2)}) copy-start(bf16[8,256,128]{2,1,0:T(8,128)(2,1)} %get-tuple-element.41) | copy-start | bytes 1572868
  159.1 33.8 %copy-start.1 = (f32[2,36,36,128]{3,2,1,0:T(8,128)S(1)}, f32[2,36,36,128]{3,2,1,0:T(8,128)}, u32[]{:S(2)}) copy-start(f32[2,36,36,128]{3,2,1,0:T(8,128)} %get-tuple-element.77) | copy-start | bytes 3981316
  159.1 8.5 %collective-permute-start = (bf16[544,128]{1,0:T(8,128)(2,1)S(1)}, bf16[544,128]{1,0:T(8,128)(2,1)S(1)}, u32[]{:S(2)}, u32[]{:S(2)}) collective-permute-start(bf16[544,128]{1,0:T(8,128)(2,1)S(1)} %reduce_sum.24), channel_id=1, source_target_pairs={{0,8},{8,16},{16,24},{24,0},{1,9},{9,17},{17,25},{25,1},{2,10},{10... | collective-permute-start | bytes 417800 | tf_op jit(solution)/shard_map/ppermute | solution.py:676
  160.7 11.7 %collective-permute-start.1 = (bf16[544,128]{1,0:T(8,128)(2,1)S(1)}, bf16[544,128]{1,0:T(8,128)(2,1)S(1)}, u32[]{:S(2)}, u32[]{:S(2)}) collective-permute-start(bf16[544,128]{1,0:T(8,128)(2,1)S(1)} %reduce_sum.24), channel_id=1, source_target_pairs={{0,16},{8,24},{16,0},{24,8},{1,17},{9,25},{17,1},{25,9},{2,18},{10... | collective-permute-start | bytes 417800 | tf_op jit(solution)/shard_map/ppermute | solution.py:676
  163.3 9.1 %collective-permute-start.2 = (bf16[544,128]{1,0:T(8,128)(2,1)S(1)}, bf16[544,128]{1,0:T(8,128)(2,1)S(1)}, u32[]{:S(2)}, u32[]{:S(2)}) collective-permute-start(bf16[544,128]{1,0:T(8,128)(2,1)S(1)} %reduce_sum.24), channel_id=1, source_target_pairs={{0,24},{8,0},{16,8},{24,16},{1,25},{9,1},{17,9},{25,17},{2,26},{10... | collective-permute-start | bytes 417800 | tf_op jit(solution)/shard_map/ppermute | solution.py:676
  186.4 9.6 %collective-permute-start.3 = (bf16[256,128]{1,0:T(8,128)(2,1)S(1)}, bf16[256,128]{1,0:T(8,128)(2,1)S(1)}, u32[]{:S(2)}, u32[]{:S(2)}) collective-permute-start(bf16[256,128]{1,0:T(8,128)(2,1)S(1)} %reduce_sum.25), channel_id=1, source_target_pairs={{0,8},{8,16},{16,24},{24,0},{1,9},{9,17},{17,25},{25,1},{2,10},{10... | collective-permute-start | bytes 196616 | tf_op jit(solution)/shard_map/ppermute | solution.py:676
  190.4 6.3 %collective-permute-start.4 = (bf16[256,128]{1,0:T(8,128)(2,1)S(1)}, bf16[256,128]{1,0:T(8,128)(2,1)S(1)}, u32[]{:S(2)}, u32[]{:S(2)}) collective-permute-start(bf16[256,128]{1,0:T(8,128)(2,1)S(1)} %reduce_sum.25), channel_id=1, source_target_pairs={{0,16},{8,24},{16,0},{24,8},{1,17},{9,25},{17,1},{25,9},{2,18},{10... | collective-permute-start | bytes 196616 | tf_op jit(solution)/shard_map/ppermute | solution.py:676
  192.1 4.8 %collective-permute-start.5 = (bf16[256,128]{1,0:T(8,128)(2,1)S(1)}, bf16[256,128]{1,0:T(8,128)(2,1)S(1)}, u32[]{:S(2)}, u32[]{:S(2)}) collective-permute-start(bf16[256,128]{1,0:T(8,128)(2,1)S(1)} %reduce_sum.25), channel_id=1, source_target_pairs={{0,24},{8,0},{16,8},{24,16},{1,25},{9,1},{17,9},{25,17},{2,26},{10... | collective-permute-start | bytes 196616 | tf_op jit(solution)/shard_map/ppermute | solution.py:676
  192.9 2.1 copy-start.3
  199.3 1.2 copy-start
Sparse Core Ops, SparseCore 0:
  173.3 25.9 all-gather.5

commit v2 on v0

v2 whole, which is shorter than its diff:
```python
from functools import partial

import jax
import jax.numpy as jnp
from jax import lax
from jax.experimental import pallas as pl
from jax.experimental.pallas import tpu as pltpu
from jax.sharding import PartitionSpec as P

F32 = jnp.float32
BF16 = jnp.bfloat16
PRECISE = lax.Precision.HIGHEST
GROUP = 8
MIB = 2**20


def dot(a, b, dims=(1, 0), precision=None):
    return lax.dot_general(
        a, b, (((dims[0],), (dims[1],)), ((), ())), precision=precision, preferred_element_type=F32
    )


def fine(a, b, dims=(1, 0)):
    return dot(a, b, dims, PRECISE)


def rows8(v):
    return v.reshape(-1, 8, v.shape[-1]).sum(axis=0)


def total(v):
    return v.sum(axis=0, keepdims=True)


def tile(v, rows):
    return jnp.broadcast_to(v[None], (rows // 8, 8, v.shape[-1])).reshape(rows, v.shape[-1])


def gelu_pair(x):
    cdf = 0.5 * lax.erf(x * 0.7071067811865476) + 0.5
    bell = jnp.exp2(x * x * (-0.5 * 1.4426950408889634))
    return x * cdf, cdf + x * bell * 0.3989422804014327


def norm_parts(v, ones):
    high = v.astype(BF16)
    low = (v - high.astype(F32)).astype(BF16)
    centred = v - dot(jnp.concatenate([high, low], axis=1), ones)
    rstd = lax.rsqrt(dot((centred * centred).astype(BF16), ones[: v.shape[1]]) + 1e-05)
    return centred * rstd, rstd


def norm_back(grad, unit, rstd, gain, ones):
    width = grad.shape[1]
    scaled = grad * gain
    first = dot(scaled.astype(BF16), ones[:width])
    second = dot((scaled * unit).astype(BF16), ones[:width])
    return rstd * (scaled - first - unit * second)


def mean_matrix(z):
    return jnp.full((2 * z.C, z.C), 1.0 / z.C, BF16)


class Sizes:
    def __init__(self, images, side, channels, hidden, red, out, layers, parts):
        self.I, self.side, self.C, self.H, self.R, self.O, self.L = images, side, channels, hidden, red, out, layers
        self.parts, self.units = parts, hidden // parts
        self.W = side * images
        self.N0 = side * self.W
        self.CH = 384
        self.N = -(-self.N0 // self.CH) * self.CH
        self.chunks = self.N // self.CH
        self.half = side // 2
        self.hp = -(-self.half // 8) * 8
        self.M = self.half * self.hp
        self.base = self.W
        self.tall = self.W * (2 * self.hp + 2)
        self.long = self.base + self.N + self.W
        self.at_project = 3 * channels
        self.at_expand = self.at_project + channels
        self.at_squeeze = self.at_expand + 3 * red
        self.at_small = self.at_squeeze + red
        self.shared = -(-(self.at_small + 16) // (16 * parts)) * 16
        self.merge = -(-(9 * out + 3) // (16 * parts)) * 16


class Refs:
    pass


def call(body, ins, outs, scratch, limit, smem=()):
    vmem = pl.BlockSpec(memory_space=pltpu.VMEM)
    scalar = pl.BlockSpec(memory_space=pltpu.SMEM)
    names = list(ins) + list(outs) + list(scratch)

    def kernel(*refs):
        r = Refs()
        for name, ref in zip(names, refs):
            setattr(r, name, ref)
        body(r)

    found = pl.pallas_call(
        kernel,
        out_shape=list(outs.values()),
        in_specs=[scalar if name in smem else vmem for name in ins],
        out_specs=[vmem] * len(outs),
        scratch_shapes=list(scratch.values()),
        compiler_params=pltpu.CompilerParams(vmem_limit_bytes=limit * MIB),
    )(*ins.values())
    return dict(zip(outs, found))


def arr(*shape, dtype=F32):
    return jax.ShapeDtypeStruct(shape, dtype)


def kept(*shape, dtype=F32):
    return pltpu.VMEM(shape, dtype)


def over(z, body):
    def step(c, carry):
        body(pl.ds(pl.multiple_of(c * z.CH, 128), z.CH), c * z.CH)
        return carry

    lax.fori_loop(0, z.chunks, step, 0)


def near(ref, start, off, size):
    return ref[pl.ds(start + off, size), :]


def parity(z, i):
    rows = lax.broadcasted_iota(jnp.int32, (8, z.C), 0)
    return jnp.where(rows % z.I == i, 1.0, 0.0)


def kinds(z, rows):
    return tile(lax.broadcasted_iota(jnp.int32, (8, z.C), 1) % 3, rows)


def weave(z, v):
    out = v[0:1] * parity(z, 0)
    for i in range(1, z.I):
        out += v[i : i + 1] * parity(z, i)
    return out


def split(z, v):
    rows = [total(v * parity(z, i)) for i in range(z.I)]
    return jnp.concatenate(rows + [jnp.zeros((GROUP - z.I, z.C), F32)], axis=0)


def front_kernel(z, r):
    rows = lax.broadcasted_iota(jnp.int32, (z.W, z.C), 0)
    lanes = lax.broadcasted_iota(jnp.int32, (z.W, z.C), 1) % 3
    image = rows % z.I
    col = rows // z.I
    high = jnp.zeros((z.W, z.C), jnp.int32)
    wide = jnp.zeros((z.W, z.C), jnp.int32)
    for i in range(z.I):
        high = jnp.where(image == i, r.sizes[i, 0], high)
        wide = jnp.where(image == i, r.sizes[i, 1], wide)
    inside = jnp.where(col < wide, 1.0, 0.0)
    first, last = col == 0, col == z.side - 1
    edge = jnp.where((first & (lanes == 2)) | (last & (lanes == 1)), 0.0, 1.0)
    back = jnp.where((last & (lanes == 2)) | (first & (lanes == 1)), 0.0, 1.0)

    def step(row, carry):
        at = pl.ds(pl.multiple_of(row * z.W, 8), z.W)
        r.mask[at, :] = jnp.where(high > row, inside, 0.0)
        r.edge[at, :] = edge
        r.back[at, :] = back
        return carry

    lax.fori_loop(0, z.side, step, 0)
    pad = jnp.zeros((z.N - z.N0, z.C), F32)
    for ref in (r.mask, r.edge, r.back):
        ref[z.N0 :, :] = pad
    pad = jnp.zeros((z.hp - z.half, z.O), F32)
    r.pgrad[z.M :, :] = jnp.zeros((8, 9 * z.C), F32)
    sums = jnp.zeros((8, z.O), F32)
    for i in range(z.I):
        for pair in range(z.half // 2):
            both = r.cotangent[i, :, 2 * pair * z.O : (2 * pair + 2) * z.O].astype(F32)
            both = jnp.concatenate([both[:, : z.O], pad, both[:, z.O :], pad], axis=0)
            at = i * z.M + 2 * pair * z.hp
            r.cot[at : at + 2 * z.hp, :] = both.astype(BF16)
            sums += rows8(both)
        step = z.M // 2
        for at in range(0, z.M, step):
            r.pgrad[at : at + step, :] = dot(r.cot[i * z.M + at : i * z.M + at + step, :], r.merge_weight[...])

        def part(dr, ds, b, down=0):
            k = 3 * dr + ds
            return r.pgrad[pl.ds(b * z.hp + down, z.hp), k * z.C : (k + 1) * z.C]

        for b in range(z.half):
            planes = [
                part(1, 1, b),
                part(2, 1, b) + part(0, 1, b, 1),
                part(1, 2, b),
                part(2, 2, b) + part(0, 2, b, 1),
            ]
            if b < z.half - 1:
                planes[2] += part(1, 0, b + 1)
                planes[3] += part(2, 0, b + 1) + part(0, 0, b + 1, 1)
            for plane, (down, right) in zip(planes, ((0, 0), (1, 0), (0, 1), (1, 1))):
                start = down * z.W + (2 * b + right) * z.I + i
                r.grad[pl.ds(start, z.hp, stride=2 * z.W), :] = plane
    r.merge_bias_sums[...] = sums


def shift_phase(z, r, cat):
    r.sums[...] = jnp.zeros_like(r.sums)

    def body(rows, at):
        start = z.base + at
        kind = kinds(z, z.CH)
        mid = near(r.normed, start, 0, z.CH)
        high = jnp.where(kind == 2, near(r.normed, start, -z.W, z.CH), near(r.normed, start, z.W, z.CH))
        wide = jnp.where(kind == 2, near(r.normed, start, -z.I, z.CH), near(r.normed, start, z.I, z.CH))
        high = jnp.where(kind == 0, mid, high).astype(BF16)
        wide = jnp.where(kind == 0, mid, wide * r.edge[rows, :]).astype(BF16)
        mask = r.mask[rows, :]
        for j, piece in enumerate((high, wide, mid.astype(BF16))):
            cat[rows, j * z.C : (j + 1) * z.C] = piece
            r.sums[j] += rows8(piece.astype(F32) * mask)

    over(z, body)


def counts_of(z, r):
    rows = []
    for i in range(GROUP):
        count = (r.sizes[i, 0] * r.sizes[i, 1]).astype(F32) if i < z.I else 1.0
        rows.append(jnp.full((1, z.C), 1.0, F32) * count)
    return jnp.concatenate(rows, axis=0)


def weigh_phase(z, r, l, o):
    pooled = r.mix_bias[l, 0:1] + r.mix_bias[l, 1:2]
    counts = counts_of(z, r)
    for j in range(3):
        pool = split(z, r.sums[j])
        o.pool[j] = pool
        pooled = pooled + fine(pool, r.mix_weight[l, j].astype(F32)) / counts
    o.pooled[...] = pooled
    act, slope = gelu_pair(fine(pooled, r.squeeze_weight[l], (1, 1)) + r.squeeze_bias[l : l + 1])
    o.act[...] = act
    o.slope[...] = slope
    logits = fine(act, r.ewp[l]) + r.ebp[l : l + 1]
    parts = [logits[:, j * z.C : (j + 1) * z.C] for j in range(3)]
    top = jnp.maximum(jnp.maximum(parts[0], parts[1]), parts[2])
    parts = [jnp.exp(part - top) for part in parts]
    whole = parts[0] + parts[1] + parts[2]
    for j in range(3):
        o.share[j] = parts[j] / whole


def mix_phase(z, r, l, o):
    ones = mean_matrix(z)
    share = [weave(z, o.share[j]) for j in range(3)]
    bias = tile(r.mix_bias[l, 0:1] * share[0] + r.mix_bias[l, 1:2] * share[1], z.CH)
    share = [tile(s, z.CH) for s in share]
    gain, shift = r.norm_gain[l, 1:2], r.norm_bias[l, 1:2]

    def body(rows, at):
        mixed = bias
        for j in range(3):
            mixed = mixed + dot(o.cat[rows, j * z.C : (j + 1) * z.C], r.mix_weight[l, j]) * share[j]
        mixed = mixed.astype(BF16)
        o.mixed[rows, :] = mixed
        token = dot(mixed, r.project_weight[l]) + r.project_bias[l : l + 1]
        halfway = r.state[rows, :] + r.mask[rows, :] * token
        unit, rstd = norm_parts(halfway, ones)
        o.unit2[rows, :] = unit
        o.rstd2[rows, :] = rstd
        o.normed2[rows, :] = (unit * gain + shift).astype(BF16)
        r.state[rows, :] = halfway

    over(z, body)


def norm_store(z, r, l, o, rows, at, state):
    unit, rstd = norm_parts(state, mean_matrix(z))
    o.unit1[rows, :] = unit
    o.rstd1[rows, :] = rstd
    r.normed[pl.ds(z.base + at, z.CH), :] = unit * r.norm_gain[l, 0:1] + r.norm_bias[l, 0:1]


def clear_edges(z, ref):
    ref[: z.base, :] = jnp.zeros((z.base, z.C), F32)
    ref[z.base + z.N0 :, :] = jnp.zeros((ref.shape[0] - z.base - z.N0, z.C), F32)


def feed_phase(z, r, l, o, after):
    def body(rows, at):
        pre = dot(o.normed2[rows, :], r.inner[l], (1, 1)) + r.inner_bias[l : l + 1]
        act, slope = gelu_pair(pre)
        act = act.astype(BF16)
        o.act_rows[rows, :] = act
        o.slope_rows[rows, :] = slope.astype(BF16)
        out = dot(act, r.outer[l]) + r.outer_bias[l : l + 1]
        state = r.state[rows, :] + r.mask[rows, :] * out
        after(rows, at, state)

    over(z, body)


def saved_early(z):
    return dict(
        unit1=kept(z.N, z.C), rstd1=kept(z.N, z.C), cat=kept(z.N, 3 * z.C, dtype=BF16), mixed=kept(z.N, z.C, dtype=BF16),
        unit2=kept(z.N, z.C), rstd2=kept(z.N, z.C), normed2=kept(z.N, z.C, dtype=BF16), pool=kept(3, GROUP, z.C),
        pooled=kept(GROUP, z.C), act=kept(GROUP, z.R), slope=kept(GROUP, z.R), share=kept(3, GROUP, z.C),
    )


def saved_late(z):
    return dict(act_rows=kept(z.N, z.H, dtype=BF16), slope_rows=kept(z.N, z.H, dtype=BF16))


def first_kernel(z, r):
    spots = lax.broadcasted_iota(jnp.int32, (3 * z.C, 3 * z.C), 0)
    ends = lax.broadcasted_iota(jnp.int32, (3 * z.C, 3 * z.C), 1)
    kind = jnp.where(ends >= 2 * z.C, 2, jnp.where(ends >= z.C, 1, 0))
    r.perm[...] = jnp.where(spots == 3 * (ends - kind * z.C) + kind, 1.0, 0.0)
    for l in range(z.L):
        r.ewp[l] = fine(r.expand_weight[l], r.perm[...])
    r.ebp[...] = fine(r.expand_bias[...], r.perm[...])
    whole = z.N0 // z.CH

    def step(c, carry):
        rows = pl.ds(pl.multiple_of(c * z.CH, 128), z.CH)
        state = r.images[rows, :].astype(F32) * r.mask[rows, :]
        r.state[rows, :] = state
        norm_store(z, r, 0, r, rows, c * z.CH, state)
        return carry

    lax.fori_loop(0, whole, step, 0)
    if whole < z.chunks:
        at = whole * z.CH
        left = z.N0 - at
        tail = r.images[at:, :].astype(F32) * r.mask[at : z.N0, :]
        state = jnp.concatenate([tail, jnp.zeros((z.CH - left, z.C), F32)], axis=0)
        r.state[at:, :] = state
        norm_store(z, r, 0, r, pl.ds(at, z.CH), at, state)
    clear_edges(z, r.normed)
    shift_phase(z, r, r.cat)
    weigh_phase(z, r, 0, r)
    mix_phase(z, r, 0, r)


def second_kernel(z, r):
    for h in range(z.parts):
        for l in range(z.L):
            at = h * z.units
            r.inner[l, at : at + z.units, :] = r.gathered[h, 2 * l * z.units : (2 * l + 1) * z.units, :]
            r.outer[l, at : at + z.units, :] = r.gathered[h, (2 * l + 1) * z.units : (2 * l + 2) * z.units, :]
    for l in range(z.L):
        row = 2 * z.L * z.units + l
        r.inner_bias[l : l + 1] = jnp.concatenate(
            [r.gathered[h, row : row + 1, : z.units].astype(F32) for h in range(z.parts)], axis=1
        )
    early, late = [Refs() for _ in range(z.L)], [Refs() for _ in range(z.L)]
    for l in range(z.L):
        early[l].normed2 = r.normed2_0 if l == 0 else r.normed2
        early[l].act_rows = r.act_rows_0 if l == 0 else r.act_rows
        early[l].slope_rows = r.slope_rows_0 if l == 0 else r.slope_rows

    def then_norm(rows, at, state):
        r.state[rows, :] = state
        norm_store(z, r, 1, r, rows, at, state)

    r.state[...] = r.state_in[...]
    feed_phase(z, r, 0, early[0], then_norm)
    clear_edges(z, r.normed)
    shift_phase(z, r, r.cat)
    weigh_phase(z, r, 1, r)
    mix_phase(z, r, 1, r)

    def then_keep(rows, at, state):
        r.normed[pl.ds(z.base + at, z.CH), :] = state

    feed_phase(z, r, 1, early[1], then_keep)
    for i in range(z.I):
        for pair in range(z.half // 2):
            at = i * z.M + 2 * pair * z.hp
            for k in range(9):
                dr, ds = divmod(k, 3)
                two = []
                for b in (2 * pair, 2 * pair + 1):
                    col = 2 * b + ds - 1
                    if col < 0:
                        two.append(jnp.zeros((z.hp, z.C), F32))
                    else:
                        two.append(r.normed[pl.ds(dr * z.W + col * z.I + i, z.hp, stride=2 * z.W), :])
                r.patch[at : at + 2 * z.hp, k * z.C : (k + 1) * z.C] = jnp.concatenate(two, axis=0).astype(BF16)
    for i in range(z.I):
        for pair in range(z.half // 2):
            at = i * z.M + 2 * pair * z.hp
            merged = dot(r.patch[at : at + 2 * z.hp, :], r.merge_weight[...], (1, 1)) + r.merge_bias[...]
            wide = jnp.concatenate([merged[: z.half], merged[z.hp : z.hp + z.half]], axis=1)
            r.features[i, :, 2 * pair * z.O : (2 * pair + 2) * z.O] = wide.astype(BF16)
    for k in range(9):
        grad = dot(r.cot[...], r.patch[:, k * z.C : (k + 1) * z.C], (0, 0))
        r.merge_rows[k * z.O : (k + 1) * z.O, :] = grad.astype(BF16)
    bias = total(r.merge_bias_sums[...])
    rest = z.O - 2 * z.C
    rows = [bias[:, : z.C], bias[:, z.C : 2 * z.C]]
    rows += [jnp.concatenate([bias[:, 2 * z.C :], jnp.zeros((1, z.C - rest), F32)], axis=1)]
    rows += [jnp.zeros((z.parts * z.merge - 9 * z.O - 3, z.C), F32)]
    r.merge_rows[9 * z.O :, :] = jnp.concatenate(rows, axis=0).astype(BF16)


def feed_back_kernel(z, l, r):
    ones = mean_matrix(z)
    gain = r.norm_gain[l, 1:2]
    sums = (r.vec, r.inner_sums, r.g_outer, r.g_inner, r.g_project, r.g_mix)
    for ref in sums:
        ref[...] = jnp.zeros_like(ref)
    even, odd = tile(parity(z, 0), z.CH), tile(parity(z, 1), z.CH)

    def body(rows, at):
        mask = r.mask[rows, :]
        grad = r.grad[rows, :]
        out = (grad * mask).astype(BF16)
        r.vec[0] += rows8(out.astype(F32))
        pre = (dot(out, r.outer[l], (1, 1)) * r.slope_rows[rows, :].astype(F32)).astype(BF16)
        r.inner_sums[...] += rows8(pre.astype(F32))
        r.g_outer[...] += dot(out, r.act_rows[rows, :], (0, 0))
        r.g_inner[...] += dot(r.normed2[rows, :], pre, (0, 0))
        normed_grad = dot(pre, r.inner[l])
        unit = r.unit2[rows, :]
        r.vec[1] += rows8(normed_grad * unit)
        r.vec[2] += rows8(normed_grad)
        grad = grad + norm_back(normed_grad, unit, r.rstd2[rows, :], gain, ones)
        r.half_grad[rows, :] = grad
        token = (grad * mask).astype(BF16)
        r.vec[3] += rows8(token.astype(F32))
        r.g_project[...] += dot(r.mixed[rows, :], token, (0, 0))
        mixed_grad = dot(token, r.project_weight[l], (1, 1))
        r.vec[4] += rows8(mixed_grad)
        both = jnp.concatenate([(mixed_grad * even).astype(BF16), (mixed_grad * odd).astype(BF16)], axis=1)
        r.mixed_grad[rows, :] = both
        r.g_mix[...] += dot(both, r.cat[rows, :], (0, 0))

    over(z, body)
    counts = counts_of(z, r)
    zeros = jnp.zeros((GROUP - z.I, z.C), F32)
    summed = split(z, r.vec[4])
    share = [r.share[j] for j in range(3)]
    mix, dp = [], []
    for j in range(3):
        weight = r.mix_weight[l, j].astype(F32)
        rows = []
        found = 0.0
        for i in range(z.I):
            block = r.g_mix[i * z.C : (i + 1) * z.C, j * z.C : (j + 1) * z.C].T
            rows.append(total(weight * block))
            found = found + block * share[j][i : i + 1]
            scaled = weight * share[j][i : i + 1]
            r.scaled[j * z.C : (j + 1) * z.C, i * z.C : (i + 1) * z.C] = scaled.astype(BF16)
        mix.append(found)
        dp.append(jnp.concatenate(rows + [zeros], axis=0))
    for j in range(2):
        dp[j] += summed * r.mix_bias[l, j : j + 1]
    even = dp[0] * share[0] + dp[1] * share[1] + dp[2] * share[2]
    dz = jnp.concatenate([share[j] * (dp[j] - even) for j in range(3)], axis=1)
    act, slope, pooled = r.act[...], r.slope[...], r.pooled[...]
    expand = fine(fine(act, dz, (0, 0)), r.perm[...], (1, 1))
    expand_bias = total(fine(dz, r.perm[...], (1, 1)))
    dact = fine(dz, r.ewp[l], (1, 1)) * slope
    squeeze = fine(dact, pooled, (0, 0))
    dpool = fine(dact, r.squeeze_weight[l])
    push = dpool / counts
    for j in range(3):
        mix[j] += fine(r.pool[j], push, (0, 0))
        r.push[j] = weave(z, fine(push, r.mix_weight[l, j].astype(F32), (1, 1)))
    for j in range(3):
        r.rows[j * z.C : (j + 1) * z.C, :] = mix[j].astype(BF16)
    r.rows[z.at_project : z.at_expand, :] = r.g_project[...].astype(BF16)
    for j in range(3):
        at = z.at_expand + j * z.R
        r.rows[at : at + z.R, :] = expand[:, j * z.C : (j + 1) * z.C].astype(BF16)
    r.rows[z.at_squeeze : z.at_small, :] = squeeze.astype(BF16)
    inner = total(r.inner_sums[...])
    small = [total(share[j] * summed + dpool) for j in range(2)]
    small += [total(r.vec[k]) for k in (3, 0, 1, 2)]
    small += [inner[:, k * z.C : (k + 1) * z.C] for k in range(z.H // z.C)]
    small += [expand_bias[:, j * z.C : (j + 1) * z.C] for j in range(3)]
    small += [jnp.concatenate([total(dact), jnp.zeros((1, z.C - z.R), F32)], axis=1)]
    small += [jnp.zeros((z.parts * z.shared - z.at_small - len(small), z.C), F32)]
    r.rows[z.at_small :, :] = jnp.concatenate(small, axis=0).astype(BF16)
    inner, outer = r.g_inner[...].T, r.g_outer[...].T
    u = z.units
    for h in range(z.parts):
        r.blocks[h, :u, :] = inner[h * u : (h + 1) * u].astype(BF16)
        r.blocks[h, u : 2 * u, :] = outer[h * u : (h + 1) * u].astype(BF16)
        r.blocks[h, 2 * u :, :] = r.rows[h * z.shared : (h + 1) * z.shared, :]


def mix_back_kernel(z, l, last, r):
    ones = mean_matrix(z)
    for ref in (r.back_h, r.back_w):
        clear_edges(z, ref)
    gain = r.norm_gain[l, 0:1]
    push = [tile(r.push[j], z.CH) for j in range(3)]

    def spread(rows, at):
        mask = r.mask[rows, :]
        parts = dot(r.mixed_grad[rows, :], r.scaled[...], (1, 1))
        for j, ref in enumerate((r.back_h, r.back_w, r.back_c)):
            ref[pl.ds(z.base + at, z.CH), :] = parts[:, j * z.C : (j + 1) * z.C] + mask * push[j]

    over(z, spread)
    r.vec[...] = jnp.zeros_like(r.vec)

    def body(rows, at):
        start = z.base + at
        kind = kinds(z, z.CH)
        high = jnp.where(kind == 2, near(r.back_h, start, z.W, z.CH), near(r.back_h, start, -z.W, z.CH))
        wide = jnp.where(kind == 2, near(r.back_w, start, z.I, z.CH), near(r.back_w, start, -z.I, z.CH))
        high = jnp.where(kind == 0, near(r.back_h, start, 0, z.CH), high)
        wide = jnp.where(kind == 0, near(r.back_w, start, 0, z.CH), wide * r.back[rows, :])
        grad = high + wide + near(r.back_c, start, 0, z.CH)
        unit = r.unit1[rows, :]
        r.vec[0] += rows8(grad * unit)
        r.vec[1] += rows8(grad)
        grad = r.half_grad[rows, :] + norm_back(grad, unit, r.rstd1[rows, :], gain, ones)
        if not last:
            r.state_grad[rows, :] = grad
            return
        grad = grad * r.mask[rows, :]
        left = z.N0 - (z.chunks - 1) * z.CH

        @pl.when(at < z.N0 - z.CH + 1)
        def _():
            r.state_grad[rows, :] = grad

        @pl.when(at > z.N0 - z.CH)
        def _():
            r.state_grad[z.N0 - left :, :] = grad[:left]

    over(z, body)
    stray = r.back_h[z.base + z.N0 - z.W : z.base + z.N0, :]
    r.vec[1] -= rows8(jnp.where(kinds(z, z.W) == 1, stray, 0.0))
    r.first_norm[...] = jnp.concatenate([total(r.vec[0]), total(r.vec[1])], axis=0)


def final_outputs(z):
    return dict(
        mix_weight=arr(z.L, 3, z.C, z.C), mix_bias=arr(z.L, 2, z.C), squeeze_weight=arr(z.L, z.R, z.C),
        squeeze_bias=arr(z.L, z.R), expand_weight=arr(z.L, z.R, 3 * z.C), expand_bias=arr(z.L, 3 * z.C),
        project_weight=arr(z.L, z.C, z.C), project_bias=arr(z.L, z.C), norm_gain=arr(z.L, 2, z.C),
        norm_bias=arr(z.L, 2, z.C), inner_weight=arr(z.L, z.units, z.C), inner_bias=arr(z.L, z.H),
        outer_weight=arr(z.L, z.units, z.C), outer_bias=arr(z.L, z.C), merge_weight=arr(z.O, 9 * z.C),
        merge_bias=arr(1, z.O),
    )


def last_kernel(z, r):
    for l in range(z.L):
        rows = r.shared_rows.at[l]

        def get(at, count):
            return rows[at : at + count, :].astype(F32)

        for j in range(3):
            r.mix_weight[l, j] = get(j * z.C, z.C)
            r.expand_weight[l, :, j * z.C : (j + 1) * z.C] = get(z.at_expand + j * z.R, z.R)
        r.project_weight[l] = get(z.at_project, z.C)
        r.squeeze_weight[l] = get(z.at_squeeze, z.R)
        small = get(z.at_small, 16)
        r.mix_bias[l] = small[0:2]
        r.project_bias[l : l + 1] = small[2:3]
        r.outer_bias[l : l + 1] = small[3:4]
        r.norm_gain[l] = jnp.concatenate([r.norms[2 * l : 2 * l + 1, :].astype(F32), small[4:5]], axis=0)
        r.norm_bias[l] = jnp.concatenate([r.norms[2 * l + 1 : 2 * l + 2, :].astype(F32), small[5:6]], axis=0)
        at = 6
        for k in range(z.H // z.C):
            r.inner_bias[l : l + 1, k * z.C : (k + 1) * z.C] = small[at : at + 1]
            at += 1
        for j in range(3):
            r.expand_bias[l : l + 1, j * z.C : (j + 1) * z.C] = small[at : at + 1]
            at += 1
        r.squeeze_bias[l : l + 1] = small[at : at + 1, : z.R]
        r.inner_weight[l] = r.feed_rows[l, : z.units, :].astype(F32)
        r.outer_weight[l] = r.feed_rows[l, z.units :, :].astype(F32)
    for k in range(9):
        r.merge_weight[:, k * z.C : (k + 1) * z.C] = r.merge_rows[k * z.O : (k + 1) * z.O, :].astype(F32)
    small = r.merge_rows[9 * z.O : 9 * z.O + 16, :].astype(F32)
    r.merge_bias[:, : z.C] = small[0:1]
    r.merge_bias[:, z.C : 2 * z.C] = small[1:2]
    r.merge_bias[:, 2 * z.C :] = small[2:3, : z.O - 2 * z.C]


def swap(x, axis, n, bit):
    return lax.ppermute(x, axis, [(a, a ^ bit) for a in range(n)])


def bits_of(n):
    return [1 << k for k in range(n.bit_length() - 1)]


def scatter_bits(x, axis, n):
    me = lax.axis_index(axis)
    for bit in bits_of(n):
        mine = (me // bit) % 2
        x = x.reshape((-1, 2) + x.shape[1:])
        away = lax.dynamic_index_in_dim(x, 1 - mine, 1, keepdims=False)
        here = lax.dynamic_index_in_dim(x, mine, 1, keepdims=False)
        x = (here.astype(F32) + swap(away, axis, n, bit).astype(F32)).astype(BF16)
    return x[0]


def sum_bits(x, axis, n):
    for bit in bits_of(n):
        x = (x.astype(F32) + swap(x, axis, n, bit).astype(F32)).astype(BF16)
    return x


def gather_bits(x, axis, n, order):
    me = lax.axis_index(axis)
    have = x[None]
    dims = []
    for bit in order:
        got = swap(have, axis, n, bit)
        mine = (me // bit) % 2
        have = jnp.where(mine == 0, jnp.stack([have, got]), jnp.stack([got, have]))
        dims.append(bit)
    count = len(dims)
    have = have.reshape((2,) * count + x.shape)
    place = [count - 1 - dims.index(bit) for bit in sorted(dims, reverse=True)]
    have = have.transpose(place + list(range(count, have.ndim)))
    return have.reshape((n,) + x.shape)


def per_device(
    img, hid, images, sizes, cotangent, mix_weight, mix_bias, squeeze_weight, squeeze_bias, expand_weight, expand_bias,
    project_weight, project_bias, norm_gain, norm_bias, inner_weight, inner_bias, outer_weight, outer_bias,
    merge_weight, merge_bias,
):
    z = Sizes(
        images.shape[0], images.shape[1], images.shape[3], inner_weight.shape[2] * hid, squeeze_weight.shape[2],
        merge_weight.shape[1], mix_weight.shape[0], hid,
    )
    flat = images.transpose(1, 2, 0, 3).reshape(z.N0, z.C)
    merge_t = merge_weight.T
    squeeze_t = squeeze_weight.transpose(0, 2, 1)
    block = jnp.stack([inner_weight.transpose(0, 2, 1), outer_weight], axis=1).reshape(-1, z.C)
    bias_rows = jnp.pad(inner_bias, ((0, 16 - z.L), (0, z.C - z.units)))
    block = jnp.concatenate([block, bias_rows], axis=0)
    order = bits_of(hid)[1:] + [1]
    gathered = gather_bits(block, "hid", hid, order)
    smem = dict(sizes=0)
    small = dict(
        mix_weight=mix_weight, mix_bias=mix_bias, squeeze_weight=squeeze_t, squeeze_bias=squeeze_bias,
        project_weight=project_weight, project_bias=project_bias, norm_gain=norm_gain, norm_bias=norm_bias,
    )
    a = call(
        partial(front_kernel, z),
        dict(sizes=sizes, cotangent=cotangent, merge_weight=merge_t),
        dict(
            mask=kept(z.N, z.C), edge=kept(z.N, z.C), back=kept(z.N, z.C), cot=kept(z.I * z.M, z.O, dtype=BF16),
            grad=kept(z.tall, z.C), merge_bias_sums=kept(8, z.O),
        ),
        dict(pgrad=kept(z.M + 8, 9 * z.C)),
        12, smem,
    )
    b = call(
        partial(first_kernel, z),
        dict(
            images=flat, sizes=sizes, mask=a["mask"], edge=a["edge"], expand_weight=expand_weight, expand_bias=expand_bias,
            **small,
        ),
        dict(
            state=kept(z.N, z.C), perm=kept(3 * z.C, 3 * z.C), ewp=kept(z.L, z.R, 3 * z.C), ebp=kept(z.L, 3 * z.C),
            **saved_early(z),
        ),
        dict(normed=kept(z.long, z.C), sums=kept(3, 8, z.C)),
        12, smem,
    )
    late = saved_late(z)
    c = call(
        partial(second_kernel, z),
        dict(
            sizes=sizes, mask=a["mask"], edge=a["edge"], state_in=b["state"], normed2_0=b["normed2"], gathered=gathered,
            ewp=b["ewp"], ebp=b["ebp"], outer_bias=outer_bias, merge_weight=merge_t, merge_bias=merge_bias.reshape(1, -1),
            cot=a["cot"], merge_bias_sums=a["merge_bias_sums"], **small,
        ),
        dict(
            features=arr(z.I, z.half, z.half * z.O, dtype=BF16),
            merge_rows=arr(z.parts * z.merge, z.C, dtype=BF16),
            inner=kept(z.L, z.H, z.C, dtype=BF16), outer=kept(z.L, z.H, z.C, dtype=BF16),
            act_rows_0=late["act_rows"], slope_rows_0=late["slope_rows"], **saved_early(z), **late,
        ),
        dict(
            state=kept(z.N, z.C), normed=kept(z.tall, z.C), sums=kept(3, 8, z.C), inner_bias=kept(z.L, z.H),
            patch=kept(z.I * z.M, 9 * z.C, dtype=BF16),
        ),
        16, smem,
    )
    first = dict(b, act_rows=c["act_rows_0"], slope_rows=c["slope_rows_0"])
    grad, blocks, norms = a["grad"], [None] * z.L, [None] * z.L
    for l in reversed(range(z.L)):
        s = c if l else first
        d = call(
            partial(feed_back_kernel, z, l),
            dict(
                sizes=sizes, mask=a["mask"], grad=grad, inner=c["inner"], outer=c["outer"], perm=b["perm"], ewp=b["ewp"],
                **{
                    name: s[name]
                    for name in dict(
                        act_rows=0, slope_rows=0, normed2=0, unit2=0, rstd2=0, mixed=0, cat=0, share=0, pool=0, pooled=0,
                        act=0, slope=0,
                    )
                },
                **small,
            ),
            dict(
                half_grad=kept(z.N, z.C), mixed_grad=kept(z.N, z.I * z.C, dtype=BF16),
                scaled=kept(3 * z.C, z.I * z.C, dtype=BF16), push=kept(3, 8, z.C),
                blocks=arr(z.parts, 2 * z.units + z.shared, z.C, dtype=BF16),
            ),
            dict(
                vec=kept(5, 8, z.C), inner_sums=kept(8, z.H), g_outer=kept(z.C, z.H), g_inner=kept(z.C, z.H),
                g_project=kept(z.C, z.C), g_mix=kept(z.I * z.C, 3 * z.C), rows=kept(z.parts * z.shared, z.C, dtype=BF16),
            ),
            12, smem,
        )
        blocks[l] = d["blocks"]
        e = call(
            partial(mix_back_kernel, z, l, l == 0),
            dict(
                mask=a["mask"], back=a["back"], mixed_grad=d["mixed_grad"], scaled=d["scaled"], push=d["push"],
                unit1=s["unit1"], rstd1=s["rstd1"], half_grad=d["half_grad"], norm_gain=norm_gain,
            ),
            dict(state_grad=kept(z.N, z.C) if l else arr(z.N0, z.C), first_norm=arr(2, z.C)),
            dict(back_h=kept(z.long, z.C), back_w=kept(z.long, z.C), back_c=kept(z.long, z.C), vec=kept(2, 8, z.C)),
            12,
        )
        grad, norms[l] = e["state_grad"], e["first_norm"]
    images_grad = grad.reshape(z.side, z.side, z.I, z.C).transpose(2, 0, 1, 3)

    back = bits_of(hid)[::-1]
    merge_rows = sum_bits(scatter_bits(c["merge_rows"].reshape(hid, z.merge, z.C), "hid", hid), "img", img)
    merge_rows = gather_bits(merge_rows, "hid", hid, back).reshape(hid * z.merge, z.C)
    both = jnp.stack(blocks, axis=1)
    norm_rows = jnp.pad(jnp.concatenate(norms, axis=0), ((0, 16 - 2 * z.L), (0, 0))).astype(BF16)
    norm_rows = jnp.broadcast_to(norm_rows[None], (hid, 16, z.C))
    every = jnp.concatenate([both.reshape(hid, -1, z.C), norm_rows], axis=1)
    every = sum_bits(scatter_bits(every, "hid", hid), "img", img)
    norm_rows = every[-16:]
    every = every[:-16].reshape(z.L, 2 * z.units + z.shared, z.C)
    feed_rows = every[:, : 2 * z.units]
    shared_rows = gather_bits(every[:, 2 * z.units :], "hid", hid, back)
    shared_rows = shared_rows.transpose(1, 0, 2, 3).reshape(z.L, hid * z.shared, z.C)
    g = call(
        partial(last_kernel, z),
        dict(shared_rows=shared_rows, feed_rows=feed_rows, merge_rows=merge_rows, norms=norm_rows),
        final_outputs(z), {}, 16,
    )
    inner_bias_grad = lax.dynamic_slice_in_dim(g["inner_bias"], lax.axis_index("hid") * z.units, z.units, axis=1)
    return (
        c["features"], images_grad, g["mix_weight"], g["mix_bias"], g["squeeze_weight"].transpose(0, 2, 1),
        g["squeeze_bias"], g["expand_weight"], g["expand_bias"], g["project_weight"], g["project_bias"], g["norm_gain"],
        g["norm_bias"], g["inner_weight"].transpose(0, 2, 1), inner_bias_grad, g["outer_weight"], g["outer_bias"],
        g["merge_weight"].T, g["merge_bias"].reshape(-1),
    )


def solution(mesh):
    maps = ("img", "hid")
    in_specs = (
        P(maps, None, None, None), P(maps, None), P(maps, None, None), P(), P(), P(), P(), P(), P(), P(), P(), P(), P(),
        P(None, None, "hid"), P(None, "hid"), P(None, "hid", None), P(), P(), P(),
    )
    out_specs = (
        P(maps, None, None), P(maps, None, None, None), P(), P(), P(), P(), P(), P(), P(), P(), P(), P(),
        P(None, None, "hid"), P(None, "hid"), P(None, "hid", None), P(), P(), P(),
    )
    return jax.shard_map(
        partial(per_device, mesh.shape["img"], mesh.shape["hid"]),
        mesh=mesh, in_specs=in_specs, out_specs=out_specs, check_vma=False,
    )
```

time: 922 us -> 136 us (0.15); the launches traced: 907 us -> 135 us
  waiting for transfers between devices: 397 us -> 26 us
  local copies, waits for them, and re-layouts: 263 us -> 3.01 us
  matrix products: 110 us -> 0 us
  Pallas kernels: 0 us -> 71.8 us
  other arithmetic: 76.5 us -> 7.17 us
  blocking collectives: 40.8 us -> 0 us
  starting transfers between devices: 1.67 us -> 26.1 us
  between operations: 17.2 us -> 1.27 us
    reduce_scatter x4 -> x0, waiting for transfers between devices: 161 us -> none  [the longest x2 111 us: per_device(): lax.psum_scatter(jnp.dot(mlp_hidden, outer_used[layer_at], preferred_elem...]
    all_gather x4 -> x0, waiting for transfers between devices: 144 us -> none  [the longest x2 83.5 us: per_device(): lax.all_gather(normed2.reshape(local_rows, channels), 'hid', axis=0, tile...]
    dot_general x51 -> x0, matrix products: 110 us -> none  [the longest x13 33.8 us: matmul_back(): lax.dot_general(left_op, right_op, (((left_op.ndim - 1,), (1,)), ((), ())...]
    psum x2 -> x0, waiting for transfers between devices: 91.9 us -> none  [the longest x1 91.9 us: per_device(): lax.psum((stacked[0], stacked[1], stacked[2], stacked[3], stacked[4], sta...]
    unnamed x406 -> x42, local copies, waits for them, and re-layouts: 87.4 us -> 1.24 us
    pad x6 -> x0, local copies, waits for them, and re-layouts: 77.1 us -> none  [the longest x3 52.8 us: patches(): padded[:, row_off:row_off + side_len:2, col_off:col_off + side_len:2, :]]
    pallas_call x0 -> x8, Pallas kernels: none -> 71.8 us  [call(): pl.pallas_call(kernel, out_shape=list(outs.values()), in_specs=[scalar if...]
    slice x13 -> x3, local copies, waits for them, and re-layouts: 71.2 us -> 0.02 us  [the longest x1 0.01 us: per_device(): every = every[:-16].reshape(z.L, 2 * z.units + z.shared, z.C)]
  transfers between devices with their start and end apart: 10 -> 19, of which waited for: 8 -> 12; matrix products, arithmetic and copies ran while one was open for 16% -> 3% of each run, Pallas kernels for 0% -> 35%
where the time goes in v2:
time: 136 us; the launch traced here: 135 us
  Pallas kernels  71.8 us (53%)
  starting transfers between devices  26.1 us (19%)
  waiting for transfers between devices  26 us (19%)
  other arithmetic  7.17 us (5%)
  local copies, waits for them, and re-layouts  3.01 us (2%)
    pallas_call x8, Pallas kernels, call(): pl.pallas_call(kernel, out_shape=list(outs.values()), in_specs=[scalar if...  71.8 us
    ppermute x19, starting transfers between devices, swap(): return lax.ppermute(x, axis, [(a, a ^ bit) for a in range(n)])  26.1 us
    ppermute x19, waiting for transfers between devices, swap(): return lax.ppermute(x, axis, [(a, a ^ bit) for a in range(n)])  26 us
  transfers between devices with their start and end apart: 19, of which 12 were waited for; matrix products, arithmetic and copies ran while one was open for 3% of the time, Pallas kernels for 35%

profile of v2, /device:TPU:0, one launch (start us, length us, event | category | flops | bytes accessed | tf_op | source)
XLA Modules:
  0.0 135.3 jit_solution(6261281542736257410)
XLA Ops:
  2.2 3.0 %collective-permute-start = (bf16[1,272,128]{2,1,0:T(8,128)(2,1)S(1)}, bf16[1,272,128]{2,1,0:T(8,128)(2,1)S(1)}, u32[]{:S(2)}, u32[]{:S(2)}) collective-permute-start(bf16[1,272,128]{2,1,0:T(8,128)(2,1)S(1)} %get-tuple-element.209), channel_id=1, source_target_pairs={{0,2},{1,3},{2,0},{3,1},{4,6},{5,7},{6,4},{7,5},{8,10},{9,11},{10,... | collective-permute-start | bytes 208904 | tf_op jit(solution)/shard_map/ppermute | solution.py:600
  5.2 2.3 %collective-permute-done = bf16[1,272,128]{2,1,0:T(8,128)(2,1)S(1)} collective-permute-done((bf16[1,272,128]{2,1,0:T(8,128)(2,1)S(1)}, bf16[1,272,128]{2,1,0:T(8,128)(2,1)S(1)}, u32[]{:S(2)}, u32[]{:S(2)}) %collective-permute-start) | collective-permute-done | bytes 69664 | tf_op jit(solution)/shard_map/ppermute | solution.py:600
  7.6 2.1 %collective-permute-start.1 = (bf16[2,1,272,128]{3,2,1,0:T(8,128)(2,1)S(1)}, bf16[2,1,272,128]{3,2,1,0:T(8,128)(2,1)S(1)}, u32[]{:S(2)}, u32[]{:S(2)}) collective-permute-start(bf16[2,1,272,128]{3,2,1,0:T(8,128)(2,1)S(1)} %maximum_select_fusion.12), channel_id=1, source_target_pairs={{0,4},{1,5},{2,6},{3,7},{4,0},{5,1},{6,2},{7,3},{8,12},{9,13},{10,... | collective-permute-start | bytes 417800 | tf_op jit(solution)/shard_map/ppermute | solution.py:600
  9.7 3.0 %collective-permute-done.1 = bf16[2,1,272,128]{3,2,1,0:T(8,128)(2,1)S(1)} collective-permute-done((bf16[2,1,272,128]{3,2,1,0:T(8,128)(2,1)S(1)}, bf16[2,1,272,128]{3,2,1,0:T(8,128)(2,1)S(1)}, u32[]{:S(2)}, u32[]{:S(2)}) %collective-permute-start.1) | collective-permute-done | bytes 139296 | tf_op jit(solution)/shard_map/ppermute | solution.py:600
  13.7 2.7 %shard_map.322 = (f32[2688,128]{1,0:T(8,128)S(1)}, f32[2688,128]{1,0:T(8,128)S(1)}, f32[2688,128]{1,0:T(8,128)S(1)}, bf16[864,320]{1,0:T(8,128)(2,1)S(1)}, f32[3...) custom-call(s32[2,2]{1,0:T(2,128)S(1)} %copy-done.11, bf16[2,18,5760]{2,1,0:T(8,128)(2,1)S(1)} %copy.45.refs_1_, ...), custom_call_target="tpu_custom_call" | custom-call | tf_op jit(solution)/shard_map/pallas_call | solution.py:103
  16.5 10.6 %shard_map.323 = (f32[2688,128]{1,0:T(8,128)S(1)}, f32[384,384]{1,0:T(8,128)S(1)}, f32[2,32,384]{2,1,0:T(8,128)S(1)}, f32[2,384]{1,0:T(2,128)S(1)}, f32[2688,128...) custom-call(bf16[2592,128]{1,0:T(8,128)(2,1)S(1)} %bitcast.108, ...), custom_call_target="tpu_custom_call" | custom-call | tf_op jit(solution)/shard_map/pallas_call | solution.py:103
  27.2 1.1 fusion.3
  28.4 22.9 %shard_map.324 = (bf16[2,18,5760]{2,1,0:T(8,128)(2,1)S(1)}, bf16[2944,128]{1,0:T(8,128)(2,1)S(1)}, bf16[2,512,128]{2,1,0:T(8,128)(2,1)S(1)}, bf16[2,512,128]{2,1...) custom-call(s32[2,2]{1,0:T(2,128)S(1)} %copy-done.11, ...), custom_call_target="tpu_custom_call" | custom-call | tf_op jit(solution)/shard_map/pallas_call | solution.py:103
  52.6 12.8 %shard_map.325 = (f32[2688,128]{1,0:T(8,128)S(1)}, bf16[2688,256]{1,0:T(8,128)(2,1)S(1)}, bf16[384,256]{1,0:T(8,128)(2,1)S(1)}, f32[3,8,128]{2,1,0:T(8,128)S(1)}, bf16[8,224,128]{2,1,0:T(8,128)(2,1)S(1)}) custom-call(s32[2,2]{1,0:T(2,128)S(1)} %copy-done.11, f32[2688,128]{1,0:T(8,128)S(1)} %get-tuple-element.90.refs_2_.refs_1_.refs_0_, ...), custom_call_target="tpu_custom_call" | custom-call | tf_op jit(solution)/shard_map/pallas_call | solution.py:103
  65.4 3.8 %shard_map.326 = (f32[2688,128]{1,0:T(8,128)S(1)}, f32[2,128]{1,0:T(2,128)S(1)}) custom-call(f32[2688,128]{1,0:T(8,128)S(1)} %get-tuple-element.90.refs_2_.refs_1_.refs_0_, f32[2688,128]{1,0:T(8,128)S(1)} %get-tuple-element.99.refs_1_, bf16[2688,256]{1,0:T(8,128)(2,1)S(1)} %get-tuple-element.116.refs_2_, bf16[384,256]{1,0:T(8,128)(2,1)S(1)} %get-tuple-element.117.refs_3_, ...), custom_call_target="tpu_custom_call" | custom-call | tf_op jit(solution)/shard_map/pallas_call | solution.py:103
  69.2 12.6 %shard_map.327 = (f32[2688,128]{1,0:T(8,128)S(1)}, bf16[2688,256]{1,0:T(8,128)(2,1)S(1)}, bf16[384,256]{1,0:T(8,128)(2,1)S(1)}, f32[3,8,128]{2,1,0:T(8,128)S(1)}, bf16[8,224,128]{2,1,0:T(8,128)(2,1)S(1)}) custom-call(s32[2,2]{1,0:T(2,128)S(1)} %copy-done.11, f32[2688,128]{1,0:T(8,128)S(1)} %get-tuple-element.90.refs_2_.refs_1_.refs_0_, ...), custom_call_target="tpu_custom_call" | custom-call | tf_op jit(solution)/shard_map/pallas_call | solution.py:103
  82.0 4.9 %shard_map.328 = (f32[2592,128]{1,0:T(8,128)}, f32[2,128]{1,0:T(2,128)S(1)}) custom-call(f32[2688,128]{1,0:T(8,128)S(1)} %get-tuple-element.90.refs_2_.refs_1_.refs_0_, f32[2688,128]{1,0:T(8,128)S(1)} %get-tuple-element.99.refs_1_, bf16[2688,256]{1,0:T(8,128)(2,1)S(1)} %get-tuple-element.134.refs_2_, bf16[384,256]{1,0:T(8,128)(2,1)S(1)} %get-tuple-element.135.refs_3_, ...), custom_call_target="tpu_custom_call" | custom-call | tf_op jit(solution)/shard_map/pallas_call | solution.py:103
  88.3 2.1 %collective-permute-start.12 = (bf16[2,368,128]{2,1,0:T(8,128)(2,1)S(1)}, bf16[2,368,128]{2,1,0:T(8,128)(2,1)S(1)}, u32[]{:S(2)}, u32[]{:S(2)}) collective-permute-start(bf16[2,368,128]{2,1,0:T(8,128)(2,1)S(1)} %dynamic-slice_bitcast_fusion.2), channel_id=1, source_target_pairs={{0,2},{1,3},{2,0},{3,1},{4,6},{5,7},{6,4},{7,5},{8,10},{9,11},{10,... | collective-permute-start | bytes 565256 | tf_op jit(solution)/shard_map/ppermute | solution.py:600
  90.3 1.2 fusion
  91.5 4.2 %collective-permute-done.12 = bf16[2,368,128]{2,1,0:T(8,128)(2,1)S(1)} collective-permute-done((bf16[2,368,128]{2,1,0:T(8,128)(2,1)S(1)}, bf16[2,368,128]{2,1,0:T(8,128)(2,1)S(1)}, u32[]{:S(2)}, u32[]{:S(2)}) %collective-permute-start.12) | collective-permute-done | bytes 188448 | tf_op jit(solution)/shard_map/ppermute | solution.py:600
  95.8 1.8 %collective-permute-start.13 = (bf16[1,368,128]{2,1,0:T(8,128)(2,1)S(1)}, bf16[1,368,128]{2,1,0:T(8,128)(2,1)S(1)}, u32[]{:S(2)}, u32[]{:S(2)}) collective-permute-start(bf16[1,368,128]{2,1,0:T(8,128)(2,1)S(1)} %constant_dynamic-slice_fusion.1), channel_id=1, source_target_pairs={{0,4},{1,5},{2,6},{3,7},{4,0},{5,1},{6,2},{7,3},{8,12},{9,13},{10,... | collective-permute-start | bytes 282632 | tf_op jit(solution)/shard_map/ppermute | solution.py:600
  97.6 1.6 %collective-permute-start.4 = (bf16[2,464,128]{2,1,0:T(8,128)(2,1)S(1)}, bf16[2,464,128]{2,1,0:T(8,128)(2,1)S(1)}, u32[]{:S(2)}, u32[]{:S(2)}) collective-permute-start(bf16[2,464,128]{2,1,0:T(8,128)(2,1)S(1)} %dynamic-slice_bitcast_fusion.1), channel_id=1, source_target_pairs={{0,2},{1,3},{2,0},{3,1},{4,6},{5,7},{6,4},{7,5},{8,10},{9,11},{10,... | collective-permute-start | bytes 712712 | tf_op jit(solution)/shard_map/ppermute | solution.py:600
  100.4 1.9 %collective-permute-start.14 = (bf16[368,128]{1,0:T(8,128)(2,1)S(1)}, bf16[368,128]{1,0:T(8,128)(2,1)S(1)}, u32[]{:S(2)}, u32[]{:S(2)}) collective-permute-start(bf16[368,128]{1,0:T(8,128)(2,1)S(1)} %fusion.13), channel_id=1, source_target_pairs={{0,8},{8,0},{16,24},{24,16},{1,9},{9,1},{17,25},{25,17},{2,10},{10... | collective-permute-start | bytes 282632 | tf_op jit(solution)/shard_map/ppermute | solution.py:600
  102.3 2.4 %collective-permute-done.4 = bf16[2,464,128]{2,1,0:T(8,128)(2,1)S(1)} collective-permute-done((bf16[2,464,128]{2,1,0:T(8,128)(2,1)S(1)}, bf16[2,464,128]{2,1,0:T(8,128)(2,1)S(1)}, u32[]{:S(2)}, u32[]{:S(2)}) %collective-permute-start.4) | collective-permute-done | bytes 237600 | tf_op jit(solution)/shard_map/ppermute | solution.py:600
  105.4 2.7 %collective-permute-start.15 = (bf16[368,128]{1,0:T(8,128)(2,1)S(1)}, bf16[368,128]{1,0:T(8,128)(2,1)S(1)}, u32[]{:S(2)}, u32[]{:S(2)}) collective-permute-start(bf16[368,128]{1,0:T(8,128)(2,1)S(1)} %add_convert_fusion.4), channel_id=1, source_target_pairs={{0,16},{8,24},{16,0},{24,8},{1,17},{9,25},{17,1},{25,9},{2,18},{10... | collective-permute-start | bytes 282632 | tf_op jit(solution)/shard_map/ppermute | solution.py:600
  108.1 1.6 %collective-permute-done.5 = bf16[1,464,128]{2,1,0:T(8,128)(2,1)S(1)} collective-permute-done((bf16[1,464,128]{2,1,0:T(8,128)(2,1)S(1)}, bf16[1,464,128]{2,1,0:T(8,128)(2,1)S(1)}, u32[]{:S(2)}, u32[]{:S(2)}) %collective-permute-start.5) | collective-permute-done | bytes 118816 | tf_op jit(solution)/shard_map/ppermute | solution.py:600
  109.8 1.6 %collective-permute-start.6 = (bf16[464,128]{1,0:T(8,128)(2,1)S(1)}, bf16[464,128]{1,0:T(8,128)(2,1)S(1)}, u32[]{:S(2)}, u32[]{:S(2)}) collective-permute-start(bf16[464,128]{1,0:T(8,128)(2,1)S(1)} %fusion.12), channel_id=1, source_target_pairs={{0,8},{8,0},{16,24},{24,16},{1,9},{9,1},{17,25},{25,17},{2,10},{10... | collective-permute-start | bytes 356360 | tf_op jit(solution)/shard_map/ppermute | solution.py:600
  111.5 1.2 collective-permute-start.16
  112.7 2.0 %collective-permute-done.6 = bf16[464,128]{1,0:T(8,128)(2,1)S(1)} collective-permute-done((bf16[464,128]{1,0:T(8,128)(2,1)S(1)}, bf16[464,128]{1,0:T(8,128)(2,1)S(1)}, u32[]{:S(2)}, u32[]{:S(2)}) %collective-permute-start.6) | collective-permute-done | bytes 118816 | tf_op jit(solution)/shard_map/ppermute | solution.py:600
  114.7 2.7 %collective-permute-start.7 = (bf16[464,128]{1,0:T(8,128)(2,1)S(1)}, bf16[464,128]{1,0:T(8,128)(2,1)S(1)}, u32[]{:S(2)}, u32[]{:S(2)}) collective-permute-start(bf16[464,128]{1,0:T(8,128)(2,1)S(1)} %add_convert_fusion.1), channel_id=1, source_target_pairs={{0,16},{8,24},{16,0},{24,8},{1,17},{9,25},{17,1},{25,9},{2,18},{10... | collective-permute-start | bytes 356360 | tf_op jit(solution)/shard_map/ppermute | solution.py:600
  117.5 4.3 %collective-permute-done.7 = bf16[464,128]{1,0:T(8,128)(2,1)S(1)} collective-permute-done((bf16[464,128]{1,0:T(8,128)(2,1)S(1)}, bf16[464,128]{1,0:T(8,128)(2,1)S(1)}, u32[]{:S(2)}, u32[]{:S(2)}) %collective-permute-start.7) | collective-permute-done | bytes 118816 | tf_op jit(solution)/shard_map/ppermute | solution.py:600
  122.8 1.6 %collective-permute-start.17 = (bf16[2,1,368,128]{3,2,1,0:T(8,128)(2,1)S(1)}, bf16[2,1,368,128]{3,2,1,0:T(8,128)(2,1)S(1)}, u32[]{:S(2)}, u32[]{:S(2)}) collective-permute-start(bf16[2,1,368,128]{3,2,1,0:T(8,128)(2,1)S(1)} %maximum_select_fusion.10), channel_id=1, source_target_pairs={{0,2},{1,3},{2,0},{3,1},{4,6},{5,7},{6,4},{7,5},{8,10},{9,11},{10,... | collective-permute-start | bytes 565256 | tf_op jit(solution)/shard_map/ppermute | solution.py:600
  124.4 1.7 %collective-permute-done.8 = bf16[1,2,96,128]{3,2,1,0:T(8,128)(2,1)S(1)} collective-permute-done((bf16[1,2,96,128]{3,2,1,0:T(8,128)(2,1)S(1)}, bf16[1,2,96,128]{3,2,1,0:T(8,128)(2,1)S(1)}, u32[]{:S(2)}, u32[]{:S(2)}) %collective-permute-start.8) | collective-permute-done | bytes 49184 | tf_op jit(solution)/shard_map/ppermute | solution.py:600
  126.1 1.6 %collective-permute-start.9 = (bf16[2,1,2,96,128]{4,3,2,1,0:T(8,128)(2,1)S(1)}, bf16[2,1,2,96,128]{4,3,2,1,0:T(8,128)(2,1)S(1)}, u32[]{:S(2)}, u32[]{:S(2)}) collective-permute-start(bf16[2,1,2,96,128]{4,3,2,1,0:T(8,128)(2,1)S(1)} %maximum_select_fusion.14), channel_id=1, source_target_pairs={{0,2},{1,3},{2,0},{3,1},{4,6},{5,7},{6,4},{7,5},{8,10},{9,11},{10,... | collective-permute-start | bytes 294920 | tf_op jit(solution)/shard_map/ppermute | solution.py:600
  128.6 2.2 %collective-permute-done.9 = bf16[2,1,2,96,128]{4,3,2,1,0:T(8,128)(2,1)S(1)} collective-permute-done((bf16[2,1,2,96,128]{4,3,2,1,0:T(8,128)(2,1)S(1)}, bf16[2,1,2,96,128]{4,3,2,1,0:T(8,128)(2,1)S(1)}, u32[]{:S(2)}, u32[]{:S(2)}) %collective-permute-start.9) | collective-permute-done | bytes 98336 | tf_op jit(solution)/shard_map/ppermute | solution.py:600
  130.9 1.3 collective-permute-done.10
  132.6 1.4 %shard_map.329 = (f32[2,3,128,128]{3,2,1,0:T(8,128)}, f32[2,2,128]{2,1,0:T(2,128)}, f32[2,32,128]{2,1,0:T(8,128)}, f32[2,32]{1,0:T(2,128)}, f32[2,32,384]{2,1,0:...) custom-call(bf16[2,768,128]{2,1,0:T(8,128)(2,1)S(1)} %bitcast.105, ...), custom_call_target="tpu_custom_call" | custom-call | tf_op jit(solution)/shard_map/pallas_call | solution.py:103
  (106 shorter events, 11.0 us)
Async XLA Ops:
  0.7 12.9 %copy-start.18 = (bf16[2,18,5760]{2,0,1:T(2,128)(2,1)S(1)}, bf16[2,18,5760]{2,0,1:T(2,128)(2,1)}, u32[]{:S(2)}) copy-start(bf16[2,18,5760]{2,0,1:T(2,128)(2,1)} %param.21) | copy-start | bytes 1244164
  0.7 13.0 %copy-start.19 = (f32[320]{0:T(512)S(1)}, f32[320]{0:T(512)}, u32[]{:S(2)}) copy-start(f32[320]{0:T(512)} %param.37) | copy-start | bytes 3844
  0.7 13.0 %copy-start.1 = (bf16[1152,320]{0,1:T(8,128)(2,1)S(1)}, bf16[1152,320]{0,1:T(8,128)(2,1)}, u32[]{:S(2)}) copy-start(bf16[1152,320]{0,1:T(8,128)(2,1)} %param.36) | copy-start | bytes 2211844
  0.7 13.0 %copy-start.11 = (s32[2,2]{1,0:T(2,128)S(1)}, s32[2,2]{1,0:T(2,128)}, u32[]{:S(2)}) copy-start(s32[2,2]{1,0:T(2,128)} %refs_0_.7) | copy-start | bytes 52
  2.2 5.3 %collective-permute-start = (bf16[1,272,128]{2,1,0:T(8,128)(2,1)S(1)}, bf16[1,272,128]{2,1,0:T(8,128)(2,1)S(1)}, u32[]{:S(2)}, u32[]{:S(2)}) collective-permute-start(bf16[1,272,128]{2,1,0:T(8,128)(2,1)S(1)} %get-tuple-element.209), channel_id=1, source_target_pairs={{0,2},{1,3},{2,0},{3,1},{4,6},{5,7},{6,4},{7,5},{8,10},{9,11},{10,... | collective-permute-start | bytes 208904 | tf_op jit(solution)/shard_map/ppermute | solution.py:600
  7.6 5.1 %collective-permute-start.1 = (bf16[2,1,272,128]{3,2,1,0:T(8,128)(2,1)S(1)}, bf16[2,1,272,128]{3,2,1,0:T(8,128)(2,1)S(1)}, u32[]{:S(2)}, u32[]{:S(2)}) collective-permute-start(bf16[2,1,272,128]{3,2,1,0:T(8,128)(2,1)S(1)} %maximum_select_fusion.12), channel_id=1, source_target_pairs={{0,4},{1,5},{2,6},{3,7},{4,0},{5,1},{6,2},{7,3},{8,12},{9,13},{10,... | collective-permute-start | bytes 417800 | tf_op jit(solution)/shard_map/ppermute | solution.py:600
  12.7 3.7 %copy-start.3 = (bf16[2,36,36,128]{3,0,2,1:T(2,128)(2,1)S(1)}, bf16[2,36,36,128]{3,0,2,1:T(2,128)(2,1)}, u32[]{:S(2)}) copy-start(bf16[2,36,36,128]{3,0,2,1:T(2,128)(2,1)} %param.19) | copy-start | bytes 1990660
  12.7 3.7 %copy-start.6 = (f32[2,128,32]{1,2,0:T(8,128)S(1)}, f32[2,128,32]{1,2,0:T(8,128)}, u32[]{:S(2)}) copy-start(f32[2,128,32]{1,2,0:T(8,128)} %param.24) | copy-start | bytes 98308
  12.7 3.7 %copy-start.7 = (f32[2,32,384]{2,1,0:T(8,128)S(1)}, f32[2,32,384]{2,1,0:T(8,128)}, u32[]{:S(2)}) copy-start(f32[2,32,384]{2,1,0:T(8,128)} %refs_4_.1) | copy-start | bytes 294916
  12.7 3.7 %copy-start.8 = (f32[2,2,128]{2,1,0:T(2,128)S(1)}, f32[2,2,128]{2,1,0:T(2,128)}, u32[]{:S(2)}) copy-start(f32[2,2,128]{2,1,0:T(2,128)} %refs_8_.5) | copy-start | bytes 6148
  12.7 3.7 %copy-start.9 = (f32[2,2,128]{2,1,0:T(2,128)S(1)}, f32[2,2,128]{2,1,0:T(2,128)}, u32[]{:S(2)}) copy-start(f32[2,2,128]{2,1,0:T(2,128)} %refs_20_.5) | copy-start | bytes 6148
  12.8 3.7 %copy-start.10 = (f32[2,2,128]{2,1,0:T(2,128)S(1)}, f32[2,2,128]{2,1,0:T(2,128)}, u32[]{:S(2)}) copy-start(f32[2,2,128]{2,1,0:T(2,128)} %refs_26_.3) | copy-start | bytes 6148
  13.6 13.6 %collective-permute-start.2 = (bf16[2,2,1,272,128]{4,3,1,2,0:T(8,128)(2,1)}, bf16[2,2,1,272,128]{4,3,1,2,0:T(8,128)(2,1)}, u32[]{:S(2)}, u32[]{:S(2)}) collective-permute-start(bf16[2,2,1,272,128]{4,3,1,2,0:T(8,128)(2,1)} %maximum_select_fusion.6), channel_id=1, source_target_pairs={{0,1},{1,0},{2,3},{3,2},{4,5},{5,4},{6,7},{7,6},{8,9},{9,8},{10,11... | collective-permute-start | bytes 835592 | tf_op jit(solution)/shard_map/ppermute | solution.py:600
  16.5 10.7 %copy-start.17 = (bf16[2,1,272,128]{3,2,1,0:T(8,128)(2,1)S(1)}, bf16[2,1,272,128]{3,2,1,0:T(8,128)(2,1)}, u32[]{:S(2)}) copy-start(bf16[2,1,272,128]{3,2,1,0:T(8,128)(2,1)} %copy-done.16) | copy-start | bytes 417796
  51.3 14.1 %copy-start.4 = (bf16[2,18,5760]{2,1,0:T(8,128)(2,1)}, bf16[2,18,5760]{2,1,0:T(8,128)(2,1)S(1)}, u32[]{:S(2)}) copy-start(bf16[2,18,5760]{2,1,0:T(8,128)(2,1)S(1)} %get-tuple-element.180) | copy-start | bytes 1244164
  52.1 35.0 %collective-permute-start.11 = (bf16[4,368,128]{2,1,0:T(8,128)(2,1)}, bf16[4,368,128]{2,1,0:T(8,128)(2,1)}, u32[]{:S(2)}, u32[]{:S(2)}) collective-permute-start(bf16[4,368,128]{2,1,0:T(8,128)(2,1)} %dynamic-slice_bitcast_fusion), channel_id=1, source_target_pairs={{0,1},{1,0},{2,3},{3,2},{4,5},{5,4},{6,7},{7,6},{8,9},{9,8},{10,11... | collective-permute-start | bytes 1130504 | tf_op jit(solution)/shard_map/ppermute | solution.py:600
  87.0 3.3 %collective-permute-start.3 = (bf16[4,464,128]{2,1,0:T(8,128)(2,1)S(1)}, bf16[4,464,128]{2,1,0:T(8,128)(2,1)}, u32[]{:S(2)}, u32[]{:S(2)}) collective-permute-start(bf16[4,464,128]{2,1,0:T(8,128)(2,1)S(1)} %fusion.5), channel_id=1, source_target_pairs={{0,1},{1,0},{2,3},{3,2},{4,5},{5,4},{6,7},{7,6},{8,9},{9,8},{10,11... | collective-permute-start | bytes 1425416 | tf_op jit(solution)/shard_map/ppermute | solution.py:600
  88.3 10.9 %copy-start.5 = (bf16[2,18,5760]{2,1,0:T(8,128)(2,1)S(1)}, bf16[2,18,5760]{2,1,0:T(8,128)(2,1)}, u32[]{:S(2)}) copy-start(bf16[2,18,5760]{2,1,0:T(8,128)(2,1)} %copy-done.4) | copy-start | bytes 1244164
  88.3 7.4 %collective-permute-start.12 = (bf16[2,368,128]{2,1,0:T(8,128)(2,1)S(1)}, bf16[2,368,128]{2,1,0:T(8,128)(2,1)S(1)}, u32[]{:S(2)}, u32[]{:S(2)}) collective-permute-start(bf16[2,368,128]{2,1,0:T(8,128)(2,1)S(1)} %dynamic-slice_bitcast_fusion.2), channel_id=1, source_target_pairs={{0,2},{1,3},{2,0},{3,1},{4,6},{5,7},{6,4},{7,5},{8,10},{9,11},{10,... | collective-permute-start | bytes 565256 | tf_op jit(solution)/shard_map/ppermute | solution.py:600
  95.8 4.6 %collective-permute-start.13 = (bf16[1,368,128]{2,1,0:T(8,128)(2,1)S(1)}, bf16[1,368,128]{2,1,0:T(8,128)(2,1)S(1)}, u32[]{:S(2)}, u32[]{:S(2)}) collective-permute-start(bf16[1,368,128]{2,1,0:T(8,128)(2,1)S(1)} %constant_dynamic-slice_fusion.1), channel_id=1, source_target_pairs={{0,4},{1,5},{2,6},{3,7},{4,0},{5,1},{6,2},{7,3},{8,12},{9,13},{10,... | collective-permute-start | bytes 282632 | tf_op jit(solution)/shard_map/ppermute | solution.py:600
  97.6 7.1 %collective-permute-start.4 = (bf16[2,464,128]{2,1,0:T(8,128)(2,1)S(1)}, bf16[2,464,128]{2,1,0:T(8,128)(2,1)S(1)}, u32[]{:S(2)}, u32[]{:S(2)}) collective-permute-start(bf16[2,464,128]{2,1,0:T(8,128)(2,1)S(1)} %dynamic-slice_bitcast_fusion.1), channel_id=1, source_target_pairs={{0,2},{1,3},{2,0},{3,1},{4,6},{5,7},{6,4},{7,5},{8,10},{9,11},{10,... | collective-permute-start | bytes 712712 | tf_op jit(solution)/shard_map/ppermute | solution.py:600
  100.4 4.9 %collective-permute-start.14 = (bf16[368,128]{1,0:T(8,128)(2,1)S(1)}, bf16[368,128]{1,0:T(8,128)(2,1)S(1)}, u32[]{:S(2)}, u32[]{:S(2)}) collective-permute-start(bf16[368,128]{1,0:T(8,128)(2,1)S(1)} %fusion.13), channel_id=1, source_target_pairs={{0,8},{8,0},{16,24},{24,16},{1,9},{9,1},{17,25},{25,17},{2,10},{10... | collective-permute-start | bytes 282632 | tf_op jit(solution)/shard_map/ppermute | solution.py:600
  104.8 4.9 %collective-permute-start.5 = (bf16[1,464,128]{2,1,0:T(8,128)(2,1)S(1)}, bf16[1,464,128]{2,1,0:T(8,128)(2,1)S(1)}, u32[]{:S(2)}, u32[]{:S(2)}) collective-permute-start(bf16[1,464,128]{2,1,0:T(8,128)(2,1)S(1)} %constant_dynamic-slice_fusion.2), channel_id=1, source_target_pairs={{0,4},{1,5},{2,6},{3,7},{4,0},{5,1},{6,2},{7,3},{8,12},{9,13},{10,... | collective-permute-start | bytes 356360 | tf_op jit(solution)/shard_map/ppermute | solution.py:600
  105.4 6.0 %collective-permute-start.15 = (bf16[368,128]{1,0:T(8,128)(2,1)S(1)}, bf16[368,128]{1,0:T(8,128)(2,1)S(1)}, u32[]{:S(2)}, u32[]{:S(2)}) collective-permute-start(bf16[368,128]{1,0:T(8,128)(2,1)S(1)} %add_convert_fusion.4), channel_id=1, source_target_pairs={{0,16},{8,24},{16,0},{24,8},{1,17},{9,25},{17,1},{25,9},{2,18},{10... | collective-permute-start | bytes 282632 | tf_op jit(solution)/shard_map/ppermute | solution.py:600
  109.8 4.9 %collective-permute-start.6 = (bf16[464,128]{1,0:T(8,128)(2,1)S(1)}, bf16[464,128]{1,0:T(8,128)(2,1)S(1)}, u32[]{:S(2)}, u32[]{:S(2)}) collective-permute-start(bf16[464,128]{1,0:T(8,128)(2,1)S(1)} %fusion.12), channel_id=1, source_target_pairs={{0,8},{8,0},{16,24},{24,16},{1,9},{9,1},{17,25},{25,17},{2,10},{10... | collective-permute-start | bytes 356360 | tf_op jit(solution)/shard_map/ppermute | solution.py:600
  111.5 6.0 %collective-permute-start.16 = (bf16[1,368,128]{2,1,0:T(8,128)(2,1)S(1)}, bf16[1,368,128]{2,1,0:T(8,128)(2,1)S(1)}, u32[]{:S(2)}, u32[]{:S(2)}) collective-permute-start(bf16[1,368,128]{2,1,0:T(8,128)(2,1)S(1)} %get-tuple-element.201), channel_id=1, source_target_pairs={{0,4},{1,5},{2,6},{3,7},{4,0},{5,1},{6,2},{7,3},{8,12},{9,13},{10,... | collective-permute-start | bytes 282632 | tf_op jit(solution)/shard_map/ppermute | solution.py:600
  114.7 7.1 %collective-permute-start.7 = (bf16[464,128]{1,0:T(8,128)(2,1)S(1)}, bf16[464,128]{1,0:T(8,128)(2,1)S(1)}, u32[]{:S(2)}, u32[]{:S(2)}) collective-permute-start(bf16[464,128]{1,0:T(8,128)(2,1)S(1)} %add_convert_fusion.1), channel_id=1, source_target_pairs={{0,16},{8,24},{16,0},{24,8},{1,17},{9,25},{17,1},{25,9},{2,18},{10... | collective-permute-start | bytes 356360 | tf_op jit(solution)/shard_map/ppermute | solution.py:600
  121.9 4.2 %collective-permute-start.8 = (bf16[1,2,96,128]{3,2,1,0:T(8,128)(2,1)S(1)}, bf16[1,2,96,128]{3,2,1,0:T(8,128)(2,1)S(1)}, u32[]{:S(2)}, u32[]{:S(2)}) collective-permute-start(bf16[1,2,96,128]{3,2,1,0:T(8,128)(2,1)S(1)} %get-tuple-element.205), channel_id=1, source_target_pairs={{0,4},{1,5},{2,6},{3,7},{4,0},{5,1},{6,2},{7,3},{8,12},{9,13},{10,... | collective-permute-start | bytes 147464 | tf_op jit(solution)/shard_map/ppermute | solution.py:600
  122.8 5.6 %collective-permute-start.17 = (bf16[2,1,368,128]{3,2,1,0:T(8,128)(2,1)S(1)}, bf16[2,1,368,128]{3,2,1,0:T(8,128)(2,1)S(1)}, u32[]{:S(2)}, u32[]{:S(2)}) collective-permute-start(bf16[2,1,368,128]{3,2,1,0:T(8,128)(2,1)S(1)} %maximum_select_fusion.10), channel_id=1, source_target_pairs={{0,2},{1,3},{2,0},{3,1},{4,6},{5,7},{6,4},{7,5},{8,10},{9,11},{10,... | collective-permute-start | bytes 565256 | tf_op jit(solution)/shard_map/ppermute | solution.py:600
  126.1 4.7 %collective-permute-start.9 = (bf16[2,1,2,96,128]{4,3,2,1,0:T(8,128)(2,1)S(1)}, bf16[2,1,2,96,128]{4,3,2,1,0:T(8,128)(2,1)S(1)}, u32[]{:S(2)}, u32[]{:S(2)}) collective-permute-start(bf16[2,1,2,96,128]{4,3,2,1,0:T(8,128)(2,1)S(1)} %maximum_select_fusion.14), channel_id=1, source_target_pairs={{0,2},{1,3},{2,0},{3,1},{4,6},{5,7},{6,4},{7,5},{8,10},{9,11},{10,... | collective-permute-start | bytes 294920 | tf_op jit(solution)/shard_map/ppermute | solution.py:600
  128.5 3.9 %collective-permute-start.18 = (bf16[2,2,1,368,128]{4,3,1,2,0:T(8,128)(2,1)S(1)}, bf16[2,2,1,368,128]{4,3,1,2,0:T(8,128)(2,1)S(1)}, u32[]{:S(2)}, u32[]{:S(2)}) collective-permute-start(bf16[2,2,1,368,128]{4,3,1,2,0:T(8,128)(2,1)S(1)} %maximum_select_fusion.4), channel_id=1, source_target_pairs={{0,1},{1,0},{2,3},{3,2},{4,5},{5,4},{6,7},{7,6},{8,9},{9,8},{10,11... | collective-permute-start | bytes 1130504 | tf_op jit(solution)/shard_map/ppermute | solution.py:600
  130.8 1.5 %collective-permute-start.10 = (bf16[2,2,1,2,96,128]{5,4,3,1,2,0:T(8,128)(2,1)S(1)}, bf16[2,2,1,2,96,128]{5,4,3,1,2,0:T(8,128)(2,1)S(1)}, u32[]{:S(2)}, u32[]{:S(2)}) collective-permute-start(bf16[2,2,1,2,96,128]{5,4,3,1,2,0:T(8,128)(2,1)S(1)} %maximum_select_fusion.8), channel_id=1, source_target_pairs={{0,1},{1,0},{2,3},{3,2},{4,5},{5,4},{6,7},{7,6},{8,9},{9,8},{10,11... | collective-permute-start | bytes 589832 | tf_op jit(solution)/shard_map/ppermute | solution.py:600
  (7 other events, 20.4 us)

commit v3 on v2

--- a/solution.py
+++ b/solution.py
@@ -9,19 +9,25 @@
 
 F32 = jnp.float32
 BF16 = jnp.bfloat16
-PRECISE = lax.Precision.HIGHEST
 GROUP = 8
 MIB = 2**20
 
 
-def dot(a, b, dims=(1, 0), precision=None):
-    return lax.dot_general(
-        a, b, (((dims[0],), (dims[1],)), ((), ())), precision=precision, preferred_element_type=F32
-    )
+def dot(a, b, dims=(1, 0)):
+    return lax.dot_general(a, b, (((dims[0],), (dims[1],)), ((), ())), preferred_element_type=F32)
+
+
+def halves(v):
+    high = v.astype(BF16)
+    return high, (v - high.astype(F32)).astype(BF16)
 
 
 def fine(a, b, dims=(1, 0)):
-    return dot(a, b, dims, PRECISE)
+    high, low = halves(a)
+    if b.dtype == BF16:
+        return dot(high, b, dims) + dot(low, b, dims)
+    b_high, b_low = halves(b)
+    return dot(high, b_high, dims) + (dot(low, b_high, dims) + dot(high, b_low, dims))
 
 
 def rows8(v):
@@ -89,9 +95,12 @@
     pass
 
 
-def call(body, ins, outs, scratch, limit, smem=()):
+def call(body, ins, outs, scratch, limit, micros, smem=(), after=None):
+    if after is not None:
+        ins = dict(ins, after=after)
     vmem = pl.BlockSpec(memory_space=pltpu.VMEM)
     scalar = pl.BlockSpec(memory_space=pltpu.SMEM)
+    waits = dict(after=0)
     names = list(ins) + list(outs) + list(scratch)
 
     def kernel(*refs):
@@ -103,10 +112,11 @@
     found = pl.pallas_call(
         kernel,
         out_shape=list(outs.values()),
-        in_specs=[scalar if name in smem else vmem for name in ins],
+        in_specs=[scalar if name in smem else (pl.BlockSpec(memory_space=pl.ANY) if name in waits else vmem) for name in ins],
         out_specs=[vmem] * len(outs),
         scratch_shapes=list(scratch.values()),
         compiler_params=pltpu.CompilerParams(vmem_limit_bytes=limit * MIB),
+        cost_estimate=pl.CostEstimate(flops=int(micros * 1.15e9), bytes_accessed=0, transcendentals=0),
     )(*ins.values())
     return dict(zip(outs, found))
 
@@ -170,14 +180,22 @@
     def step(row, carry):
         at = pl.ds(pl.multiple_of(row * z.W, 8), z.W)
         r.mask[at, :] = jnp.where(high > row, inside, 0.0)
+        return carry
+
+    lax.fori_loop(0, z.side, step, 0)
+    edge = jnp.concatenate([edge, edge], axis=0).astype(BF16)
+    back = jnp.concatenate([back, back], axis=0).astype(BF16)
+
+    def step2(row, carry):
+        at = pl.ds(pl.multiple_of(row * 2 * z.W, 16), 2 * z.W)
         r.edge[at, :] = edge
         r.back[at, :] = back
         return carry
 
-    lax.fori_loop(0, z.side, step, 0)
+    lax.fori_loop(0, z.side // 2, step2, 0)
     pad = jnp.zeros((z.N - z.N0, z.C), F32)
     for ref in (r.mask, r.edge, r.back):
-        ref[z.N0 :, :] = pad
+        ref[z.N0 :, :] = pad.astype(ref.dtype)
     pad = jnp.zeros((z.hp - z.half, z.O), F32)
     r.pgrad[z.M :, :] = jnp.zeros((8, 9 * z.C), F32)
     sums = jnp.zeros((8, z.O), F32)
@@ -210,6 +228,7 @@
                 start = down * z.W + (2 * b + right) * z.I + i
                 r.grad[pl.ds(start, z.hp, stride=2 * z.W), :] = plane
     r.merge_bias_sums[...] = sums
+    r.token[...] = jnp.zeros_like(r.token)
 
 
 def shift_phase(z, r, cat):
@@ -222,7 +241,7 @@
         high = jnp.where(kind == 2, near(r.normed, start, -z.W, z.CH), near(r.normed, start, z.W, z.CH))
         wide = jnp.where(kind == 2, near(r.normed, start, -z.I, z.CH), near(r.normed, start, z.I, z.CH))
         high = jnp.where(kind == 0, mid, high).astype(BF16)
-        wide = jnp.where(kind == 0, mid, wide * r.edge[rows, :]).astype(BF16)
+        wide = jnp.where(kind == 0, mid, wide * r.edge[rows, :].astype(F32)).astype(BF16)
         mask = r.mask[rows, :]
         for j, piece in enumerate((high, wide, mid.astype(BF16))):
             cat[rows, j * z.C : (j + 1) * z.C] = piece
@@ -245,7 +264,7 @@
     for j in range(3):
         pool = split(z, r.sums[j])
         o.pool[j] = pool
-        pooled = pooled + fine(pool, r.mix_weight[l, j].astype(F32)) / counts
+        pooled = pooled + fine(pool, r.mix_weight[l, j]) / counts
     o.pooled[...] = pooled
     act, slope = gelu_pair(fine(pooled, r.squeeze_weight[l], (1, 1)) + r.squeeze_bias[l : l + 1])
     o.act[...] = act
@@ -275,8 +294,8 @@
         token = dot(mixed, r.project_weight[l]) + r.project_bias[l : l + 1]
         halfway = r.state[rows, :] + r.mask[rows, :] * token
         unit, rstd = norm_parts(halfway, ones)
-        o.unit2[rows, :] = unit
-        o.rstd2[rows, :] = rstd
+        o.unit2[rows, :] = unit.astype(BF16)
+        o.rstd2[rows, :] = rstd.astype(BF16)
         o.normed2[rows, :] = (unit * gain + shift).astype(BF16)
         r.state[rows, :] = halfway
 
@@ -285,8 +304,8 @@
 
 def norm_store(z, r, l, o, rows, at, state):
     unit, rstd = norm_parts(state, mean_matrix(z))
-    o.unit1[rows, :] = unit
-    o.rstd1[rows, :] = rstd
+    o.unit1[rows, :] = unit.astype(BF16)
+    o.rstd1[rows, :] = rstd.astype(BF16)
     r.normed[pl.ds(z.base + at, z.CH), :] = unit * r.norm_gain[l, 0:1] + r.norm_bias[l, 0:1]
 
 
@@ -311,8 +330,8 @@
 
 def saved_early(z):
     return dict(
-        unit1=kept(z.N, z.C), rstd1=kept(z.N, z.C), cat=kept(z.N, 3 * z.C, dtype=BF16), mixed=kept(z.N, z.C, dtype=BF16),
-        unit2=kept(z.N, z.C), rstd2=kept(z.N, z.C), normed2=kept(z.N, z.C, dtype=BF16), pool=kept(3, GROUP, z.C),
+        unit1=kept(z.N, z.C, dtype=BF16), rstd1=kept(z.N, z.C, dtype=BF16), cat=kept(z.N, 3 * z.C, dtype=BF16), mixed=kept(z.N, z.C, dtype=BF16),
+        unit2=kept(z.N, z.C, dtype=BF16), rstd2=kept(z.N, z.C, dtype=BF16), normed2=kept(z.N, z.C, dtype=BF16), pool=kept(3, GROUP, z.C),
         pooled=kept(GROUP, z.C), act=kept(GROUP, z.R), slope=kept(GROUP, z.R), share=kept(3, GROUP, z.C),
     )
 
@@ -325,7 +344,7 @@
     spots = lax.broadcasted_iota(jnp.int32, (3 * z.C, 3 * z.C), 0)
     ends = lax.broadcasted_iota(jnp.int32, (3 * z.C, 3 * z.C), 1)
     kind = jnp.where(ends >= 2 * z.C, 2, jnp.where(ends >= z.C, 1, 0))
-    r.perm[...] = jnp.where(spots == 3 * (ends - kind * z.C) + kind, 1.0, 0.0)
+    r.perm[...] = jnp.where(spots == 3 * (ends - kind * z.C) + kind, 1.0, 0.0).astype(BF16)
     for l in range(z.L):
         r.ewp[l] = fine(r.expand_weight[l], r.perm[...])
     r.ebp[...] = fine(r.expand_bias[...], r.perm[...])
@@ -350,19 +369,38 @@
     shift_phase(z, r, r.cat)
     weigh_phase(z, r, 0, r)
     mix_phase(z, r, 0, r)
+    r.token[...] = jnp.zeros_like(r.token)
+
+
+def rank(z, e):
+    at, half = 0, z.parts // 2
+    while half:
+        at, e, half = at + half * (e % 2), e // 2, half // 2
+    return at
+
+
+def put_blocks(z, me, rows, size, here, away, start=0):
+    half = z.parts // 2
+    for e in range(z.parts):
+        at = rank(z, e)
+        block = rows[pl.ds(pl.multiple_of((me ^ e) * size, 16), size), :]
+        if at < half:
+            here[at, start : start + size, :] = block
+        else:
+            away[at - half, start : start + size, :] = block
 
 
 def second_kernel(z, r):
-    for h in range(z.parts):
+    me = r.place[0]
+    for k, e in enumerate(z.found):
+        at = pl.multiple_of((me ^ e) * z.units, z.units)
         for l in range(z.L):
-            at = h * z.units
-            r.inner[l, at : at + z.units, :] = r.gathered[h, 2 * l * z.units : (2 * l + 1) * z.units, :]
-            r.outer[l, at : at + z.units, :] = r.gathered[h, (2 * l + 1) * z.units : (2 * l + 2) * z.units, :]
+            r.inner[l, pl.ds(at, z.units), :] = r.gathered[k, 2 * l * z.units : (2 * l + 1) * z.units, :]
+            r.outer[l, pl.ds(at, z.units), :] = r.gathered[k, (2 * l + 1) * z.units : (2 * l + 2) * z.units, :]
+        at = 2 * z.L * z.units
+        r.bias_rows[me ^ e] = r.gathered[k, at : at + 16, :].astype(F32)
     for l in range(z.L):
-        row = 2 * z.L * z.units + l
-        r.inner_bias[l : l + 1] = jnp.concatenate(
-            [r.gathered[h, row : row + 1, : z.units].astype(F32) for h in range(z.parts)], axis=1
-        )
+        r.inner_bias[l : l + 1] = jnp.concatenate([r.bias_rows[h, l : l + 1, : z.units] for h in range(z.parts)], axis=1)
     early, late = [Refs() for _ in range(z.L)], [Refs() for _ in range(z.L)]
     for l in range(z.L):
         early[l].normed2 = r.normed2_0 if l == 0 else r.normed2
@@ -412,15 +450,14 @@
     rows += [jnp.concatenate([bias[:, 2 * z.C :], jnp.zeros((1, z.C - rest), F32)], axis=1)]
     rows += [jnp.zeros((z.parts * z.merge - 9 * z.O - 3, z.C), F32)]
     r.merge_rows[9 * z.O :, :] = jnp.concatenate(rows, axis=0).astype(BF16)
+    put_blocks(z, me, r.merge_rows, z.merge, r.merge_here, r.merge_away)
 
 
 def feed_back_kernel(z, l, r):
     ones = mean_matrix(z)
     gain = r.norm_gain[l, 1:2]
-    sums = (r.vec, r.inner_sums, r.g_outer, r.g_inner, r.g_project, r.g_mix)
-    for ref in sums:
+    for ref in (r.vec, r.inner_sums, r.g_outer, r.g_inner):
         ref[...] = jnp.zeros_like(ref)
-    even, odd = tile(parity(z, 0), z.CH), tile(parity(z, 1), z.CH)
 
     def body(rows, at):
         mask = r.mask[rows, :]
@@ -432,16 +469,35 @@
         r.g_outer[...] += dot(out, r.act_rows[rows, :], (0, 0))
         r.g_inner[...] += dot(r.normed2[rows, :], pre, (0, 0))
         normed_grad = dot(pre, r.inner[l])
-        unit = r.unit2[rows, :]
+        unit = r.unit2[rows, :].astype(F32)
         r.vec[1] += rows8(normed_grad * unit)
         r.vec[2] += rows8(normed_grad)
-        grad = grad + norm_back(normed_grad, unit, r.rstd2[rows, :], gain, ones)
-        r.half_grad[rows, :] = grad
-        token = (grad * mask).astype(BF16)
-        r.vec[3] += rows8(token.astype(F32))
+        r.half_grad[rows, :] = grad + norm_back(normed_grad, unit, r.rstd2[rows, :].astype(F32), gain, ones)
+
+    over(z, body)
+    inner = total(r.inner_sums[...])
+    small = [total(r.vec[k]) for k in range(3)]
+    small += [inner[:, k * z.C : (k + 1) * z.C] for k in range(z.H // z.C)]
+    small += [jnp.zeros((1, z.C), F32)]
+    r.feed_small[...] = jnp.concatenate(small, axis=0)
+    r.turned[0] = r.g_inner[...].T.astype(BF16)
+    r.turned[1] = r.g_outer[...].T.astype(BF16)
+    for k in range(2):
+        put_blocks(z, r.place[0], r.turned.at[k], z.units, r.here, r.away, k * z.units)
+    r.token[...] = jnp.zeros_like(r.token)
+
+
+def token_back_kernel(z, l, r):
+    for ref in (r.vec, r.g_project, r.g_mix):
+        ref[...] = jnp.zeros_like(ref)
+    even, odd = tile(parity(z, 0), z.CH), tile(parity(z, 1), z.CH)
+
+    def body(rows, at):
+        token = (r.half_grad[rows, :] * r.mask[rows, :]).astype(BF16)
+        r.vec[0] += rows8(token.astype(F32))
         r.g_project[...] += dot(r.mixed[rows, :], token, (0, 0))
         mixed_grad = dot(token, r.project_weight[l], (1, 1))
-        r.vec[4] += rows8(mixed_grad)
+        r.vec[1] += rows8(mixed_grad)
         both = jnp.concatenate([(mixed_grad * even).astype(BF16), (mixed_grad * odd).astype(BF16)], axis=1)
         r.mixed_grad[rows, :] = both
         r.g_mix[...] += dot(both, r.cat[rows, :], (0, 0))
@@ -449,7 +505,7 @@
     over(z, body)
     counts = counts_of(z, r)
     zeros = jnp.zeros((GROUP - z.I, z.C), F32)
-    summed = split(z, r.vec[4])
+    summed = split(z, r.vec[1])
     share = [r.share[j] for j in range(3)]
     mix, dp = [], []
     for j in range(3):
@@ -477,7 +533,7 @@
     push = dpool / counts
     for j in range(3):
         mix[j] += fine(r.pool[j], push, (0, 0))
-        r.push[j] = weave(z, fine(push, r.mix_weight[l, j].astype(F32), (1, 1)))
+        r.push[j] = weave(z, fine(push, r.mix_weight[l, j], (1, 1)))
     for j in range(3):
         r.rows[j * z.C : (j + 1) * z.C, :] = mix[j].astype(BF16)
     r.rows[z.at_project : z.at_expand, :] = r.g_project[...].astype(BF16)
@@ -485,20 +541,15 @@
         at = z.at_expand + j * z.R
         r.rows[at : at + z.R, :] = expand[:, j * z.C : (j + 1) * z.C].astype(BF16)
     r.rows[z.at_squeeze : z.at_small, :] = squeeze.astype(BF16)
-    inner = total(r.inner_sums[...])
     small = [total(share[j] * summed + dpool) for j in range(2)]
-    small += [total(r.vec[k]) for k in (3, 0, 1, 2)]
-    small += [inner[:, k * z.C : (k + 1) * z.C] for k in range(z.H // z.C)]
+    small += [total(r.vec[0]), r.feed_small[: 3 + z.H // z.C, :]]
     small += [expand_bias[:, j * z.C : (j + 1) * z.C] for j in range(3)]
     small += [jnp.concatenate([total(dact), jnp.zeros((1, z.C - z.R), F32)], axis=1)]
-    small += [jnp.zeros((z.parts * z.shared - z.at_small - len(small), z.C), F32)]
+    used = sum(row.shape[0] for row in small)
+    small += [jnp.zeros((z.parts * z.shared - z.at_small - used, z.C), F32)]
     r.rows[z.at_small :, :] = jnp.concatenate(small, axis=0).astype(BF16)
-    inner, outer = r.g_inner[...].T, r.g_outer[...].T
-    u = z.units
-    for h in range(z.parts):
-        r.blocks[h, :u, :] = inner[h * u : (h + 1) * u].astype(BF16)
-        r.blocks[h, u : 2 * u, :] = outer[h * u : (h + 1) * u].astype(BF16)
-        r.blocks[h, 2 * u :, :] = r.rows[h * z.shared : (h + 1) * z.shared, :]
+    put_blocks(z, r.place[0], r.rows, z.shared, r.here, r.away)
+    r.token[...] = jnp.zeros_like(r.token)
 
 
 def mix_back_kernel(z, l, last, r):
@@ -523,12 +574,12 @@
         high = jnp.where(kind == 2, near(r.back_h, start, z.W, z.CH), near(r.back_h, start, -z.W, z.CH))
         wide = jnp.where(kind == 2, near(r.back_w, start, z.I, z.CH), near(r.back_w, start, -z.I, z.CH))
         high = jnp.where(kind == 0, near(r.back_h, start, 0, z.CH), high)
-        wide = jnp.where(kind == 0, near(r.back_w, start, 0, z.CH), wide * r.back[rows, :])
+        wide = jnp.where(kind == 0, near(r.back_w, start, 0, z.CH), wide * r.back[rows, :].astype(F32))
         grad = high + wide + near(r.back_c, start, 0, z.CH)
-        unit = r.unit1[rows, :]
+        unit = r.unit1[rows, :].astype(F32)
         r.vec[0] += rows8(grad * unit)
         r.vec[1] += rows8(grad)
-        grad = r.half_grad[rows, :] + norm_back(grad, unit, r.rstd1[rows, :], gain, ones)
+        grad = r.half_grad[rows, :] + norm_back(grad, unit, r.rstd1[rows, :].astype(F32), gain, ones)
         if not last:
             r.state_grad[rows, :] = grad
             return
@@ -547,6 +598,7 @@
     stray = r.back_h[z.base + z.N0 - z.W : z.base + z.N0, :]
     r.vec[1] -= rows8(jnp.where(kinds(z, z.W) == 1, stray, 0.0))
     r.first_norm[...] = jnp.concatenate([total(r.vec[0]), total(r.vec[1])], axis=0)
+    r.token[...] = jnp.zeros_like(r.token)
 
 
 def final_outputs(z):
@@ -554,15 +606,27 @@
         mix_weight=arr(z.L, 3, z.C, z.C), mix_bias=arr(z.L, 2, z.C), squeeze_weight=arr(z.L, z.R, z.C),
         squeeze_bias=arr(z.L, z.R), expand_weight=arr(z.L, z.R, 3 * z.C), expand_bias=arr(z.L, 3 * z.C),
         project_weight=arr(z.L, z.C, z.C), project_bias=arr(z.L, z.C), norm_gain=arr(z.L, 2, z.C),
-        norm_bias=arr(z.L, 2, z.C), inner_weight=arr(z.L, z.units, z.C), inner_bias=arr(z.L, z.H),
+        norm_bias=arr(z.L, 2, z.C), inner_weight=arr(z.L, z.units, z.C), inner_bias=arr(z.L, z.units),
         outer_weight=arr(z.L, z.units, z.C), outer_bias=arr(z.L, z.C), merge_weight=arr(z.O, 9 * z.C),
         merge_bias=arr(1, z.O),
     )
 
 
 def last_kernel(z, r):
+    me = r.place[0]
+    half = z.parts // 2
+    size = z.shared
+    for at in range(z.parts):
+        spot = me ^ z.ranks[at]
+        have, merge = (r.have, r.merge_have) if at < half else (r.got, r.merge_got)
+        k = at % half
+        rows = pl.ds(pl.multiple_of(spot * z.shared, 16), z.shared)
+        r.rows[0, rows, :] = have[k * size : (k + 1) * size, :]
+        r.rows[1, rows, :] = merge[k, :size, :]
+        r.merge_rows[pl.ds(pl.multiple_of(spot * z.merge, 16), z.merge), :] = merge[k, size:, :]
+    norms = r.have[half * size :, :].astype(F32) + r.got[half * size :, :].astype(F32)
     for l in range(z.L):
-        rows = r.shared_rows.at[l]
+        rows = r.rows.at[l]
 
         def get(at, count):
             return rows[at : at + count, :].astype(F32)
@@ -576,18 +640,23 @@
         r.mix_bias[l] = small[0:2]
         r.project_bias[l : l + 1] = small[2:3]
         r.outer_bias[l : l + 1] = small[3:4]
-        r.norm_gain[l] = jnp.concatenate([r.norms[2 * l : 2 * l + 1, :].astype(F32), small[4:5]], axis=0)
-        r.norm_bias[l] = jnp.concatenate([r.norms[2 * l + 1 : 2 * l + 2, :].astype(F32), small[5:6]], axis=0)
+        r.norm_gain[l] = jnp.concatenate([norms[2 * l : 2 * l + 1], small[4:5]], axis=0)
+        r.norm_bias[l] = jnp.concatenate([norms[2 * l + 1 : 2 * l + 2], small[5:6]], axis=0)
         at = 6
+        inner = jnp.zeros((1, z.units), F32)
         for k in range(z.H // z.C):
-            r.inner_bias[l : l + 1, k * z.C : (k + 1) * z.C] = small[at : at + 1]
+            for c in range(0, z.C, z.units):
+                mine = jnp.where(me == (k * z.C + c) // z.units, 1.0, 0.0)
+                inner = inner + small[at : at + 1, c : c + z.units] * mine
             at += 1
+        r.inner_bias[l : l + 1] = inner
         for j in range(3):
             r.expand_bias[l : l + 1, j * z.C : (j + 1) * z.C] = small[at : at + 1]
             at += 1
         r.squeeze_bias[l : l + 1] = small[at : at + 1, : z.R]
-        r.inner_weight[l] = r.feed_rows[l, : z.units, :].astype(F32)
-        r.outer_weight[l] = r.feed_rows[l, z.units :, :].astype(F32)
+        feed = r.feed_rows[2 * l * z.units : 2 * (l + 1) * z.units, :].astype(F32)
+        r.inner_weight[l] = feed[: z.units]
+        r.outer_weight[l] = feed[z.units :]
     for k in range(9):
         r.merge_weight[:, k * z.C : (k + 1) * z.C] = r.merge_rows[k * z.O : (k + 1) * z.O, :].astype(F32)
     small = r.merge_rows[9 * z.O : 9 * z.O + 16, :].astype(F32)
@@ -596,6 +665,18 @@
     r.merge_bias[:, 2 * z.C :] = small[2:3, : z.O - 2 * z.C]
 
 
+def pack_kernel(z, r):
+    u = z.units
+    for l in range(z.L):
+        r.block[2 * l * u : (2 * l + 1) * u, :] = r.inner_weight[l]
+        r.block[(2 * l + 1) * u : (2 * l + 2) * u, :] = r.outer_weight[l]
+    bias = r.inner_bias[...].astype(F32)
+    if u < z.C:
+        bias = jnp.concatenate([bias, jnp.zeros((z.L, z.C - u), F32)], axis=1)
+    bias = jnp.concatenate([bias, jnp.zeros((16 - z.L, z.C), F32)], axis=0)
+    r.block[2 * z.L * u :, :] = bias.astype(BF16)
+
+
 def swap(x, axis, n, bit):
     return lax.ppermute(x, axis, [(a, a ^ bit) for a in range(n)])
 
@@ -604,37 +685,41 @@
     return [1 << k for k in range(n.bit_length() - 1)]
 
 
-def scatter_bits(x, axis, n):
-    me = lax.axis_index(axis)
-    for bit in bits_of(n):
-        mine = (me // bit) % 2
-        x = x.reshape((-1, 2) + x.shape[1:])
-        away = lax.dynamic_index_in_dim(x, 1 - mine, 1, keepdims=False)
-        here = lax.dynamic_index_in_dim(x, mine, 1, keepdims=False)
-        x = (here.astype(F32) + swap(away, axis, n, bit).astype(F32)).astype(BF16)
-    return x[0]
-
-
-def sum_bits(x, axis, n):
-    for bit in bits_of(n):
-        x = (x.astype(F32) + swap(x, axis, n, bit).astype(F32)).astype(BF16)
-    return x
-
-
-def gather_bits(x, axis, n, order):
-    me = lax.axis_index(axis)
-    have = x[None]
-    dims = []
-    for bit in order:
-        got = swap(have, axis, n, bit)
-        mine = (me // bit) % 2
-        have = jnp.where(mine == 0, jnp.stack([have, got]), jnp.stack([got, have]))
-        dims.append(bit)
-    count = len(dims)
-    have = have.reshape((2,) * count + x.shape)
-    place = [count - 1 - dims.index(bit) for bit in sorted(dims, reverse=True)]
-    have = have.transpose(place + list(range(count, have.ndim)))
-    return have.reshape((n,) + x.shape)
+def add(here, got, token):
+    out = here.astype(F32) + got.astype(F32)
+    if token is not None:
+        out = out + token[0]
+    return out.astype(BF16)
+
+
+def take(tokens):
+    return tokens.pop(0) if tokens else None
+
+
+class Chain:
+    def __init__(self, parts, hid, img):
+        self.here = jnp.concatenate([part["here"] for part in parts], axis=1)
+        self.away = jnp.concatenate([part["away"] for part in parts], axis=1)
+        self.left = [("hid", hid, bit) for bit in bits_of(hid)] + [("img", img, bit) for bit in bits_of(img)]
+
+    def held(self):
+        return self.here
+
+    def step(self, token=None, extra=None):
+        axis, n, bit = self.left.pop(0)
+        x = add(self.here, swap(self.away, axis, n, bit), token)
+        if x.shape[0] > 1:
+            half = x.shape[0] // 2
+            self.here, self.away = x[:half], x[half:]
+        else:
+            if extra is not None and axis == "hid":
+                x = jnp.concatenate([x, extra[None]], axis=1)
+            self.here = self.away = x
+
+    def finish(self, extra=None):
+        while self.left:
+            self.step(None, extra)
+        return self.here[0]
 
 
 def per_device(
@@ -646,29 +731,43 @@
         images.shape[0], images.shape[1], images.shape[3], inner_weight.shape[2] * hid, squeeze_weight.shape[2],
         merge_weight.shape[1], mix_weight.shape[0], hid,
     )
+    z.ranks = sorted(range(hid), key=partial(rank, z))
+    place = lax.axis_index("hid").reshape(1)
     flat = images.transpose(1, 2, 0, 3).reshape(z.N0, z.C)
     merge_t = merge_weight.T
     squeeze_t = squeeze_weight.transpose(0, 2, 1)
-    block = jnp.stack([inner_weight.transpose(0, 2, 1), outer_weight], axis=1).reshape(-1, z.C)
-    bias_rows = jnp.pad(inner_bias, ((0, 16 - z.L), (0, z.C - z.units)))
-    block = jnp.concatenate([block, bias_rows], axis=0)
-    order = bits_of(hid)[1:] + [1]
-    gathered = gather_bits(block, "hid", hid, order)
-    smem = dict(sizes=0)
+    block = call(
+        partial(pack_kernel, z),
+        dict(inner_weight=inner_weight.transpose(0, 2, 1), outer_weight=outer_weight, inner_bias=inner_bias, place=place),
+        dict(block=kept(2 * z.L * z.units + 16, z.C, dtype=BF16)), {}, 2, 1, dict(place=0),
+    )
+    block = block["block"]
+    smem = dict(sizes=0, place=0)
     small = dict(
         mix_weight=mix_weight, mix_bias=mix_bias, squeeze_weight=squeeze_t, squeeze_bias=squeeze_bias,
         project_weight=project_weight, project_bias=project_bias, norm_gain=norm_gain, norm_bias=norm_bias,
     )
+    token = dict(token=arr(1, z.C))
     a = call(
         partial(front_kernel, z),
         dict(sizes=sizes, cotangent=cotangent, merge_weight=merge_t),
         dict(
-            mask=kept(z.N, z.C), edge=kept(z.N, z.C), back=kept(z.N, z.C), cot=kept(z.I * z.M, z.O, dtype=BF16),
-            grad=kept(z.tall, z.C), merge_bias_sums=kept(8, z.O),
+            mask=kept(z.N, z.C), edge=kept(z.N, z.C, dtype=BF16), back=kept(z.N, z.C, dtype=BF16), cot=kept(z.I * z.M, z.O, dtype=BF16),
+            grad=kept(z.tall, z.C), merge_bias_sums=kept(8, z.O), **token,
         ),
         dict(pgrad=kept(z.M + 8, 9 * z.C)),
-        12, smem,
-    )
+        4, 3, smem,
+    )
+    order = bits_of(hid)[1:] + [1]
+
+    def widen(have, bit, token):
+        got = swap(have, "hid", hid, bit)
+        return jnp.concatenate([have, got if token is None else got + token.astype(BF16)], axis=0)
+
+    z.found = [0]
+    for bit in order:
+        z.found = z.found + [e ^ bit for e in z.found]
+    have = widen(block[None], order[0], a["token"])
     b = call(
         partial(first_kernel, z),
         dict(
@@ -676,97 +775,129 @@
             **small,
         ),
         dict(
-            state=kept(z.N, z.C), perm=kept(3 * z.C, 3 * z.C), ewp=kept(z.L, z.R, 3 * z.C), ebp=kept(z.L, 3 * z.C),
-            **saved_early(z),
+            state=kept(z.N, z.C), perm=kept(3 * z.C, 3 * z.C, dtype=BF16), ewp=kept(z.L, z.R, 3 * z.C),
+            ebp=kept(z.L, 3 * z.C), **saved_early(z), **token,
         ),
         dict(normed=kept(z.long, z.C), sums=kept(3, 8, z.C)),
-        12, smem,
-    )
+        5, 10, smem, have,
+    )
+    for bit in order[1:]:
+        have = widen(have, bit, b["token"] if bit == order[1] else None)
     late = saved_late(z)
     c = call(
         partial(second_kernel, z),
         dict(
-            sizes=sizes, mask=a["mask"], edge=a["edge"], state_in=b["state"], normed2_0=b["normed2"], gathered=gathered,
+            sizes=sizes, mask=a["mask"], edge=a["edge"], state_in=b["state"], normed2_0=b["normed2"], gathered=have, place=place,
             ewp=b["ewp"], ebp=b["ebp"], outer_bias=outer_bias, merge_weight=merge_t, merge_bias=merge_bias.reshape(1, -1),
             cot=a["cot"], merge_bias_sums=a["merge_bias_sums"], **small,
         ),
         dict(
             features=arr(z.I, z.half, z.half * z.O, dtype=BF16),
-            merge_rows=arr(z.parts * z.merge, z.C, dtype=BF16),
+            merge_here=kept(z.parts // 2, z.merge, z.C, dtype=BF16), merge_away=kept(z.parts // 2, z.merge, z.C, dtype=BF16),
             inner=kept(z.L, z.H, z.C, dtype=BF16), outer=kept(z.L, z.H, z.C, dtype=BF16),
             act_rows_0=late["act_rows"], slope_rows_0=late["slope_rows"], **saved_early(z), **late,
         ),
         dict(
-            state=kept(z.N, z.C), normed=kept(z.tall, z.C), sums=kept(3, 8, z.C), inner_bias=kept(z.L, z.H),
-            patch=kept(z.I * z.M, 9 * z.C, dtype=BF16),
+            state=kept(z.N, z.C), normed=kept(z.tall, z.C), sums=kept(3, 8, z.C), inner_bias=kept(z.L, z.H), bias_rows=kept(z.parts, 16, z.C),
+            patch=kept(z.I * z.M, 9 * z.C, dtype=BF16), merge_rows=kept(z.parts * z.merge, z.C, dtype=BF16),
         ),
-        16, smem,
+        13, 22, smem,
     )
     first = dict(b, act_rows=c["act_rows_0"], slope_rows=c["slope_rows_0"])
-    grad, blocks, norms = a["grad"], [None] * z.L, [None] * z.L
+
+    def some(s, **names):
+        return {name: s[name] for name in names}
+
+    grad = a["grad"]
+    shares, norms = [None] * z.L, [None] * z.L
+    chain = None
     for l in reversed(range(z.L)):
         s = c if l else first
         d = call(
             partial(feed_back_kernel, z, l),
             dict(
-                sizes=sizes, mask=a["mask"], grad=grad, inner=c["inner"], outer=c["outer"], perm=b["perm"], ewp=b["ewp"],
-                **{
-                    name: s[name]
-                    for name in dict(
-                        act_rows=0, slope_rows=0, normed2=0, unit2=0, rstd2=0, mixed=0, cat=0, share=0, pool=0, pooled=0,
-                        act=0, slope=0,
-                    )
-                },
-                **small,
+                place=place, mask=a["mask"], grad=grad, inner=c["inner"], outer=c["outer"], norm_gain=norm_gain,
+                **some(s, act_rows=0, slope_rows=0, normed2=0, unit2=0, rstd2=0),
             ),
             dict(
-                half_grad=kept(z.N, z.C), mixed_grad=kept(z.N, z.I * z.C, dtype=BF16),
-                scaled=kept(3 * z.C, z.I * z.C, dtype=BF16), push=kept(3, 8, z.C),
-                blocks=arr(z.parts, 2 * z.units + z.shared, z.C, dtype=BF16),
+                half_grad=kept(z.N, z.C), feed_small=arr(8, z.C), here=kept(z.parts // 2, 2 * z.units, z.C, dtype=BF16),
+                away=kept(z.parts // 2, 2 * z.units, z.C, dtype=BF16), **token,
             ),
             dict(
-                vec=kept(5, 8, z.C), inner_sums=kept(8, z.H), g_outer=kept(z.C, z.H), g_inner=kept(z.C, z.H),
-                g_project=kept(z.C, z.C), g_mix=kept(z.I * z.C, 3 * z.C), rows=kept(z.parts * z.shared, z.C, dtype=BF16),
+                vec=kept(3, 8, z.C), inner_sums=kept(8, z.H), g_outer=kept(z.C, z.H), g_inner=kept(z.C, z.H),
+                turned=kept(2, z.H, z.C, dtype=BF16),
             ),
-            12, smem,
+            6, 6, smem, chain and chain.held(),
         )
-        blocks[l] = d["blocks"]
+        if chain:
+            chain.step(d["token"])
+        t = call(
+            partial(token_back_kernel, z, l),
+            dict(
+                sizes=sizes, place=place, mask=a["mask"], half_grad=d["half_grad"], feed_small=d["feed_small"],
+                perm=b["perm"], ewp=b["ewp"], **some(s, mixed=0, cat=0, share=0, pool=0, pooled=0, act=0, slope=0), **small,
+            ),
+            dict(
+                mixed_grad=kept(z.N, z.I * z.C, dtype=BF16), scaled=kept(3 * z.C, z.I * z.C, dtype=BF16),
+                push=kept(3, 8, z.C), here=kept(z.parts // 2, z.shared, z.C, dtype=BF16),
+                away=kept(z.parts // 2, z.shared, z.C, dtype=BF16), **token,
+            ),
+            dict(
+                vec=kept(2, 8, z.C), g_project=kept(z.C, z.C), g_mix=kept(z.I * z.C, 3 * z.C),
+                rows=kept(z.parts * z.shared, z.C, dtype=BF16),
+            ),
+            5, 6, smem, chain and chain.held(),
+        )
+        parts = [d, t]
+        if chain:
+            chain.step(t["token"])
+        elif l:
+            parts += [dict(here=c["merge_here"], away=c["merge_away"])]
+            chain = Chain(parts, hid, img)
+        if not l:
+            tail = Chain(parts, hid, img)
         e = call(
             partial(mix_back_kernel, z, l, l == 0),
             dict(
-                mask=a["mask"], back=a["back"], mixed_grad=d["mixed_grad"], scaled=d["scaled"], push=d["push"],
-                unit1=s["unit1"], rstd1=s["rstd1"], half_grad=d["half_grad"], norm_gain=norm_gain,
+                mask=a["mask"], back=a["back"], norm_gain=norm_gain, half_grad=d["half_grad"],
+                **some(t, mixed_grad=0, scaled=0, push=0), **some(s, unit1=0, rstd1=0),
             ),
-            dict(state_grad=kept(z.N, z.C) if l else arr(z.N0, z.C), first_norm=arr(2, z.C)),
+            dict(state_grad=kept(z.N, z.C) if l else arr(z.N0, z.C), first_norm=arr(2, z.C), **token),
             dict(back_h=kept(z.long, z.C), back_w=kept(z.long, z.C), back_c=kept(z.long, z.C), vec=kept(2, 8, z.C)),
-            12,
+            6, 4, (), chain and chain.held(),
         )
+        if chain:
+            chain.step(e["token"])
         grad, norms[l] = e["state_grad"], e["first_norm"]
     images_grad = grad.reshape(z.side, z.side, z.I, z.C).transpose(2, 0, 1, 3)
 
-    back = bits_of(hid)[::-1]
-    merge_rows = sum_bits(scatter_bits(c["merge_rows"].reshape(hid, z.merge, z.C), "hid", hid), "img", img)
-    merge_rows = gather_bits(merge_rows, "hid", hid, back).reshape(hid * z.merge, z.C)
-    both = jnp.stack(blocks, axis=1)
+    early = chain.finish()
+    tail.step(e["token"])
     norm_rows = jnp.pad(jnp.concatenate(norms, axis=0), ((0, 16 - 2 * z.L), (0, 0))).astype(BF16)
-    norm_rows = jnp.broadcast_to(norm_rows[None], (hid, 16, z.C))
-    every = jnp.concatenate([both.reshape(hid, -1, z.C), norm_rows], axis=1)
-    every = sum_bits(scatter_bits(every, "hid", hid), "img", img)
-    norm_rows = every[-16:]
-    every = every[:-16].reshape(z.L, 2 * z.units + z.shared, z.C)
-    feed_rows = every[:, : 2 * z.units]
-    shared_rows = gather_bits(every[:, 2 * z.units :], "hid", hid, back)
-    shared_rows = shared_rows.transpose(1, 0, 2, 3).reshape(z.L, hid * z.shared, z.C)
+    late_rows = tail.finish(norm_rows)
+    feed = 2 * z.units
+    cut = feed + z.shared
+    feed_rows = jnp.concatenate([late_rows[:feed], early[:feed]], axis=0)
+    have, norm_rows = late_rows[feed:cut], late_rows[cut:]
+    merge = early[None, feed:]
+    for bit in bits_of(hid)[::-1]:
+        sent = jnp.concatenate([have, norm_rows], axis=0)
+        got, merge_got = swap(sent, "hid", hid, bit), swap(merge, "hid", hid, bit)
+        if bit > 1:
+            have = jnp.concatenate([have, got[:-16]], axis=0)
+            norm_rows = add(norm_rows, got[-16:], None)
+            merge = jnp.concatenate([merge, merge_got], axis=0)
     g = call(
         partial(last_kernel, z),
-        dict(shared_rows=shared_rows, feed_rows=feed_rows, merge_rows=merge_rows, norms=norm_rows),
-        final_outputs(z), {}, 16,
-    )
-    inner_bias_grad = lax.dynamic_slice_in_dim(g["inner_bias"], lax.axis_index("hid") * z.units, z.units, axis=1)
+        dict(place=place, have=sent, got=got, merge_have=merge, merge_got=merge_got, feed_rows=feed_rows),
+        final_outputs(z),
+        dict(rows=kept(z.L, z.parts * z.shared, z.C, dtype=BF16), merge_rows=kept(z.parts * z.merge, z.C, dtype=BF16)),
+        8, 2, smem,
+    )
     return (
         c["features"], images_grad, g["mix_weight"], g["mix_bias"], g["squeeze_weight"].transpose(0, 2, 1),
         g["squeeze_bias"], g["expand_weight"], g["expand_bias"], g["project_weight"], g["project_bias"], g["norm_gain"],
-        g["norm_bias"], g["inner_weight"].transpose(0, 2, 1), inner_bias_grad, g["outer_weight"], g["outer_bias"],
+        g["norm_bias"], g["inner_weight"].transpose(0, 2, 1), g["inner_bias"], g["outer_weight"], g["outer_bias"],
         g["merge_weight"].T, g["merge_bias"].reshape(-1),
     )
 

time: 136 us -> 122 us (0.90)
  other arithmetic: 7.17 us -> 1.57 us
  starting transfers between devices: 26.1 us -> 22.4 us
  waiting for transfers between devices: 26 us -> 22.7 us
    ppermute x19, starting transfers between devices: 26.1 us -> 22.4 us  [swap(): return lax.ppermute(x, axis, [(a, a ^ bit) for a in range(n)])]
    ppermute x19, waiting for transfers between devices: 26 us -> 22.7 us  [swap(): return lax.ppermute(x, axis, [(a, a ^ bit) for a in range(n)])]
    unnamed x42, local copies, waits for them, and re-layouts: 1.24 us -> 3.41 us
    convert_element_type x7 -> x12, other arithmetic: 2.47 us -> 0.66 us  [add(): return out.astype(BF16)]
    another operation x9 -> x2, other arithmetic: 1.73 us -> 0.01 us  [the longest x1 0.87 us: per_device(): jnp.stack([inner_weight.transpose(0, 2, 1), outer_weight], axis=1)]
    pallas_call x8 -> x11, Pallas kernels: 71.8 us -> 70.5 us  [call(): pl.pallas_call(kernel, out_shape=list(outs.values()), in_specs=[scalar if...]
  transfers between devices with their start and end apart: 19 -> 19, of which waited for: 12 -> 10; matrix products, arithmetic and copies ran while one was open for 3% -> 1% of each run, Pallas kernels for 35% -> 27%
where the time goes in v3:
time: 122 us
  Pallas kernels  70.5 us (58%)
  waiting for transfers between devices  22.7 us (19%)
  starting transfers between devices  22.4 us (18%)
  local copies, waits for them, and re-layouts  3.57 us (3%)
  other arithmetic  1.57 us (1%)
    pallas_call x11, Pallas kernels, call(): pl.pallas_call(kernel, out_shape=list(outs.values()), in_specs=[scalar if...  70.5 us
    ppermute x19, waiting for transfers between devices, swap(): return lax.ppermute(x, axis, [(a, a ^ bit) for a in range(n)])  22.7 us
    ppermute x19, starting transfers between devices, swap(): return lax.ppermute(x, axis, [(a, a ^ bit) for a in range(n)])  22.4 us
    unnamed x42, local copies, waits for them, and re-layouts  3.41 us
  transfers between devices with their start and end apart: 19, of which 10 were waited for; matrix products, arithmetic and copies ran while one was open for 1% of the time, Pallas kernels for 27%

profile of v3, /device:TPU:0, one launch (start us, length us, event | category | flops | bytes accessed | tf_op | source)
XLA Modules:
  0.0 122.0 jit_solution(13507589364667482450)
XLA Ops:
  1.4 0.8 copy-done.6
  2.9 3.0 %collective-permute-start = (bf16[1,272,128]{2,1,0:T(8,128)(2,1)S(1)}, bf16[1,272,128]{2,1,0:T(8,128)(2,1)S(1)}, u32[]{:S(2)}, u32[]{:S(2)}) collective-permute-start(bf16[1,272,128]{2,1,0:T(8,128)(2,1)S(1)} %bitcast.34), channel_id=1, source_target_pairs={{0,2},{1,3},{2,0},{3,1},{4,6},{5,7},{6,4},{7,5},{8,10},{9,11},{10,... | collective-permute-start | bytes 208904 | tf_op jit(solution)/shard_map/ppermute | solution.py:681
  6.1 2.8 %shard_map.322 = (f32[2688,128]{1,0:T(8,128)S(1)}, bf16[2688,128]{1,0:T(8,128)(2,1)S(1)}, bf16[2688,128]{1,0:T(8,128)(2,1)S(1)}, bf16[864,320]{1,0:T(8,128)(2,1)...) custom-call(s32[2,2]{1,0:T(2,128)S(1)} %copy-done.13, ...), custom_call_target="tpu_custom_call" | custom-call | flops 3449999872 | tf_op jit(solution)/shard_map/pallas_call | solution.py:112
  8.9 1.6 %collective-permute-start.1 = (bf16[2,272,128]{2,1,0:T(8,128)(2,1)S(1)}, bf16[2,272,128]{2,1,0:T(8,128)(2,1)S(1)}, u32[]{:S(2)}, u32[]{:S(2)}) collective-permute-start(bf16[2,272,128]{2,1,0:T(8,128)(2,1)S(1)} %pad_maximum_fusion.6.refs_14_), channel_id=1, source_target_pairs={{0,4},{1,5},{2,6},{3,7},{4,0},{5,1},{6,2},{7,3},{8,12},{9,13},{10,... | collective-permute-start | bytes 417800 | tf_op jit(solution)/shard_map/ppermute | solution.py:681
  10.6 9.8 %shard_map.324 = (f32[2688,128]{1,0:T(8,128)S(1)}, bf16[384,384]{1,0:T(8,128)(2,1)S(1)}, f32[2,32,384]{2,1,0:T(8,128)S(1)}, f32[2,384]{1,0:T(2,128)S(1)}, bf16[2...) custom-call(bf16[2592,128]{1,0:T(8,128)(2,1)S(1)} %bitcast.45, ...), custom_call_target="tpu_custom_call" | custom-call | flops 11500000256 | tf_op jit(solution)/shard_map/pallas_call | solution.py:112
  20.7 1.5 %collective-permute-done.2 = bf16[4,272,128]{2,1,0:T(8,128)(2,1)S(1)} collective-permute-done((bf16[4,272,128]{2,1,0:T(8,128)(2,1)S(1)}, bf16[4,272,128]{2,1,0:T(8,128)(2,1)S(1)}, u32[]{:S(2)}, u32[]{:S(2)}) %collective-permute-start.2) | collective-permute-done | bytes 278560 | tf_op jit(solution)/shard_map/ppermute | solution.py:681
  22.3 23.2 %shard_map.325 = (bf16[2,18,5760]{2,1,0:T(8,128)(2,1)S(1)}, bf16[4,368,128]{2,1,0:T(8,128)(2,1)S(1)}, bf16[4,368,128]{2,1,0:T(8,128)(2,1)S(1)}, bf16[2,512,128]{...) custom-call(s32[2,2]{1,0:T(2,128)S(1)} %copy-done.13, ...), custom_call_target="tpu_custom_call" | custom-call | flops 25300000768 | tf_op jit(solution)/shard_map/pallas_call | solution.py:112
  45.5 6.4 %shard_map.326 = (f32[2688,128]{1,0:T(8,128)S(1)}, f32[8,128]{1,0:T(8,128)S(1)}, bf16[4,128,128]{2,1,0:T(8,128)(2,1)S(1)}, bf16[4,128,128]{2,1,0:T(8,128)(2,1)S(1)}, f32[1,128]{1,0:T(1,128)}) custom-call(s32[1]{0:T(128)} %bitcast.5.refs_3_.refs_6_.refs_0_.refs_1_, f32[2688,128]{1,0:T(8,128)S(1)} %get-tuple-element.105.refs_2_.refs_1_.refs_0_, ...), custom_call_target="tpu_custom_call" | custom-call | flops 6899999744 | tf_op jit(solution)/shard_map/pallas_call | solution.py:112
  51.9 6.1 %shard_map.327 = (bf16[2688,256]{1,0:T(8,128)(2,1)S(1)}, bf16[384,256]{1,0:T(8,128)(2,1)S(1)}, f32[3,8,128]{2,1,0:T(8,128)S(1)}, bf16[4,96,128]{2,1,0:T(8,128)(2...) custom-call(s32[2,2]{1,0:T(2,128)S(1)} %copy-done.13, s32[1]{0:T(128)} %bitcast.5.refs_3_.refs_6_.refs_0_.refs_1_, ...), custom_call_target="tpu_custom_call" | custom-call | flops 6899999744 | tf_op jit(solution)/shard_map/pallas_call | solution.py:112
  58.3 3.8 %shard_map.328 = (f32[2688,128]{1,0:T(8,128)S(1)}, f32[2,128]{1,0:T(2,128)S(1)}, f32[1,128]{1,0:T(1,128)S(1)}) custom-call(f32[2688,128]{1,0:T(8,128)S(1)} %get-tuple-element.105.refs_2_.refs_1_.refs_0_, bf16[2688,128]{1,0:T(8,128)(2,1)S(1)} %get-tuple-element.116.refs_1_, f32[2,2,128]{2,1,0:T(2,128)S(1)} %copy-done.11, ...), custom_call_target="tpu_custom_call" | custom-call | flops 4600000000 | tf_op jit(solution)/shard_map/pallas_call | solution.py:112
  62.4 1.3 %collective-permute-start.4 = (bf16[2,592,128]{2,1,0:T(8,128)(2,1)S(1)}, bf16[2,592,128]{2,1,0:T(8,128)(2,1)S(1)}, u32[]{:S(2)}, u32[]{:S(2)}) collective-permute-start(bf16[2,592,128]{2,1,0:T(8,128)(2,1)S(1)} %get-tuple-element.210), channel_id=1, source_target_pairs={{0,2},{1,3},{2,0},{3,1},{4,6},{5,7},{6,4},{7,5},{8,10},{9,11},{10,... | collective-permute-start | bytes 909320 | tf_op jit(solution)/shard_map/ppermute | solution.py:681
  63.8 5.9 %shard_map.329 = (f32[2688,128]{1,0:T(8,128)S(1)}, f32[8,128]{1,0:T(8,128)S(1)}, bf16[4,128,128]{2,1,0:T(8,128)(2,1)S(1)}, bf16[4,128,128]{2,1,0:T(8,128)(2,1)S(1)}, f32[1,128]{1,0:T(1,128)S(1)}) custom-call(s32[1]{0:T(128)} %bitcast.5.refs_3_.refs_6_.refs_0_.refs_1_, f32[2688,128]{1,0:T(8,128)S(1)} %get-tuple-element.105.refs_2_.refs_1_.refs_0_, ...), custom_call_target="tpu_custom_call" | custom-call | flops 6899999744 | tf_op jit(solution)/shard_map/pallas_call | solution.py:112
  69.7 2.2 %collective-permute-done.4 = bf16[2,592,128]{2,1,0:T(8,128)(2,1)S(1)} collective-permute-done((bf16[2,592,128]{2,1,0:T(8,128)(2,1)S(1)}, bf16[2,592,128]{2,1,0:T(8,128)(2,1)S(1)}, u32[]{:S(2)}, u32[]{:S(2)}) %collective-permute-start.4) | collective-permute-done | bytes 303136 | tf_op jit(solution)/shard_map/ppermute | solution.py:681
  72.7 5.9 %shard_map.330 = (bf16[2688,256]{1,0:T(8,128)(2,1)S(1)}, bf16[384,256]{1,0:T(8,128)(2,1)S(1)}, f32[3,8,128]{2,1,0:T(8,128)S(1)}, bf16[4,96,128]{2,1,0:T(8,128)(2...) custom-call(s32[2,2]{1,0:T(2,128)S(1)} %copy-done.13, s32[1]{0:T(128)} %bitcast.5.refs_3_.refs_6_.refs_0_.refs_1_, ...), custom_call_target="tpu_custom_call" | custom-call | flops 6899999744 | tf_op jit(solution)/shard_map/pallas_call | solution.py:112
  78.8 4.9 %shard_map.331 = (f32[2592,128]{1,0:T(8,128)}, f32[2,128]{1,0:T(2,128)S(1)}, f32[1,128]{1,0:T(1,128)S(1)}) custom-call(f32[2688,128]{1,0:T(8,128)S(1)} %get-tuple-element.105.refs_2_.refs_1_.refs_0_, bf16[2688,128]{1,0:T(8,128)(2,1)S(1)} %get-tuple-element.116.refs_1_, f32[2,2,128]{2,1,0:T(2,128)S(1)} %copy-done.11, ...), custom_call_target="tpu_custom_call" | custom-call | flops 4600000000 | tf_op jit(solution)/shard_map/pallas_call | solution.py:112
  83.8 1.3 %collective-permute-start.7 = (bf16[2,224,128]{2,1,0:T(8,128)(2,1)S(1)}, bf16[2,224,128]{2,1,0:T(8,128)(2,1)S(1)}, u32[]{:S(2)}, u32[]{:S(2)}) collective-permute-start(bf16[2,224,128]{2,1,0:T(8,128)(2,1)S(1)} %slice.90), channel_id=1, source_target_pairs={{0,2},{1,3},{2,0},{3,1},{4,6},{5,7},{6,4},{7,5},{8,10},{9,11},{10,... | collective-permute-start | bytes 344072 | tf_op jit(solution)/shard_map/ppermute | solution.py:681
  85.2 1.1 copy.38
  86.2 1.6 %collective-permute-start.14 = (bf16[1,592,128]{2,1,0:T(8,128)(2,1)S(1)}, bf16[1,592,128]{2,1,0:T(8,128)(2,1)S(1)}, u32[]{:S(2)}, u32[]{:S(2)}) collective-permute-start(bf16[1,592,128]{2,1,0:T(8,128)(2,1)S(1)} %add_convert_fusion.5.refs_9_), channel_id=1, source_target_pairs={{0,8},{8,0},{16,24},{24,16},{1,9},{9,1},{17,25},{25,17},{2,10},{10... | collective-permute-start | bytes 454664 | tf_op jit(solution)/shard_map/ppermute | solution.py:681
  87.8 1.6 %collective-permute-done.7 = bf16[2,224,128]{2,1,0:T(8,128)(2,1)S(1)} collective-permute-done((bf16[2,224,128]{2,1,0:T(8,128)(2,1)S(1)}, bf16[2,224,128]{2,1,0:T(8,128)(2,1)S(1)}, u32[]{:S(2)}, u32[]{:S(2)}) %collective-permute-start.7) | collective-permute-done | bytes 114720 | tf_op jit(solution)/shard_map/ppermute | solution.py:681
  89.5 1.6 %collective-permute-start.8 = (bf16[1,224,128]{2,1,0:T(8,128)(2,1)S(1)}, bf16[1,224,128]{2,1,0:T(8,128)(2,1)S(1)}, u32[]{:S(2)}, u32[]{:S(2)}) collective-permute-start(bf16[1,224,128]{2,1,0:T(8,128)(2,1)S(1)} %slice.92), channel_id=1, source_target_pairs={{0,4},{1,5},{2,6},{3,7},{4,0},{5,1},{6,2},{7,3},{8,12},{9,13},{10,... | collective-permute-start | bytes 172040 | tf_op jit(solution)/shard_map/ppermute | solution.py:681
  91.1 2.6 %collective-permute-done.8 = bf16[1,224,128]{2,1,0:T(8,128)(2,1)S(1)} collective-permute-done((bf16[1,224,128]{2,1,0:T(8,128)(2,1)S(1)}, bf16[1,224,128]{2,1,0:T(8,128)(2,1)S(1)}, u32[]{:S(2)}, u32[]{:S(2)}) %collective-permute-start.8) | collective-permute-done | bytes 57376 | tf_op jit(solution)/shard_map/ppermute | solution.py:681
  93.8 1.7 %collective-permute-start.9 = (bf16[1,240,128]{2,1,0:T(8,128)(2,1)S(1)}, bf16[1,240,128]{2,1,0:T(8,128)(2,1)S(1)}, u32[]{:S(2)}, u32[]{:S(2)}) collective-permute-start(bf16[1,240,128]{2,1,0:T(8,128)(2,1)S(1)} %pad_maximum_fusion.9), channel_id=1, source_target_pairs={{0,8},{8,0},{16,24},{24,16},{1,9},{9,1},{17,25},{25,17},{2,10},{10... | collective-permute-start | bytes 184328 | tf_op jit(solution)/shard_map/ppermute | solution.py:681
  95.5 2.7 %collective-permute-start.15 = (bf16[1,592,128]{2,1,0:T(8,128)(2,1)S(1)}, bf16[1,592,128]{2,1,0:T(8,128)(2,1)S(1)}, u32[]{:S(2)}, u32[]{:S(2)}) collective-permute-start(bf16[1,592,128]{2,1,0:T(8,128)(2,1)S(1)} %add_convert_fusion.4), channel_id=1, source_target_pairs={{0,16},{8,24},{16,0},{24,8},{1,17},{9,25},{17,1},{25,9},{2,18},{10... | collective-permute-start | bytes 454664 | tf_op jit(solution)/shard_map/ppermute | solution.py:681
  98.5 2.2 %collective-permute-start.10 = (bf16[1,240,128]{2,1,0:T(8,128)(2,1)S(1)}, bf16[1,240,128]{2,1,0:T(8,128)(2,1)S(1)}, u32[]{:S(2)}, u32[]{:S(2)}) collective-permute-start(bf16[1,240,128]{2,1,0:T(8,128)(2,1)S(1)} %add_convert_fusion.8), channel_id=1, source_target_pairs={{0,16},{8,24},{16,0},{24,8},{1,17},{9,25},{17,1},{25,9},{2,18},{10... | collective-permute-start | bytes 184328 | tf_op jit(solution)/shard_map/ppermute | solution.py:681
  100.8 5.1 %collective-permute-done.15 = bf16[1,592,128]{2,1,0:T(8,128)(2,1)S(1)} collective-permute-done((bf16[1,592,128]{2,1,0:T(8,128)(2,1)S(1)}, bf16[1,592,128]{2,1,0:T(8,128)(2,1)S(1)}, u32[]{:S(2)}, u32[]{:S(2)}) %collective-permute-start.15) | collective-permute-done | bytes 151584 | tf_op jit(solution)/shard_map/ppermute | solution.py:681
  106.0 1.6 %collective-permute-start.16 = (bf16[1,464,128]{2,1,0:T(8,128)(2,1)S(1)}, bf16[1,464,128]{2,1,0:T(8,128)(2,1)S(1)}, u32[]{:S(2)}, u32[]{:S(2)}) collective-permute-start(bf16[1,464,128]{2,1,0:T(8,128)(2,1)S(1)} %slice.99), channel_id=1, source_target_pairs={{0,4},{1,5},{2,6},{3,7},{4,0},{5,1},{6,2},{7,3},{8,12},{9,13},{10,... | collective-permute-start | bytes 356360 | tf_op jit(solution)/shard_map/ppermute | solution.py:681
  108.2 3.3 %collective-permute-done.11 = bf16[112,128]{1,0:T(8,128)(2,1)S(1)} collective-permute-done((bf16[112,128]{1,0:T(8,128)(2,1)S(1)}, bf16[112,128]{1,0:T(8,128)(2,1)S(1)}, u32[]{:S(2)}, u32[]{:S(2)}) %collective-permute-start.11) | collective-permute-done | bytes 28704 | tf_op jit(solution)/shard_map/ppermute | solution.py:681
  111.6 1.2 collective-permute-start.17
  112.8 0.9 collective-permute-start.12
  113.7 4.0 %collective-permute-done.17 = bf16[2,464,128]{2,1,0:T(8,128)(2,1)S(1)} collective-permute-done((bf16[2,464,128]{2,1,0:T(8,128)(2,1)S(1)}, bf16[2,464,128]{2,1,0:T(8,128)(2,1)S(1)}, u32[]{:S(2)}, u32[]{:S(2)}) %collective-permute-start.17) | collective-permute-done | bytes 237600 | tf_op jit(solution)/shard_map/ppermute | solution.py:681
  118.5 1.4 %collective-permute-done.13.refs_2_ = bf16[400,128]{1,0:T(8,128)(2,1)S(1)} collective-permute-done((bf16[400,128]{1,0:T(8,128)(2,1)S(1)}, bf16[400,128]{1,0:T(8,128)(2,1)S(1)}, u32[]{:S(2)}, u32[]{:S(2)}) %collective-permute-start.13) | collective-permute-done | bytes 102432 | tf_op jit(solution)/shard_map/ppermute | solution.py:681
  119.9 1.5 %shard_map.332 = (f32[2,3,128,128]{3,2,1,0:T(8,128)}, f32[2,2,128]{2,1,0:T(2,128)}, f32[2,32,128]{2,1,0:T(8,128)}, f32[2,32]{1,0:T(2,128)}, f32[2,32,384]{2,1,0:...) custom-call(s32[1]{0:T(128)} %bitcast.5.refs_3_.refs_6_.refs_0_.refs, ...), custom_call_target="tpu_custom_call" | custom-call | flops 2300000000 | tf_op jit(solution)/shard_map/pallas_call | solution.py:112
  (104 shorter events, 5.8 us)
Async XLA Ops:
  2.8 3.1 %copy-start.13 = (s32[2,2]{1,0:T(2,128)S(1)}, s32[2,2]{1,0:T(2,128)}, u32[]{:S(2)}) copy-start(s32[2,2]{1,0:T(2,128)} %refs_0_.7) | copy-start | bytes 52
  2.9 6.0 %collective-permute-start = (bf16[1,272,128]{2,1,0:T(8,128)(2,1)S(1)}, bf16[1,272,128]{2,1,0:T(8,128)(2,1)S(1)}, u32[]{:S(2)}, u32[]{:S(2)}) collective-permute-start(bf16[1,272,128]{2,1,0:T(8,128)(2,1)S(1)} %bitcast.34), channel_id=1, source_target_pairs={{0,2},{1,3},{2,0},{3,1},{4,6},{5,7},{6,4},{7,5},{8,10},{9,11},{10,... | collective-permute-start | bytes 208904 | tf_op jit(solution)/shard_map/ppermute | solution.py:681
  5.9 4.6 %copy-start.1 = (bf16[2,36,36,128]{3,0,2,1:T(2,128)(2,1)S(1)}, bf16[2,36,36,128]{3,0,2,1:T(2,128)(2,1)}, u32[]{:S(2)}) copy-start(bf16[2,36,36,128]{3,0,2,1:T(2,128)(2,1)} %param.19) | copy-start | bytes 1990660
  6.0 4.6 %copy-start.2 = (bf16[2,3,128,128]{3,2,1,0:T(8,128)(2,1)S(1)}, bf16[2,3,128,128]{3,2,1,0:T(8,128)(2,1)}, u32[]{:S(2)}) copy-start(bf16[2,3,128,128]{3,2,1,0:T(8,128)(2,1)} %refs_14_.5) | copy-start | bytes 589828
  6.0 4.6 %copy-start.3 = (f32[2,32,384]{2,1,0:T(8,128)S(1)}, f32[2,32,384]{2,1,0:T(8,128)}, u32[]{:S(2)}) copy-start(f32[2,32,384]{2,1,0:T(8,128)} %refs_4_.1) | copy-start | bytes 294916
  6.0 4.6 %copy-start.4 = (bf16[2,128,128]{2,1,0:T(8,128)(2,1)S(1)}, bf16[2,128,128]{2,1,0:T(8,128)(2,1)}, u32[]{:S(2)}) copy-start(bf16[2,128,128]{2,1,0:T(8,128)(2,1)} %refs_18_.5) | copy-start | bytes 196612
  6.0 4.6 %copy-start.7 = (f32[2,128,32]{1,2,0:T(8,128)S(1)}, f32[2,128,32]{1,2,0:T(8,128)}, u32[]{:S(2)}) copy-start(f32[2,128,32]{1,2,0:T(8,128)} %param.24) | copy-start | bytes 98308
  6.0 4.6 %copy-start.8 = (f32[2,384]{1,0:T(2,128)S(1)}, f32[2,384]{1,0:T(2,128)}, u32[]{:S(2)}) copy-start(f32[2,384]{1,0:T(2,128)} %refs_5_.3) | copy-start | bytes 9220
  6.0 4.6 %copy-start.9 = (f32[2,2,128]{2,1,0:T(2,128)S(1)}, f32[2,2,128]{2,1,0:T(2,128)}, u32[]{:S(2)}) copy-start(f32[2,2,128]{2,1,0:T(2,128)} %refs_15_.5) | copy-start | bytes 6148
  6.0 4.6 %copy-start.10 = (f32[2,2,128]{2,1,0:T(2,128)S(1)}, f32[2,2,128]{2,1,0:T(2,128)}, u32[]{:S(2)}) copy-start(f32[2,2,128]{2,1,0:T(2,128)} %refs_21_.5) | copy-start | bytes 6148
  6.0 4.5 %copy-start.11 = (f32[2,2,128]{2,1,0:T(2,128)S(1)}, f32[2,2,128]{2,1,0:T(2,128)}, u32[]{:S(2)}) copy-start(f32[2,2,128]{2,1,0:T(2,128)} %refs_2_.5) | copy-start | bytes 6148
  6.0 4.5 %copy-start.14 = (f32[2,32]{1,0:T(2,128)S(1)}, f32[2,32]{1,0:T(2,128)}, u32[]{:S(2)}) copy-start(f32[2,32]{1,0:T(2,128)} %refs_17_.5) | copy-start | bytes 772
  6.1 4.5 %copy-start.15 = (f32[2,128]{1,0:T(2,128)S(1)}, f32[2,128]{1,0:T(2,128)}, u32[]{:S(2)}) copy-start(f32[2,128]{1,0:T(2,128)} %refs_19_.5) | copy-start | bytes 3076
  8.9 11.6 %collective-permute-start.1 = (bf16[2,272,128]{2,1,0:T(8,128)(2,1)S(1)}, bf16[2,272,128]{2,1,0:T(8,128)(2,1)S(1)}, u32[]{:S(2)}, u32[]{:S(2)}) collective-permute-start(bf16[2,272,128]{2,1,0:T(8,128)(2,1)S(1)} %pad_maximum_fusion.6.refs_14_), channel_id=1, source_target_pairs={{0,4},{1,5},{2,6},{3,7},{4,0},{5,1},{6,2},{7,3},{8,12},{9,13},{10,... | collective-permute-start | bytes 417800 | tf_op jit(solution)/shard_map/ppermute | solution.py:681
  10.6 10.0 %copy-start.18 = (f32[320]{0:T(512)S(1)}, f32[320]{0:T(512)}, u32[]{:S(2)}) copy-start(f32[320]{0:T(512)} %param.37) | copy-start | bytes 3844
  20.6 1.6 %collective-permute-start.2 = (bf16[4,272,128]{2,1,0:T(8,128)(2,1)S(1)}, bf16[4,272,128]{2,1,0:T(8,128)(2,1)S(1)}, u32[]{:S(2)}, u32[]{:S(2)}) collective-permute-start(bf16[4,272,128]{2,1,0:T(8,128)(2,1)S(1)} %pad_maximum_fusion.3), channel_id=1, source_target_pairs={{0,1},{1,0},{2,3},{3,2},{4,5},{5,4},{6,7},{7,6},{8,9},{9,8},{10,11... | collective-permute-start | bytes 835592 | tf_op jit(solution)/shard_map/ppermute | solution.py:681
  58.1 4.1 %collective-permute-start.3 = (bf16[4,592,128]{2,1,0:T(8,128)(2,1)S(1)}, bf16[4,592,128]{2,1,0:T(8,128)(2,1)S(1)}, u32[]{:S(2)}, u32[]{:S(2)}) collective-permute-start(bf16[4,592,128]{2,1,0:T(8,128)(2,1)S(1)} %pad_maximum_fusion), channel_id=1, source_target_pairs={{0,1},{1,0},{2,3},{3,2},{4,5},{5,4},{6,7},{7,6},{8,9},{9,8},{10,11... | collective-permute-start | bytes 1818632 | tf_op jit(solution)/shard_map/ppermute | solution.py:681
  62.4 9.5 %collective-permute-start.4 = (bf16[2,592,128]{2,1,0:T(8,128)(2,1)S(1)}, bf16[2,592,128]{2,1,0:T(8,128)(2,1)S(1)}, u32[]{:S(2)}, u32[]{:S(2)}) collective-permute-start(bf16[2,592,128]{2,1,0:T(8,128)(2,1)S(1)} %get-tuple-element.210), channel_id=1, source_target_pairs={{0,2},{1,3},{2,0},{3,1},{4,6},{5,7},{6,4},{7,5},{8,10},{9,11},{10,... | collective-permute-start | bytes 909320 | tf_op jit(solution)/shard_map/ppermute | solution.py:681
  72.1 6.6 %collective-permute-start.5 = (bf16[1,592,128]{2,1,0:T(8,128)(2,1)S(1)}, bf16[1,592,128]{2,1,0:T(8,128)(2,1)S(1)}, u32[]{:S(2)}, u32[]{:S(2)}) collective-permute-start(bf16[1,592,128]{2,1,0:T(8,128)(2,1)S(1)} %get-tuple-element.212), channel_id=1, source_target_pairs={{0,4},{1,5},{2,6},{3,7},{4,0},{5,1},{6,2},{7,3},{8,12},{9,13},{10,... | collective-permute-start | bytes 454664 | tf_op jit(solution)/shard_map/ppermute | solution.py:681
  78.6 5.1 %collective-permute-start.6 = (bf16[4,224,128]{2,1,0:T(8,128)(2,1)S(1)}, bf16[4,224,128]{2,1,0:T(8,128)(2,1)S(1)}, u32[]{:S(2)}, u32[]{:S(2)}) collective-permute-start(bf16[4,224,128]{2,1,0:T(8,128)(2,1)S(1)} %pad_maximum_fusion.5), channel_id=1, source_target_pairs={{0,1},{1,0},{2,3},{3,2},{4,5},{5,4},{6,7},{7,6},{8,9},{9,8},{10,11... | collective-permute-start | bytes 688136 | tf_op jit(solution)/shard_map/ppermute | solution.py:681
  83.8 5.6 %collective-permute-start.7 = (bf16[2,224,128]{2,1,0:T(8,128)(2,1)S(1)}, bf16[2,224,128]{2,1,0:T(8,128)(2,1)S(1)}, u32[]{:S(2)}, u32[]{:S(2)}) collective-permute-start(bf16[2,224,128]{2,1,0:T(8,128)(2,1)S(1)} %slice.90), channel_id=1, source_target_pairs={{0,2},{1,3},{2,0},{3,1},{4,6},{5,7},{6,4},{7,5},{8,10},{9,11},{10,... | collective-permute-start | bytes 344072 | tf_op jit(solution)/shard_map/ppermute | solution.py:681
  86.2 9.2 %collective-permute-start.14 = (bf16[1,592,128]{2,1,0:T(8,128)(2,1)S(1)}, bf16[1,592,128]{2,1,0:T(8,128)(2,1)S(1)}, u32[]{:S(2)}, u32[]{:S(2)}) collective-permute-start(bf16[1,592,128]{2,1,0:T(8,128)(2,1)S(1)} %add_convert_fusion.5.refs_9_), channel_id=1, source_target_pairs={{0,8},{8,0},{16,24},{24,16},{1,9},{9,1},{17,25},{25,17},{2,10},{10... | collective-permute-start | bytes 454664 | tf_op jit(solution)/shard_map/ppermute | solution.py:681
  89.5 4.2 %collective-permute-start.8 = (bf16[1,224,128]{2,1,0:T(8,128)(2,1)S(1)}, bf16[1,224,128]{2,1,0:T(8,128)(2,1)S(1)}, u32[]{:S(2)}, u32[]{:S(2)}) collective-permute-start(bf16[1,224,128]{2,1,0:T(8,128)(2,1)S(1)} %slice.92), channel_id=1, source_target_pairs={{0,4},{1,5},{2,6},{3,7},{4,0},{5,1},{6,2},{7,3},{8,12},{9,13},{10,... | collective-permute-start | bytes 172040 | tf_op jit(solution)/shard_map/ppermute | solution.py:681
  93.8 4.7 %collective-permute-start.9 = (bf16[1,240,128]{2,1,0:T(8,128)(2,1)S(1)}, bf16[1,240,128]{2,1,0:T(8,128)(2,1)S(1)}, u32[]{:S(2)}, u32[]{:S(2)}) collective-permute-start(bf16[1,240,128]{2,1,0:T(8,128)(2,1)S(1)} %pad_maximum_fusion.9), channel_id=1, source_target_pairs={{0,8},{8,0},{16,24},{24,16},{1,9},{9,1},{17,25},{25,17},{2,10},{10... | collective-permute-start | bytes 184328 | tf_op jit(solution)/shard_map/ppermute | solution.py:681
  95.5 10.4 %collective-permute-start.15 = (bf16[1,592,128]{2,1,0:T(8,128)(2,1)S(1)}, bf16[1,592,128]{2,1,0:T(8,128)(2,1)S(1)}, u32[]{:S(2)}, u32[]{:S(2)}) collective-permute-start(bf16[1,592,128]{2,1,0:T(8,128)(2,1)S(1)} %add_convert_fusion.4), channel_id=1, source_target_pairs={{0,16},{8,24},{16,0},{24,8},{1,17},{9,25},{17,1},{25,9},{2,18},{10... | collective-permute-start | bytes 454664 | tf_op jit(solution)/shard_map/ppermute | solution.py:681
  98.5 9.0 %collective-permute-start.10 = (bf16[1,240,128]{2,1,0:T(8,128)(2,1)S(1)}, bf16[1,240,128]{2,1,0:T(8,128)(2,1)S(1)}, u32[]{:S(2)}, u32[]{:S(2)}) collective-permute-start(bf16[1,240,128]{2,1,0:T(8,128)(2,1)S(1)} %add_convert_fusion.8), channel_id=1, source_target_pairs={{0,16},{8,24},{16,0},{24,8},{1,17},{9,25},{17,1},{25,9},{2,18},{10... | collective-permute-start | bytes 184328 | tf_op jit(solution)/shard_map/ppermute | solution.py:681
  106.0 5.6 %collective-permute-start.16 = (bf16[1,464,128]{2,1,0:T(8,128)(2,1)S(1)}, bf16[1,464,128]{2,1,0:T(8,128)(2,1)S(1)}, u32[]{:S(2)}, u32[]{:S(2)}) collective-permute-start(bf16[1,464,128]{2,1,0:T(8,128)(2,1)S(1)} %slice.99), channel_id=1, source_target_pairs={{0,4},{1,5},{2,6},{3,7},{4,0},{5,1},{6,2},{7,3},{8,12},{9,13},{10,... | collective-permute-start | bytes 356360 | tf_op jit(solution)/shard_map/ppermute | solution.py:681
  107.6 3.9 %collective-permute-start.11 = (bf16[112,128]{1,0:T(8,128)(2,1)S(1)}, bf16[112,128]{1,0:T(8,128)(2,1)S(1)}, u32[]{:S(2)}, u32[]{:S(2)}) collective-permute-start(bf16[112,128]{1,0:T(8,128)(2,1)S(1)} %pad_maximum_fusion.11), channel_id=1, source_target_pairs={{0,4},{1,5},{2,6},{3,7},{4,0},{5,1},{6,2},{7,3},{8,12},{9,13},{10,... | collective-permute-start | bytes 86024 | tf_op jit(solution)/shard_map/ppermute | solution.py:681
  111.6 6.2 %collective-permute-start.17 = (bf16[2,464,128]{2,1,0:T(8,128)(2,1)S(1)}, bf16[2,464,128]{2,1,0:T(8,128)(2,1)S(1)}, u32[]{:S(2)}, u32[]{:S(2)}) collective-permute-start(bf16[2,464,128]{2,1,0:T(8,128)(2,1)S(1)} %pad_maximum_fusion.4), channel_id=1, source_target_pairs={{0,2},{1,3},{2,0},{3,1},{4,6},{5,7},{6,4},{7,5},{8,10},{9,11},{10,... | collective-permute-start | bytes 712712 | tf_op jit(solution)/shard_map/ppermute | solution.py:681
  112.8 5.5 %collective-permute-start.12 = (bf16[208,128]{1,0:T(8,128)(2,1)S(1)}, bf16[208,128]{1,0:T(8,128)(2,1)S(1)}, u32[]{:S(2)}, u32[]{:S(2)}) collective-permute-start(bf16[208,128]{1,0:T(8,128)(2,1)S(1)} %pad_maximum_fusion.10), channel_id=1, source_target_pairs={{0,2},{1,3},{2,0},{3,1},{4,6},{5,7},{6,4},{7,5},{8,10},{9,11},{10,... | collective-permute-start | bytes 159752 | tf_op jit(solution)/shard_map/ppermute | solution.py:681
  117.8 2.1 %collective-permute-start.18 = (bf16[4,464,128]{2,1,0:T(8,128)(2,1)S(1)}, bf16[4,464,128]{2,1,0:T(8,128)(2,1)S(1)}, u32[]{:S(2)}, u32[]{:S(2)}) collective-permute-start(bf16[4,464,128]{2,1,0:T(8,128)(2,1)S(1)} %pad_maximum_fusion.2.refs_3_), channel_id=1, source_target_pairs={{0,1},{1,0},{2,3},{3,2},{4,5},{5,4},{6,7},{7,6},{8,9},{9,8},{10,11... | collective-permute-start | bytes 1425416 | tf_op jit(solution)/shard_map/ppermute | solution.py:681
  118.3 1.5 %collective-permute-start.13 = (bf16[400,128]{1,0:T(8,128)(2,1)S(1)}, bf16[400,128]{1,0:T(8,128)(2,1)S(1)}, u32[]{:S(2)}, u32[]{:S(2)}) collective-permute-start(bf16[400,128]{1,0:T(8,128)(2,1)S(1)} %pad_maximum_fusion.7.refs_1_), channel_id=1, source_target_pairs={{0,1},{1,0},{2,3},{3,2},{4,5},{5,4},{6,7},{7,6},{8,9},{9,8},{10,11... | collective-permute-start | bytes 307208 | tf_op jit(solution)/shard_map/ppermute | solution.py:681
  (6 other events, 10.1 us)

commit v4 on v3

--- a/solution.py
+++ b/solution.py
@@ -48,24 +48,17 @@
     return x * cdf, cdf + x * bell * 0.3989422804014327
 
 
-def norm_parts(v, ones):
-    high = v.astype(BF16)
-    low = (v - high.astype(F32)).astype(BF16)
-    centred = v - dot(jnp.concatenate([high, low], axis=1), ones)
-    rstd = lax.rsqrt(dot((centred * centred).astype(BF16), ones[: v.shape[1]]) + 1e-05)
-    return centred * rstd, rstd
-
-
-def norm_back(grad, unit, rstd, gain, ones):
-    width = grad.shape[1]
+def norm_parts(v):
+    centred = v - jnp.mean(v, axis=-1, keepdims=True)
+    rstd = lax.rsqrt(jnp.mean(centred * centred, axis=-1, keepdims=True) + 1e-05)
+    return centred * rstd, jnp.broadcast_to(rstd, v.shape)
+
+
+def norm_back(grad, unit, rstd, gain):
     scaled = grad * gain
-    first = dot(scaled.astype(BF16), ones[:width])
-    second = dot((scaled * unit).astype(BF16), ones[:width])
+    first = jnp.mean(scaled, axis=-1, keepdims=True)
+    second = jnp.mean(scaled * unit, axis=-1, keepdims=True)
     return rstd * (scaled - first - unit * second)
-
-
-def mean_matrix(z):
-    return jnp.full((2 * z.C, z.C), 1.0 / z.C, BF16)
 
 
 class Sizes:
@@ -74,9 +67,9 @@
         self.parts, self.units = parts, hidden // parts
         self.W = side * images
         self.N0 = side * self.W
-        self.CH = 384
-        self.N = -(-self.N0 // self.CH) * self.CH
-        self.chunks = self.N // self.CH
+        self.N = -(-self.N0 // 384) * 384
+        self.run_first = self.run_back = self.run_mix = self.N
+        self.run_second = self.N // 7
         self.half = side // 2
         self.hp = -(-self.half // 8) * 8
         self.M = self.half * self.hp
@@ -129,16 +122,13 @@
     return pltpu.VMEM(shape, dtype)
 
 
-def over(z, body):
-    def step(c, carry):
-        body(pl.ds(pl.multiple_of(c * z.CH, 128), z.CH), c * z.CH)
-        return carry
-
-    lax.fori_loop(0, z.chunks, step, 0)
+def over(z, body, size):
+    for at in range(0, z.N, size):
+        body(slice(at, at + size), at)
 
 
 def near(ref, start, off, size):
-    return ref[pl.ds(start + off, size), :]
+    return ref[start + off : start + off + size, :]
 
 
 def parity(z, i):
@@ -231,15 +221,15 @@
     r.token[...] = jnp.zeros_like(r.token)
 
 
-def shift_phase(z, r, cat):
+def shift_phase(z, r, cat, size):
     r.sums[...] = jnp.zeros_like(r.sums)
 
     def body(rows, at):
         start = z.base + at
-        kind = kinds(z, z.CH)
-        mid = near(r.normed, start, 0, z.CH)
-        high = jnp.where(kind == 2, near(r.normed, start, -z.W, z.CH), near(r.normed, start, z.W, z.CH))
-        wide = jnp.where(kind == 2, near(r.normed, start, -z.I, z.CH), near(r.normed, start, z.I, z.CH))
+        kind = kinds(z, size)
+        mid = near(r.normed, start, 0, size)
+        high = jnp.where(kind == 2, near(r.normed, start, -z.W, size), near(r.normed, start, z.W, size))
+        wide = jnp.where(kind == 2, near(r.normed, start, -z.I, size), near(r.normed, start, z.I, size))
         high = jnp.where(kind == 0, mid, high).astype(BF16)
         wide = jnp.where(kind == 0, mid, wide * r.edge[rows, :].astype(F32)).astype(BF16)
         mask = r.mask[rows, :]
@@ -247,7 +237,7 @@
             cat[rows, j * z.C : (j + 1) * z.C] = piece
             r.sums[j] += rows8(piece.astype(F32) * mask)
 
-    over(z, body)
+    over(z, body, size)
 
 
 def counts_of(z, r):
@@ -278,11 +268,10 @@
         o.share[j] = parts[j] / whole
 
 
-def mix_phase(z, r, l, o):
-    ones = mean_matrix(z)
+def mix_phase(z, r, l, o, size):
     share = [weave(z, o.share[j]) for j in range(3)]
-    bias = tile(r.mix_bias[l, 0:1] * share[0] + r.mix_bias[l, 1:2] * share[1], z.CH)
-    share = [tile(s, z.CH) for s in share]
+    bias = tile(r.mix_bias[l, 0:1] * share[0] + r.mix_bias[l, 1:2] * share[1], size)
+    share = [tile(s, size) for s in share]
     gain, shift = r.norm_gain[l, 1:2], r.norm_bias[l, 1:2]
 
     def body(rows, at):
@@ -293,20 +282,20 @@
         o.mixed[rows, :] = mixed
         token = dot(mixed, r.project_weight[l]) + r.project_bias[l : l + 1]
         halfway = r.state[rows, :] + r.mask[rows, :] * token
-        unit, rstd = norm_parts(halfway, ones)
+        unit, rstd = norm_parts(halfway)
         o.unit2[rows, :] = unit.astype(BF16)
         o.rstd2[rows, :] = rstd.astype(BF16)
         o.normed2[rows, :] = (unit * gain + shift).astype(BF16)
         r.state[rows, :] = halfway
 
-    over(z, body)
+    over(z, body, size)
 
 
 def norm_store(z, r, l, o, rows, at, state):
-    unit, rstd = norm_parts(state, mean_matrix(z))
+    unit, rstd = norm_parts(state)
     o.unit1[rows, :] = unit.astype(BF16)
     o.rstd1[rows, :] = rstd.astype(BF16)
-    r.normed[pl.ds(z.base + at, z.CH), :] = unit * r.norm_gain[l, 0:1] + r.norm_bias[l, 0:1]
+    r.normed[z.base + at : z.base + at + rows.stop - rows.start, :] = unit * r.norm_gain[l, 0:1] + r.norm_bias[l, 0:1]
 
 
 def clear_edges(z, ref):
@@ -325,7 +314,7 @@
         state = r.state[rows, :] + r.mask[rows, :] * out
         after(rows, at, state)
 
-    over(z, body)
+    over(z, body, z.run_second)
 
 
 def saved_early(z):
@@ -348,27 +337,20 @@
     for l in range(z.L):
         r.ewp[l] = fine(r.expand_weight[l], r.perm[...])
     r.ebp[...] = fine(r.expand_bias[...], r.perm[...])
-    whole = z.N0 // z.CH
-
-    def step(c, carry):
-        rows = pl.ds(pl.multiple_of(c * z.CH, 128), z.CH)
-        state = r.images[rows, :].astype(F32) * r.mask[rows, :]
+
+    def begin(rows, at):
+        real = min(rows.stop, z.N0) - at
+        state = r.images[at : at + real, :].astype(F32) * r.mask[at : at + real, :]
+        if real < rows.stop - at:
+            state = jnp.concatenate([state, jnp.zeros((rows.stop - at - real, z.C), F32)], axis=0)
         r.state[rows, :] = state
-        norm_store(z, r, 0, r, rows, c * z.CH, state)
-        return carry
-
-    lax.fori_loop(0, whole, step, 0)
-    if whole < z.chunks:
-        at = whole * z.CH
-        left = z.N0 - at
-        tail = r.images[at:, :].astype(F32) * r.mask[at : z.N0, :]
-        state = jnp.concatenate([tail, jnp.zeros((z.CH - left, z.C), F32)], axis=0)
-        r.state[at:, :] = state
-        norm_store(z, r, 0, r, pl.ds(at, z.CH), at, state)
+        norm_store(z, r, 0, r, rows, at, state)
+
+    over(z, begin, z.run_first)
     clear_edges(z, r.normed)
-    shift_phase(z, r, r.cat)
+    shift_phase(z, r, r.cat, z.run_first)
     weigh_phase(z, r, 0, r)
-    mix_phase(z, r, 0, r)
+    mix_phase(z, r, 0, r, z.run_first)
     r.token[...] = jnp.zeros_like(r.token)
 
 
@@ -414,12 +396,12 @@
     r.state[...] = r.state_in[...]
     feed_phase(z, r, 0, early[0], then_norm)
     clear_edges(z, r.normed)
-    shift_phase(z, r, r.cat)
+    shift_phase(z, r, r.cat, z.run_second)
     weigh_phase(z, r, 1, r)
-    mix_phase(z, r, 1, r)
+    mix_phase(z, r, 1, r, z.run_second)
 
     def then_keep(rows, at, state):
-        r.normed[pl.ds(z.base + at, z.CH), :] = state
+        r.normed[z.base + at : z.base + at + rows.stop - rows.start, :] = state
 
     feed_phase(z, r, 1, early[1], then_keep)
     for i in range(z.I):
@@ -454,7 +436,6 @@
 
 
 def feed_back_kernel(z, l, r):
-    ones = mean_matrix(z)
     gain = r.norm_gain[l, 1:2]
     for ref in (r.vec, r.inner_sums, r.g_outer, r.g_inner):
         ref[...] = jnp.zeros_like(ref)
@@ -472,9 +453,9 @@
         unit = r.unit2[rows, :].astype(F32)
         r.vec[1] += rows8(normed_grad * unit)
         r.vec[2] += rows8(normed_grad)
-        r.half_grad[rows, :] = grad + norm_back(normed_grad, unit, r.rstd2[rows, :].astype(F32), gain, ones)
-
-    over(z, body)
+        r.half_grad[rows, :] = grad + norm_back(normed_grad, unit, r.rstd2[rows, :].astype(F32), gain)
+
+    over(z, body, z.run_back)
     inner = total(r.inner_sums[...])
     small = [total(r.vec[k]) for k in range(3)]
     small += [inner[:, k * z.C : (k + 1) * z.C] for k in range(z.H // z.C)]
@@ -490,7 +471,7 @@
 def token_back_kernel(z, l, r):
     for ref in (r.vec, r.g_project, r.g_mix):
         ref[...] = jnp.zeros_like(ref)
-    even, odd = tile(parity(z, 0), z.CH), tile(parity(z, 1), z.CH)
+    even, odd = tile(parity(z, 0), z.run_back), tile(parity(z, 1), z.run_back)
 
     def body(rows, at):
         token = (r.half_grad[rows, :] * r.mask[rows, :]).astype(BF16)
@@ -502,7 +483,7 @@
         r.mixed_grad[rows, :] = both
         r.g_mix[...] += dot(both, r.cat[rows, :], (0, 0))
 
-    over(z, body)
+    over(z, body, z.run_back)
     counts = counts_of(z, r)
     zeros = jnp.zeros((GROUP - z.I, z.C), F32)
     summed = split(z, r.vec[1])
@@ -553,48 +534,40 @@
 
 
 def mix_back_kernel(z, l, last, r):
-    ones = mean_matrix(z)
     for ref in (r.back_h, r.back_w):
         clear_edges(z, ref)
     gain = r.norm_gain[l, 0:1]
-    push = [tile(r.push[j], z.CH) for j in range(3)]
+    size = z.run_mix
+    push = [tile(r.push[j], size) for j in range(3)]
 
     def spread(rows, at):
         mask = r.mask[rows, :]
         parts = dot(r.mixed_grad[rows, :], r.scaled[...], (1, 1))
         for j, ref in enumerate((r.back_h, r.back_w, r.back_c)):
-            ref[pl.ds(z.base + at, z.CH), :] = parts[:, j * z.C : (j + 1) * z.C] + mask * push[j]
-
-    over(z, spread)
+            ref[z.base + at : z.base + at + size, :] = parts[:, j * z.C : (j + 1) * z.C] + mask * push[j]
+
+    over(z, spread, size)
     r.vec[...] = jnp.zeros_like(r.vec)
 
     def body(rows, at):
         start = z.base + at
-        kind = kinds(z, z.CH)
-        high = jnp.where(kind == 2, near(r.back_h, start, z.W, z.CH), near(r.back_h, start, -z.W, z.CH))
-        wide = jnp.where(kind == 2, near(r.back_w, start, z.I, z.CH), near(r.back_w, start, -z.I, z.CH))
-        high = jnp.where(kind == 0, near(r.back_h, start, 0, z.CH), high)
-        wide = jnp.where(kind == 0, near(r.back_w, start, 0, z.CH), wide * r.back[rows, :].astype(F32))
-        grad = high + wide + near(r.back_c, start, 0, z.CH)
+        kind = kinds(z, size)
+        high = jnp.where(kind == 2, near(r.back_h, start, z.W, size), near(r.back_h, start, -z.W, size))
+        wide = jnp.where(kind == 2, near(r.back_w, start, z.I, size), near(r.back_w, start, -z.I, size))
+        high = jnp.where(kind == 0, near(r.back_h, start, 0, size), high)
+        wide = jnp.where(kind == 0, near(r.back_w, start, 0, size), wide * r.back[rows, :].astype(F32))
+        grad = high + wide + near(r.back_c, start, 0, size)
         unit = r.unit1[rows, :].astype(F32)
         r.vec[0] += rows8(grad * unit)
         r.vec[1] += rows8(grad)
-        grad = r.half_grad[rows, :] + norm_back(grad, unit, r.rstd1[rows, :].astype(F32), gain, ones)
-        if not last:
+        grad = r.half_grad[rows, :] + norm_back(grad, unit, r.rstd1[rows, :].astype(F32), gain)
+        if last:
+            real = min(rows.stop, z.N0) - at
+            r.state_grad[at : at + real, :] = (grad * r.mask[rows, :])[:real]
+        else:
             r.state_grad[rows, :] = grad
-            return
-        grad = grad * r.mask[rows, :]
-        left = z.N0 - (z.chunks - 1) * z.CH
-
-        @pl.when(at < z.N0 - z.CH + 1)
-        def _():
-            r.state_grad[rows, :] = grad
-
-        @pl.when(at > z.N0 - z.CH)
-        def _():
-            r.state_grad[z.N0 - left :, :] = grad[:left]
-
-    over(z, body)
+
+    over(z, body, size)
     stray = r.back_h[z.base + z.N0 - z.W : z.base + z.N0, :]
     r.vec[1] -= rows8(jnp.where(kinds(z, z.W) == 1, stray, 0.0))
     r.first_norm[...] = jnp.concatenate([total(r.vec[0]), total(r.vec[1])], axis=0)
@@ -779,7 +752,7 @@
             ebp=kept(z.L, 3 * z.C), **saved_early(z), **token,
         ),
         dict(normed=kept(z.long, z.C), sums=kept(3, 8, z.C)),
-        5, 10, smem, have,
+        5, 5, smem, have,
     )
     for bit in order[1:]:
         have = widen(have, bit, b["token"] if bit == order[1] else None)
@@ -801,7 +774,7 @@
             state=kept(z.N, z.C), normed=kept(z.tall, z.C), sums=kept(3, 8, z.C), inner_bias=kept(z.L, z.H), bias_rows=kept(z.parts, 16, z.C),
             patch=kept(z.I * z.M, 9 * z.C, dtype=BF16), merge_rows=kept(z.parts * z.merge, z.C, dtype=BF16),
         ),
-        13, 22, smem,
+        11, 16, smem,
     )
     first = dict(b, act_rows=c["act_rows_0"], slope_rows=c["slope_rows_0"])
 
@@ -827,7 +800,7 @@
                 vec=kept(3, 8, z.C), inner_sums=kept(8, z.H), g_outer=kept(z.C, z.H), g_inner=kept(z.C, z.H),
                 turned=kept(2, z.H, z.C, dtype=BF16),
             ),
-            6, 6, smem, chain and chain.held(),
+            6, 4, smem, chain and chain.held(),
         )
         if chain:
             chain.step(d["token"])
@@ -846,7 +819,7 @@
                 vec=kept(2, 8, z.C), g_project=kept(z.C, z.C), g_mix=kept(z.I * z.C, 3 * z.C),
                 rows=kept(z.parts * z.shared, z.C, dtype=BF16),
             ),
-            5, 6, smem, chain and chain.held(),
+            4, 4, smem, chain and chain.held(),
         )
         parts = [d, t]
         if chain:
@@ -864,7 +837,7 @@
             ),
             dict(state_grad=kept(z.N, z.C) if l else arr(z.N0, z.C), first_norm=arr(2, z.C), **token),
             dict(back_h=kept(z.long, z.C), back_w=kept(z.long, z.C), back_c=kept(z.long, z.C), vec=kept(2, 8, z.C)),
-            6, 4, (), chain and chain.held(),
+            5, 3, (), chain and chain.held(),
         )
         if chain:
             chain.step(e["token"])
@@ -892,7 +865,7 @@
         dict(place=place, have=sent, got=got, merge_have=merge, merge_got=merge_got, feed_rows=feed_rows),
         final_outputs(z),
         dict(rows=kept(z.L, z.parts * z.shared, z.C, dtype=BF16), merge_rows=kept(z.parts * z.merge, z.C, dtype=BF16)),
-        8, 2, smem,
+        5, 2, smem,
     )
     return (
         c["features"], images_grad, g["mix_weight"], g["mix_bias"], g["squeeze_weight"].transpose(0, 2, 1),

time: 122 us -> 96.9 us (0.79)
  Pallas kernels: 70.5 us -> 42.4 us
  waiting for transfers between devices: 22.7 us -> 25 us
    pallas_call x11, Pallas kernels: 70.5 us -> 42.4 us  [call(): pl.pallas_call(kernel, out_shape=list(outs.values()), in_specs=[scalar if...]
    ppermute x19, waiting for transfers between devices: 22.7 us -> 25 us  [swap(): return lax.ppermute(x, axis, [(a, a ^ bit) for a in range(n)])]
  transfers between devices with their start and end apart: 19 -> 19, of which waited for: 10 -> 10; matrix products, arithmetic and copies ran while one was open for 1% -> 2% of each run, Pallas kernels for 27% -> 19%
where the time goes in v4:
time: 96.9 us; the launch traced here: 96.7 us
  Pallas kernels  42.4 us (44%)
  waiting for transfers between devices  25 us (26%)
  starting transfers between devices  22.8 us (24%)
  local copies, waits for them, and re-layouts  3.79 us (4%)
  other arithmetic  1.55 us (2%)
  between operations  1.21 us (1%)
    pallas_call x11, Pallas kernels, call(): pl.pallas_call(kernel, out_shape=list(outs.values()), in_specs=[scalar if...  42.4 us
    ppermute x19, waiting for transfers between devices, swap(): return lax.ppermute(x, axis, [(a, a ^ bit) for a in range(n)])  25 us
    ppermute x19, starting transfers between devices, swap(): return lax.ppermute(x, axis, [(a, a ^ bit) for a in range(n)])  22.8 us
    unnamed x42, local copies, waits for them, and re-layouts  3.41 us
  transfers between devices with their start and end apart: 19, of which 10 were waited for; matrix products, arithmetic and copies ran while one was open for 2% of the time, Pallas kernels for 19%

profile of v4, /device:TPU:0, one launch (start us, length us, event | category | flops | bytes accessed | tf_op | source)
XLA Modules:
  0.0 96.7 jit_solution(1014628023861510964)
XLA Ops:
  1.4 0.8 copy-done.6
  2.9 3.0 %collective-permute-start = (bf16[1,272,128]{2,1,0:T(8,128)(2,1)S(1)}, bf16[1,272,128]{2,1,0:T(8,128)(2,1)S(1)}, u32[]{:S(2)}, u32[]{:S(2)}) collective-permute-start(bf16[1,272,128]{2,1,0:T(8,128)(2,1)S(1)} %bitcast.34), channel_id=1, source_target_pairs={{0,2},{1,3},{2,0},{3,1},{4,6},{5,7},{6,4},{7,5},{8,10},{9,11},{10,... | collective-permute-start | bytes 208904 | tf_op jit(solution)/shard_map/ppermute | solution.py:654
  6.1 2.8 %shard_map.322 = (f32[2688,128]{1,0:T(8,128)S(1)}, bf16[2688,128]{1,0:T(8,128)(2,1)S(1)}, bf16[2688,128]{1,0:T(8,128)(2,1)S(1)}, bf16[864,320]{1,0:T(8,128)(2,1)...) custom-call(s32[2,2]{1,0:T(2,128)S(1)} %copy-done.13, ...), custom_call_target="tpu_custom_call" | custom-call | flops 3449999872 | tf_op jit(solution)/shard_map/pallas_call | solution.py:105
  9.0 1.6 %collective-permute-start.1 = (bf16[2,272,128]{2,1,0:T(8,128)(2,1)S(1)}, bf16[2,272,128]{2,1,0:T(8,128)(2,1)S(1)}, u32[]{:S(2)}, u32[]{:S(2)}) collective-permute-start(bf16[2,272,128]{2,1,0:T(8,128)(2,1)S(1)} %pad_maximum_fusion.6.refs_14_), channel_id=1, source_target_pairs={{0,4},{1,5},{2,6},{3,7},{4,0},{5,1},{6,2},{7,3},{8,12},{9,13},{10,... | collective-permute-start | bytes 417800 | tf_op jit(solution)/shard_map/ppermute | solution.py:654
  10.6 4.5 %shard_map.324 = (f32[2688,128]{1,0:T(8,128)S(1)}, bf16[384,384]{1,0:T(8,128)(2,1)S(1)}, f32[2,32,384]{2,1,0:T(8,128)S(1)}, f32[2,384]{1,0:T(2,128)S(1)}, bf16[2...) custom-call(bf16[2592,128]{1,0:T(8,128)(2,1)S(1)} %bitcast.45, ...), custom_call_target="tpu_custom_call" | custom-call | flops 5750000128 | tf_op jit(solution)/shard_map/pallas_call | solution.py:105
  15.3 1.5 %collective-permute-done.2 = bf16[4,272,128]{2,1,0:T(8,128)(2,1)S(1)} collective-permute-done((bf16[4,272,128]{2,1,0:T(8,128)(2,1)S(1)}, bf16[4,272,128]{2,1,0:T(8,128)(2,1)S(1)}, u32[]{:S(2)}, u32[]{:S(2)}) %collective-permute-start.2) | collective-permute-done | bytes 278560 | tf_op jit(solution)/shard_map/ppermute | solution.py:654
  16.9 15.9 %shard_map.325 = (bf16[2,18,5760]{2,1,0:T(8,128)(2,1)S(1)}, bf16[4,368,128]{2,1,0:T(8,128)(2,1)S(1)}, bf16[4,368,128]{2,1,0:T(8,128)(2,1)S(1)}, bf16[2,512,128]{...) custom-call(s32[2,2]{1,0:T(2,128)S(1)} %copy-done.13, ...), custom_call_target="tpu_custom_call" | custom-call | flops 18400000000 | tf_op jit(solution)/shard_map/pallas_call | solution.py:105
  32.9 3.4 %shard_map.326 = (f32[2688,128]{1,0:T(8,128)S(1)}, f32[8,128]{1,0:T(8,128)S(1)}, bf16[4,128,128]{2,1,0:T(8,128)(2,1)S(1)}, bf16[4,128,128]{2,1,0:T(8,128)(2,1)S(1)}, f32[1,128]{1,0:T(1,128)}) custom-call(s32[1]{0:T(128)} %bitcast.5.refs_3_.refs_6_.refs_0_.refs_1_, f32[2688,128]{1,0:T(8,128)S(1)} %get-tuple-element.105.refs_2_.refs_1_.refs_0_, ...), custom_call_target="tpu_custom_call" | custom-call | flops 4600000000 | tf_op jit(solution)/shard_map/pallas_call | solution.py:105
  36.3 3.6 %shard_map.327 = (bf16[2688,256]{1,0:T(8,128)(2,1)S(1)}, bf16[384,256]{1,0:T(8,128)(2,1)S(1)}, f32[3,8,128]{2,1,0:T(8,128)S(1)}, bf16[4,96,128]{2,1,0:T(8,128)(2...) custom-call(s32[2,2]{1,0:T(2,128)S(1)} %copy-done.13, s32[1]{0:T(128)} %bitcast.5.refs_3_.refs_6_.refs_0_.refs_1_, ...), custom_call_target="tpu_custom_call" | custom-call | flops 4600000000 | tf_op jit(solution)/shard_map/pallas_call | solution.py:105
  40.4 1.8 %shard_map.328 = (f32[2688,128]{1,0:T(8,128)S(1)}, f32[2,128]{1,0:T(2,128)S(1)}, f32[1,128]{1,0:T(1,128)S(1)}) custom-call(f32[2688,128]{1,0:T(8,128)S(1)} %get-tuple-element.105.refs_2_.refs_1_.refs_0_, bf16[2688,128]{1,0:T(8,128)(2,1)S(1)} %get-tuple-element.116.refs_1_, f32[2,2,128]{2,1,0:T(2,128)S(1)} %copy-done.11, ...), custom_call_target="tpu_custom_call" | custom-call | flops 3449999872 | tf_op jit(solution)/shard_map/pallas_call | solution.py:105
  42.4 1.3 %collective-permute-start.4 = (bf16[2,592,128]{2,1,0:T(8,128)(2,1)S(1)}, bf16[2,592,128]{2,1,0:T(8,128)(2,1)S(1)}, u32[]{:S(2)}, u32[]{:S(2)}) collective-permute-start(bf16[2,592,128]{2,1,0:T(8,128)(2,1)S(1)} %get-tuple-element.210), channel_id=1, source_target_pairs={{0,2},{1,3},{2,0},{3,1},{4,6},{5,7},{6,4},{7,5},{8,10},{9,11},{10,... | collective-permute-start | bytes 909320 | tf_op jit(solution)/shard_map/ppermute | solution.py:654
  43.7 2.8 %shard_map.329 = (f32[2688,128]{1,0:T(8,128)S(1)}, f32[8,128]{1,0:T(8,128)S(1)}, bf16[4,128,128]{2,1,0:T(8,128)(2,1)S(1)}, bf16[4,128,128]{2,1,0:T(8,128)(2,1)S(1)}, f32[1,128]{1,0:T(1,128)S(1)}) custom-call(s32[1]{0:T(128)} %bitcast.5.refs_3_.refs_6_.refs_0_.refs_1_, f32[2688,128]{1,0:T(8,128)S(1)} %get-tuple-element.105.refs_2_.refs_1_.refs_0_, ...), custom_call_target="tpu_custom_call" | custom-call | flops 4600000000 | tf_op jit(solution)/shard_map/pallas_call | solution.py:105
  46.6 5.4 %collective-permute-done.4 = bf16[2,592,128]{2,1,0:T(8,128)(2,1)S(1)} collective-permute-done((bf16[2,592,128]{2,1,0:T(8,128)(2,1)S(1)}, bf16[2,592,128]{2,1,0:T(8,128)(2,1)S(1)}, u32[]{:S(2)}, u32[]{:S(2)}) %collective-permute-start.4) | collective-permute-done | bytes 303136 | tf_op jit(solution)/shard_map/ppermute | solution.py:654
  52.6 3.2 %shard_map.330 = (bf16[2688,256]{1,0:T(8,128)(2,1)S(1)}, bf16[384,256]{1,0:T(8,128)(2,1)S(1)}, f32[3,8,128]{2,1,0:T(8,128)S(1)}, bf16[4,96,128]{2,1,0:T(8,128)(2...) custom-call(s32[2,2]{1,0:T(2,128)S(1)} %copy-done.13, s32[1]{0:T(128)} %bitcast.5.refs_3_.refs_6_.refs_0_.refs_1_, ...), custom_call_target="tpu_custom_call" | custom-call | flops 4600000000 | tf_op jit(solution)/shard_map/pallas_call | solution.py:105
  55.9 1.6 %collective-permute-done.5 = bf16[1,592,128]{2,1,0:T(8,128)(2,1)S(1)} collective-permute-done((bf16[1,592,128]{2,1,0:T(8,128)(2,1)S(1)}, bf16[1,592,128]{2,1,0:T(8,128)(2,1)S(1)}, u32[]{:S(2)}, u32[]{:S(2)}) %collective-permute-start.5) | collective-permute-done | bytes 151584 | tf_op jit(solution)/shard_map/ppermute | solution.py:654
  57.6 2.9 %shard_map.331 = (f32[2592,128]{1,0:T(8,128)}, f32[2,128]{1,0:T(2,128)S(1)}, f32[1,128]{1,0:T(1,128)S(1)}) custom-call(f32[2688,128]{1,0:T(8,128)S(1)} %get-tuple-element.105.refs_2_.refs_1_.refs_0_, bf16[2688,128]{1,0:T(8,128)(2,1)S(1)} %get-tuple-element.116.refs_1_, f32[2,2,128]{2,1,0:T(2,128)S(1)} %copy-done.11, ...), custom_call_target="tpu_custom_call" | custom-call | flops 3449999872 | tf_op jit(solution)/shard_map/pallas_call | solution.py:105
  60.6 1.3 %collective-permute-start.7 = (bf16[2,224,128]{2,1,0:T(8,128)(2,1)S(1)}, bf16[2,224,128]{2,1,0:T(8,128)(2,1)S(1)}, u32[]{:S(2)}, u32[]{:S(2)}) collective-permute-start(bf16[2,224,128]{2,1,0:T(8,128)(2,1)S(1)} %slice.90), channel_id=1, source_target_pairs={{0,2},{1,3},{2,0},{3,1},{4,6},{5,7},{6,4},{7,5},{8,10},{9,11},{10,... | collective-permute-start | bytes 344072 | tf_op jit(solution)/shard_map/ppermute | solution.py:654
  61.9 1.1 %copy.38 = bf16[2,18,5760]{2,0,1:T(2,128)(2,1)} copy(bf16[2,18,5760]{2,1,0:T(8,128)(2,1)S(1)} %get-tuple-element.192) | data formatting | bytes 829440
  63.0 1.6 %collective-permute-start.14 = (bf16[1,592,128]{2,1,0:T(8,128)(2,1)S(1)}, bf16[1,592,128]{2,1,0:T(8,128)(2,1)S(1)}, u32[]{:S(2)}, u32[]{:S(2)}) collective-permute-start(bf16[1,592,128]{2,1,0:T(8,128)(2,1)S(1)} %add_convert_fusion.5.refs_9_), channel_id=1, source_target_pairs={{0,8},{8,0},{16,24},{24,16},{1,9},{9,1},{17,25},{25,17},{2,10},{10... | collective-permute-start | bytes 454664 | tf_op jit(solution)/shard_map/ppermute | solution.py:654
  64.6 0.9 collective-permute-done.7
  66.3 3.5 %collective-permute-done.8 = bf16[1,224,128]{2,1,0:T(8,128)(2,1)S(1)} collective-permute-done((bf16[1,224,128]{2,1,0:T(8,128)(2,1)S(1)}, bf16[1,224,128]{2,1,0:T(8,128)(2,1)S(1)}, u32[]{:S(2)}, u32[]{:S(2)}) %collective-permute-start.8) | collective-permute-done | bytes 57376 | tf_op jit(solution)/shard_map/ppermute | solution.py:654
  69.8 1.6 %collective-permute-start.9 = (bf16[1,240,128]{2,1,0:T(8,128)(2,1)S(1)}, bf16[1,240,128]{2,1,0:T(8,128)(2,1)S(1)}, u32[]{:S(2)}, u32[]{:S(2)}) collective-permute-start(bf16[1,240,128]{2,1,0:T(8,128)(2,1)S(1)} %pad_maximum_fusion.9), channel_id=1, source_target_pairs={{0,8},{8,0},{16,24},{24,16},{1,9},{9,1},{17,25},{25,17},{2,10},{10... | collective-permute-start | bytes 184328 | tf_op jit(solution)/shard_map/ppermute | solution.py:654
  71.5 2.7 %collective-permute-start.15 = (bf16[1,592,128]{2,1,0:T(8,128)(2,1)S(1)}, bf16[1,592,128]{2,1,0:T(8,128)(2,1)S(1)}, u32[]{:S(2)}, u32[]{:S(2)}) collective-permute-start(bf16[1,592,128]{2,1,0:T(8,128)(2,1)S(1)} %add_convert_fusion.4), channel_id=1, source_target_pairs={{0,16},{8,24},{16,0},{24,8},{1,17},{9,25},{17,1},{25,9},{2,18},{10... | collective-permute-start | bytes 454664 | tf_op jit(solution)/shard_map/ppermute | solution.py:654
  74.2 2.6 %collective-permute-start.10 = (bf16[1,240,128]{2,1,0:T(8,128)(2,1)S(1)}, bf16[1,240,128]{2,1,0:T(8,128)(2,1)S(1)}, u32[]{:S(2)}, u32[]{:S(2)}) collective-permute-start(bf16[1,240,128]{2,1,0:T(8,128)(2,1)S(1)} %add_convert_fusion.8), channel_id=1, source_target_pairs={{0,16},{8,24},{16,0},{24,8},{1,17},{9,25},{17,1},{25,9},{2,18},{10... | collective-permute-start | bytes 184328 | tf_op jit(solution)/shard_map/ppermute | solution.py:654
  76.8 3.0 %collective-permute-done.15 = bf16[1,592,128]{2,1,0:T(8,128)(2,1)S(1)} collective-permute-done((bf16[1,592,128]{2,1,0:T(8,128)(2,1)S(1)}, bf16[1,592,128]{2,1,0:T(8,128)(2,1)S(1)}, u32[]{:S(2)}, u32[]{:S(2)}) %collective-permute-start.15) | collective-permute-done | bytes 151584 | tf_op jit(solution)/shard_map/ppermute | solution.py:654
  79.8 2.5 %collective-permute-start.16 = (bf16[1,464,128]{2,1,0:T(8,128)(2,1)S(1)}, bf16[1,464,128]{2,1,0:T(8,128)(2,1)S(1)}, u32[]{:S(2)}, u32[]{:S(2)}) collective-permute-start(bf16[1,464,128]{2,1,0:T(8,128)(2,1)S(1)} %slice.99), channel_id=1, source_target_pairs={{0,4},{1,5},{2,6},{3,7},{4,0},{5,1},{6,2},{7,3},{8,12},{9,13},{10,... | collective-permute-start | bytes 356360 | tf_op jit(solution)/shard_map/ppermute | solution.py:654
  82.9 3.3 %collective-permute-done.11 = bf16[112,128]{1,0:T(8,128)(2,1)S(1)} collective-permute-done((bf16[112,128]{1,0:T(8,128)(2,1)S(1)}, bf16[112,128]{1,0:T(8,128)(2,1)S(1)}, u32[]{:S(2)}, u32[]{:S(2)}) %collective-permute-start.11) | collective-permute-done | bytes 28704 | tf_op jit(solution)/shard_map/ppermute | solution.py:654
  86.3 1.2 %collective-permute-start.17 = (bf16[2,464,128]{2,1,0:T(8,128)(2,1)S(1)}, bf16[2,464,128]{2,1,0:T(8,128)(2,1)S(1)}, u32[]{:S(2)}, u32[]{:S(2)}) collective-permute-start(bf16[2,464,128]{2,1,0:T(8,128)(2,1)S(1)} %pad_maximum_fusion.4), channel_id=1, source_target_pairs={{0,2},{1,3},{2,0},{3,1},{4,6},{5,7},{6,4},{7,5},{8,10},{9,11},{10,... | collective-permute-start | bytes 712712 | tf_op jit(solution)/shard_map/ppermute | solution.py:654
  87.5 0.9 collective-permute-start.12
  88.5 4.0 %collective-permute-done.17 = bf16[2,464,128]{2,1,0:T(8,128)(2,1)S(1)} collective-permute-done((bf16[2,464,128]{2,1,0:T(8,128)(2,1)S(1)}, bf16[2,464,128]{2,1,0:T(8,128)(2,1)S(1)}, u32[]{:S(2)}, u32[]{:S(2)}) %collective-permute-start.17) | collective-permute-done | bytes 237600 | tf_op jit(solution)/shard_map/ppermute | solution.py:654
  93.2 1.4 %collective-permute-done.13.refs_2_ = bf16[400,128]{1,0:T(8,128)(2,1)S(1)} collective-permute-done((bf16[400,128]{1,0:T(8,128)(2,1)S(1)}, bf16[400,128]{1,0:T(8,128)(2,1)S(1)}, u32[]{:S(2)}, u32[]{:S(2)}) %collective-permute-start.13) | collective-permute-done | bytes 102432 | tf_op jit(solution)/shard_map/ppermute | solution.py:654
  94.6 1.5 %shard_map.332 = (f32[2,3,128,128]{3,2,1,0:T(8,128)}, f32[2,2,128]{2,1,0:T(2,128)}, f32[2,32,128]{2,1,0:T(8,128)}, f32[2,32]{1,0:T(2,128)}, f32[2,32,384]{2,1,0:...) custom-call(s32[1]{0:T(128)} %bitcast.5.refs_3_.refs_6_.refs_0_.refs, ...), custom_call_target="tpu_custom_call" | custom-call | flops 2300000000 | tf_op jit(solution)/shard_map/pallas_call | solution.py:105
  (104 shorter events, 6.4 us)
Async XLA Ops:
  2.8 3.1 %copy-start.13 = (s32[2,2]{1,0:T(2,128)S(1)}, s32[2,2]{1,0:T(2,128)}, u32[]{:S(2)}) copy-start(s32[2,2]{1,0:T(2,128)} %refs_0_.7) | copy-start | bytes 52
  2.9 6.1 %collective-permute-start = (bf16[1,272,128]{2,1,0:T(8,128)(2,1)S(1)}, bf16[1,272,128]{2,1,0:T(8,128)(2,1)S(1)}, u32[]{:S(2)}, u32[]{:S(2)}) collective-permute-start(bf16[1,272,128]{2,1,0:T(8,128)(2,1)S(1)} %bitcast.34), channel_id=1, source_target_pairs={{0,2},{1,3},{2,0},{3,1},{4,6},{5,7},{6,4},{7,5},{8,10},{9,11},{10,... | collective-permute-start | bytes 208904 | tf_op jit(solution)/shard_map/ppermute | solution.py:654
  5.9 4.6 %copy-start.1 = (bf16[2,36,36,128]{3,0,2,1:T(2,128)(2,1)S(1)}, bf16[2,36,36,128]{3,0,2,1:T(2,128)(2,1)}, u32[]{:S(2)}) copy-start(bf16[2,36,36,128]{3,0,2,1:T(2,128)(2,1)} %param.19) | copy-start | bytes 1990660
  6.0 4.6 %copy-start.2 = (bf16[2,3,128,128]{3,2,1,0:T(8,128)(2,1)S(1)}, bf16[2,3,128,128]{3,2,1,0:T(8,128)(2,1)}, u32[]{:S(2)}) copy-start(bf16[2,3,128,128]{3,2,1,0:T(8,128)(2,1)} %refs_14_.5) | copy-start | bytes 589828
  6.0 4.6 %copy-start.3 = (f32[2,32,384]{2,1,0:T(8,128)S(1)}, f32[2,32,384]{2,1,0:T(8,128)}, u32[]{:S(2)}) copy-start(f32[2,32,384]{2,1,0:T(8,128)} %refs_4_.1) | copy-start | bytes 294916
  6.0 4.6 %copy-start.4 = (bf16[2,128,128]{2,1,0:T(8,128)(2,1)S(1)}, bf16[2,128,128]{2,1,0:T(8,128)(2,1)}, u32[]{:S(2)}) copy-start(bf16[2,128,128]{2,1,0:T(8,128)(2,1)} %refs_18_.5) | copy-start | bytes 196612
  6.0 4.6 %copy-start.7 = (f32[2,128,32]{1,2,0:T(8,128)S(1)}, f32[2,128,32]{1,2,0:T(8,128)}, u32[]{:S(2)}) copy-start(f32[2,128,32]{1,2,0:T(8,128)} %param.24) | copy-start | bytes 98308
  6.0 4.6 %copy-start.8 = (f32[2,384]{1,0:T(2,128)S(1)}, f32[2,384]{1,0:T(2,128)}, u32[]{:S(2)}) copy-start(f32[2,384]{1,0:T(2,128)} %refs_5_.3) | copy-start | bytes 9220
  6.0 4.6 %copy-start.9 = (f32[2,2,128]{2,1,0:T(2,128)S(1)}, f32[2,2,128]{2,1,0:T(2,128)}, u32[]{:S(2)}) copy-start(f32[2,2,128]{2,1,0:T(2,128)} %refs_15_.5) | copy-start | bytes 6148
  6.0 4.6 %copy-start.10 = (f32[2,2,128]{2,1,0:T(2,128)S(1)}, f32[2,2,128]{2,1,0:T(2,128)}, u32[]{:S(2)}) copy-start(f32[2,2,128]{2,1,0:T(2,128)} %refs_21_.5) | copy-start | bytes 6148
  6.0 4.6 %copy-start.11 = (f32[2,2,128]{2,1,0:T(2,128)S(1)}, f32[2,2,128]{2,1,0:T(2,128)}, u32[]{:S(2)}) copy-start(f32[2,2,128]{2,1,0:T(2,128)} %refs_2_.5) | copy-start | bytes 6148
  6.0 4.6 %copy-start.14 = (f32[2,32]{1,0:T(2,128)S(1)}, f32[2,32]{1,0:T(2,128)}, u32[]{:S(2)}) copy-start(f32[2,32]{1,0:T(2,128)} %refs_17_.5) | copy-start | bytes 772
  6.1 4.6 %copy-start.15 = (f32[2,128]{1,0:T(2,128)S(1)}, f32[2,128]{1,0:T(2,128)}, u32[]{:S(2)}) copy-start(f32[2,128]{1,0:T(2,128)} %refs_19_.5) | copy-start | bytes 3076
  9.0 6.2 %collective-permute-start.1 = (bf16[2,272,128]{2,1,0:T(8,128)(2,1)S(1)}, bf16[2,272,128]{2,1,0:T(8,128)(2,1)S(1)}, u32[]{:S(2)}, u32[]{:S(2)}) collective-permute-start(bf16[2,272,128]{2,1,0:T(8,128)(2,1)S(1)} %pad_maximum_fusion.6.refs_14_), channel_id=1, source_target_pairs={{0,4},{1,5},{2,6},{3,7},{4,0},{5,1},{6,2},{7,3},{8,12},{9,13},{10,... | collective-permute-start | bytes 417800 | tf_op jit(solution)/shard_map/ppermute | solution.py:654
  10.6 4.7 %copy-start.18 = (f32[320]{0:T(512)S(1)}, f32[320]{0:T(512)}, u32[]{:S(2)}) copy-start(f32[320]{0:T(512)} %param.37) | copy-start | bytes 3844
  15.2 1.6 %collective-permute-start.2 = (bf16[4,272,128]{2,1,0:T(8,128)(2,1)S(1)}, bf16[4,272,128]{2,1,0:T(8,128)(2,1)S(1)}, u32[]{:S(2)}, u32[]{:S(2)}) collective-permute-start(bf16[4,272,128]{2,1,0:T(8,128)(2,1)S(1)} %pad_maximum_fusion.3), channel_id=1, source_target_pairs={{0,1},{1,0},{2,3},{3,2},{4,5},{5,4},{6,7},{7,6},{8,9},{9,8},{10,11... | collective-permute-start | bytes 835592 | tf_op jit(solution)/shard_map/ppermute | solution.py:654
  39.9 2.3 %collective-permute-start.3 = (bf16[4,592,128]{2,1,0:T(8,128)(2,1)S(1)}, bf16[4,592,128]{2,1,0:T(8,128)(2,1)S(1)}, u32[]{:S(2)}, u32[]{:S(2)}) collective-permute-start(bf16[4,592,128]{2,1,0:T(8,128)(2,1)S(1)} %pad_maximum_fusion), channel_id=1, source_target_pairs={{0,1},{1,0},{2,3},{3,2},{4,5},{5,4},{6,7},{7,6},{8,9},{9,8},{10,11... | collective-permute-start | bytes 1818632 | tf_op jit(solution)/shard_map/ppermute | solution.py:654
  42.4 9.5 %collective-permute-start.4 = (bf16[2,592,128]{2,1,0:T(8,128)(2,1)S(1)}, bf16[2,592,128]{2,1,0:T(8,128)(2,1)S(1)}, u32[]{:S(2)}, u32[]{:S(2)}) collective-permute-start(bf16[2,592,128]{2,1,0:T(8,128)(2,1)S(1)} %get-tuple-element.210), channel_id=1, source_target_pairs={{0,2},{1,3},{2,0},{3,1},{4,6},{5,7},{6,4},{7,5},{8,10},{9,11},{10,... | collective-permute-start | bytes 909320 | tf_op jit(solution)/shard_map/ppermute | solution.py:654
  52.1 5.5 %collective-permute-start.5 = (bf16[1,592,128]{2,1,0:T(8,128)(2,1)S(1)}, bf16[1,592,128]{2,1,0:T(8,128)(2,1)S(1)}, u32[]{:S(2)}, u32[]{:S(2)}) collective-permute-start(bf16[1,592,128]{2,1,0:T(8,128)(2,1)S(1)} %get-tuple-element.212), channel_id=1, source_target_pairs={{0,4},{1,5},{2,6},{3,7},{4,0},{5,1},{6,2},{7,3},{8,12},{9,13},{10,... | collective-permute-start | bytes 454664 | tf_op jit(solution)/shard_map/ppermute | solution.py:654
  55.9 4.7 %collective-permute-start.6 = (bf16[4,224,128]{2,1,0:T(8,128)(2,1)S(1)}, bf16[4,224,128]{2,1,0:T(8,128)(2,1)S(1)}, u32[]{:S(2)}, u32[]{:S(2)}) collective-permute-start(bf16[4,224,128]{2,1,0:T(8,128)(2,1)S(1)} %pad_maximum_fusion.5), channel_id=1, source_target_pairs={{0,1},{1,0},{2,3},{3,2},{4,5},{5,4},{6,7},{7,6},{8,9},{9,8},{10,11... | collective-permute-start | bytes 688136 | tf_op jit(solution)/shard_map/ppermute | solution.py:654
  60.6 4.9 %collective-permute-start.7 = (bf16[2,224,128]{2,1,0:T(8,128)(2,1)S(1)}, bf16[2,224,128]{2,1,0:T(8,128)(2,1)S(1)}, u32[]{:S(2)}, u32[]{:S(2)}) collective-permute-start(bf16[2,224,128]{2,1,0:T(8,128)(2,1)S(1)} %slice.90), channel_id=1, source_target_pairs={{0,2},{1,3},{2,0},{3,1},{4,6},{5,7},{6,4},{7,5},{8,10},{9,11},{10,... | collective-permute-start | bytes 344072 | tf_op jit(solution)/shard_map/ppermute | solution.py:654
  63.0 8.4 %collective-permute-start.14 = (bf16[1,592,128]{2,1,0:T(8,128)(2,1)S(1)}, bf16[1,592,128]{2,1,0:T(8,128)(2,1)S(1)}, u32[]{:S(2)}, u32[]{:S(2)}) collective-permute-start(bf16[1,592,128]{2,1,0:T(8,128)(2,1)S(1)} %add_convert_fusion.5.refs_9_), channel_id=1, source_target_pairs={{0,8},{8,0},{16,24},{24,16},{1,9},{9,1},{17,25},{25,17},{2,10},{10... | collective-permute-start | bytes 454664 | tf_op jit(solution)/shard_map/ppermute | solution.py:654
  65.5 4.2 %collective-permute-start.8 = (bf16[1,224,128]{2,1,0:T(8,128)(2,1)S(1)}, bf16[1,224,128]{2,1,0:T(8,128)(2,1)S(1)}, u32[]{:S(2)}, u32[]{:S(2)}) collective-permute-start(bf16[1,224,128]{2,1,0:T(8,128)(2,1)S(1)} %slice.92), channel_id=1, source_target_pairs={{0,4},{1,5},{2,6},{3,7},{4,0},{5,1},{6,2},{7,3},{8,12},{9,13},{10,... | collective-permute-start | bytes 172040 | tf_op jit(solution)/shard_map/ppermute | solution.py:654
  69.8 4.4 %collective-permute-start.9 = (bf16[1,240,128]{2,1,0:T(8,128)(2,1)S(1)}, bf16[1,240,128]{2,1,0:T(8,128)(2,1)S(1)}, u32[]{:S(2)}, u32[]{:S(2)}) collective-permute-start(bf16[1,240,128]{2,1,0:T(8,128)(2,1)S(1)} %pad_maximum_fusion.9), channel_id=1, source_target_pairs={{0,8},{8,0},{16,24},{24,16},{1,9},{9,1},{17,25},{25,17},{2,10},{10... | collective-permute-start | bytes 184328 | tf_op jit(solution)/shard_map/ppermute | solution.py:654
  71.5 8.2 %collective-permute-start.15 = (bf16[1,592,128]{2,1,0:T(8,128)(2,1)S(1)}, bf16[1,592,128]{2,1,0:T(8,128)(2,1)S(1)}, u32[]{:S(2)}, u32[]{:S(2)}) collective-permute-start(bf16[1,592,128]{2,1,0:T(8,128)(2,1)S(1)} %add_convert_fusion.4), channel_id=1, source_target_pairs={{0,16},{8,24},{16,0},{24,8},{1,17},{9,25},{17,1},{25,9},{2,18},{10... | collective-permute-start | bytes 454664 | tf_op jit(solution)/shard_map/ppermute | solution.py:654
  74.2 8.1 %collective-permute-start.10 = (bf16[1,240,128]{2,1,0:T(8,128)(2,1)S(1)}, bf16[1,240,128]{2,1,0:T(8,128)(2,1)S(1)}, u32[]{:S(2)}, u32[]{:S(2)}) collective-permute-start(bf16[1,240,128]{2,1,0:T(8,128)(2,1)S(1)} %add_convert_fusion.8), channel_id=1, source_target_pairs={{0,16},{8,24},{16,0},{24,8},{1,17},{9,25},{17,1},{25,9},{2,18},{10... | collective-permute-start | bytes 184328 | tf_op jit(solution)/shard_map/ppermute | solution.py:654
  79.8 6.5 %collective-permute-start.16 = (bf16[1,464,128]{2,1,0:T(8,128)(2,1)S(1)}, bf16[1,464,128]{2,1,0:T(8,128)(2,1)S(1)}, u32[]{:S(2)}, u32[]{:S(2)}) collective-permute-start(bf16[1,464,128]{2,1,0:T(8,128)(2,1)S(1)} %slice.99), channel_id=1, source_target_pairs={{0,4},{1,5},{2,6},{3,7},{4,0},{5,1},{6,2},{7,3},{8,12},{9,13},{10,... | collective-permute-start | bytes 356360 | tf_op jit(solution)/shard_map/ppermute | solution.py:654
  82.3 3.9 %collective-permute-start.11 = (bf16[112,128]{1,0:T(8,128)(2,1)S(1)}, bf16[112,128]{1,0:T(8,128)(2,1)S(1)}, u32[]{:S(2)}, u32[]{:S(2)}) collective-permute-start(bf16[112,128]{1,0:T(8,128)(2,1)S(1)} %pad_maximum_fusion.11), channel_id=1, source_target_pairs={{0,4},{1,5},{2,6},{3,7},{4,0},{5,1},{6,2},{7,3},{8,12},{9,13},{10,... | collective-permute-start | bytes 86024 | tf_op jit(solution)/shard_map/ppermute | solution.py:654
  86.3 6.2 %collective-permute-start.17 = (bf16[2,464,128]{2,1,0:T(8,128)(2,1)S(1)}, bf16[2,464,128]{2,1,0:T(8,128)(2,1)S(1)}, u32[]{:S(2)}, u32[]{:S(2)}) collective-permute-start(bf16[2,464,128]{2,1,0:T(8,128)(2,1)S(1)} %pad_maximum_fusion.4), channel_id=1, source_target_pairs={{0,2},{1,3},{2,0},{3,1},{4,6},{5,7},{6,4},{7,5},{8,10},{9,11},{10,... | collective-permute-start | bytes 712712 | tf_op jit(solution)/shard_map/ppermute | solution.py:654
  87.5 5.5 %collective-permute-start.12 = (bf16[208,128]{1,0:T(8,128)(2,1)S(1)}, bf16[208,128]{1,0:T(8,128)(2,1)S(1)}, u32[]{:S(2)}, u32[]{:S(2)}) collective-permute-start(bf16[208,128]{1,0:T(8,128)(2,1)S(1)} %pad_maximum_fusion.10), channel_id=1, source_target_pairs={{0,2},{1,3},{2,0},{3,1},{4,6},{5,7},{6,4},{7,5},{8,10},{9,11},{10,... | collective-permute-start | bytes 159752 | tf_op jit(solution)/shard_map/ppermute | solution.py:654
  92.5 2.1 %collective-permute-start.18 = (bf16[4,464,128]{2,1,0:T(8,128)(2,1)S(1)}, bf16[4,464,128]{2,1,0:T(8,128)(2,1)S(1)}, u32[]{:S(2)}, u32[]{:S(2)}) collective-permute-start(bf16[4,464,128]{2,1,0:T(8,128)(2,1)S(1)} %pad_maximum_fusion.2.refs_3_), channel_id=1, source_target_pairs={{0,1},{1,0},{2,3},{3,2},{4,5},{5,4},{6,7},{7,6},{8,9},{9,8},{10,11... | collective-permute-start | bytes 1425416 | tf_op jit(solution)/shard_map/ppermute | solution.py:654
  93.1 1.5 %collective-permute-start.13 = (bf16[400,128]{1,0:T(8,128)(2,1)S(1)}, bf16[400,128]{1,0:T(8,128)(2,1)S(1)}, u32[]{:S(2)}, u32[]{:S(2)}) collective-permute-start(bf16[400,128]{1,0:T(8,128)(2,1)S(1)} %pad_maximum_fusion.7.refs_1_), channel_id=1, source_target_pairs={{0,1},{1,0},{2,3},{3,2},{4,5},{5,4},{6,7},{7,6},{8,9},{9,8},{10,11... | collective-permute-start | bytes 307208 | tf_op jit(solution)/shard_map/ppermute | solution.py:654
  (6 other events, 10.1 us)

commit v5 on v4

--- a/solution.py
+++ b/solution.py
@@ -88,12 +88,15 @@
     pass
 
 
-def call(body, ins, outs, scratch, limit, micros, smem=(), after=None):
-    if after is not None:
-        ins = dict(ins, after=after)
+def call(body, ins, outs, scratch, limit, micros, smem=(), after=(), far=()):
+    waits = {f"after{k}": array for k, array in enumerate(after)}
+    ins = dict(ins, **waits)
     vmem = pl.BlockSpec(memory_space=pltpu.VMEM)
-    scalar = pl.BlockSpec(memory_space=pltpu.SMEM)
-    waits = dict(after=0)
+    scalar, anywhere = pl.BlockSpec(memory_space=pltpu.SMEM), pl.BlockSpec(memory_space=pl.ANY)
+
+    def place(name):
+        return scalar if name in smem else anywhere if name in waits or name in far else vmem
+
     names = list(ins) + list(outs) + list(scratch)
 
     def kernel(*refs):
@@ -105,7 +108,7 @@
     found = pl.pallas_call(
         kernel,
         out_shape=list(outs.values()),
-        in_specs=[scalar if name in smem else (pl.BlockSpec(memory_space=pl.ANY) if name in waits else vmem) for name in ins],
+        in_specs=[place(name) for name in ins],
         out_specs=[vmem] * len(outs),
         scratch_shapes=list(scratch.values()),
         compiler_params=pltpu.CompilerParams(vmem_limit_bytes=limit * MIB),
@@ -354,17 +357,19 @@
     r.token[...] = jnp.zeros_like(r.token)
 
 
-def rank(z, e):
-    at, half = 0, z.parts // 2
-    while half:
-        at, e, half = at + half * (e % 2), e // 2, half // 2
-    return at
+def exchange_order(n):
+    bits = bits_of(n)
+    return bits[:1] + bits[:0:-1]
+
+
+def rank(n, e):
+    return sum((n >> k + 1) * (e // bit % 2) for k, bit in enumerate(exchange_order(n)))
 
 
 def put_blocks(z, me, rows, size, here, away, start=0):
     half = z.parts // 2
     for e in range(z.parts):
-        at = rank(z, e)
+        at = rank(z.parts, e)
         block = rows[pl.ds(pl.multiple_of((me ^ e) * size, 16), size), :]
         if at < half:
             here[at, start : start + size, :] = block
@@ -374,7 +379,7 @@
 
 def second_kernel(z, r):
     me = r.place[0]
-    for k, e in enumerate(z.found):
+    for k, e in enumerate(z.gathered):
         at = pl.multiple_of((me ^ e) * z.units, z.units)
         for l in range(z.L):
             r.inner[l, pl.ds(at, z.units), :] = r.gathered[k, 2 * l * z.units : (2 * l + 1) * z.units, :]
@@ -417,12 +422,6 @@
                     else:
                         two.append(r.normed[pl.ds(dr * z.W + col * z.I + i, z.hp, stride=2 * z.W), :])
                 r.patch[at : at + 2 * z.hp, k * z.C : (k + 1) * z.C] = jnp.concatenate(two, axis=0).astype(BF16)
-    for i in range(z.I):
-        for pair in range(z.half // 2):
-            at = i * z.M + 2 * pair * z.hp
-            merged = dot(r.patch[at : at + 2 * z.hp, :], r.merge_weight[...], (1, 1)) + r.merge_bias[...]
-            wide = jnp.concatenate([merged[: z.half], merged[z.hp : z.hp + z.half]], axis=1)
-            r.features[i, :, 2 * pair * z.O : (2 * pair + 2) * z.O] = wide.astype(BF16)
     for k in range(9):
         grad = dot(r.cot[...], r.patch[:, k * z.C : (k + 1) * z.C], (0, 0))
         r.merge_rows[k * z.O : (k + 1) * z.O, :] = grad.astype(BF16)
@@ -433,6 +432,17 @@
     rows += [jnp.zeros((z.parts * z.merge - 9 * z.O - 3, z.C), F32)]
     r.merge_rows[9 * z.O :, :] = jnp.concatenate(rows, axis=0).astype(BF16)
     put_blocks(z, me, r.merge_rows, z.merge, r.merge_here, r.merge_away)
+
+
+def features_kernel(z, r):
+    r.merged[...] = dot(r.patch[...], r.merge_weight[...], (1, 1)) + r.merge_bias[...]
+    r.token[...] = jnp.zeros_like(r.token)
+    for i in range(z.I):
+        for pair in range(z.half // 2):
+            at = i * z.M + 2 * pair * z.hp
+            wide = [r.merged[at : at + z.half, :], r.merged[at + z.hp : at + z.hp + z.half, :]]
+            wide = jnp.concatenate(wide, axis=1).astype(BF16)
+            r.features[i, :, 2 * pair * z.O : (2 * pair + 2) * z.O] = wide
 
 
 def feed_back_kernel(z, l, r):
@@ -588,15 +598,15 @@
 def last_kernel(z, r):
     me = r.place[0]
     half = z.parts // 2
-    size = z.shared
+    size = z.L * z.shared
     for at in range(z.parts):
-        spot = me ^ z.ranks[at]
+        k = at % half
         have, merge = (r.have, r.merge_have) if at < half else (r.got, r.merge_got)
-        k = at % half
-        rows = pl.ds(pl.multiple_of(spot * z.shared, 16), z.shared)
-        r.rows[0, rows, :] = have[k * size : (k + 1) * size, :]
-        r.rows[1, rows, :] = merge[k, :size, :]
-        r.merge_rows[pl.ds(pl.multiple_of(spot * z.merge, 16), z.merge), :] = merge[k, size:, :]
+        rows = pl.ds(pl.multiple_of((me ^ z.found[0][at]) * z.shared, 16), z.shared)
+        for l in range(z.L):
+            r.rows[l, rows, :] = have[k * size + l * z.shared : k * size + (l + 1) * z.shared, :]
+        rows = pl.ds(pl.multiple_of((me ^ z.found[1][at]) * z.merge, 16), z.merge)
+        r.merge_rows[rows, :] = merge[k]
     norms = r.have[half * size :, :].astype(F32) + r.got[half * size :, :].astype(F32)
     for l in range(z.L):
         rows = r.rows.at[l]
@@ -640,10 +650,16 @@
 
 def pack_kernel(z, r):
     u = z.units
+    copies = [pltpu.make_async_copy(r.inner_bias, r.bias, r.sem.at[2 * z.L])]
     for l in range(z.L):
-        r.block[2 * l * u : (2 * l + 1) * u, :] = r.inner_weight[l]
-        r.block[(2 * l + 1) * u : (2 * l + 2) * u, :] = r.outer_weight[l]
-    bias = r.inner_bias[...].astype(F32)
+        for k, ref in enumerate((r.inner_weight, r.outer_weight)):
+            at = (2 * l + k) * u
+            copies.append(pltpu.make_async_copy(ref.at[l], r.block.at[at : at + u], r.sem.at[2 * l + k]))
+    for copy in copies:
+        copy.start()
+    for copy in copies:
+        copy.wait()
+    bias = r.bias[...].astype(F32)
     if u < z.C:
         bias = jnp.concatenate([bias, jnp.zeros((z.L, z.C - u), F32)], axis=1)
     bias = jnp.concatenate([bias, jnp.zeros((16 - z.L, z.C), F32)], axis=0)
@@ -670,29 +686,28 @@
 
 
 class Chain:
-    def __init__(self, parts, hid, img):
+    def __init__(self, parts, hid):
         self.here = jnp.concatenate([part["here"] for part in parts], axis=1)
         self.away = jnp.concatenate([part["away"] for part in parts], axis=1)
-        self.left = [("hid", hid, bit) for bit in bits_of(hid)] + [("img", img, bit) for bit in bits_of(img)]
-
-    def held(self):
-        return self.here
-
-    def step(self, token=None, extra=None):
+        self.left = [("hid", hid, bit) for bit in exchange_order(hid)]
+
+    def step(self, token=None):
         axis, n, bit = self.left.pop(0)
         x = add(self.here, swap(self.away, axis, n, bit), token)
-        if x.shape[0] > 1:
-            half = x.shape[0] // 2
-            self.here, self.away = x[:half], x[half:]
-        else:
-            if extra is not None and axis == "hid":
-                x = jnp.concatenate([x, extra[None]], axis=1)
+        if axis == "img":
             self.here = self.away = x
-
-    def finish(self, extra=None):
+            return
+        half = x.shape[0] // 2
+        self.here, self.away = (x[:half], x[half:]) if half else (x[0], None)
+
+    def halve(self, token):
         while self.left:
-            self.step(None, extra)
-        return self.here[0]
+            self.step(token)
+        return self.here
+
+    def widen(self, rows, img):
+        self.here = self.away = rows
+        self.left = [("img", img, bit) for bit in bits_of(img)]
 
 
 def per_device(
@@ -704,15 +719,17 @@
         images.shape[0], images.shape[1], images.shape[3], inner_weight.shape[2] * hid, squeeze_weight.shape[2],
         merge_weight.shape[1], mix_weight.shape[0], hid,
     )
-    z.ranks = sorted(range(hid), key=partial(rank, z))
     place = lax.axis_index("hid").reshape(1)
     flat = images.transpose(1, 2, 0, 3).reshape(z.N0, z.C)
     merge_t = merge_weight.T
     squeeze_t = squeeze_weight.transpose(0, 2, 1)
+    far = [pltpu.with_memory_space_constraint(v, pltpu.HBM) for v in (inner_weight.transpose(0, 2, 1), outer_weight, inner_bias)]
     block = call(
         partial(pack_kernel, z),
-        dict(inner_weight=inner_weight.transpose(0, 2, 1), outer_weight=outer_weight, inner_bias=inner_bias, place=place),
-        dict(block=kept(2 * z.L * z.units + 16, z.C, dtype=BF16)), {}, 2, 1, dict(place=0),
+        dict(place=place, inner_weight=far[0], outer_weight=far[1], inner_bias=far[2]),
+        dict(block=kept(2 * z.L * z.units + 16, z.C, dtype=BF16)),
+        dict(bias=kept(z.L, z.units, dtype=BF16), sem=pltpu.SemaphoreType.DMA((2 * z.L + 1,))),
+        2, 1, dict(place=0), far=dict(inner_weight=0, outer_weight=0, inner_bias=0),
     )
     block = block["block"]
     smem = dict(sizes=0, place=0)
@@ -723,7 +740,7 @@
     token = dict(token=arr(1, z.C))
     a = call(
         partial(front_kernel, z),
-        dict(sizes=sizes, cotangent=cotangent, merge_weight=merge_t),
+        dict(sizes=sizes, place=place, cotangent=cotangent, merge_weight=merge_t),
         dict(
             mask=kept(z.N, z.C), edge=kept(z.N, z.C, dtype=BF16), back=kept(z.N, z.C, dtype=BF16), cot=kept(z.I * z.M, z.O, dtype=BF16),
             grad=kept(z.tall, z.C), merge_bias_sums=kept(8, z.O), **token,
@@ -737,9 +754,9 @@
         got = swap(have, "hid", hid, bit)
         return jnp.concatenate([have, got if token is None else got + token.astype(BF16)], axis=0)
 
-    z.found = [0]
+    z.gathered = [0]
     for bit in order:
-        z.found = z.found + [e ^ bit for e in z.found]
+        z.gathered = z.gathered + [e ^ bit for e in z.gathered]
     have = widen(block[None], order[0], a["token"])
     b = call(
         partial(first_kernel, z),
@@ -752,7 +769,7 @@
             ebp=kept(z.L, 3 * z.C), **saved_early(z), **token,
         ),
         dict(normed=kept(z.long, z.C), sums=kept(3, 8, z.C)),
-        5, 5, smem, have,
+        5, 5, smem, [have],
     )
     for bit in order[1:]:
         have = widen(have, bit, b["token"] if bit == order[1] else None)
@@ -761,18 +778,17 @@
         partial(second_kernel, z),
         dict(
             sizes=sizes, mask=a["mask"], edge=a["edge"], state_in=b["state"], normed2_0=b["normed2"], gathered=have, place=place,
-            ewp=b["ewp"], ebp=b["ebp"], outer_bias=outer_bias, merge_weight=merge_t, merge_bias=merge_bias.reshape(1, -1),
-            cot=a["cot"], merge_bias_sums=a["merge_bias_sums"], **small,
+            ewp=b["ewp"], ebp=b["ebp"], outer_bias=outer_bias, cot=a["cot"], merge_bias_sums=a["merge_bias_sums"], **small,
         ),
         dict(
-            features=arr(z.I, z.half, z.half * z.O, dtype=BF16),
+            patch=kept(z.I * z.M, 9 * z.C, dtype=BF16),
             merge_here=kept(z.parts // 2, z.merge, z.C, dtype=BF16), merge_away=kept(z.parts // 2, z.merge, z.C, dtype=BF16),
             inner=kept(z.L, z.H, z.C, dtype=BF16), outer=kept(z.L, z.H, z.C, dtype=BF16),
             act_rows_0=late["act_rows"], slope_rows_0=late["slope_rows"], **saved_early(z), **late,
         ),
         dict(
             state=kept(z.N, z.C), normed=kept(z.tall, z.C), sums=kept(3, 8, z.C), inner_bias=kept(z.L, z.H), bias_rows=kept(z.parts, 16, z.C),
-            patch=kept(z.I * z.M, 9 * z.C, dtype=BF16), merge_rows=kept(z.parts * z.merge, z.C, dtype=BF16),
+            merge_rows=kept(z.parts * z.merge, z.C, dtype=BF16),
         ),
         11, 16, smem,
     )
@@ -782,8 +798,8 @@
         return {name: s[name] for name in names}
 
     grad = a["grad"]
-    shares, norms = [None] * z.L, [None] * z.L
-    chain = None
+    norms, chain = [None] * z.L, None
+    merge = Chain([dict(here=c["merge_here"], away=c["merge_away"])], hid)
     for l in reversed(range(z.L)):
         s = c if l else first
         d = call(
@@ -800,10 +816,9 @@
                 vec=kept(3, 8, z.C), inner_sums=kept(8, z.H), g_outer=kept(z.C, z.H), g_inner=kept(z.C, z.H),
                 turned=kept(2, z.H, z.C, dtype=BF16),
             ),
-            6, 4, smem, chain and chain.held(),
+            6, 2, smem, [merge.here] + ([chain.here] if chain else []),
         )
-        if chain:
-            chain.step(d["token"])
+        (chain or merge).step(d["token"])
         t = call(
             partial(token_back_kernel, z, l),
             dict(
@@ -819,16 +834,13 @@
                 vec=kept(2, 8, z.C), g_project=kept(z.C, z.C), g_mix=kept(z.I * z.C, 3 * z.C),
                 rows=kept(z.parts * z.shared, z.C, dtype=BF16),
             ),
-            4, 4, smem, chain and chain.held(),
+            4, 1, smem, [(chain or merge).here],
         )
-        parts = [d, t]
+        own = Chain([d, t], hid)
         if chain:
-            chain.step(t["token"])
-        elif l:
-            parts += [dict(here=c["merge_here"], away=c["merge_away"])]
-            chain = Chain(parts, hid, img)
-        if not l:
-            tail = Chain(parts, hid, img)
+            rows = jnp.concatenate([chain.halve(t["token"]), merge.halve(t["token"])], axis=0)
+            chain.widen(rows, img)
+        held = [own.here] + ([chain.here] if chain else [])
         e = call(
             partial(mix_back_kernel, z, l, l == 0),
             dict(
@@ -837,26 +849,39 @@
             ),
             dict(state_grad=kept(z.N, z.C) if l else arr(z.N0, z.C), first_norm=arr(2, z.C), **token),
             dict(back_h=kept(z.long, z.C), back_w=kept(z.long, z.C), back_c=kept(z.long, z.C), vec=kept(2, 8, z.C)),
-            5, 3, (), chain and chain.held(),
+            5, 0.05, (), held,
         )
-        if chain:
-            chain.step(e["token"])
+        own.step(e["token"])
+        (chain or merge).step(e["token"])
+        chain, last = chain or own, own
         grad, norms[l] = e["state_grad"], e["first_norm"]
     images_grad = grad.reshape(z.side, z.side, z.I, z.C).transpose(2, 0, 1, 3)
 
-    early = chain.finish()
-    tail.step(e["token"])
+    f = call(
+        partial(features_kernel, z),
+        dict(patch=c["patch"], merge_weight=merge_t, merge_bias=merge_bias.reshape(1, -1)),
+        dict(features=arr(z.I, z.half, z.half * z.O, dtype=BF16), **token), dict(merged=kept(z.I * z.M, z.O)), 6, 2, (), [last.here],
+    )
     norm_rows = jnp.pad(jnp.concatenate(norms, axis=0), ((0, 16 - 2 * z.L), (0, 0))).astype(BF16)
-    late_rows = tail.finish(norm_rows)
-    feed = 2 * z.units
-    cut = feed + z.shared
-    feed_rows = jnp.concatenate([late_rows[:feed], early[:feed]], axis=0)
-    have, norm_rows = late_rows[feed:cut], late_rows[cut:]
-    merge = early[None, feed:]
-    for bit in bits_of(hid)[::-1]:
+    last.widen(jnp.concatenate([last.halve(None), norm_rows], axis=0), img)
+    shown = f["token"]
+    while chain.left or last.left:
+        for each in (chain, last):
+            if each.left:
+                each.step(shown if each is last else None)
+        shown = None
+    feed, cut = 2 * z.units, 2 * z.units + z.shared
+    feed_rows = jnp.concatenate([last.here[:feed], chain.here[:feed]], axis=0)
+    have = jnp.concatenate([last.here[feed:cut], chain.here[feed:cut]], axis=0)
+    norm_rows, merge = last.here[cut:], chain.here[None, cut:]
+    bits = bits_of(hid)
+    orders = bits[::-1], bits[1:] + bits[:1]
+    z.found = [[0], [0]]
+    for step, (bit, merge_bit) in enumerate(zip(*orders)):
         sent = jnp.concatenate([have, norm_rows], axis=0)
-        got, merge_got = swap(sent, "hid", hid, bit), swap(merge, "hid", hid, bit)
-        if bit > 1:
+        got, merge_got = swap(sent, "hid", hid, bit), swap(merge, "hid", hid, merge_bit)
+        z.found = [found + [e ^ b for e in found] for found, b in zip(z.found, (bit, merge_bit))]
+        if step < len(bits) - 1:
             have = jnp.concatenate([have, got[:-16]], axis=0)
             norm_rows = add(norm_rows, got[-16:], None)
             merge = jnp.concatenate([merge, merge_got], axis=0)
@@ -868,7 +893,7 @@
         5, 2, smem,
     )
     return (
-        c["features"], images_grad, g["mix_weight"], g["mix_bias"], g["squeeze_weight"].transpose(0, 2, 1),
+        f["features"], images_grad, g["mix_weight"], g["mix_bias"], g["squeeze_weight"].transpose(0, 2, 1),
         g["squeeze_bias"], g["expand_weight"], g["expand_bias"], g["project_weight"], g["project_bias"], g["norm_gain"],
         g["norm_bias"], g["inner_weight"].transpose(0, 2, 1), g["inner_bias"], g["outer_weight"], g["outer_bias"],
         g["merge_weight"].T, g["merge_bias"].reshape(-1),

time: 96.9 us -> 86.8 us (0.90)
  waiting for transfers between devices: 25 us -> 18 us
  local copies, waits for them, and re-layouts: 3.79 us -> 1.43 us
  Pallas kernels: 42.4 us -> 41.1 us
    ppermute x19 -> x22, waiting for transfers between devices: 25 us -> 18 us  [swap(): return lax.ppermute(x, axis, [(a, a ^ bit) for a in range(n)])]
    unnamed x42 -> x37, local copies, waits for them, and re-layouts: 3.41 us -> 1.26 us
    pallas_call x11 -> x12, Pallas kernels: 42.4 us -> 41.1 us  [call(): pl.pallas_call(kernel, out_shape=list(outs.values()), in_specs=[place(nam...]
    ppermute x19 -> x22, starting transfers between devices: 22.8 us -> 23.3 us  [swap(): return lax.ppermute(x, axis, [(a, a ^ bit) for a in range(n)])]
  transfers between devices with their start and end apart: 19 -> 22, of which waited for: 10 -> 15; matrix products, arithmetic and copies ran while one was open for 2% -> 2% of each run, Pallas kernels for 19% -> 30%
where the time goes in v5:
time: 86.8 us; the launch traced here: 86.6 us
  Pallas kernels  41.1 us (47%)
  starting transfers between devices  23.3 us (27%)
  waiting for transfers between devices  18 us (21%)
  other arithmetic  1.56 us (2%)
  local copies, waits for them, and re-layouts  1.43 us (2%)
  between operations  1.3 us (1%)
    pallas_call x12, Pallas kernels, call(): pl.pallas_call(kernel, out_shape=list(outs.values()), in_specs=[place(nam...  41.1 us
    ppermute x22, starting transfers between devices, swap(): return lax.ppermute(x, axis, [(a, a ^ bit) for a in range(n)])  23.3 us
    ppermute x22, waiting for transfers between devices, swap(): return lax.ppermute(x, axis, [(a, a ^ bit) for a in range(n)])  18 us
  transfers between devices with their start and end apart: 22, of which 15 were waited for; matrix products, arithmetic and copies ran while one was open for 2% of the time, Pallas kernels for 30%

profile of v5, /device:TPU:0, one launch (start us, length us, event | category | flops | bytes accessed | tf_op | source)
XLA Modules:
  0.0 86.6 jit_solution(5891745677854798588)
XLA Ops:
  1.6 3.0 %collective-permute-start = (bf16[1,272,128]{2,1,0:T(8,128)(2,1)S(1)}, bf16[1,272,128]{2,1,0:T(8,128)(2,1)S(1)}, u32[]{:S(2)}, u32[]{:S(2)}) collective-permute-start(bf16[1,272,128]{2,1,0:T(8,128)(2,1)S(1)} %bitcast.32), channel_id=1, source_target_pairs={{0,2},{1,3},{2,0},{3,1},{4,6},{5,7},{6,4},{7,5},{8,10},{9,11},{10,... | collective-permute-start | bytes 208904 | tf_op jit(solution)/shard_map/ppermute | solution.py:670
  4.8 2.8 %shard_map.322 = (f32[2688,128]{1,0:T(8,128)S(1)}, bf16[2688,128]{1,0:T(8,128)(2,1)S(1)}, bf16[2688,128]{1,0:T(8,128)(2,1)S(1)}, bf16[864,320]{1,0:T(8,128)(2,1)...) custom-call(s32[2,2]{1,0:T(2,128)S(1)} %copy-done.6, s32[1]{0:T(128)} %bitcast.refs_1_.refs_0_.refs_6_, ...), custom_call_target="tpu_custom_call" | custom-call | flops 3449999872 | tf_op jit(solution)/shard_map/pallas_call | solution.py:108
  7.7 1.6 %collective-permute-start.1 = (bf16[2,272,128]{2,1,0:T(8,128)(2,1)S(1)}, bf16[2,272,128]{2,1,0:T(8,128)(2,1)S(1)}, u32[]{:S(2)}, u32[]{:S(2)}) collective-permute-start(bf16[2,272,128]{2,1,0:T(8,128)(2,1)S(1)} %pad_maximum_fusion.7.refs_14_), channel_id=1, source_target_pairs={{0,4},{1,5},{2,6},{3,7},{4,0},{5,1},{6,2},{7,3},{8,12},{9,13},{10,... | collective-permute-start | bytes 417800 | tf_op jit(solution)/shard_map/ppermute | solution.py:670
  9.4 4.4 %shard_map.324 = (f32[2688,128]{1,0:T(8,128)S(1)}, bf16[384,384]{1,0:T(8,128)(2,1)S(1)}, f32[2,32,384]{2,1,0:T(8,128)S(1)}, f32[2,384]{1,0:T(2,128)S(1)}, bf16[2...) custom-call(bf16[2592,128]{1,0:T(8,128)(2,1)S(1)} %bitcast.51, ...), custom_call_target="tpu_custom_call" | custom-call | flops 5750000128 | tf_op jit(solution)/shard_map/pallas_call | solution.py:108
  14.0 1.5 %collective-permute-done.2 = bf16[4,272,128]{2,1,0:T(8,128)(2,1)S(1)} collective-permute-done((bf16[4,272,128]{2,1,0:T(8,128)(2,1)S(1)}, bf16[4,272,128]{2,1,0:T(8,128)(2,1)S(1)}, u32[]{:S(2)}, u32[]{:S(2)}) %collective-permute-start.2) | collective-permute-done | bytes 278560 | tf_op jit(solution)/shard_map/ppermute | solution.py:670
  15.6 12.7 %shard_map.325 = (bf16[864,1152]{1,0:T(8,128)(2,1)S(1)}, bf16[4,368,128]{2,1,0:T(8,128)(2,1)S(1)}, bf16[4,368,128]{2,1,0:T(8,128)(2,1)S(1)}, bf16[2,512,128]{2,1...) custom-call(s32[2,2]{1,0:T(2,128)S(1)} %copy-done.6, ...), custom_call_target="tpu_custom_call" | custom-call | flops 18400000000 | tf_op jit(solution)/shard_map/pallas_call | solution.py:108
  28.5 2.9 %shard_map.326 = (f32[2688,128]{1,0:T(8,128)S(1)}, f32[8,128]{1,0:T(8,128)S(1)}, bf16[4,128,128]{2,1,0:T(8,128)(2,1)S(1)}, bf16[4,128,128]{2,1,0:T(8,128)(2,1)S(1)}, f32[1,128]{1,0:T(1,128)S(1)}) custom-call(s32[1]{0:T(128)} %bitcast.refs_1_.refs_0_.refs_6_, f32[2688,128]{1,0:T(8,128)S(1)} %get-tuple-element.108.refs_2_.refs_1_.refs_0_, ...), custom_call_target="tpu_custom_call" | custom-call | flops 2300000000 | tf_op jit(solution)/shard_map/pallas_call | solution.py:108
  32.2 3.5 %shard_map.327 = (bf16[2688,256]{1,0:T(8,128)(2,1)S(1)}, bf16[384,256]{1,0:T(8,128)(2,1)S(1)}, f32[3,8,128]{2,1,0:T(8,128)S(1)}, bf16[4,96,128]{2,1,0:T(8,128)(2...) custom-call(s32[2,2]{1,0:T(2,128)S(1)} %copy-done.6, s32[1]{0:T(128)} %bitcast.refs_1_.refs_0_.refs_6_, ...), custom_call_target="tpu_custom_call" | custom-call | flops 1150000000 | tf_op jit(solution)/shard_map/pallas_call | solution.py:108
  35.9 1.7 %shard_map.328 = (f32[2688,128]{1,0:T(8,128)S(1)}, f32[2,128]{1,0:T(2,128)S(1)}, f32[1,128]{1,0:T(1,128)S(1)}) custom-call(f32[2688,128]{1,0:T(8,128)S(1)} %get-tuple-element.108.refs_2_.refs_1_.refs_0_, bf16[2688,128]{1,0:T(8,128)(2,1)S(1)} %get-tuple-element.119.refs_1_, f32[2,2,128]{2,1,0:T(2,128)S(1)} %copy-done.3, ...), custom_call_target="tpu_custom_call" | custom-call | flops 57500000 | tf_op jit(solution)/shard_map/pallas_call | solution.py:108
  38.7 1.3 %collective-permute-start.9 = (bf16[1,368,128]{2,1,0:T(8,128)(2,1)S(1)}, bf16[1,368,128]{2,1,0:T(8,128)(2,1)S(1)}, u32[]{:S(2)}, u32[]{:S(2)}) collective-permute-start(bf16[1,368,128]{2,1,0:T(8,128)(2,1)S(1)} %get-tuple-element.222), channel_id=1, source_target_pairs={{0,2},{1,3},{2,0},{3,1},{4,6},{5,7},{6,4},{7,5},{8,10},{9,11},{10,... | collective-permute-start | bytes 282632 | tf_op jit(solution)/shard_map/ppermute | solution.py:670
  40.7 3.1 %shard_map.329 = (f32[2688,128]{1,0:T(8,128)S(1)}, f32[8,128]{1,0:T(8,128)S(1)}, bf16[4,128,128]{2,1,0:T(8,128)(2,1)S(1)}, bf16[4,128,128]{2,1,0:T(8,128)(2,1)S(1)}, f32[1,128]{1,0:T(1,128)S(1)}) custom-call(s32[1]{0:T(128)} %bitcast.refs_1_.refs_0_.refs_6_, f32[2688,128]{1,0:T(8,128)S(1)} %get-tuple-element.108.refs_2_.refs_1_.refs_0_, ...), custom_call_target="tpu_custom_call" | custom-call | flops 2300000000 | tf_op jit(solution)/shard_map/pallas_call | solution.py:108
  43.8 1.2 %collective-permute-done.6 = bf16[2,224,128]{2,1,0:T(8,128)(2,1)S(1)} collective-permute-done((bf16[2,224,128]{2,1,0:T(8,128)(2,1)S(1)}, bf16[2,224,128]{2,1,0:T(8,128)(2,1)S(1)}, u32[]{:S(2)}, u32[]{:S(2)}) %collective-permute-start.6) | collective-permute-done | bytes 114720 | tf_op jit(solution)/shard_map/ppermute | solution.py:670
  45.9 3.2 %shard_map.330 = (bf16[2688,256]{1,0:T(8,128)(2,1)S(1)}, bf16[384,256]{1,0:T(8,128)(2,1)S(1)}, f32[3,8,128]{2,1,0:T(8,128)S(1)}, bf16[4,96,128]{2,1,0:T(8,128)(2...) custom-call(s32[2,2]{1,0:T(2,128)S(1)} %copy-done.6, s32[1]{0:T(128)} %bitcast.refs_1_.refs_0_.refs_6_, ...), custom_call_target="tpu_custom_call" | custom-call | flops 1150000000 | tf_op jit(solution)/shard_map/pallas_call | solution.py:108
  49.4 1.6 %collective-permute-start.14 = (bf16[592,128]{1,0:T(8,128)(2,1)S(1)}, bf16[592,128]{1,0:T(8,128)(2,1)S(1)}, u32[]{:S(2)}, u32[]{:S(2)}) collective-permute-start(bf16[592,128]{1,0:T(8,128)(2,1)S(1)} %pad_maximum_fusion.6.refs_10_), channel_id=1, source_target_pairs={{0,8},{8,0},{16,24},{24,16},{1,9},{9,1},{17,25},{25,17},{2,10},{10... | collective-permute-start | bytes 454664 | tf_op jit(solution)/shard_map/ppermute | solution.py:670
  51.0 3.0 %shard_map.331 = (f32[2592,128]{1,0:T(8,128)}, f32[2,128]{1,0:T(2,128)S(1)}, f32[1,128]{1,0:T(1,128)S(1)}) custom-call(f32[2688,128]{1,0:T(8,128)S(1)} %get-tuple-element.108.refs_2_.refs_1_.refs_0_, bf16[2688,128]{1,0:T(8,128)(2,1)S(1)} %get-tuple-element.119.refs_1_, f32[2,2,128]{2,1,0:T(2,128)S(1)} %copy-done.3, ...), custom_call_target="tpu_custom_call" | custom-call | flops 57500000 | tf_op jit(solution)/shard_map/pallas_call | solution.py:108
  54.1 1.0 %collective-permute-start.10 = (bf16[2,224,128]{2,1,0:T(8,128)(2,1)S(1)}, bf16[2,224,128]{2,1,0:T(8,128)(2,1)S(1)}, u32[]{:S(2)}, u32[]{:S(2)}) collective-permute-start(bf16[2,224,128]{2,1,0:T(8,128)(2,1)S(1)} %get-tuple-element.218), channel_id=1, source_target_pairs={{0,4},{1,5},{2,6},{3,7},{4,0},{5,1},{6,2},{7,3},{8,12},{9,13},{10,... | collective-permute-start | bytes 344072 | tf_op jit(solution)/shard_map/ppermute | solution.py:670
  55.8 2.7 %collective-permute-start.15 = (bf16[592,128]{1,0:T(8,128)(2,1)S(1)}, bf16[592,128]{1,0:T(8,128)(2,1)S(1)}, u32[]{:S(2)}, u32[]{:S(2)}) collective-permute-start(bf16[592,128]{1,0:T(8,128)(2,1)S(1)} %add_convert_fusion.5), channel_id=1, source_target_pairs={{0,16},{8,24},{16,0},{24,8},{1,17},{9,25},{17,1},{25,9},{2,18},{10... | collective-permute-start | bytes 454664 | tf_op jit(solution)/shard_map/ppermute | solution.py:670
  59.4 1.3 %collective-permute-start.11 = (bf16[1,224,128]{2,1,0:T(8,128)(2,1)S(1)}, bf16[1,224,128]{2,1,0:T(8,128)(2,1)S(1)}, u32[]{:S(2)}, u32[]{:S(2)}) collective-permute-start(bf16[1,224,128]{2,1,0:T(8,128)(2,1)S(1)} %slice.99), channel_id=1, source_target_pairs={{0,2},{1,3},{2,0},{3,1},{4,6},{5,7},{6,4},{7,5},{8,10},{9,11},{10,... | collective-permute-start | bytes 172040 | tf_op jit(solution)/shard_map/ppermute | solution.py:670
  60.8 1.4 %shard_map.332 = (bf16[2,18,5760]{2,1,0:T(8,128)(2,1)S(1)}, f32[1,128]{1,0:T(1,128)S(1)}) custom-call(bf16[864,1152]{1,0:T(8,128)(2,1)S(1)} %get-tuple-element.118.refs_0_, bf16[320,1152]{1,0:T(8,128)(2,1)S(1)} %bitcast.50, f32[1,320]{1,0:T(1,128)S(1)} %reshape.65.refs_2_, bf16[2,224,128]{2,1,0:T(8,128)(2,1)S(1)} %get-tuple-element.219.refs_3_), custom_call_target="tpu_custom_call" | custom-call | flops 2300000000 | tf_op jit(solution)/shard_map/pallas_call | solution.py:108
  62.2 1.5 %collective-permute-done.11 = bf16[1,224,128]{2,1,0:T(8,128)(2,1)S(1)} collective-permute-done((bf16[1,224,128]{2,1,0:T(8,128)(2,1)S(1)}, bf16[1,224,128]{2,1,0:T(8,128)(2,1)S(1)}, u32[]{:S(2)}, u32[]{:S(2)}) %collective-permute-start.11) | collective-permute-done | bytes 57376 | tf_op jit(solution)/shard_map/ppermute | solution.py:670
  64.4 1.2 %collective-permute-done.15 = bf16[592,128]{1,0:T(8,128)(2,1)S(1)} collective-permute-done((bf16[592,128]{1,0:T(8,128)(2,1)S(1)}, bf16[592,128]{1,0:T(8,128)(2,1)S(1)}, u32[]{:S(2)}, u32[]{:S(2)}) %collective-permute-start.15) | collective-permute-done | bytes 151584 | tf_op jit(solution)/shard_map/ppermute | solution.py:670
  65.6 2.4 %collective-permute-done.12 = bf16[240,128]{1,0:T(8,128)(2,1)S(1)} collective-permute-done((bf16[240,128]{1,0:T(8,128)(2,1)S(1)}, bf16[240,128]{1,0:T(8,128)(2,1)S(1)}, u32[]{:S(2)}, u32[]{:S(2)}) %collective-permute-start.12) | collective-permute-done | bytes 61472 | tf_op jit(solution)/shard_map/ppermute | solution.py:670
  68.0 2.7 %collective-permute-start.13 = (bf16[240,128]{1,0:T(8,128)(2,1)S(1)}, bf16[240,128]{1,0:T(8,128)(2,1)S(1)}, u32[]{:S(2)}, u32[]{:S(2)}) collective-permute-start(bf16[240,128]{1,0:T(8,128)(2,1)S(1)} %add_convert_fusion.10), channel_id=1, source_target_pairs={{0,16},{8,24},{16,0},{24,8},{1,17},{9,25},{17,1},{25,9},{2,18},{10... | collective-permute-start | bytes 184328 | tf_op jit(solution)/shard_map/ppermute | solution.py:670
  70.7 1.3 %collective-permute-start.19 = (bf16[1,368,128]{2,1,0:T(8,128)(2,1)S(1)}, bf16[1,368,128]{2,1,0:T(8,128)(2,1)S(1)}, u32[]{:S(2)}, u32[]{:S(2)}) collective-permute-start(bf16[1,368,128]{2,1,0:T(8,128)(2,1)S(1)} %slice_bitcast_fusion), channel_id=1, source_target_pairs={{0,2},{1,3},{2,0},{3,1},{4,6},{5,7},{6,4},{7,5},{8,10},{9,11},{10,... | collective-permute-start | bytes 282632 | tf_op jit(solution)/shard_map/ppermute | solution.py:670
  72.0 1.9 %collective-permute-done.13 = bf16[240,128]{1,0:T(8,128)(2,1)S(1)} collective-permute-done((bf16[240,128]{1,0:T(8,128)(2,1)S(1)}, bf16[240,128]{1,0:T(8,128)(2,1)S(1)}, u32[]{:S(2)}, u32[]{:S(2)}) %collective-permute-start.13) | collective-permute-done | bytes 61472 | tf_op jit(solution)/shard_map/ppermute | solution.py:670
  74.0 1.0 %collective-permute-start.16 = (bf16[208,128]{1,0:T(8,128)(2,1)S(1)}, bf16[208,128]{1,0:T(8,128)(2,1)S(1)}, u32[]{:S(2)}, u32[]{:S(2)}) collective-permute-start(bf16[208,128]{1,0:T(8,128)(2,1)S(1)} %pad_maximum_fusion.11), channel_id=1, source_target_pairs={{0,4},{1,5},{2,6},{3,7},{4,0},{5,1},{6,2},{7,3},{8,12},{9,13},{10,... | collective-permute-start | bytes 159752 | tf_op jit(solution)/shard_map/ppermute | solution.py:670
  76.3 1.8 %collective-permute-done.16 = bf16[208,128]{1,0:T(8,128)(2,1)S(1)} collective-permute-done((bf16[208,128]{1,0:T(8,128)(2,1)S(1)}, bf16[208,128]{1,0:T(8,128)(2,1)S(1)}, u32[]{:S(2)}, u32[]{:S(2)}) %collective-permute-start.16) | collective-permute-done | bytes 53280 | tf_op jit(solution)/shard_map/ppermute | solution.py:670
  78.2 1.3 %collective-permute-start.17 = (bf16[400,128]{1,0:T(8,128)(2,1)S(1)}, bf16[400,128]{1,0:T(8,128)(2,1)S(1)}, u32[]{:S(2)}, u32[]{:S(2)}) collective-permute-start(bf16[400,128]{1,0:T(8,128)(2,1)S(1)} %pad_maximum_fusion.8), channel_id=1, source_target_pairs={{0,2},{1,3},{2,0},{3,1},{4,6},{5,7},{6,4},{7,5},{8,10},{9,11},{10,... | collective-permute-start | bytes 307208 | tf_op jit(solution)/shard_map/ppermute | solution.py:670
  79.5 1.5 %collective-permute-done.20 = bf16[2,368,128]{2,1,0:T(8,128)(2,1)S(1)} collective-permute-done((bf16[2,368,128]{2,1,0:T(8,128)(2,1)S(1)}, bf16[2,368,128]{2,1,0:T(8,128)(2,1)S(1)}, u32[]{:S(2)}, u32[]{:S(2)}) %collective-permute-start.20) | collective-permute-done | bytes 188448 | tf_op jit(solution)/shard_map/ppermute | solution.py:670
  81.1 1.8 %collective-permute-done.17 = bf16[400,128]{1,0:T(8,128)(2,1)S(1)} collective-permute-done((bf16[400,128]{1,0:T(8,128)(2,1)S(1)}, bf16[400,128]{1,0:T(8,128)(2,1)S(1)}, u32[]{:S(2)}, u32[]{:S(2)}) %collective-permute-start.17) | collective-permute-done | bytes 102432 | tf_op jit(solution)/shard_map/ppermute | solution.py:670
  83.0 1.1 %copy.38 = bf16[2,18,5760]{2,0,1:T(2,128)(2,1)} copy(bf16[2,18,5760]{2,1,0:T(8,128)(2,1)S(1)} %get-tuple-element.198) | data formatting | bytes 829440
  84.5 1.5 %shard_map.333 = (f32[2,3,128,128]{3,2,1,0:T(8,128)}, f32[2,2,128]{2,1,0:T(2,128)}, f32[2,32,128]{2,1,0:T(8,128)}, f32[2,32]{1,0:T(2,128)}, f32[2,32,384]{2,1,0:...) custom-call(s32[1]{0:T(128)} %bitcast.refs_1_.refs_0_.refs_6_, ...), custom_call_target="tpu_custom_call" | custom-call | flops 2300000000 | tf_op jit(solution)/shard_map/pallas_call | solution.py:108
  (112 shorter events, 10.5 us)
Async XLA Ops:
  1.6 6.1 %collective-permute-start = (bf16[1,272,128]{2,1,0:T(8,128)(2,1)S(1)}, bf16[1,272,128]{2,1,0:T(8,128)(2,1)S(1)}, u32[]{:S(2)}, u32[]{:S(2)}) collective-permute-start(bf16[1,272,128]{2,1,0:T(8,128)(2,1)S(1)} %bitcast.32), channel_id=1, source_target_pairs={{0,2},{1,3},{2,0},{3,1},{4,6},{5,7},{6,4},{7,5},{8,10},{9,11},{10,... | collective-permute-start | bytes 208904 | tf_op jit(solution)/shard_map/ppermute | solution.py:670
  4.7 4.6 %copy-start = (bf16[2,3,128,128]{3,2,1,0:T(8,128)(2,1)S(1)}, bf16[2,3,128,128]{3,2,1,0:T(8,128)(2,1)}, u32[]{:S(2)}) copy-start(bf16[2,3,128,128]{3,2,1,0:T(8,128)(2,1)} %refs_14_.3) | copy-start | bytes 589828
  4.7 4.6 %copy-start.1 = (bf16[2,128,128]{2,1,0:T(8,128)(2,1)S(1)}, bf16[2,128,128]{2,1,0:T(8,128)(2,1)}, u32[]{:S(2)}) copy-start(bf16[2,128,128]{2,1,0:T(8,128)(2,1)} %refs_18_.5) | copy-start | bytes 196612
  4.7 4.6 %copy-start.2 = (f32[2,128,32]{1,2,0:T(8,128)S(1)}, f32[2,128,32]{1,2,0:T(8,128)}, u32[]{:S(2)}) copy-start(f32[2,128,32]{1,2,0:T(8,128)} %param.24) | copy-start | bytes 98308
  4.7 4.6 %copy-start.3 = (f32[2,2,128]{2,1,0:T(2,128)S(1)}, f32[2,2,128]{2,1,0:T(2,128)}, u32[]{:S(2)}) copy-start(f32[2,2,128]{2,1,0:T(2,128)} %refs_2_.6) | copy-start | bytes 6148
  4.8 4.6 %copy-start.4 = (f32[2,2,128]{2,1,0:T(2,128)S(1)}, f32[2,2,128]{2,1,0:T(2,128)}, u32[]{:S(2)}) copy-start(f32[2,2,128]{2,1,0:T(2,128)} %refs_15_.5) | copy-start | bytes 6148
  4.8 4.6 %copy-start.5 = (f32[2,2,128]{2,1,0:T(2,128)S(1)}, f32[2,2,128]{2,1,0:T(2,128)}, u32[]{:S(2)}) copy-start(f32[2,2,128]{2,1,0:T(2,128)} %refs_21_.3) | copy-start | bytes 6148
  4.8 4.6 %copy-start.7 = (f32[2,32]{1,0:T(2,128)S(1)}, f32[2,32]{1,0:T(2,128)}, u32[]{:S(2)}) copy-start(f32[2,32]{1,0:T(2,128)} %refs_17_.5) | copy-start | bytes 772
  4.8 4.6 %copy-start.8 = (f32[2,128]{1,0:T(2,128)S(1)}, f32[2,128]{1,0:T(2,128)}, u32[]{:S(2)}) copy-start(f32[2,128]{1,0:T(2,128)} %refs_19_.5) | copy-start | bytes 3076
  4.8 4.6 %copy-start.10 = (bf16[2,36,36,128]{3,0,2,1:T(2,128)(2,1)S(1)}, bf16[2,36,36,128]{3,0,2,1:T(2,128)(2,1)}, u32[]{:S(2)}) copy-start(bf16[2,36,36,128]{3,0,2,1:T(2,128)(2,1)} %param.19) | copy-start | bytes 1990660
  7.7 6.1 %collective-permute-start.1 = (bf16[2,272,128]{2,1,0:T(8,128)(2,1)S(1)}, bf16[2,272,128]{2,1,0:T(8,128)(2,1)S(1)}, u32[]{:S(2)}, u32[]{:S(2)}) collective-permute-start(bf16[2,272,128]{2,1,0:T(8,128)(2,1)S(1)} %pad_maximum_fusion.7.refs_14_), channel_id=1, source_target_pairs={{0,4},{1,5},{2,6},{3,7},{4,0},{5,1},{6,2},{7,3},{8,12},{9,13},{10,... | collective-permute-start | bytes 417800 | tf_op jit(solution)/shard_map/ppermute | solution.py:670
  13.9 1.6 %collective-permute-start.2 = (bf16[4,272,128]{2,1,0:T(8,128)(2,1)S(1)}, bf16[4,272,128]{2,1,0:T(8,128)(2,1)S(1)}, u32[]{:S(2)}, u32[]{:S(2)}) collective-permute-start(bf16[4,272,128]{2,1,0:T(8,128)(2,1)S(1)} %pad_maximum_fusion.2), channel_id=1, source_target_pairs={{0,1},{1,0},{2,3},{3,2},{4,5},{5,4},{6,7},{7,6},{8,9},{9,8},{10,11... | collective-permute-start | bytes 835592 | tf_op jit(solution)/shard_map/ppermute | solution.py:670
  15.6 12.9 %copy-start.15 = (f32[320]{0:T(512)S(1)}, f32[320]{0:T(512)}, u32[]{:S(2)}) copy-start(f32[320]{0:T(512)} %param.37) | copy-start | bytes 3844
  28.3 3.1 %collective-permute-start.3 = (bf16[4,368,128]{2,1,0:T(8,128)(2,1)S(1)}, bf16[4,368,128]{2,1,0:T(8,128)(2,1)S(1)}, u32[]{:S(2)}, u32[]{:S(2)}) collective-permute-start(bf16[4,368,128]{2,1,0:T(8,128)(2,1)S(1)} %get-tuple-element.139), channel_id=1, source_target_pairs={{0,1},{1,0},{2,3},{3,2},{4,5},{5,4},{6,7},{7,6},{8,9},{9,8},{10,11... | collective-permute-start | bytes 1130504 | tf_op jit(solution)/shard_map/ppermute | solution.py:670
  31.6 7.1 %collective-permute-start.4 = (bf16[2,368,128]{2,1,0:T(8,128)(2,1)S(1)}, bf16[2,368,128]{2,1,0:T(8,128)(2,1)S(1)}, u32[]{:S(2)}, u32[]{:S(2)}) collective-permute-start(bf16[2,368,128]{2,1,0:T(8,128)(2,1)S(1)} %get-tuple-element.216), channel_id=1, source_target_pairs={{0,4},{1,5},{2,6},{3,7},{4,0},{5,1},{6,2},{7,3},{8,12},{9,13},{10,... | collective-permute-start | bytes 565256 | tf_op jit(solution)/shard_map/ppermute | solution.py:670
  35.8 4.3 %collective-permute-start.5 = (bf16[4,224,128]{2,1,0:T(8,128)(2,1)S(1)}, bf16[4,224,128]{2,1,0:T(8,128)(2,1)S(1)}, u32[]{:S(2)}, u32[]{:S(2)}) collective-permute-start(bf16[4,224,128]{2,1,0:T(8,128)(2,1)S(1)} %pad_maximum_fusion.3), channel_id=1, source_target_pairs={{0,1},{1,0},{2,3},{3,2},{4,5},{5,4},{6,7},{7,6},{8,9},{9,8},{10,11... | collective-permute-start | bytes 688136 | tf_op jit(solution)/shard_map/ppermute | solution.py:670
  38.7 10.5 %collective-permute-start.9 = (bf16[1,368,128]{2,1,0:T(8,128)(2,1)S(1)}, bf16[1,368,128]{2,1,0:T(8,128)(2,1)S(1)}, u32[]{:S(2)}, u32[]{:S(2)}) collective-permute-start(bf16[1,368,128]{2,1,0:T(8,128)(2,1)S(1)} %get-tuple-element.222), channel_id=1, source_target_pairs={{0,2},{1,3},{2,0},{3,1},{4,6},{5,7},{6,4},{7,5},{8,10},{9,11},{10,... | collective-permute-start | bytes 282632 | tf_op jit(solution)/shard_map/ppermute | solution.py:670
  40.1 4.9 %collective-permute-start.6 = (bf16[2,224,128]{2,1,0:T(8,128)(2,1)S(1)}, bf16[2,224,128]{2,1,0:T(8,128)(2,1)S(1)}, u32[]{:S(2)}, u32[]{:S(2)}) collective-permute-start(bf16[2,224,128]{2,1,0:T(8,128)(2,1)S(1)} %get-tuple-element.220), channel_id=1, source_target_pairs={{0,4},{1,5},{2,6},{3,7},{4,0},{5,1},{6,2},{7,3},{8,12},{9,13},{10,... | collective-permute-start | bytes 344072 | tf_op jit(solution)/shard_map/ppermute | solution.py:670
  45.1 4.2 %collective-permute-start.8 = (bf16[1,224,128]{2,1,0:T(8,128)(2,1)S(1)}, bf16[1,224,128]{2,1,0:T(8,128)(2,1)S(1)}, u32[]{:S(2)}, u32[]{:S(2)}) collective-permute-start(bf16[1,224,128]{2,1,0:T(8,128)(2,1)S(1)} %get-tuple-element.226), channel_id=1, source_target_pairs={{0,2},{1,3},{2,0},{3,1},{4,6},{5,7},{6,4},{7,5},{8,10},{9,11},{10,... | collective-permute-start | bytes 172040 | tf_op jit(solution)/shard_map/ppermute | solution.py:670
  49.1 4.9 %collective-permute-start.7 = (bf16[4,224,128]{2,1,0:T(8,128)(2,1)S(1)}, bf16[4,224,128]{2,1,0:T(8,128)(2,1)S(1)}, u32[]{:S(2)}, u32[]{:S(2)}) collective-permute-start(bf16[4,224,128]{2,1,0:T(8,128)(2,1)S(1)} %pad_maximum_fusion.4), channel_id=1, source_target_pairs={{0,1},{1,0},{2,3},{3,2},{4,5},{5,4},{6,7},{7,6},{8,9},{9,8},{10,11... | collective-permute-start | bytes 688136 | tf_op jit(solution)/shard_map/ppermute | solution.py:670
  49.4 6.4 %collective-permute-start.14 = (bf16[592,128]{1,0:T(8,128)(2,1)S(1)}, bf16[592,128]{1,0:T(8,128)(2,1)S(1)}, u32[]{:S(2)}, u32[]{:S(2)}) collective-permute-start(bf16[592,128]{1,0:T(8,128)(2,1)S(1)} %pad_maximum_fusion.6.refs_10_), channel_id=1, source_target_pairs={{0,8},{8,0},{16,24},{24,16},{1,9},{9,1},{17,25},{25,17},{2,10},{10... | collective-permute-start | bytes 454664 | tf_op jit(solution)/shard_map/ppermute | solution.py:670
  54.1 5.3 %collective-permute-start.10 = (bf16[2,224,128]{2,1,0:T(8,128)(2,1)S(1)}, bf16[2,224,128]{2,1,0:T(8,128)(2,1)S(1)}, u32[]{:S(2)}, u32[]{:S(2)}) collective-permute-start(bf16[2,224,128]{2,1,0:T(8,128)(2,1)S(1)} %get-tuple-element.218), channel_id=1, source_target_pairs={{0,4},{1,5},{2,6},{3,7},{4,0},{5,1},{6,2},{7,3},{8,12},{9,13},{10,... | collective-permute-start | bytes 344072 | tf_op jit(solution)/shard_map/ppermute | solution.py:670
  55.8 9.8 %collective-permute-start.15 = (bf16[592,128]{1,0:T(8,128)(2,1)S(1)}, bf16[592,128]{1,0:T(8,128)(2,1)S(1)}, u32[]{:S(2)}, u32[]{:S(2)}) collective-permute-start(bf16[592,128]{1,0:T(8,128)(2,1)S(1)} %add_convert_fusion.5), channel_id=1, source_target_pairs={{0,16},{8,24},{16,0},{24,8},{1,17},{9,25},{17,1},{25,9},{2,18},{10... | collective-permute-start | bytes 454664 | tf_op jit(solution)/shard_map/ppermute | solution.py:670
  59.4 4.2 %collective-permute-start.11 = (bf16[1,224,128]{2,1,0:T(8,128)(2,1)S(1)}, bf16[1,224,128]{2,1,0:T(8,128)(2,1)S(1)}, u32[]{:S(2)}, u32[]{:S(2)}) collective-permute-start(bf16[1,224,128]{2,1,0:T(8,128)(2,1)S(1)} %slice.99), channel_id=1, source_target_pairs={{0,2},{1,3},{2,0},{3,1},{4,6},{5,7},{6,4},{7,5},{8,10},{9,11},{10,... | collective-permute-start | bytes 172040 | tf_op jit(solution)/shard_map/ppermute | solution.py:670
  63.7 4.3 %collective-permute-start.12 = (bf16[240,128]{1,0:T(8,128)(2,1)S(1)}, bf16[240,128]{1,0:T(8,128)(2,1)S(1)}, u32[]{:S(2)}, u32[]{:S(2)}) collective-permute-start(bf16[240,128]{1,0:T(8,128)(2,1)S(1)} %pad_maximum_fusion.10), channel_id=1, source_target_pairs={{0,8},{8,0},{16,24},{24,16},{1,9},{9,1},{17,25},{25,17},{2,10},{10... | collective-permute-start | bytes 184328 | tf_op jit(solution)/shard_map/ppermute | solution.py:670
  68.0 5.8 %collective-permute-start.13 = (bf16[240,128]{1,0:T(8,128)(2,1)S(1)}, bf16[240,128]{1,0:T(8,128)(2,1)S(1)}, u32[]{:S(2)}, u32[]{:S(2)}) collective-permute-start(bf16[240,128]{1,0:T(8,128)(2,1)S(1)} %add_convert_fusion.10), channel_id=1, source_target_pairs={{0,16},{8,24},{16,0},{24,8},{1,17},{9,25},{17,1},{25,9},{2,18},{10... | collective-permute-start | bytes 184328 | tf_op jit(solution)/shard_map/ppermute | solution.py:670
  70.7 4.6 %collective-permute-start.19 = (bf16[1,368,128]{2,1,0:T(8,128)(2,1)S(1)}, bf16[1,368,128]{2,1,0:T(8,128)(2,1)S(1)}, u32[]{:S(2)}, u32[]{:S(2)}) collective-permute-start(bf16[1,368,128]{2,1,0:T(8,128)(2,1)S(1)} %slice_bitcast_fusion), channel_id=1, source_target_pairs={{0,2},{1,3},{2,0},{3,1},{4,6},{5,7},{6,4},{7,5},{8,10},{9,11},{10,... | collective-permute-start | bytes 282632 | tf_op jit(solution)/shard_map/ppermute | solution.py:670
  74.0 4.2 %collective-permute-start.16 = (bf16[208,128]{1,0:T(8,128)(2,1)S(1)}, bf16[208,128]{1,0:T(8,128)(2,1)S(1)}, u32[]{:S(2)}, u32[]{:S(2)}) collective-permute-start(bf16[208,128]{1,0:T(8,128)(2,1)S(1)} %pad_maximum_fusion.11), channel_id=1, source_target_pairs={{0,4},{1,5},{2,6},{3,7},{4,0},{5,1},{6,2},{7,3},{8,12},{9,13},{10,... | collective-permute-start | bytes 159752 | tf_op jit(solution)/shard_map/ppermute | solution.py:670
  75.4 5.6 %collective-permute-start.20 = (bf16[2,368,128]{2,1,0:T(8,128)(2,1)S(1)}, bf16[2,368,128]{2,1,0:T(8,128)(2,1)S(1)}, u32[]{:S(2)}, u32[]{:S(2)}) collective-permute-start(bf16[2,368,128]{2,1,0:T(8,128)(2,1)S(1)} %pad_maximum_fusion.5), channel_id=1, source_target_pairs={{0,4},{1,5},{2,6},{3,7},{4,0},{5,1},{6,2},{7,3},{8,12},{9,13},{10,... | collective-permute-start | bytes 565256 | tf_op jit(solution)/shard_map/ppermute | solution.py:670
  78.2 4.7 %collective-permute-start.17 = (bf16[400,128]{1,0:T(8,128)(2,1)S(1)}, bf16[400,128]{1,0:T(8,128)(2,1)S(1)}, u32[]{:S(2)}, u32[]{:S(2)}) collective-permute-start(bf16[400,128]{1,0:T(8,128)(2,1)S(1)} %pad_maximum_fusion.8), channel_id=1, source_target_pairs={{0,2},{1,3},{2,0},{3,1},{4,6},{5,7},{6,4},{7,5},{8,10},{9,11},{10,... | collective-permute-start | bytes 307208 | tf_op jit(solution)/shard_map/ppermute | solution.py:670
  81.1 3.4 %collective-permute-start.21 = (bf16[4,368,128]{2,1,0:T(8,128)(2,1)S(1)}, bf16[4,368,128]{2,1,0:T(8,128)(2,1)S(1)}, u32[]{:S(2)}, u32[]{:S(2)}) collective-permute-start(bf16[4,368,128]{2,1,0:T(8,128)(2,1)S(1)} %pad_maximum_fusion.1.refs_3_), channel_id=1, source_target_pairs={{0,1},{1,0},{2,3},{3,2},{4,5},{5,4},{6,7},{7,6},{8,9},{9,8},{10,11... | collective-permute-start | bytes 1130504 | tf_op jit(solution)/shard_map/ppermute | solution.py:670
  83.0 1.5 %collective-permute-start.18 = (bf16[784,128]{1,0:T(8,128)(2,1)S(1)}, bf16[784,128]{1,0:T(8,128)(2,1)S(1)}, u32[]{:S(2)}, u32[]{:S(2)}) collective-permute-start(bf16[784,128]{1,0:T(8,128)(2,1)S(1)} %constant_dynamic-update-slice_fusion.4.refs_1_), channel_id=1, source_target_pairs={{0,1},{1,0},{2,3},{3,2},{4,5},{5,4},{6,7},{7,6},{8,9},{9,8},{10,11... | collective-permute-start | bytes 602120 | tf_op jit(solution)/shard_map/ppermute | solution.py:670
  (6 other events, 22.9 us)

commit v6 on v5

--- a/solution.py
+++ b/solution.py
@@ -24,10 +24,17 @@
 
 def fine(a, b, dims=(1, 0)):
     high, low = halves(a)
+    if dims == (0, 0):
+        b_high, b_low = halves(b)
+        return dot(jnp.concatenate([high, low, high], axis=0), jnp.concatenate([b_high, b_high, b_low], axis=0), dims)
+    rows = a.shape[0]
+    both = jnp.concatenate([high, low], axis=0)
     if b.dtype == BF16:
-        return dot(high, b, dims) + dot(low, b, dims)
+        out = dot(both, b, dims)
+        return out[:rows] + out[rows:]
     b_high, b_low = halves(b)
-    return dot(high, b_high, dims) + (dot(low, b_high, dims) + dot(high, b_low, dims))
+    out = dot(both, b_high, dims)
+    return out[:rows] + (out[rows:] + dot(high, b_low, dims))
 
 
 def rows8(v):
@@ -233,12 +240,12 @@
         mid = near(r.normed, start, 0, size)
         high = jnp.where(kind == 2, near(r.normed, start, -z.W, size), near(r.normed, start, z.W, size))
         wide = jnp.where(kind == 2, near(r.normed, start, -z.I, size), near(r.normed, start, z.I, size))
-        high = jnp.where(kind == 0, mid, high).astype(BF16)
-        wide = jnp.where(kind == 0, mid, wide * r.edge[rows, :].astype(F32)).astype(BF16)
+        high = jnp.where(kind == 0, mid, high)
+        wide = jnp.where(kind == 0, mid, wide * r.edge[rows, :].astype(F32))
         mask = r.mask[rows, :]
-        for j, piece in enumerate((high, wide, mid.astype(BF16))):
-            cat[rows, j * z.C : (j + 1) * z.C] = piece
-            r.sums[j] += rows8(piece.astype(F32) * mask)
+        for j, piece in enumerate((high, wide, mid)):
+            cat[rows, j * z.C : (j + 1) * z.C] = piece.astype(BF16)
+            r.sums[j] += rows8(piece * mask)
 
     over(z, body, size)
 
@@ -306,7 +313,7 @@
     ref[z.base + z.N0 :, :] = jnp.zeros((ref.shape[0] - z.base - z.N0, z.C), F32)
 
 
-def feed_phase(z, r, l, o, after):
+def feed_phase(z, r, l, o, source, after):
     def body(rows, at):
         pre = dot(o.normed2[rows, :], r.inner[l], (1, 1)) + r.inner_bias[l : l + 1]
         act, slope = gelu_pair(pre)
@@ -314,7 +321,7 @@
         o.act_rows[rows, :] = act
         o.slope_rows[rows, :] = slope.astype(BF16)
         out = dot(act, r.outer[l]) + r.outer_bias[l : l + 1]
-        state = r.state[rows, :] + r.mask[rows, :] * out
+        state = source[rows, :] + r.mask[rows, :] * out
         after(rows, at, state)
 
     over(z, body, z.run_second)
@@ -337,9 +344,12 @@
     ends = lax.broadcasted_iota(jnp.int32, (3 * z.C, 3 * z.C), 1)
     kind = jnp.where(ends >= 2 * z.C, 2, jnp.where(ends >= z.C, 1, 0))
     r.perm[...] = jnp.where(spots == 3 * (ends - kind * z.C) + kind, 1.0, 0.0).astype(BF16)
+    blank = jnp.zeros((8 - z.L, 3 * z.C), F32)
+    rows = [r.expand_weight[l] for l in range(z.L)] + [r.expand_bias[...], blank]
+    rows = fine(jnp.concatenate(rows, axis=0), r.perm[...])
     for l in range(z.L):
-        r.ewp[l] = fine(r.expand_weight[l], r.perm[...])
-    r.ebp[...] = fine(r.expand_bias[...], r.perm[...])
+        r.ewp[l] = rows[l * z.R : (l + 1) * z.R]
+    r.ebp[...] = rows[z.L * z.R : z.L * z.R + z.L]
 
     def begin(rows, at):
         real = min(rows.stop, z.N0) - at
@@ -398,8 +408,7 @@
         r.state[rows, :] = state
         norm_store(z, r, 1, r, rows, at, state)
 
-    r.state[...] = r.state_in[...]
-    feed_phase(z, r, 0, early[0], then_norm)
+    feed_phase(z, r, 0, early[0], r.state_in, then_norm)
     clear_edges(z, r.normed)
     shift_phase(z, r, r.cat, z.run_second)
     weigh_phase(z, r, 1, r)
@@ -408,7 +417,7 @@
     def then_keep(rows, at, state):
         r.normed[z.base + at : z.base + at + rows.stop - rows.start, :] = state
 
-    feed_phase(z, r, 1, early[1], then_keep)
+    feed_phase(z, r, 1, early[1], r.state, then_keep)
     for i in range(z.I):
         for pair in range(z.half // 2):
             at = i * z.M + 2 * pair * z.hp
@@ -453,10 +462,12 @@
     def body(rows, at):
         mask = r.mask[rows, :]
         grad = r.grad[rows, :]
-        out = (grad * mask).astype(BF16)
-        r.vec[0] += rows8(out.astype(F32))
-        pre = (dot(out, r.outer[l], (1, 1)) * r.slope_rows[rows, :].astype(F32)).astype(BF16)
-        r.inner_sums[...] += rows8(pre.astype(F32))
+        out = grad * mask
+        r.vec[0] += rows8(out)
+        out = out.astype(BF16)
+        pre = dot(out, r.outer[l], (1, 1)) * r.slope_rows[rows, :].astype(F32)
+        r.inner_sums[...] += rows8(pre)
+        pre = pre.astype(BF16)
         r.g_outer[...] += dot(out, r.act_rows[rows, :], (0, 0))
         r.g_inner[...] += dot(r.normed2[rows, :], pre, (0, 0))
         normed_grad = dot(pre, r.inner[l])
@@ -484,8 +495,9 @@
     even, odd = tile(parity(z, 0), z.run_back), tile(parity(z, 1), z.run_back)
 
     def body(rows, at):
-        token = (r.half_grad[rows, :] * r.mask[rows, :]).astype(BF16)
-        r.vec[0] += rows8(token.astype(F32))
+        token = r.half_grad[rows, :] * r.mask[rows, :]
+        r.vec[0] += rows8(token)
+        token = token.astype(BF16)
         r.g_project[...] += dot(r.mixed[rows, :], token, (0, 0))
         mixed_grad = dot(token, r.project_weight[l], (1, 1))
         r.vec[1] += rows8(mixed_grad)
@@ -516,8 +528,8 @@
     even = dp[0] * share[0] + dp[1] * share[1] + dp[2] * share[2]
     dz = jnp.concatenate([share[j] * (dp[j] - even) for j in range(3)], axis=1)
     act, slope, pooled = r.act[...], r.slope[...], r.pooled[...]
-    expand = fine(fine(act, dz, (0, 0)), r.perm[...], (1, 1))
-    expand_bias = total(fine(dz, r.perm[...], (1, 1)))
+    expand = fine(jnp.concatenate([fine(act, dz, (0, 0)), dz], axis=0), r.perm[...], (1, 1))
+    expand, expand_bias = expand[: z.R], total(expand[z.R :])
     dact = fine(dz, r.ewp[l], (1, 1)) * slope
     squeeze = fine(dact, pooled, (0, 0))
     dpool = fine(dact, r.squeeze_weight[l])
@@ -591,22 +603,22 @@
         project_weight=arr(z.L, z.C, z.C), project_bias=arr(z.L, z.C), norm_gain=arr(z.L, 2, z.C),
         norm_bias=arr(z.L, 2, z.C), inner_weight=arr(z.L, z.units, z.C), inner_bias=arr(z.L, z.units),
         outer_weight=arr(z.L, z.units, z.C), outer_bias=arr(z.L, z.C), merge_weight=arr(z.O, 9 * z.C),
-        merge_bias=arr(1, z.O),
+        merge_bias=arr(z.O),
     )
 
 
 def last_kernel(z, r):
     me = r.place[0]
     half = z.parts // 2
-    size = z.L * z.shared
+    size = z.shared
     for at in range(z.parts):
         k = at % half
         have, merge = (r.have, r.merge_have) if at < half else (r.got, r.merge_got)
-        rows = pl.ds(pl.multiple_of((me ^ z.found[0][at]) * z.shared, 16), z.shared)
-        for l in range(z.L):
-            r.rows[l, rows, :] = have[k * size + l * z.shared : k * size + (l + 1) * z.shared, :]
-        rows = pl.ds(pl.multiple_of((me ^ z.found[1][at]) * z.merge, 16), z.merge)
-        r.merge_rows[rows, :] = merge[k]
+        rows = pl.ds(pl.multiple_of((me ^ z.found[at]) * z.shared, 16), z.shared)
+        r.rows[0, rows, :] = have[k * size : (k + 1) * size, :]
+        r.rows[1, rows, :] = merge[k, :size, :]
+        rows = pl.ds(pl.multiple_of((me ^ z.found[at]) * z.merge, 16), z.merge)
+        r.merge_rows[rows, :] = merge[k, size:, :]
     norms = r.have[half * size :, :].astype(F32) + r.got[half * size :, :].astype(F32)
     for l in range(z.L):
         rows = r.rows.at[l]
@@ -643,9 +655,9 @@
     for k in range(9):
         r.merge_weight[:, k * z.C : (k + 1) * z.C] = r.merge_rows[k * z.O : (k + 1) * z.O, :].astype(F32)
     small = r.merge_rows[9 * z.O : 9 * z.O + 16, :].astype(F32)
-    r.merge_bias[:, : z.C] = small[0:1]
-    r.merge_bias[:, z.C : 2 * z.C] = small[1:2]
-    r.merge_bias[:, 2 * z.C :] = small[2:3, : z.O - 2 * z.C]
+    r.merge_bias[: z.C] = small[0]
+    r.merge_bias[z.C : 2 * z.C] = small[1]
+    r.merge_bias[2 * z.C :] = small[2, : z.O - 2 * z.C]
 
 
 def pack_kernel(z, r):
@@ -691,14 +703,18 @@
         self.away = jnp.concatenate([part["away"] for part in parts], axis=1)
         self.left = [("hid", hid, bit) for bit in exchange_order(hid)]
 
-    def step(self, token=None):
+    def step(self, token=None, tie=None):
         axis, n, bit = self.left.pop(0)
-        x = add(self.here, swap(self.away, axis, n, bit), token)
+        got = swap(self.away, axis, n, bit)
+        if tie is not None:
+            got, tie = lax.optimization_barrier((got, tie))
+        x = add(self.here, got, token)
         if axis == "img":
             self.here = self.away = x
-            return
+            return tie
         half = x.shape[0] // 2
         self.here, self.away = (x[:half], x[half:]) if half else (x[0], None)
+        return tie
 
     def halve(self, token):
         while self.left:
@@ -840,6 +856,8 @@
         if chain:
             rows = jnp.concatenate([chain.halve(t["token"]), merge.halve(t["token"])], axis=0)
             chain.widen(rows, img)
+        if chain:
+            own.step()
         held = [own.here] + ([chain.here] if chain else [])
         e = call(
             partial(mix_back_kernel, z, l, l == 0),
@@ -852,7 +870,10 @@
             5, 0.05, (), held,
         )
         own.step(e["token"])
-        (chain or merge).step(e["token"])
+        if chain:
+            chain.step(None, own.here)
+        else:
+            merge.step(e["token"])
         chain, last = chain or own, own
         grad, norms[l] = e["state_grad"], e["first_norm"]
     images_grad = grad.reshape(z.side, z.side, z.I, z.C).transpose(2, 0, 1, 3)
@@ -863,28 +884,37 @@
         dict(features=arr(z.I, z.half, z.half * z.O, dtype=BF16), **token), dict(merged=kept(z.I * z.M, z.O)), 6, 2, (), [last.here],
     )
     norm_rows = jnp.pad(jnp.concatenate(norms, axis=0), ((0, 16 - 2 * z.L), (0, 0))).astype(BF16)
-    last.widen(jnp.concatenate([last.halve(None), norm_rows], axis=0), img)
-    shown = f["token"]
-    while chain.left or last.left:
-        for each in (chain, last):
-            if each.left:
-                each.step(shown if each is last else None)
-        shown = None
+    last.widen(jnp.concatenate([last.halve(f["token"]), norm_rows], axis=0), img)
+    while chain.left:
+        chain.step(None, last.here)
     feed, cut = 2 * z.units, 2 * z.units + z.shared
+    merge = chain.here[None, feed:]
+    bits = bits_of(hid)
+    bits = bits[1:] + bits[:1]
+
+    def widen_merge(merge, bit):
+        return jnp.concatenate([merge, swap(merge, "hid", hid, bit)], axis=0)
+
+    merge = widen_merge(merge, bits[0])
+    while len(last.left) > 1:
+        last.step()
+    last.step(None, merge)
     feed_rows = jnp.concatenate([last.here[:feed], chain.here[:feed]], axis=0)
-    have = jnp.concatenate([last.here[feed:cut], chain.here[feed:cut]], axis=0)
-    norm_rows, merge = last.here[cut:], chain.here[None, cut:]
-    bits = bits_of(hid)
-    orders = bits[::-1], bits[1:] + bits[:1]
-    z.found = [[0], [0]]
-    for step, (bit, merge_bit) in enumerate(zip(*orders)):
+    have = last.here[feed:cut]
+    norm_rows = last.here[cut:]
+    z.found = [0]
+    for step, bit in enumerate(bits):
         sent = jnp.concatenate([have, norm_rows], axis=0)
-        got, merge_got = swap(sent, "hid", hid, bit), swap(merge, "hid", hid, merge_bit)
-        z.found = [found + [e ^ b for e in found] for found, b in zip(z.found, (bit, merge_bit))]
-        if step < len(bits) - 1:
+        got = swap(sent, "hid", hid, bit)
+        z.found = z.found + [e ^ bit for e in z.found]
+        if step + 2 < len(bits):
+            merge = widen_merge(merge, bits[step + 1])
+            got, _ = lax.optimization_barrier((got, merge))
+        elif step + 2 == len(bits):
+            merge_got = swap(merge, "hid", hid, bits[-1])
+        if step + 1 < len(bits):
             have = jnp.concatenate([have, got[:-16]], axis=0)
             norm_rows = add(norm_rows, got[-16:], None)
-            merge = jnp.concatenate([merge, merge_got], axis=0)
     g = call(
         partial(last_kernel, z),
         dict(place=place, have=sent, got=got, merge_have=merge, merge_got=merge_got, feed_rows=feed_rows),
@@ -896,7 +926,7 @@
         f["features"], images_grad, g["mix_weight"], g["mix_bias"], g["squeeze_weight"].transpose(0, 2, 1),
         g["squeeze_bias"], g["expand_weight"], g["expand_bias"], g["project_weight"], g["project_bias"], g["norm_gain"],
         g["norm_bias"], g["inner_weight"].transpose(0, 2, 1), g["inner_bias"], g["outer_weight"], g["outer_bias"],
-        g["merge_weight"].T, g["merge_bias"].reshape(-1),
+        g["merge_weight"].T, g["merge_bias"],
     )
 
 

time: 86.8 us -> 83.8 us (0.965)
  starting transfers between devices: 23.3 us -> 21.7 us
  Pallas kernels: 41.1 us -> 40.1 us
    ppermute x22, starting transfers between devices: 23.3 us -> 21.7 us  [swap(): return lax.ppermute(x, axis, [(a, a ^ bit) for a in range(n)])]
    pallas_call x12, Pallas kernels: 41.1 us -> 40.1 us  [call(): pl.pallas_call(kernel, out_shape=list(outs.values()), in_specs=[place(nam...]
  transfers between devices with their start and end apart: 22 -> 22, of which waited for: 15 -> 13; matrix products, arithmetic and copies ran while one was open for 2% -> 2% of each run, Pallas kernels for 30% -> 30%
where the time goes in v6:
time: 83.8 us; the launch traced here: 83.6 us
  Pallas kernels  40.1 us (48%)
  starting transfers between devices  21.7 us (26%)
  waiting for transfers between devices  18.1 us (22%)
  local copies, waits for them, and re-layouts  1.38 us (2%)
  between operations  1.3 us (2%)
  other arithmetic  0.96 us (1%)
    pallas_call x12, Pallas kernels, call(): pl.pallas_call(kernel, out_shape=list(outs.values()), in_specs=[place(nam...  40.1 us
    ppermute x22, starting transfers between devices, swap(): return lax.ppermute(x, axis, [(a, a ^ bit) for a in range(n)])  21.7 us
    ppermute x22, waiting for transfers between devices, swap(): return lax.ppermute(x, axis, [(a, a ^ bit) for a in range(n)])  18.1 us
  transfers between devices with their start and end apart: 22, of which 13 were waited for; matrix products, arithmetic and copies ran while one was open for 2% of the time, Pallas kernels for 30%

profile of v6, /device:TPU:0, one launch (start us, length us, event | category | flops | bytes accessed | tf_op | source)
XLA Modules:
  0.0 83.6 jit_solution(11373993387477612210)
XLA Ops:
  1.6 3.0 %collective-permute-start = (bf16[1,272,128]{2,1,0:T(8,128)(2,1)S(1)}, bf16[1,272,128]{2,1,0:T(8,128)(2,1)S(1)}, u32[]{:S(2)}, u32[]{:S(2)}) collective-permute-start(bf16[1,272,128]{2,1,0:T(8,128)(2,1)S(1)} %bitcast.32), channel_id=1, source_target_pairs={{0,2},{1,3},{2,0},{3,1},{4,6},{5,7},{6,4},{7,5},{8,10},{9,11},{10,... | collective-permute-start | bytes 208904 | tf_op jit(solution)/shard_map/ppermute | solution.py:682
  4.8 2.8 %shard_map.322 = (f32[2688,128]{1,0:T(8,128)S(1)}, bf16[2688,128]{1,0:T(8,128)(2,1)S(1)}, bf16[2688,128]{1,0:T(8,128)(2,1)S(1)}, bf16[864,320]{1,0:T(8,128)(2,1)...) custom-call(s32[2,2]{1,0:T(2,128)S(1)} %copy-done.6, s32[1]{0:T(128)} %bitcast.refs_1_.refs_0_.refs_6_, ...), custom_call_target="tpu_custom_call" | custom-call | flops 3449999872 | tf_op jit(solution)/shard_map/pallas_call | solution.py:115
  7.7 1.6 %collective-permute-start.1 = (bf16[2,272,128]{2,1,0:T(8,128)(2,1)S(1)}, bf16[2,272,128]{2,1,0:T(8,128)(2,1)S(1)}, u32[]{:S(2)}, u32[]{:S(2)}) collective-permute-start(bf16[2,272,128]{2,1,0:T(8,128)(2,1)S(1)} %pad_maximum_fusion.7.refs_14_), channel_id=1, source_target_pairs={{0,4},{1,5},{2,6},{3,7},{4,0},{5,1},{6,2},{7,3},{8,12},{9,13},{10,... | collective-permute-start | bytes 417800 | tf_op jit(solution)/shard_map/ppermute | solution.py:682
  9.4 4.3 %shard_map.324 = (f32[2688,128]{1,0:T(8,128)S(1)}, bf16[384,384]{1,0:T(8,128)(2,1)S(1)}, f32[2,32,384]{2,1,0:T(8,128)S(1)}, f32[2,384]{1,0:T(2,128)S(1)}, bf16[2...) custom-call(bf16[2592,128]{1,0:T(8,128)(2,1)S(1)} %bitcast.50, ...), custom_call_target="tpu_custom_call" | custom-call | flops 5750000128 | tf_op jit(solution)/shard_map/pallas_call | solution.py:115
  13.9 1.5 %collective-permute-done.2 = bf16[4,272,128]{2,1,0:T(8,128)(2,1)S(1)} collective-permute-done((bf16[4,272,128]{2,1,0:T(8,128)(2,1)S(1)}, bf16[4,272,128]{2,1,0:T(8,128)(2,1)S(1)}, u32[]{:S(2)}, u32[]{:S(2)}) %collective-permute-start.2) | collective-permute-done | bytes 278560 | tf_op jit(solution)/shard_map/ppermute | solution.py:682
  15.5 12.5 %shard_map.325 = (bf16[864,1152]{1,0:T(8,128)(2,1)S(1)}, bf16[4,368,128]{2,1,0:T(8,128)(2,1)S(1)}, bf16[4,368,128]{2,1,0:T(8,128)(2,1)S(1)}, bf16[2,512,128]{2,1...) custom-call(s32[2,2]{1,0:T(2,128)S(1)} %copy-done.6, ...), custom_call_target="tpu_custom_call" | custom-call | flops 18400000000 | tf_op jit(solution)/shard_map/pallas_call | solution.py:115
  28.2 2.8 %shard_map.326 = (f32[2688,128]{1,0:T(8,128)S(1)}, f32[8,128]{1,0:T(8,128)S(1)}, bf16[4,128,128]{2,1,0:T(8,128)(2,1)S(1)}, bf16[4,128,128]{2,1,0:T(8,128)(2,1)S(1)}, f32[1,128]{1,0:T(1,128)S(1)}) custom-call(s32[1]{0:T(128)} %bitcast.refs_1_.refs_0_.refs_6_, f32[2688,128]{1,0:T(8,128)S(1)} %get-tuple-element.112.refs_2_.refs_1_.refs_0_, ...), custom_call_target="tpu_custom_call" | custom-call | flops 2300000000 | tf_op jit(solution)/shard_map/pallas_call | solution.py:115
  32.1 3.2 %shard_map.327 = (bf16[2688,256]{1,0:T(8,128)(2,1)S(1)}, bf16[384,256]{1,0:T(8,128)(2,1)S(1)}, f32[3,8,128]{2,1,0:T(8,128)S(1)}, bf16[4,96,128]{2,1,0:T(8,128)(2...) custom-call(s32[2,2]{1,0:T(2,128)S(1)} %copy-done.6, s32[1]{0:T(128)} %bitcast.refs_1_.refs_0_.refs_6_, ...), custom_call_target="tpu_custom_call" | custom-call | flops 1150000000 | tf_op jit(solution)/shard_map/pallas_call | solution.py:115
  35.4 1.7 %shard_map.328 = (f32[2688,128]{1,0:T(8,128)S(1)}, f32[2,128]{1,0:T(2,128)S(1)}, f32[1,128]{1,0:T(1,128)S(1)}) custom-call(f32[2688,128]{1,0:T(8,128)S(1)} %get-tuple-element.112.refs_2_.refs_1_.refs_0_, bf16[2688,128]{1,0:T(8,128)(2,1)S(1)} %get-tuple-element.123.refs_1_, f32[2,2,128]{2,1,0:T(2,128)S(1)} %copy-done.3, ...), custom_call_target="tpu_custom_call" | custom-call | flops 57500000 | tf_op jit(solution)/shard_map/pallas_call | solution.py:115
  37.2 1.2 %collective-permute-done.4 = bf16[2,368,128]{2,1,0:T(8,128)(2,1)S(1)} collective-permute-done((bf16[2,368,128]{2,1,0:T(8,128)(2,1)S(1)}, bf16[2,368,128]{2,1,0:T(8,128)(2,1)S(1)}, u32[]{:S(2)}, u32[]{:S(2)}) %collective-permute-start.4) | collective-permute-done | bytes 188448 | tf_op jit(solution)/shard_map/ppermute | solution.py:682
  38.4 1.3 %collective-permute-start.10 = (bf16[1,368,128]{2,1,0:T(8,128)(2,1)S(1)}, bf16[1,368,128]{2,1,0:T(8,128)(2,1)S(1)}, u32[]{:S(2)}, u32[]{:S(2)}) collective-permute-start(bf16[1,368,128]{2,1,0:T(8,128)(2,1)S(1)} %get-tuple-element.230), channel_id=1, source_target_pairs={{0,2},{1,3},{2,0},{3,1},{4,6},{5,7},{6,4},{7,5},{8,10},{9,11},{10,... | collective-permute-start | bytes 282632 | tf_op jit(solution)/shard_map/ppermute | solution.py:682
  40.6 3.1 %shard_map.329 = (f32[2688,128]{1,0:T(8,128)S(1)}, f32[8,128]{1,0:T(8,128)S(1)}, bf16[4,128,128]{2,1,0:T(8,128)(2,1)S(1)}, bf16[4,128,128]{2,1,0:T(8,128)(2,1)S(1)}, f32[1,128]{1,0:T(1,128)S(1)}) custom-call(s32[1]{0:T(128)} %bitcast.refs_1_.refs_0_.refs_6_, f32[2688,128]{1,0:T(8,128)S(1)} %get-tuple-element.112.refs_2_.refs_1_.refs_0_, ...), custom_call_target="tpu_custom_call" | custom-call | flops 2300000000 | tf_op jit(solution)/shard_map/pallas_call | solution.py:115
  43.7 1.0 %collective-permute-done.6 = bf16[2,224,128]{2,1,0:T(8,128)(2,1)S(1)} collective-permute-done((bf16[2,224,128]{2,1,0:T(8,128)(2,1)S(1)}, bf16[2,224,128]{2,1,0:T(8,128)(2,1)S(1)}, u32[]{:S(2)}, u32[]{:S(2)}) %collective-permute-start.6) | collective-permute-done | bytes 114720 | tf_op jit(solution)/shard_map/ppermute | solution.py:682
  45.6 2.8 %shard_map.330 = (bf16[2688,256]{1,0:T(8,128)(2,1)S(1)}, bf16[384,256]{1,0:T(8,128)(2,1)S(1)}, f32[3,8,128]{2,1,0:T(8,128)S(1)}, bf16[4,96,128]{2,1,0:T(8,128)(2...) custom-call(s32[2,2]{1,0:T(2,128)S(1)} %copy-done.6, s32[1]{0:T(128)} %bitcast.refs_1_.refs_0_.refs_6_, ...), custom_call_target="tpu_custom_call" | custom-call | flops 1150000000 | tf_op jit(solution)/shard_map/pallas_call | solution.py:115
  49.1 1.6 %collective-permute-start.14 = (bf16[592,128]{1,0:T(8,128)(2,1)S(1)}, bf16[592,128]{1,0:T(8,128)(2,1)S(1)}, u32[]{:S(2)}, u32[]{:S(2)}) collective-permute-start(bf16[592,128]{1,0:T(8,128)(2,1)S(1)} %pad_maximum_fusion.6.refs_10_), channel_id=1, source_target_pairs={{0,8},{8,0},{16,24},{24,16},{1,9},{9,1},{17,25},{25,17},{2,10},{10... | collective-permute-start | bytes 454664 | tf_op jit(solution)/shard_map/ppermute | solution.py:682
  51.5 2.9 %shard_map.331 = (f32[2592,128]{1,0:T(8,128)}, f32[2,128]{1,0:T(2,128)S(1)}, f32[1,128]{1,0:T(1,128)S(1)}) custom-call(f32[2688,128]{1,0:T(8,128)S(1)} %get-tuple-element.112.refs_2_.refs_1_.refs_0_, bf16[2688,128]{1,0:T(8,128)(2,1)S(1)} %get-tuple-element.123.refs_1_, f32[2,2,128]{2,1,0:T(2,128)S(1)} %copy-done.3, ...), custom_call_target="tpu_custom_call" | custom-call | flops 57500000 | tf_op jit(solution)/shard_map/pallas_call | solution.py:115
  54.5 1.3 %collective-permute-done.8 = bf16[2,224,128]{2,1,0:T(8,128)(2,1)S(1)} collective-permute-done((bf16[2,224,128]{2,1,0:T(8,128)(2,1)S(1)}, bf16[2,224,128]{2,1,0:T(8,128)(2,1)S(1)}, u32[]{:S(2)}, u32[]{:S(2)}) %collective-permute-start.8) | collective-permute-done | bytes 114720 | tf_op jit(solution)/shard_map/ppermute | solution.py:682
  55.9 2.7 %collective-permute-start.15 = (bf16[592,128]{1,0:T(8,128)(2,1)S(1)}, bf16[592,128]{1,0:T(8,128)(2,1)S(1)}, u32[]{:S(2)}, u32[]{:S(2)}) collective-permute-start(bf16[592,128]{1,0:T(8,128)(2,1)S(1)} %add_convert_fusion.5), channel_id=1, source_target_pairs={{0,16},{8,24},{16,0},{24,8},{1,17},{9,25},{17,1},{25,9},{2,18},{10... | collective-permute-start | bytes 454664 | tf_op jit(solution)/shard_map/ppermute | solution.py:682
  58.5 1.3 %collective-permute-start.11 = (bf16[1,224,128]{2,1,0:T(8,128)(2,1)S(1)}, bf16[1,224,128]{2,1,0:T(8,128)(2,1)S(1)}, u32[]{:S(2)}, u32[]{:S(2)}) collective-permute-start(bf16[1,224,128]{2,1,0:T(8,128)(2,1)S(1)} %get-tuple-element.232), channel_id=1, source_target_pairs={{0,2},{1,3},{2,0},{3,1},{4,6},{5,7},{6,4},{7,5},{8,10},{9,11},{10,... | collective-permute-start | bytes 172040 | tf_op jit(solution)/shard_map/ppermute | solution.py:682
  59.8 1.4 %shard_map.332 = (bf16[2,18,5760]{2,1,0:T(8,128)(2,1)S(1)}, f32[1,128]{1,0:T(1,128)S(1)}) custom-call(bf16[864,1152]{1,0:T(8,128)(2,1)S(1)} %get-tuple-element.122.refs_0_, bf16[320,1152]{1,0:T(8,128)(2,1)S(1)} %bitcast.49, f32[1,320]{1,0:T(1,128)S(1)} %reshape.65.refs_2_, bf16[1,224,128]{2,1,0:T(8,128)(2,1)S(1)} %get-tuple-element.233.refs_3_), custom_call_target="tpu_custom_call" | custom-call | flops 2300000000 | tf_op jit(solution)/shard_map/pallas_call | solution.py:115
  61.2 1.5 %collective-permute-done.11 = bf16[1,224,128]{2,1,0:T(8,128)(2,1)S(1)} collective-permute-done((bf16[1,224,128]{2,1,0:T(8,128)(2,1)S(1)}, bf16[1,224,128]{2,1,0:T(8,128)(2,1)S(1)}, u32[]{:S(2)}, u32[]{:S(2)}) %collective-permute-start.11) | collective-permute-done | bytes 57376 | tf_op jit(solution)/shard_map/ppermute | solution.py:682
  62.7 1.3 %collective-permute-start.12 = (bf16[240,128]{1,0:T(8,128)(2,1)S(1)}, bf16[240,128]{1,0:T(8,128)(2,1)S(1)}, u32[]{:S(2)}, u32[]{:S(2)}) collective-permute-start(bf16[240,128]{1,0:T(8,128)(2,1)S(1)} %pad_maximum_fusion.10), channel_id=1, source_target_pairs={{0,8},{8,0},{16,24},{24,16},{1,9},{9,1},{17,25},{25,17},{2,10},{10... | collective-permute-start | bytes 184328 | tf_op jit(solution)/shard_map/ppermute | solution.py:682
  65.0 1.8 %collective-permute-start.16 = (bf16[1,464,128]{2,1,0:T(8,128)(2,1)S(1)}, bf16[1,464,128]{2,1,0:T(8,128)(2,1)S(1)}, u32[]{:S(2)}, u32[]{:S(2)}) collective-permute-start(bf16[1,464,128]{2,1,0:T(8,128)(2,1)S(1)} %slice_bitcast_fusion), channel_id=1, source_target_pairs={{0,2},{1,3},{2,0},{3,1},{4,6},{5,7},{6,4},{7,5},{8,10},{9,11},{10,... | collective-permute-start | bytes 356360 | tf_op jit(solution)/shard_map/ppermute | solution.py:682
  67.5 2.5 %collective-permute-done.16 = bf16[1,464,128]{2,1,0:T(8,128)(2,1)S(1)} collective-permute-done((bf16[1,464,128]{2,1,0:T(8,128)(2,1)S(1)}, bf16[1,464,128]{2,1,0:T(8,128)(2,1)S(1)}, u32[]{:S(2)}, u32[]{:S(2)}) %collective-permute-start.16) | collective-permute-done | bytes 118816 | tf_op jit(solution)/shard_map/ppermute | solution.py:682
  70.8 1.4 %collective-permute-done.13 = bf16[240,128]{1,0:T(8,128)(2,1)S(1)} collective-permute-done((bf16[240,128]{1,0:T(8,128)(2,1)S(1)}, bf16[240,128]{1,0:T(8,128)(2,1)S(1)}, u32[]{:S(2)}, u32[]{:S(2)}) %collective-permute-start.13) | collective-permute-done | bytes 61472 | tf_op jit(solution)/shard_map/ppermute | solution.py:682
  72.3 1.3 %collective-permute-start.17 = (bf16[112,128]{1,0:T(8,128)(2,1)S(1)}, bf16[112,128]{1,0:T(8,128)(2,1)S(1)}, u32[]{:S(2)}, u32[]{:S(2)}) collective-permute-start(bf16[112,128]{1,0:T(8,128)(2,1)S(1)} %concatenate.71), channel_id=1, source_target_pairs={{0,2},{1,3},{2,0},{3,1},{4,6},{5,7},{6,4},{7,5},{8,10},{9,11},{10,... | collective-permute-start | bytes 86024 | tf_op jit(solution)/shard_map/ppermute | solution.py:682
  73.6 2.7 %collective-permute-done.18 = bf16[2,464,128]{2,1,0:T(8,128)(2,1)S(1)} collective-permute-done((bf16[2,464,128]{2,1,0:T(8,128)(2,1)S(1)}, bf16[2,464,128]{2,1,0:T(8,128)(2,1)S(1)}, u32[]{:S(2)}, u32[]{:S(2)}) %collective-permute-start.18) | collective-permute-done | bytes 237600 | tf_op jit(solution)/shard_map/ppermute | solution.py:682
  76.5 1.1 %collective-permute-start.19 = (bf16[208,128]{1,0:T(8,128)(2,1)S(1)}, bf16[208,128]{1,0:T(8,128)(2,1)S(1)}, u32[]{:S(2)}, u32[]{:S(2)}) collective-permute-start(bf16[208,128]{1,0:T(8,128)(2,1)S(1)} %pad_maximum_fusion.11), channel_id=1, source_target_pairs={{0,4},{1,5},{2,6},{3,7},{4,0},{5,1},{6,2},{7,3},{8,12},{9,13},{10,... | collective-permute-start | bytes 159752 | tf_op jit(solution)/shard_map/ppermute | solution.py:682
  77.5 1.1 %copy.38 = bf16[2,18,5760]{2,0,1:T(2,128)(2,1)} copy(bf16[2,18,5760]{2,1,0:T(8,128)(2,1)S(1)} %get-tuple-element.206) | data formatting | bytes 829440
  78.6 2.1 %collective-permute-done.19 = bf16[208,128]{1,0:T(8,128)(2,1)S(1)} collective-permute-done((bf16[208,128]{1,0:T(8,128)(2,1)S(1)}, bf16[208,128]{1,0:T(8,128)(2,1)S(1)}, u32[]{:S(2)}, u32[]{:S(2)}) %collective-permute-start.19) | collective-permute-done | bytes 53280 | tf_op jit(solution)/shard_map/ppermute | solution.py:682
  80.8 1.3 %collective-permute-done.20.refs_2_ = bf16[400,128]{1,0:T(8,128)(2,1)S(1)} collective-permute-done((bf16[400,128]{1,0:T(8,128)(2,1)S(1)}, bf16[400,128]{1,0:T(8,128)(2,1)S(1)}, u32[]{:S(2)}, u32[]{:S(2)}) %collective-permute-start.20) | collective-permute-done | bytes 102432 | tf_op jit(solution)/shard_map/ppermute | solution.py:682
  82.1 1.5 %shard_map.333 = (f32[2,3,128,128]{3,2,1,0:T(8,128)}, f32[2,2,128]{2,1,0:T(2,128)}, f32[2,32,128]{2,1,0:T(8,128)}, f32[2,32]{1,0:T(2,128)}, f32[2,32,384]{2,1,0:...) custom-call(s32[1]{0:T(128)} %bitcast.refs_1_.refs_0_.refs_6_, ...), custom_call_target="tpu_custom_call" | custom-call | flops 2300000000 | tf_op jit(solution)/shard_map/pallas_call | solution.py:115
  (108 shorter events, 8.6 us)
Async XLA Ops:
  1.6 6.1 %collective-permute-start = (bf16[1,272,128]{2,1,0:T(8,128)(2,1)S(1)}, bf16[1,272,128]{2,1,0:T(8,128)(2,1)S(1)}, u32[]{:S(2)}, u32[]{:S(2)}) collective-permute-start(bf16[1,272,128]{2,1,0:T(8,128)(2,1)S(1)} %bitcast.32), channel_id=1, source_target_pairs={{0,2},{1,3},{2,0},{3,1},{4,6},{5,7},{6,4},{7,5},{8,10},{9,11},{10,... | collective-permute-start | bytes 208904 | tf_op jit(solution)/shard_map/ppermute | solution.py:682
  4.7 4.6 %copy-start = (bf16[2,3,128,128]{3,2,1,0:T(8,128)(2,1)S(1)}, bf16[2,3,128,128]{3,2,1,0:T(8,128)(2,1)}, u32[]{:S(2)}) copy-start(bf16[2,3,128,128]{3,2,1,0:T(8,128)(2,1)} %refs_14_.3) | copy-start | bytes 589828
  4.7 4.6 %copy-start.1 = (bf16[2,128,128]{2,1,0:T(8,128)(2,1)S(1)}, bf16[2,128,128]{2,1,0:T(8,128)(2,1)}, u32[]{:S(2)}) copy-start(bf16[2,128,128]{2,1,0:T(8,128)(2,1)} %refs_18_.5) | copy-start | bytes 196612
  4.7 4.6 %copy-start.2 = (f32[2,128,32]{1,2,0:T(8,128)S(1)}, f32[2,128,32]{1,2,0:T(8,128)}, u32[]{:S(2)}) copy-start(f32[2,128,32]{1,2,0:T(8,128)} %param.24) | copy-start | bytes 98308
  4.7 4.6 %copy-start.3 = (f32[2,2,128]{2,1,0:T(2,128)S(1)}, f32[2,2,128]{2,1,0:T(2,128)}, u32[]{:S(2)}) copy-start(f32[2,2,128]{2,1,0:T(2,128)} %refs_2_.6) | copy-start | bytes 6148
  4.8 4.6 %copy-start.4 = (f32[2,2,128]{2,1,0:T(2,128)S(1)}, f32[2,2,128]{2,1,0:T(2,128)}, u32[]{:S(2)}) copy-start(f32[2,2,128]{2,1,0:T(2,128)} %refs_15_.5) | copy-start | bytes 6148
  4.8 4.6 %copy-start.5 = (f32[2,2,128]{2,1,0:T(2,128)S(1)}, f32[2,2,128]{2,1,0:T(2,128)}, u32[]{:S(2)}) copy-start(f32[2,2,128]{2,1,0:T(2,128)} %refs_21_.3) | copy-start | bytes 6148
  4.8 4.6 %copy-start.7 = (f32[2,32]{1,0:T(2,128)S(1)}, f32[2,32]{1,0:T(2,128)}, u32[]{:S(2)}) copy-start(f32[2,32]{1,0:T(2,128)} %refs_17_.5) | copy-start | bytes 772
  4.8 4.6 %copy-start.8 = (f32[2,128]{1,0:T(2,128)S(1)}, f32[2,128]{1,0:T(2,128)}, u32[]{:S(2)}) copy-start(f32[2,128]{1,0:T(2,128)} %refs_19_.5) | copy-start | bytes 3076
  4.8 4.6 %copy-start.10 = (bf16[2,36,36,128]{3,0,2,1:T(2,128)(2,1)S(1)}, bf16[2,36,36,128]{3,0,2,1:T(2,128)(2,1)}, u32[]{:S(2)}) copy-start(bf16[2,36,36,128]{3,0,2,1:T(2,128)(2,1)} %param.19) | copy-start | bytes 1990660
  7.7 6.0 %collective-permute-start.1 = (bf16[2,272,128]{2,1,0:T(8,128)(2,1)S(1)}, bf16[2,272,128]{2,1,0:T(8,128)(2,1)S(1)}, u32[]{:S(2)}, u32[]{:S(2)}) collective-permute-start(bf16[2,272,128]{2,1,0:T(8,128)(2,1)S(1)} %pad_maximum_fusion.7.refs_14_), channel_id=1, source_target_pairs={{0,4},{1,5},{2,6},{3,7},{4,0},{5,1},{6,2},{7,3},{8,12},{9,13},{10,... | collective-permute-start | bytes 417800 | tf_op jit(solution)/shard_map/ppermute | solution.py:682
  13.8 1.6 %collective-permute-start.2 = (bf16[4,272,128]{2,1,0:T(8,128)(2,1)S(1)}, bf16[4,272,128]{2,1,0:T(8,128)(2,1)S(1)}, u32[]{:S(2)}, u32[]{:S(2)}) collective-permute-start(bf16[4,272,128]{2,1,0:T(8,128)(2,1)S(1)} %pad_maximum_fusion.2), channel_id=1, source_target_pairs={{0,1},{1,0},{2,3},{3,2},{4,5},{5,4},{6,7},{7,6},{8,9},{9,8},{10,11... | collective-permute-start | bytes 835592 | tf_op jit(solution)/shard_map/ppermute | solution.py:682
  15.5 12.8 %copy-start.15 = (f32[320]{0:T(512)S(1)}, f32[320]{0:T(512)}, u32[]{:S(2)}) copy-start(f32[320]{0:T(512)} %param.37) | copy-start | bytes 3844
  28.0 3.1 %collective-permute-start.3 = (bf16[4,368,128]{2,1,0:T(8,128)(2,1)S(1)}, bf16[4,368,128]{2,1,0:T(8,128)(2,1)S(1)}, u32[]{:S(2)}, u32[]{:S(2)}) collective-permute-start(bf16[4,368,128]{2,1,0:T(8,128)(2,1)S(1)} %get-tuple-element.143), channel_id=1, source_target_pairs={{0,1},{1,0},{2,3},{3,2},{4,5},{5,4},{6,7},{7,6},{8,9},{9,8},{10,11... | collective-permute-start | bytes 1130504 | tf_op jit(solution)/shard_map/ppermute | solution.py:682
  31.3 7.1 %collective-permute-start.4 = (bf16[2,368,128]{2,1,0:T(8,128)(2,1)S(1)}, bf16[2,368,128]{2,1,0:T(8,128)(2,1)S(1)}, u32[]{:S(2)}, u32[]{:S(2)}) collective-permute-start(bf16[2,368,128]{2,1,0:T(8,128)(2,1)S(1)} %get-tuple-element.224), channel_id=1, source_target_pairs={{0,4},{1,5},{2,6},{3,7},{4,0},{5,1},{6,2},{7,3},{8,12},{9,13},{10,... | collective-permute-start | bytes 565256 | tf_op jit(solution)/shard_map/ppermute | solution.py:682
  35.2 4.5 %collective-permute-start.5 = (bf16[4,224,128]{2,1,0:T(8,128)(2,1)S(1)}, bf16[4,224,128]{2,1,0:T(8,128)(2,1)S(1)}, u32[]{:S(2)}, u32[]{:S(2)}) collective-permute-start(bf16[4,224,128]{2,1,0:T(8,128)(2,1)S(1)} %pad_maximum_fusion.4), channel_id=1, source_target_pairs={{0,1},{1,0},{2,3},{3,2},{4,5},{5,4},{6,7},{7,6},{8,9},{9,8},{10,11... | collective-permute-start | bytes 688136 | tf_op jit(solution)/shard_map/ppermute | solution.py:682
  38.4 10.1 %collective-permute-start.10 = (bf16[1,368,128]{2,1,0:T(8,128)(2,1)S(1)}, bf16[1,368,128]{2,1,0:T(8,128)(2,1)S(1)}, u32[]{:S(2)}, u32[]{:S(2)}) collective-permute-start(bf16[1,368,128]{2,1,0:T(8,128)(2,1)S(1)} %get-tuple-element.230), channel_id=1, source_target_pairs={{0,2},{1,3},{2,0},{3,1},{4,6},{5,7},{6,4},{7,5},{8,10},{9,11},{10,... | collective-permute-start | bytes 282632 | tf_op jit(solution)/shard_map/ppermute | solution.py:682
  39.9 4.9 %collective-permute-start.6 = (bf16[2,224,128]{2,1,0:T(8,128)(2,1)S(1)}, bf16[2,224,128]{2,1,0:T(8,128)(2,1)S(1)}, u32[]{:S(2)}, u32[]{:S(2)}) collective-permute-start(bf16[2,224,128]{2,1,0:T(8,128)(2,1)S(1)} %get-tuple-element.228), channel_id=1, source_target_pairs={{0,4},{1,5},{2,6},{3,7},{4,0},{5,1},{6,2},{7,3},{8,12},{9,13},{10,... | collective-permute-start | bytes 344072 | tf_op jit(solution)/shard_map/ppermute | solution.py:682
  44.8 4.2 %collective-permute-start.9 = (bf16[1,224,128]{2,1,0:T(8,128)(2,1)S(1)}, bf16[1,224,128]{2,1,0:T(8,128)(2,1)S(1)}, u32[]{:S(2)}, u32[]{:S(2)}) collective-permute-start(bf16[1,224,128]{2,1,0:T(8,128)(2,1)S(1)} %get-tuple-element.234), channel_id=1, source_target_pairs={{0,2},{1,3},{2,0},{3,1},{4,6},{5,7},{6,4},{7,5},{8,10},{9,11},{10,... | collective-permute-start | bytes 172040 | tf_op jit(solution)/shard_map/ppermute | solution.py:682
  48.5 2.2 %collective-permute-start.7 = (bf16[4,224,128]{2,1,0:T(8,128)(2,1)S(1)}, bf16[4,224,128]{2,1,0:T(8,128)(2,1)S(1)}, u32[]{:S(2)}, u32[]{:S(2)}) collective-permute-start(bf16[4,224,128]{2,1,0:T(8,128)(2,1)S(1)} %pad_maximum_fusion.5), channel_id=1, source_target_pairs={{0,1},{1,0},{2,3},{3,2},{4,5},{5,4},{6,7},{7,6},{8,9},{9,8},{10,11... | collective-permute-start | bytes 688136 | tf_op jit(solution)/shard_map/ppermute | solution.py:682
  49.1 6.7 %collective-permute-start.14 = (bf16[592,128]{1,0:T(8,128)(2,1)S(1)}, bf16[592,128]{1,0:T(8,128)(2,1)S(1)}, u32[]{:S(2)}, u32[]{:S(2)}) collective-permute-start(bf16[592,128]{1,0:T(8,128)(2,1)S(1)} %pad_maximum_fusion.6.refs_10_), channel_id=1, source_target_pairs={{0,8},{8,0},{16,24},{24,16},{1,9},{9,1},{17,25},{25,17},{2,10},{10... | collective-permute-start | bytes 454664 | tf_op jit(solution)/shard_map/ppermute | solution.py:682
  50.8 4.9 %collective-permute-start.8 = (bf16[2,224,128]{2,1,0:T(8,128)(2,1)S(1)}, bf16[2,224,128]{2,1,0:T(8,128)(2,1)S(1)}, u32[]{:S(2)}, u32[]{:S(2)}) collective-permute-start(bf16[2,224,128]{2,1,0:T(8,128)(2,1)S(1)} %get-tuple-element.227), channel_id=1, source_target_pairs={{0,4},{1,5},{2,6},{3,7},{4,0},{5,1},{6,2},{7,3},{8,12},{9,13},{10,... | collective-permute-start | bytes 344072 | tf_op jit(solution)/shard_map/ppermute | solution.py:682
  55.9 9.1 %collective-permute-start.15 = (bf16[592,128]{1,0:T(8,128)(2,1)S(1)}, bf16[592,128]{1,0:T(8,128)(2,1)S(1)}, u32[]{:S(2)}, u32[]{:S(2)}) collective-permute-start(bf16[592,128]{1,0:T(8,128)(2,1)S(1)} %add_convert_fusion.5), channel_id=1, source_target_pairs={{0,16},{8,24},{16,0},{24,8},{1,17},{9,25},{17,1},{25,9},{2,18},{10... | collective-permute-start | bytes 454664 | tf_op jit(solution)/shard_map/ppermute | solution.py:682
  58.5 4.2 %collective-permute-start.11 = (bf16[1,224,128]{2,1,0:T(8,128)(2,1)S(1)}, bf16[1,224,128]{2,1,0:T(8,128)(2,1)S(1)}, u32[]{:S(2)}, u32[]{:S(2)}) collective-permute-start(bf16[1,224,128]{2,1,0:T(8,128)(2,1)S(1)} %get-tuple-element.232), channel_id=1, source_target_pairs={{0,2},{1,3},{2,0},{3,1},{4,6},{5,7},{6,4},{7,5},{8,10},{9,11},{10,... | collective-permute-start | bytes 172040 | tf_op jit(solution)/shard_map/ppermute | solution.py:682
  62.7 4.3 %collective-permute-start.12 = (bf16[240,128]{1,0:T(8,128)(2,1)S(1)}, bf16[240,128]{1,0:T(8,128)(2,1)S(1)}, u32[]{:S(2)}, u32[]{:S(2)}) collective-permute-start(bf16[240,128]{1,0:T(8,128)(2,1)S(1)} %pad_maximum_fusion.10), channel_id=1, source_target_pairs={{0,8},{8,0},{16,24},{24,16},{1,9},{9,1},{17,25},{25,17},{2,10},{10... | collective-permute-start | bytes 184328 | tf_op jit(solution)/shard_map/ppermute | solution.py:682
  65.0 4.9 %collective-permute-start.16 = (bf16[1,464,128]{2,1,0:T(8,128)(2,1)S(1)}, bf16[1,464,128]{2,1,0:T(8,128)(2,1)S(1)}, u32[]{:S(2)}, u32[]{:S(2)}) collective-permute-start(bf16[1,464,128]{2,1,0:T(8,128)(2,1)S(1)} %slice_bitcast_fusion), channel_id=1, source_target_pairs={{0,2},{1,3},{2,0},{3,1},{4,6},{5,7},{6,4},{7,5},{8,10},{9,11},{10,... | collective-permute-start | bytes 356360 | tf_op jit(solution)/shard_map/ppermute | solution.py:682
  67.1 5.2 %collective-permute-start.13 = (bf16[240,128]{1,0:T(8,128)(2,1)S(1)}, bf16[240,128]{1,0:T(8,128)(2,1)S(1)}, u32[]{:S(2)}, u32[]{:S(2)}) collective-permute-start(bf16[240,128]{1,0:T(8,128)(2,1)S(1)} %add_convert_fusion.10), channel_id=1, source_target_pairs={{0,16},{8,24},{16,0},{24,8},{1,17},{9,25},{17,1},{25,9},{2,18},{10... | collective-permute-start | bytes 184328 | tf_op jit(solution)/shard_map/ppermute | solution.py:682
  69.9 6.4 %collective-permute-start.18 = (bf16[2,464,128]{2,1,0:T(8,128)(2,1)S(1)}, bf16[2,464,128]{2,1,0:T(8,128)(2,1)S(1)}, u32[]{:S(2)}, u32[]{:S(2)}) collective-permute-start(bf16[2,464,128]{2,1,0:T(8,128)(2,1)S(1)} %pad_maximum_fusion.3), channel_id=1, source_target_pairs={{0,4},{1,5},{2,6},{3,7},{4,0},{5,1},{6,2},{7,3},{8,12},{9,13},{10,... | collective-permute-start | bytes 712712 | tf_op jit(solution)/shard_map/ppermute | solution.py:682
  72.3 4.1 %collective-permute-start.17 = (bf16[112,128]{1,0:T(8,128)(2,1)S(1)}, bf16[112,128]{1,0:T(8,128)(2,1)S(1)}, u32[]{:S(2)}, u32[]{:S(2)}) collective-permute-start(bf16[112,128]{1,0:T(8,128)(2,1)S(1)} %concatenate.71), channel_id=1, source_target_pairs={{0,2},{1,3},{2,0},{3,1},{4,6},{5,7},{6,4},{7,5},{8,10},{9,11},{10,... | collective-permute-start | bytes 86024 | tf_op jit(solution)/shard_map/ppermute | solution.py:682
  76.5 4.2 %collective-permute-start.19 = (bf16[208,128]{1,0:T(8,128)(2,1)S(1)}, bf16[208,128]{1,0:T(8,128)(2,1)S(1)}, u32[]{:S(2)}, u32[]{:S(2)}) collective-permute-start(bf16[208,128]{1,0:T(8,128)(2,1)S(1)} %pad_maximum_fusion.11), channel_id=1, source_target_pairs={{0,4},{1,5},{2,6},{3,7},{4,0},{5,1},{6,2},{7,3},{8,12},{9,13},{10,... | collective-permute-start | bytes 159752 | tf_op jit(solution)/shard_map/ppermute | solution.py:682
  77.5 4.5 %collective-permute-start.21 = (bf16[4,464,128]{2,1,0:T(8,128)(2,1)S(1)}, bf16[4,464,128]{2,1,0:T(8,128)(2,1)S(1)}, u32[]{:S(2)}, u32[]{:S(2)}) collective-permute-start(bf16[4,464,128]{2,1,0:T(8,128)(2,1)S(1)} %pad_maximum_fusion.1.refs_3_), channel_id=1, source_target_pairs={{0,1},{1,0},{2,3},{3,2},{4,5},{5,4},{6,7},{7,6},{8,9},{9,8},{10,11... | collective-permute-start | bytes 1425416 | tf_op jit(solution)/shard_map/ppermute | solution.py:682
  80.7 1.4 %collective-permute-start.20 = (bf16[400,128]{1,0:T(8,128)(2,1)S(1)}, bf16[400,128]{1,0:T(8,128)(2,1)S(1)}, u32[]{:S(2)}, u32[]{:S(2)}) collective-permute-start(bf16[400,128]{1,0:T(8,128)(2,1)S(1)} %pad_maximum_fusion.8.refs_1_), channel_id=1, source_target_pairs={{0,1},{1,0},{2,3},{3,2},{4,5},{5,4},{6,7},{7,6},{8,9},{9,8},{10,11... | collective-permute-start | bytes 307208 | tf_op jit(solution)/shard_map/ppermute | solution.py:682
  (6 other events, 22.9 us)

commit v7 on v6

--- a/solution.py
+++ b/solution.py
@@ -313,14 +313,38 @@
     ref[z.base + z.N0 :, :] = jnp.zeros((ref.shape[0] - z.base - z.N0, z.C), F32)
 
 
+def unit_bias(z, blocks, l, which):
+    at = 2 * z.L * z.units + l
+    return jnp.concatenate([blocks[k, at : at + 1, : z.units].astype(F32) for k in which], axis=1)
+
+
+def feed_some(o, rows, inner, bias, outer):
+    act, slope = gelu_pair(dot(o.normed2[rows, :], inner, (1, 1)) + bias)
+    act = act.astype(BF16)
+    o.act_rows[rows, :] = act
+    o.slope_rows[rows, :] = slope.astype(BF16)
+    return dot(act, outer)
+
+
+def half_kernel(z, r):
+    which, u = range(z.parts // 2), z.units
+    inner = jnp.concatenate([r.gathered[k, :u, :] for k in which], axis=0)
+    outer = jnp.concatenate([r.gathered[k, u : 2 * u, :] for k in which], axis=0)
+    bias = unit_bias(z, r.gathered, 0, which)
+
+    def body(rows, at):
+        r.partial[rows, :] = feed_some(r, rows, inner, bias, outer) + r.outer_bias[0:1]
+
+    over(z, body, z.run_second)
+    r.token[...] = jnp.zeros_like(r.token)
+
+
 def feed_phase(z, r, l, o, source, after):
+    first = 0 if l else z.H // 2
+
     def body(rows, at):
-        pre = dot(o.normed2[rows, :], r.inner[l], (1, 1)) + r.inner_bias[l : l + 1]
-        act, slope = gelu_pair(pre)
-        act = act.astype(BF16)
-        o.act_rows[rows, :] = act
-        o.slope_rows[rows, :] = slope.astype(BF16)
-        out = dot(act, r.outer[l]) + r.outer_bias[l : l + 1]
+        out = feed_some(o, rows, r.inner[l, first:, :], r.inner_bias[l : l + 1, first:], r.outer[l, first:, :])
+        out = out + (r.outer_bias[l : l + 1] if l else r.partial[rows, :])
         state = source[rows, :] + r.mask[rows, :] * out
         after(rows, at, state)
 
@@ -376,28 +400,28 @@
     return sum((n >> k + 1) * (e // bit % 2) for k, bit in enumerate(exchange_order(n)))
 
 
-def put_blocks(z, me, rows, size, here, away, start=0):
-    half = z.parts // 2
+def put_blocks(z, me, rows, size, here, away):
     for e in range(z.parts):
-        at = rank(z.parts, e)
-        block = rows[pl.ds(pl.multiple_of((me ^ e) * size, 16), size), :]
-        if at < half:
-            here[at, start : start + size, :] = block
-        else:
-            away[at - half, start : start + size, :] = block
+        put_block(z, e, rows[pl.ds(pl.multiple_of((me ^ e) * size, 16), size), :], here, away)
+
+
+def put_block(z, e, block, here, away, start=0):
+    at, half, stop = rank(z.parts, e), z.parts // 2, start + block.shape[0]
+    if at < half:
+        here[at, start:stop, :] = block
+    else:
+        away[at - half, start:stop, :] = block
 
 
 def second_kernel(z, r):
     me = r.place[0]
-    for k, e in enumerate(z.gathered):
-        at = pl.multiple_of((me ^ e) * z.units, z.units)
+    for k in range(z.parts):
+        at = k * z.units
         for l in range(z.L):
-            r.inner[l, pl.ds(at, z.units), :] = r.gathered[k, 2 * l * z.units : (2 * l + 1) * z.units, :]
-            r.outer[l, pl.ds(at, z.units), :] = r.gathered[k, (2 * l + 1) * z.units : (2 * l + 2) * z.units, :]
-        at = 2 * z.L * z.units
-        r.bias_rows[me ^ e] = r.gathered[k, at : at + 16, :].astype(F32)
+            r.inner[l, at : at + z.units, :] = r.gathered[k, 2 * l * z.units : (2 * l + 1) * z.units, :]
+            r.outer[l, at : at + z.units, :] = r.gathered[k, (2 * l + 1) * z.units : (2 * l + 2) * z.units, :]
     for l in range(z.L):
-        r.inner_bias[l : l + 1] = jnp.concatenate([r.bias_rows[h, l : l + 1, : z.units] for h in range(z.parts)], axis=1)
+        r.inner_bias[l : l + 1] = unit_bias(z, r.gathered, l, range(z.parts))
     early, late = [Refs() for _ in range(z.L)], [Refs() for _ in range(z.L)]
     for l in range(z.L):
         early[l].normed2 = r.normed2_0 if l == 0 else r.normed2
@@ -459,16 +483,21 @@
     for ref in (r.vec, r.inner_sums, r.g_outer, r.g_inner):
         ref[...] = jnp.zeros_like(ref)
 
+    def units(late, early, rows):
+        return late[rows, :] if l else jnp.concatenate([early[rows, :], late[rows, :]], axis=1)
+
     def body(rows, at):
         mask = r.mask[rows, :]
         grad = r.grad[rows, :]
+        slope = units(r.slope_rows, None if l else r.slope_before, rows)
+        act = units(r.act_rows, None if l else r.act_before, rows)
         out = grad * mask
         r.vec[0] += rows8(out)
         out = out.astype(BF16)
-        pre = dot(out, r.outer[l], (1, 1)) * r.slope_rows[rows, :].astype(F32)
+        pre = dot(out, r.outer[l], (1, 1)) * slope.astype(F32)
         r.inner_sums[...] += rows8(pre)
         pre = pre.astype(BF16)
-        r.g_outer[...] += dot(out, r.act_rows[rows, :], (0, 0))
+        r.g_outer[...] += dot(out, act, (0, 0))
         r.g_inner[...] += dot(r.normed2[rows, :], pre, (0, 0))
         normed_grad = dot(pre, r.inner[l])
         unit = r.unit2[rows, :].astype(F32)
@@ -477,7 +506,10 @@
         r.half_grad[rows, :] = grad + norm_back(normed_grad, unit, r.rstd2[rows, :].astype(F32), gain)
 
     over(z, body, z.run_back)
-    inner = total(r.inner_sums[...])
+    inner, me = total(r.inner_sums[...]), r.place[0]
+    for k, e in enumerate(z.gathered):
+        r.unit_sums[me ^ e] = inner[:, k * z.units : (k + 1) * z.units]
+    inner = jnp.concatenate([r.unit_sums[k] for k in range(z.parts)], axis=1)
     small = [total(r.vec[k]) for k in range(3)]
     small += [inner[:, k * z.C : (k + 1) * z.C] for k in range(z.H // z.C)]
     small += [jnp.zeros((1, z.C), F32)]
@@ -485,7 +517,9 @@
     r.turned[0] = r.g_inner[...].T.astype(BF16)
     r.turned[1] = r.g_outer[...].T.astype(BF16)
     for k in range(2):
-        put_blocks(z, r.place[0], r.turned.at[k], z.units, r.here, r.away, k * z.units)
+        for spot, e in enumerate(z.gathered):
+            block = r.turned[k, spot * z.units : (spot + 1) * z.units, :]
+            put_block(z, e, block, r.here, r.away, k * z.units)
     r.token[...] = jnp.zeros_like(r.token)
 
 
@@ -787,28 +821,36 @@
         dict(normed=kept(z.long, z.C), sums=kept(3, 8, z.C)),
         5, 5, smem, [have],
     )
-    for bit in order[1:]:
+    for bit in order[1:-1]:
         have = widen(have, bit, b["token"] if bit == order[1] else None)
-    late = saved_late(z)
+    late, some_units = saved_late(z), kept(z.N, z.H // 2, dtype=BF16)
+    h = call(
+        partial(half_kernel, z),
+        dict(gathered=have, normed2=b["normed2"], outer_bias=outer_bias),
+        dict(partial=kept(z.N, z.C), act_rows=some_units, slope_rows=some_units, **token), {}, 4, 2,
+    )
+    have = widen(have, order[-1], h["token"])
     c = call(
         partial(second_kernel, z),
         dict(
-            sizes=sizes, mask=a["mask"], edge=a["edge"], state_in=b["state"], normed2_0=b["normed2"], gathered=have, place=place,
+            sizes=sizes, mask=a["mask"], edge=a["edge"], state_in=b["state"], normed2_0=b["normed2"], gathered=have,
+            partial=h["partial"], place=place,
             ewp=b["ewp"], ebp=b["ebp"], outer_bias=outer_bias, cot=a["cot"], merge_bias_sums=a["merge_bias_sums"], **small,
         ),
         dict(
             patch=kept(z.I * z.M, 9 * z.C, dtype=BF16),
             merge_here=kept(z.parts // 2, z.merge, z.C, dtype=BF16), merge_away=kept(z.parts // 2, z.merge, z.C, dtype=BF16),
             inner=kept(z.L, z.H, z.C, dtype=BF16), outer=kept(z.L, z.H, z.C, dtype=BF16),
-            act_rows_0=late["act_rows"], slope_rows_0=late["slope_rows"], **saved_early(z), **late,
+            act_rows_0=some_units, slope_rows_0=some_units, **saved_early(z), **late,
         ),
         dict(
-            state=kept(z.N, z.C), normed=kept(z.tall, z.C), sums=kept(3, 8, z.C), inner_bias=kept(z.L, z.H), bias_rows=kept(z.parts, 16, z.C),
+            state=kept(z.N, z.C), normed=kept(z.tall, z.C), sums=kept(3, 8, z.C), inner_bias=kept(z.L, z.H),
             merge_rows=kept(z.parts * z.merge, z.C, dtype=BF16),
         ),
         11, 16, smem,
     )
     first = dict(b, act_rows=c["act_rows_0"], slope_rows=c["slope_rows_0"])
+    before = dict(act_before=h["act_rows"], slope_before=h["slope_rows"])
 
     def some(s, **names):
         return {name: s[name] for name in names}
@@ -822,7 +864,7 @@
             partial(feed_back_kernel, z, l),
             dict(
                 place=place, mask=a["mask"], grad=grad, inner=c["inner"], outer=c["outer"], norm_gain=norm_gain,
-                **some(s, act_rows=0, slope_rows=0, normed2=0, unit2=0, rstd2=0),
+                **some(s, act_rows=0, slope_rows=0, normed2=0, unit2=0, rstd2=0), **({} if l else before),
             ),
             dict(
                 half_grad=kept(z.N, z.C), feed_small=arr(8, z.C), here=kept(z.parts // 2, 2 * z.units, z.C, dtype=BF16),
@@ -830,7 +872,7 @@
             ),
             dict(
                 vec=kept(3, 8, z.C), inner_sums=kept(8, z.H), g_outer=kept(z.C, z.H), g_inner=kept(z.C, z.H),
-                turned=kept(2, z.H, z.C, dtype=BF16),
+                turned=kept(2, z.H, z.C, dtype=BF16), unit_sums=kept(z.parts, 1, z.units),
             ),
             6, 2, smem, [merge.here] + ([chain.here] if chain else []),
         )

time: 83.8 us -> 83 us (level)
  waiting for transfers between devices: 18.1 us -> 16 us
    ppermute x22, waiting for transfers between devices: 18.1 us -> 16 us  [swap(): return lax.ppermute(x, axis, [(a, a ^ bit) for a in range(n)])]
    pallas_call x12 -> x13, Pallas kernels: 40.1 us -> 40.8 us  [call(): pl.pallas_call(kernel, out_shape=list(outs.values()), in_specs=[place(nam...]
  transfers between devices with their start and end apart: 22 -> 22, of which waited for: 13 -> 12; matrix products, arithmetic and copies ran while one was open for 2% -> 2% of each run, Pallas kernels for 30% -> 32%
where the time goes in v7:
time: 83 us; the launch traced here: 82.7 us
  Pallas kernels  40.8 us (49%)
  starting transfers between devices  22.3 us (27%)
  waiting for transfers between devices  16 us (19%)
  local copies, waits for them, and re-layouts  1.39 us (2%)
  between operations  1.34 us (2%)
  other arithmetic  0.99 us (1%)
    pallas_call x13, Pallas kernels, call(): pl.pallas_call(kernel, out_shape=list(outs.values()), in_specs=[place(nam...  40.8 us
    ppermute x22, starting transfers between devices, swap(): return lax.ppermute(x, axis, [(a, a ^ bit) for a in range(n)])  22.3 us
    ppermute x22, waiting for transfers between devices, swap(): return lax.ppermute(x, axis, [(a, a ^ bit) for a in range(n)])  16 us
  transfers between devices with their start and end apart: 22, of which 12 were waited for; matrix products, arithmetic and copies ran while one was open for 2% of the time, Pallas kernels for 32%

profile of v7, /device:TPU:0, one launch (start us, length us, event | category | flops | bytes accessed | tf_op | source)
XLA Modules:
  0.0 82.7 jit_solution(16834866898489695002)
XLA Ops:
  1.6 3.0 %collective-permute-start = (bf16[1,272,128]{2,1,0:T(8,128)(2,1)S(1)}, bf16[1,272,128]{2,1,0:T(8,128)(2,1)S(1)}, u32[]{:S(2)}, u32[]{:S(2)}) collective-permute-start(bf16[1,272,128]{2,1,0:T(8,128)(2,1)S(1)} %bitcast.34), channel_id=1, source_target_pairs={{0,2},{1,3},{2,0},{3,1},{4,6},{5,7},{6,4},{7,5},{8,10},{9,11},{10,... | collective-permute-start | bytes 208904 | tf_op jit(solution)/shard_map/ppermute | solution.py:716
  4.8 2.8 %shard_map.322 = (f32[2688,128]{1,0:T(8,128)S(1)}, bf16[2688,128]{1,0:T(8,128)(2,1)S(1)}, bf16[2688,128]{1,0:T(8,128)(2,1)S(1)}, bf16[864,320]{1,0:T(8,128)(2,1)...) custom-call(s32[2,2]{1,0:T(2,128)S(1)} %copy-done.6, s32[1]{0:T(128)} %bitcast.refs_1_.refs_0_.refs_7_, ...), custom_call_target="tpu_custom_call" | custom-call | flops 3449999872 | tf_op jit(solution)/shard_map/pallas_call | solution.py:115
  7.7 1.6 %collective-permute-start.1 = (bf16[2,272,128]{2,1,0:T(8,128)(2,1)S(1)}, bf16[2,272,128]{2,1,0:T(8,128)(2,1)S(1)}, u32[]{:S(2)}, u32[]{:S(2)}) collective-permute-start(bf16[2,272,128]{2,1,0:T(8,128)(2,1)S(1)} %pad_maximum_fusion.7.refs_14_), channel_id=1, source_target_pairs={{0,4},{1,5},{2,6},{3,7},{4,0},{5,1},{6,2},{7,3},{8,12},{9,13},{10,... | collective-permute-start | bytes 417800 | tf_op jit(solution)/shard_map/ppermute | solution.py:716
  9.4 4.3 %shard_map.324 = (f32[2688,128]{1,0:T(8,128)S(1)}, bf16[384,384]{1,0:T(8,128)(2,1)S(1)}, f32[2,32,384]{2,1,0:T(8,128)S(1)}, f32[2,384]{1,0:T(2,128)S(1)}, bf16[2...) custom-call(bf16[2592,128]{1,0:T(8,128)(2,1)S(1)} %bitcast.52, ...), custom_call_target="tpu_custom_call" | custom-call | flops 5750000128 | tf_op jit(solution)/shard_map/pallas_call | solution.py:115
  13.9 1.6 %shard_map.325 = (f32[2688,128]{1,0:T(8,128)S(1)}, bf16[2688,256]{1,0:T(8,128)(2,1)S(1)}, bf16[2688,256]{1,0:T(8,128)(2,1)S(1)}, f32[1,128]{1,0:T(1,128)S(1)}) custom-call(bf16[4,272,128]{2,1,0:T(8,128)(2,1)S(1)} %pad_maximum_fusion.2.refs_0_, bf16[2688,128]{1,0:T(8,128)(2,1)S(1)} %get-tuple-element.120.refs_1_.refs_4_.refs_8_, f32[2,128]{1,0:T(2,128)S(1)} %copy-done.13), custom_call_target="tpu_custom_call" | custom-call | flops 2300000000 | tf_op jit(solution)/shard_map/pallas_call | solution.py:115
  15.6 11.6 %shard_map.326 = (bf16[864,1152]{1,0:T(8,128)(2,1)S(1)}, bf16[4,368,128]{2,1,0:T(8,128)(2,1)S(1)}, bf16[4,368,128]{2,1,0:T(8,128)(2,1)S(1)}, bf16[2,512,128]{2,1...) custom-call(s32[2,2]{1,0:T(2,128)S(1)} %copy-done.6, ...), custom_call_target="tpu_custom_call" | custom-call | flops 18400000000 | tf_op jit(solution)/shard_map/pallas_call | solution.py:115
  27.7 2.9 %shard_map.327 = (f32[2688,128]{1,0:T(8,128)S(1)}, f32[8,128]{1,0:T(8,128)S(1)}, bf16[4,128,128]{2,1,0:T(8,128)(2,1)S(1)}, bf16[4,128,128]{2,1,0:T(8,128)(2,1)S(1)}, f32[1,128]{1,0:T(1,128)S(1)}) custom-call(s32[1]{0:T(128)} %bitcast.refs_1_.refs_0_.refs_7_, f32[2688,128]{1,0:T(8,128)S(1)} %get-tuple-element.116.refs_2_.refs_1_.refs_0_, ...), custom_call_target="tpu_custom_call" | custom-call | flops 2300000000 | tf_op jit(solution)/shard_map/pallas_call | solution.py:115
  31.6 3.2 %shard_map.328 = (bf16[2688,256]{1,0:T(8,128)(2,1)S(1)}, bf16[384,256]{1,0:T(8,128)(2,1)S(1)}, f32[3,8,128]{2,1,0:T(8,128)S(1)}, bf16[4,96,128]{2,1,0:T(8,128)(2...) custom-call(s32[2,2]{1,0:T(2,128)S(1)} %copy-done.6, s32[1]{0:T(128)} %bitcast.refs_1_.refs_0_.refs_7_, ...), custom_call_target="tpu_custom_call" | custom-call | flops 1150000000 | tf_op jit(solution)/shard_map/pallas_call | solution.py:115
  34.9 1.7 %shard_map.329 = (f32[2688,128]{1,0:T(8,128)S(1)}, f32[2,128]{1,0:T(2,128)S(1)}, f32[1,128]{1,0:T(1,128)S(1)}) custom-call(f32[2688,128]{1,0:T(8,128)S(1)} %get-tuple-element.116.refs_2_.refs_1_.refs_0_, bf16[2688,128]{1,0:T(8,128)(2,1)S(1)} %get-tuple-element.129.refs_1_, f32[2,2,128]{2,1,0:T(2,128)S(1)} %copy-done.3, ...), custom_call_target="tpu_custom_call" | custom-call | flops 57500000 | tf_op jit(solution)/shard_map/pallas_call | solution.py:115
  37.6 1.3 %collective-permute-start.10 = (bf16[1,368,128]{2,1,0:T(8,128)(2,1)S(1)}, bf16[1,368,128]{2,1,0:T(8,128)(2,1)S(1)}, u32[]{:S(2)}, u32[]{:S(2)}) collective-permute-start(bf16[1,368,128]{2,1,0:T(8,128)(2,1)S(1)} %get-tuple-element.238), channel_id=1, source_target_pairs={{0,2},{1,3},{2,0},{3,1},{4,6},{5,7},{6,4},{7,5},{8,10},{9,11},{10,... | collective-permute-start | bytes 282632 | tf_op jit(solution)/shard_map/ppermute | solution.py:716
  39.8 3.1 %shard_map.330 = (f32[2688,128]{1,0:T(8,128)S(1)}, f32[8,128]{1,0:T(8,128)S(1)}, bf16[4,128,128]{2,1,0:T(8,128)(2,1)S(1)}, bf16[4,128,128]{2,1,0:T(8,128)(2,1)S(1)}, f32[1,128]{1,0:T(1,128)S(1)}) custom-call(s32[1]{0:T(128)} %bitcast.refs_1_.refs_0_.refs_7_, f32[2688,128]{1,0:T(8,128)S(1)} %get-tuple-element.116.refs_2_.refs_1_.refs_0_, ...), custom_call_target="tpu_custom_call" | custom-call | flops 2300000000 | tf_op jit(solution)/shard_map/pallas_call | solution.py:115
  42.9 1.0 %collective-permute-done.6 = bf16[2,224,128]{2,1,0:T(8,128)(2,1)S(1)} collective-permute-done((bf16[2,224,128]{2,1,0:T(8,128)(2,1)S(1)}, bf16[2,224,128]{2,1,0:T(8,128)(2,1)S(1)}, u32[]{:S(2)}, u32[]{:S(2)}) %collective-permute-start.6) | collective-permute-done | bytes 114720 | tf_op jit(solution)/shard_map/ppermute | solution.py:716
  44.8 2.8 %shard_map.331 = (bf16[2688,256]{1,0:T(8,128)(2,1)S(1)}, bf16[384,256]{1,0:T(8,128)(2,1)S(1)}, f32[3,8,128]{2,1,0:T(8,128)S(1)}, bf16[4,96,128]{2,1,0:T(8,128)(2...) custom-call(s32[2,2]{1,0:T(2,128)S(1)} %copy-done.6, s32[1]{0:T(128)} %bitcast.refs_1_.refs_0_.refs_7_, ...), custom_call_target="tpu_custom_call" | custom-call | flops 1150000000 | tf_op jit(solution)/shard_map/pallas_call | solution.py:115
  48.3 1.7 %collective-permute-start.14 = (bf16[592,128]{1,0:T(8,128)(2,1)S(1)}, bf16[592,128]{1,0:T(8,128)(2,1)S(1)}, u32[]{:S(2)}, u32[]{:S(2)}) collective-permute-start(bf16[592,128]{1,0:T(8,128)(2,1)S(1)} %pad_maximum_fusion.6.refs_10_), channel_id=1, source_target_pairs={{0,8},{8,0},{16,24},{24,16},{1,9},{9,1},{17,25},{25,17},{2,10},{10... | collective-permute-start | bytes 454664 | tf_op jit(solution)/shard_map/ppermute | solution.py:716
  51.0 3.0 %shard_map.332 = (f32[2592,128]{1,0:T(8,128)}, f32[2,128]{1,0:T(2,128)S(1)}, f32[1,128]{1,0:T(1,128)S(1)}) custom-call(f32[2688,128]{1,0:T(8,128)S(1)} %get-tuple-element.116.refs_2_.refs_1_.refs_0_, bf16[2688,128]{1,0:T(8,128)(2,1)S(1)} %get-tuple-element.129.refs_1_, f32[2,2,128]{2,1,0:T(2,128)S(1)} %copy-done.3, ...), custom_call_target="tpu_custom_call" | custom-call | flops 57500000 | tf_op jit(solution)/shard_map/pallas_call | solution.py:115
  54.0 1.0 %collective-permute-done.8 = bf16[2,224,128]{2,1,0:T(8,128)(2,1)S(1)} collective-permute-done((bf16[2,224,128]{2,1,0:T(8,128)(2,1)S(1)}, bf16[2,224,128]{2,1,0:T(8,128)(2,1)S(1)}, u32[]{:S(2)}, u32[]{:S(2)}) %collective-permute-start.8) | collective-permute-done | bytes 114720 | tf_op jit(solution)/shard_map/ppermute | solution.py:716
  55.1 2.7 %collective-permute-start.15 = (bf16[592,128]{1,0:T(8,128)(2,1)S(1)}, bf16[592,128]{1,0:T(8,128)(2,1)S(1)}, u32[]{:S(2)}, u32[]{:S(2)}) collective-permute-start(bf16[592,128]{1,0:T(8,128)(2,1)S(1)} %add_convert_fusion.5), channel_id=1, source_target_pairs={{0,16},{8,24},{16,0},{24,8},{1,17},{9,25},{17,1},{25,9},{2,18},{10... | collective-permute-start | bytes 454664 | tf_op jit(solution)/shard_map/ppermute | solution.py:716
  57.7 1.3 %collective-permute-start.11 = (bf16[1,224,128]{2,1,0:T(8,128)(2,1)S(1)}, bf16[1,224,128]{2,1,0:T(8,128)(2,1)S(1)}, u32[]{:S(2)}, u32[]{:S(2)}) collective-permute-start(bf16[1,224,128]{2,1,0:T(8,128)(2,1)S(1)} %get-tuple-element.240), channel_id=1, source_target_pairs={{0,2},{1,3},{2,0},{3,1},{4,6},{5,7},{6,4},{7,5},{8,10},{9,11},{10,... | collective-permute-start | bytes 172040 | tf_op jit(solution)/shard_map/ppermute | solution.py:716
  59.0 1.4 %shard_map.333 = (bf16[2,18,5760]{2,1,0:T(8,128)(2,1)S(1)}, f32[1,128]{1,0:T(1,128)S(1)}) custom-call(bf16[864,1152]{1,0:T(8,128)(2,1)S(1)} %get-tuple-element.128.refs_0_, bf16[320,1152]{1,0:T(8,128)(2,1)S(1)} %bitcast.51, f32[1,320]{1,0:T(1,128)S(1)} %reshape.66.refs_2_, bf16[1,224,128]{2,1,0:T(8,128)(2,1)S(1)} %get-tuple-element.241.refs_3_), custom_call_target="tpu_custom_call" | custom-call | flops 2300000000 | tf_op jit(solution)/shard_map/pallas_call | solution.py:115
  60.4 1.5 %collective-permute-done.11 = bf16[1,224,128]{2,1,0:T(8,128)(2,1)S(1)} collective-permute-done((bf16[1,224,128]{2,1,0:T(8,128)(2,1)S(1)}, bf16[1,224,128]{2,1,0:T(8,128)(2,1)S(1)}, u32[]{:S(2)}, u32[]{:S(2)}) %collective-permute-start.11) | collective-permute-done | bytes 57376 | tf_op jit(solution)/shard_map/ppermute | solution.py:716
  62.0 1.3 %collective-permute-start.12 = (bf16[240,128]{1,0:T(8,128)(2,1)S(1)}, bf16[240,128]{1,0:T(8,128)(2,1)S(1)}, u32[]{:S(2)}, u32[]{:S(2)}) collective-permute-start(bf16[240,128]{1,0:T(8,128)(2,1)S(1)} %pad_maximum_fusion.10), channel_id=1, source_target_pairs={{0,8},{8,0},{16,24},{24,16},{1,9},{9,1},{17,25},{25,17},{2,10},{10... | collective-permute-start | bytes 184328 | tf_op jit(solution)/shard_map/ppermute | solution.py:716
  64.2 1.8 %collective-permute-start.16 = (bf16[1,464,128]{2,1,0:T(8,128)(2,1)S(1)}, bf16[1,464,128]{2,1,0:T(8,128)(2,1)S(1)}, u32[]{:S(2)}, u32[]{:S(2)}) collective-permute-start(bf16[1,464,128]{2,1,0:T(8,128)(2,1)S(1)} %slice_bitcast_fusion), channel_id=1, source_target_pairs={{0,2},{1,3},{2,0},{3,1},{4,6},{5,7},{6,4},{7,5},{8,10},{9,11},{10,... | collective-permute-start | bytes 356360 | tf_op jit(solution)/shard_map/ppermute | solution.py:716
  66.7 2.4 %collective-permute-done.16 = bf16[1,464,128]{2,1,0:T(8,128)(2,1)S(1)} collective-permute-done((bf16[1,464,128]{2,1,0:T(8,128)(2,1)S(1)}, bf16[1,464,128]{2,1,0:T(8,128)(2,1)S(1)}, u32[]{:S(2)}, u32[]{:S(2)}) %collective-permute-start.16) | collective-permute-done | bytes 118816 | tf_op jit(solution)/shard_map/ppermute | solution.py:716
  69.1 1.0 %collective-permute-start.18 = (bf16[2,464,128]{2,1,0:T(8,128)(2,1)S(1)}, bf16[2,464,128]{2,1,0:T(8,128)(2,1)S(1)}, u32[]{:S(2)}, u32[]{:S(2)}) collective-permute-start(bf16[2,464,128]{2,1,0:T(8,128)(2,1)S(1)} %pad_maximum_fusion.3), channel_id=1, source_target_pairs={{0,4},{1,5},{2,6},{3,7},{4,0},{5,1},{6,2},{7,3},{8,12},{9,13},{10,... | collective-permute-start | bytes 712712 | tf_op jit(solution)/shard_map/ppermute | solution.py:716
  70.1 1.4 %collective-permute-done.13 = bf16[240,128]{1,0:T(8,128)(2,1)S(1)} collective-permute-done((bf16[240,128]{1,0:T(8,128)(2,1)S(1)}, bf16[240,128]{1,0:T(8,128)(2,1)S(1)}, u32[]{:S(2)}, u32[]{:S(2)}) %collective-permute-start.13) | collective-permute-done | bytes 61472 | tf_op jit(solution)/shard_map/ppermute | solution.py:716
  71.5 1.3 %collective-permute-start.17 = (bf16[112,128]{1,0:T(8,128)(2,1)S(1)}, bf16[112,128]{1,0:T(8,128)(2,1)S(1)}, u32[]{:S(2)}, u32[]{:S(2)}) collective-permute-start(bf16[112,128]{1,0:T(8,128)(2,1)S(1)} %concatenate.71), channel_id=1, source_target_pairs={{0,2},{1,3},{2,0},{3,1},{4,6},{5,7},{6,4},{7,5},{8,10},{9,11},{10,... | collective-permute-start | bytes 86024 | tf_op jit(solution)/shard_map/ppermute | solution.py:716
  72.8 2.7 %collective-permute-done.18 = bf16[2,464,128]{2,1,0:T(8,128)(2,1)S(1)} collective-permute-done((bf16[2,464,128]{2,1,0:T(8,128)(2,1)S(1)}, bf16[2,464,128]{2,1,0:T(8,128)(2,1)S(1)}, u32[]{:S(2)}, u32[]{:S(2)}) %collective-permute-start.18) | collective-permute-done | bytes 237600 | tf_op jit(solution)/shard_map/ppermute | solution.py:716
  75.6 1.0 %collective-permute-start.19 = (bf16[208,128]{1,0:T(8,128)(2,1)S(1)}, bf16[208,128]{1,0:T(8,128)(2,1)S(1)}, u32[]{:S(2)}, u32[]{:S(2)}) collective-permute-start(bf16[208,128]{1,0:T(8,128)(2,1)S(1)} %pad_maximum_fusion.11), channel_id=1, source_target_pairs={{0,4},{1,5},{2,6},{3,7},{4,0},{5,1},{6,2},{7,3},{8,12},{9,13},{10,... | collective-permute-start | bytes 159752 | tf_op jit(solution)/shard_map/ppermute | solution.py:716
  76.6 1.1 %copy.38 = bf16[2,18,5760]{2,0,1:T(2,128)(2,1)} copy(bf16[2,18,5760]{2,1,0:T(8,128)(2,1)S(1)} %get-tuple-element.214) | data formatting | bytes 829440
  77.7 2.1 %collective-permute-done.19 = bf16[208,128]{1,0:T(8,128)(2,1)S(1)} collective-permute-done((bf16[208,128]{1,0:T(8,128)(2,1)S(1)}, bf16[208,128]{1,0:T(8,128)(2,1)S(1)}, u32[]{:S(2)}, u32[]{:S(2)}) %collective-permute-start.19) | collective-permute-done | bytes 53280 | tf_op jit(solution)/shard_map/ppermute | solution.py:716
  79.9 1.3 %collective-permute-done.20.refs_2_ = bf16[400,128]{1,0:T(8,128)(2,1)S(1)} collective-permute-done((bf16[400,128]{1,0:T(8,128)(2,1)S(1)}, bf16[400,128]{1,0:T(8,128)(2,1)S(1)}, u32[]{:S(2)}, u32[]{:S(2)}) %collective-permute-start.20) | collective-permute-done | bytes 102432 | tf_op jit(solution)/shard_map/ppermute | solution.py:716
  81.2 1.5 %shard_map.334 = (f32[2,3,128,128]{3,2,1,0:T(8,128)}, f32[2,2,128]{2,1,0:T(2,128)}, f32[2,32,128]{2,1,0:T(8,128)}, f32[2,32]{1,0:T(2,128)}, f32[2,32,384]{2,1,0:...) custom-call(s32[1]{0:T(128)} %bitcast.refs_1_.refs_0_.refs_7_, ...), custom_call_target="tpu_custom_call" | custom-call | flops 2300000000 | tf_op jit(solution)/shard_map/pallas_call | solution.py:115
  (111 shorter events, 9.2 us)
Async XLA Ops:
  1.6 6.1 %collective-permute-start = (bf16[1,272,128]{2,1,0:T(8,128)(2,1)S(1)}, bf16[1,272,128]{2,1,0:T(8,128)(2,1)S(1)}, u32[]{:S(2)}, u32[]{:S(2)}) collective-permute-start(bf16[1,272,128]{2,1,0:T(8,128)(2,1)S(1)} %bitcast.34), channel_id=1, source_target_pairs={{0,2},{1,3},{2,0},{3,1},{4,6},{5,7},{6,4},{7,5},{8,10},{9,11},{10,... | collective-permute-start | bytes 208904 | tf_op jit(solution)/shard_map/ppermute | solution.py:716
  4.7 4.6 %copy-start = (bf16[2,3,128,128]{3,2,1,0:T(8,128)(2,1)S(1)}, bf16[2,3,128,128]{3,2,1,0:T(8,128)(2,1)}, u32[]{:S(2)}) copy-start(bf16[2,3,128,128]{3,2,1,0:T(8,128)(2,1)} %refs_14_.5) | copy-start | bytes 589828
  4.7 4.6 %copy-start.1 = (bf16[2,128,128]{2,1,0:T(8,128)(2,1)S(1)}, bf16[2,128,128]{2,1,0:T(8,128)(2,1)}, u32[]{:S(2)}) copy-start(bf16[2,128,128]{2,1,0:T(8,128)(2,1)} %refs_18_.5) | copy-start | bytes 196612
  4.7 4.6 %copy-start.2 = (f32[2,128,32]{1,2,0:T(8,128)S(1)}, f32[2,128,32]{1,2,0:T(8,128)}, u32[]{:S(2)}) copy-start(f32[2,128,32]{1,2,0:T(8,128)} %param.24) | copy-start | bytes 98308
  4.7 4.6 %copy-start.3 = (f32[2,2,128]{2,1,0:T(2,128)S(1)}, f32[2,2,128]{2,1,0:T(2,128)}, u32[]{:S(2)}) copy-start(f32[2,2,128]{2,1,0:T(2,128)} %refs_2_.8) | copy-start | bytes 6148
  4.8 4.6 %copy-start.4 = (f32[2,2,128]{2,1,0:T(2,128)S(1)}, f32[2,2,128]{2,1,0:T(2,128)}, u32[]{:S(2)}) copy-start(f32[2,2,128]{2,1,0:T(2,128)} %refs_15_.3) | copy-start | bytes 6148
  4.8 4.6 %copy-start.5 = (f32[2,2,128]{2,1,0:T(2,128)S(1)}, f32[2,2,128]{2,1,0:T(2,128)}, u32[]{:S(2)}) copy-start(f32[2,2,128]{2,1,0:T(2,128)} %refs_21_.3) | copy-start | bytes 6148
  4.8 4.6 %copy-start.7 = (f32[2,32]{1,0:T(2,128)S(1)}, f32[2,32]{1,0:T(2,128)}, u32[]{:S(2)}) copy-start(f32[2,32]{1,0:T(2,128)} %refs_17_.5) | copy-start | bytes 772
  4.8 4.6 %copy-start.8 = (f32[2,128]{1,0:T(2,128)S(1)}, f32[2,128]{1,0:T(2,128)}, u32[]{:S(2)}) copy-start(f32[2,128]{1,0:T(2,128)} %refs_19_.5) | copy-start | bytes 3076
  4.8 4.6 %copy-start.10 = (bf16[2,36,36,128]{3,0,2,1:T(2,128)(2,1)S(1)}, bf16[2,36,36,128]{3,0,2,1:T(2,128)(2,1)}, u32[]{:S(2)}) copy-start(bf16[2,36,36,128]{3,0,2,1:T(2,128)(2,1)} %param.19) | copy-start | bytes 1990660
  7.7 6.0 %collective-permute-start.1 = (bf16[2,272,128]{2,1,0:T(8,128)(2,1)S(1)}, bf16[2,272,128]{2,1,0:T(8,128)(2,1)S(1)}, u32[]{:S(2)}, u32[]{:S(2)}) collective-permute-start(bf16[2,272,128]{2,1,0:T(8,128)(2,1)S(1)} %pad_maximum_fusion.7.refs_14_), channel_id=1, source_target_pairs={{0,4},{1,5},{2,6},{3,7},{4,0},{5,1},{6,2},{7,3},{8,12},{9,13},{10,... | collective-permute-start | bytes 417800 | tf_op jit(solution)/shard_map/ppermute | solution.py:716
  13.8 1.7 %collective-permute-start.2 = (bf16[4,272,128]{2,1,0:T(8,128)(2,1)S(1)}, bf16[4,272,128]{2,1,0:T(8,128)(2,1)S(1)}, u32[]{:S(2)}, u32[]{:S(2)}) collective-permute-start(bf16[4,272,128]{2,1,0:T(8,128)(2,1)S(1)} %pad_maximum_fusion.2.refs_0_), channel_id=1, source_target_pairs={{0,1},{1,0},{2,3},{3,2},{4,5},{5,4},{6,7},{7,6},{8,9},{9,8},{10,11... | collective-permute-start | bytes 835592 | tf_op jit(solution)/shard_map/ppermute | solution.py:716
  15.6 12.1 %copy-start.15 = (f32[320]{0:T(512)S(1)}, f32[320]{0:T(512)}, u32[]{:S(2)}) copy-start(f32[320]{0:T(512)} %param.37) | copy-start | bytes 3844
  27.2 3.5 %collective-permute-start.3 = (bf16[4,368,128]{2,1,0:T(8,128)(2,1)S(1)}, bf16[4,368,128]{2,1,0:T(8,128)(2,1)S(1)}, u32[]{:S(2)}, u32[]{:S(2)}) collective-permute-start(bf16[4,368,128]{2,1,0:T(8,128)(2,1)S(1)} %get-tuple-element.149), channel_id=1, source_target_pairs={{0,1},{1,0},{2,3},{3,2},{4,5},{5,4},{6,7},{7,6},{8,9},{9,8},{10,11... | collective-permute-start | bytes 1130504 | tf_op jit(solution)/shard_map/ppermute | solution.py:716
  30.8 6.7 %collective-permute-start.4 = (bf16[2,368,128]{2,1,0:T(8,128)(2,1)S(1)}, bf16[2,368,128]{2,1,0:T(8,128)(2,1)S(1)}, u32[]{:S(2)}, u32[]{:S(2)}) collective-permute-start(bf16[2,368,128]{2,1,0:T(8,128)(2,1)S(1)} %get-tuple-element.232), channel_id=1, source_target_pairs={{0,4},{1,5},{2,6},{3,7},{4,0},{5,1},{6,2},{7,3},{8,12},{9,13},{10,... | collective-permute-start | bytes 565256 | tf_op jit(solution)/shard_map/ppermute | solution.py:716
  34.8 4.2 %collective-permute-start.5 = (bf16[4,224,128]{2,1,0:T(8,128)(2,1)S(1)}, bf16[4,224,128]{2,1,0:T(8,128)(2,1)S(1)}, u32[]{:S(2)}, u32[]{:S(2)}) collective-permute-start(bf16[4,224,128]{2,1,0:T(8,128)(2,1)S(1)} %pad_maximum_fusion.4), channel_id=1, source_target_pairs={{0,1},{1,0},{2,3},{3,2},{4,5},{5,4},{6,7},{7,6},{8,9},{9,8},{10,11... | collective-permute-start | bytes 688136 | tf_op jit(solution)/shard_map/ppermute | solution.py:716
  37.6 10.1 %collective-permute-start.10 = (bf16[1,368,128]{2,1,0:T(8,128)(2,1)S(1)}, bf16[1,368,128]{2,1,0:T(8,128)(2,1)S(1)}, u32[]{:S(2)}, u32[]{:S(2)}) collective-permute-start(bf16[1,368,128]{2,1,0:T(8,128)(2,1)S(1)} %get-tuple-element.238), channel_id=1, source_target_pairs={{0,2},{1,3},{2,0},{3,1},{4,6},{5,7},{6,4},{7,5},{8,10},{9,11},{10,... | collective-permute-start | bytes 282632 | tf_op jit(solution)/shard_map/ppermute | solution.py:716
  39.1 4.9 %collective-permute-start.6 = (bf16[2,224,128]{2,1,0:T(8,128)(2,1)S(1)}, bf16[2,224,128]{2,1,0:T(8,128)(2,1)S(1)}, u32[]{:S(2)}, u32[]{:S(2)}) collective-permute-start(bf16[2,224,128]{2,1,0:T(8,128)(2,1)S(1)} %get-tuple-element.236), channel_id=1, source_target_pairs={{0,4},{1,5},{2,6},{3,7},{4,0},{5,1},{6,2},{7,3},{8,12},{9,13},{10,... | collective-permute-start | bytes 344072 | tf_op jit(solution)/shard_map/ppermute | solution.py:716
  44.0 4.2 %collective-permute-start.9 = (bf16[1,224,128]{2,1,0:T(8,128)(2,1)S(1)}, bf16[1,224,128]{2,1,0:T(8,128)(2,1)S(1)}, u32[]{:S(2)}, u32[]{:S(2)}) collective-permute-start(bf16[1,224,128]{2,1,0:T(8,128)(2,1)S(1)} %get-tuple-element.242), channel_id=1, source_target_pairs={{0,2},{1,3},{2,0},{3,1},{4,6},{5,7},{6,4},{7,5},{8,10},{9,11},{10,... | collective-permute-start | bytes 172040 | tf_op jit(solution)/shard_map/ppermute | solution.py:716
  47.7 2.3 %collective-permute-start.7 = (bf16[4,224,128]{2,1,0:T(8,128)(2,1)S(1)}, bf16[4,224,128]{2,1,0:T(8,128)(2,1)S(1)}, u32[]{:S(2)}, u32[]{:S(2)}) collective-permute-start(bf16[4,224,128]{2,1,0:T(8,128)(2,1)S(1)} %pad_maximum_fusion.5), channel_id=1, source_target_pairs={{0,1},{1,0},{2,3},{3,2},{4,5},{5,4},{6,7},{7,6},{8,9},{9,8},{10,11... | collective-permute-start | bytes 688136 | tf_op jit(solution)/shard_map/ppermute | solution.py:716
  48.3 6.7 %collective-permute-start.14 = (bf16[592,128]{1,0:T(8,128)(2,1)S(1)}, bf16[592,128]{1,0:T(8,128)(2,1)S(1)}, u32[]{:S(2)}, u32[]{:S(2)}) collective-permute-start(bf16[592,128]{1,0:T(8,128)(2,1)S(1)} %pad_maximum_fusion.6.refs_10_), channel_id=1, source_target_pairs={{0,8},{8,0},{16,24},{24,16},{1,9},{9,1},{17,25},{25,17},{2,10},{10... | collective-permute-start | bytes 454664 | tf_op jit(solution)/shard_map/ppermute | solution.py:716
  50.0 4.9 %collective-permute-start.8 = (bf16[2,224,128]{2,1,0:T(8,128)(2,1)S(1)}, bf16[2,224,128]{2,1,0:T(8,128)(2,1)S(1)}, u32[]{:S(2)}, u32[]{:S(2)}) collective-permute-start(bf16[2,224,128]{2,1,0:T(8,128)(2,1)S(1)} %get-tuple-element.235), channel_id=1, source_target_pairs={{0,4},{1,5},{2,6},{3,7},{4,0},{5,1},{6,2},{7,3},{8,12},{9,13},{10,... | collective-permute-start | bytes 344072 | tf_op jit(solution)/shard_map/ppermute | solution.py:716
  55.1 9.1 %collective-permute-start.15 = (bf16[592,128]{1,0:T(8,128)(2,1)S(1)}, bf16[592,128]{1,0:T(8,128)(2,1)S(1)}, u32[]{:S(2)}, u32[]{:S(2)}) collective-permute-start(bf16[592,128]{1,0:T(8,128)(2,1)S(1)} %add_convert_fusion.5), channel_id=1, source_target_pairs={{0,16},{8,24},{16,0},{24,8},{1,17},{9,25},{17,1},{25,9},{2,18},{10... | collective-permute-start | bytes 454664 | tf_op jit(solution)/shard_map/ppermute | solution.py:716
  57.7 4.2 %collective-permute-start.11 = (bf16[1,224,128]{2,1,0:T(8,128)(2,1)S(1)}, bf16[1,224,128]{2,1,0:T(8,128)(2,1)S(1)}, u32[]{:S(2)}, u32[]{:S(2)}) collective-permute-start(bf16[1,224,128]{2,1,0:T(8,128)(2,1)S(1)} %get-tuple-element.240), channel_id=1, source_target_pairs={{0,2},{1,3},{2,0},{3,1},{4,6},{5,7},{6,4},{7,5},{8,10},{9,11},{10,... | collective-permute-start | bytes 172040 | tf_op jit(solution)/shard_map/ppermute | solution.py:716
  62.0 4.3 %collective-permute-start.12 = (bf16[240,128]{1,0:T(8,128)(2,1)S(1)}, bf16[240,128]{1,0:T(8,128)(2,1)S(1)}, u32[]{:S(2)}, u32[]{:S(2)}) collective-permute-start(bf16[240,128]{1,0:T(8,128)(2,1)S(1)} %pad_maximum_fusion.10), channel_id=1, source_target_pairs={{0,8},{8,0},{16,24},{24,16},{1,9},{9,1},{17,25},{25,17},{2,10},{10... | collective-permute-start | bytes 184328 | tf_op jit(solution)/shard_map/ppermute | solution.py:716
  64.2 4.9 %collective-permute-start.16 = (bf16[1,464,128]{2,1,0:T(8,128)(2,1)S(1)}, bf16[1,464,128]{2,1,0:T(8,128)(2,1)S(1)}, u32[]{:S(2)}, u32[]{:S(2)}) collective-permute-start(bf16[1,464,128]{2,1,0:T(8,128)(2,1)S(1)} %slice_bitcast_fusion), channel_id=1, source_target_pairs={{0,2},{1,3},{2,0},{3,1},{4,6},{5,7},{6,4},{7,5},{8,10},{9,11},{10,... | collective-permute-start | bytes 356360 | tf_op jit(solution)/shard_map/ppermute | solution.py:716
  66.3 5.2 %collective-permute-start.13 = (bf16[240,128]{1,0:T(8,128)(2,1)S(1)}, bf16[240,128]{1,0:T(8,128)(2,1)S(1)}, u32[]{:S(2)}, u32[]{:S(2)}) collective-permute-start(bf16[240,128]{1,0:T(8,128)(2,1)S(1)} %add_convert_fusion.10), channel_id=1, source_target_pairs={{0,16},{8,24},{16,0},{24,8},{1,17},{9,25},{17,1},{25,9},{2,18},{10... | collective-permute-start | bytes 184328 | tf_op jit(solution)/shard_map/ppermute | solution.py:716
  69.1 6.4 %collective-permute-start.18 = (bf16[2,464,128]{2,1,0:T(8,128)(2,1)S(1)}, bf16[2,464,128]{2,1,0:T(8,128)(2,1)S(1)}, u32[]{:S(2)}, u32[]{:S(2)}) collective-permute-start(bf16[2,464,128]{2,1,0:T(8,128)(2,1)S(1)} %pad_maximum_fusion.3), channel_id=1, source_target_pairs={{0,4},{1,5},{2,6},{3,7},{4,0},{5,1},{6,2},{7,3},{8,12},{9,13},{10,... | collective-permute-start | bytes 712712 | tf_op jit(solution)/shard_map/ppermute | solution.py:716
  71.5 4.1 %collective-permute-start.17 = (bf16[112,128]{1,0:T(8,128)(2,1)S(1)}, bf16[112,128]{1,0:T(8,128)(2,1)S(1)}, u32[]{:S(2)}, u32[]{:S(2)}) collective-permute-start(bf16[112,128]{1,0:T(8,128)(2,1)S(1)} %concatenate.71), channel_id=1, source_target_pairs={{0,2},{1,3},{2,0},{3,1},{4,6},{5,7},{6,4},{7,5},{8,10},{9,11},{10,... | collective-permute-start | bytes 86024 | tf_op jit(solution)/shard_map/ppermute | solution.py:716
  75.6 4.2 %collective-permute-start.19 = (bf16[208,128]{1,0:T(8,128)(2,1)S(1)}, bf16[208,128]{1,0:T(8,128)(2,1)S(1)}, u32[]{:S(2)}, u32[]{:S(2)}) collective-permute-start(bf16[208,128]{1,0:T(8,128)(2,1)S(1)} %pad_maximum_fusion.11), channel_id=1, source_target_pairs={{0,4},{1,5},{2,6},{3,7},{4,0},{5,1},{6,2},{7,3},{8,12},{9,13},{10,... | collective-permute-start | bytes 159752 | tf_op jit(solution)/shard_map/ppermute | solution.py:716
  76.6 4.6 %collective-permute-start.21 = (bf16[4,464,128]{2,1,0:T(8,128)(2,1)S(1)}, bf16[4,464,128]{2,1,0:T(8,128)(2,1)S(1)}, u32[]{:S(2)}, u32[]{:S(2)}) collective-permute-start(bf16[4,464,128]{2,1,0:T(8,128)(2,1)S(1)} %pad_maximum_fusion.1.refs_3_), channel_id=1, source_target_pairs={{0,1},{1,0},{2,3},{3,2},{4,5},{5,4},{6,7},{7,6},{8,9},{9,8},{10,11... | collective-permute-start | bytes 1425416 | tf_op jit(solution)/shard_map/ppermute | solution.py:716
  79.9 1.4 %collective-permute-start.20 = (bf16[400,128]{1,0:T(8,128)(2,1)S(1)}, bf16[400,128]{1,0:T(8,128)(2,1)S(1)}, u32[]{:S(2)}, u32[]{:S(2)}) collective-permute-start(bf16[400,128]{1,0:T(8,128)(2,1)S(1)} %pad_maximum_fusion.8.refs_1_), channel_id=1, source_target_pairs={{0,1},{1,0},{2,3},{3,2},{4,5},{5,4},{6,7},{7,6},{8,9},{9,8},{10,11... | collective-permute-start | bytes 307208 | tf_op jit(solution)/shard_map/ppermute | solution.py:716
  (6 other events, 25.6 us)

commit v8 on v7

--- a/solution.py
+++ b/solution.py
@@ -74,9 +74,9 @@
         self.parts, self.units = parts, hidden // parts
         self.W = side * images
         self.N0 = side * self.W
-        self.N = -(-self.N0 // 384) * 384
+        self.N = -(-self.N0 // 432) * 432
         self.run_first = self.run_back = self.run_mix = self.N
-        self.run_second = self.N // 7
+        self.run_second = self.N // 6
         self.half = side // 2
         self.hp = -(-self.half // 8) * 8
         self.M = self.half * self.hp
@@ -193,9 +193,10 @@
         return carry
 
     lax.fori_loop(0, z.side // 2, step2, 0)
-    pad = jnp.zeros((z.N - z.N0, z.C), F32)
-    for ref in (r.mask, r.edge, r.back):
-        ref[z.N0 :, :] = pad.astype(ref.dtype)
+    if z.N > z.N0:
+        pad = jnp.zeros((z.N - z.N0, z.C), F32)
+        for ref in (r.mask, r.edge, r.back):
+            ref[z.N0 :, :] = pad.astype(ref.dtype)
     pad = jnp.zeros((z.hp - z.half, z.O), F32)
     r.pgrad[z.M :, :] = jnp.zeros((8, 9 * z.C), F32)
     sums = jnp.zeros((8, z.O), F32)
@@ -624,8 +625,9 @@
             r.state_grad[rows, :] = grad
 
     over(z, body, size)
-    stray = r.back_h[z.base + z.N0 - z.W : z.base + z.N0, :]
-    r.vec[1] -= rows8(jnp.where(kinds(z, z.W) == 1, stray, 0.0))
+    if z.N > z.N0:
+        stray = r.back_h[z.base + z.N0 - z.W : z.base + z.N0, :]
+        r.vec[1] -= rows8(jnp.where(kinds(z, z.W) == 1, stray, 0.0))
     r.first_norm[...] = jnp.concatenate([total(r.vec[0]), total(r.vec[1])], axis=0)
     r.token[...] = jnp.zeros_like(r.token)
 

time: 83 us -> 82.6 us (level)
  no operation moved by 1% of the time
where the time goes in v8:
time: 82.6 us; the launch traced here: 82.4 us
  Pallas kernels  40.4 us (49%)
  starting transfers between devices  22.4 us (27%)
  waiting for transfers between devices  15.9 us (19%)
  local copies, waits for them, and re-layouts  1.38 us (2%)
  between operations  1.34 us (2%)
  other arithmetic  1 us (1%)
    pallas_call x13, Pallas kernels, call(): pl.pallas_call(kernel, out_shape=list(outs.values()), in_specs=[place(nam...  40.4 us
    ppermute x22, starting transfers between devices, swap(): return lax.ppermute(x, axis, [(a, a ^ bit) for a in range(n)])  22.4 us
    ppermute x22, waiting for transfers between devices, swap(): return lax.ppermute(x, axis, [(a, a ^ bit) for a in range(n)])  15.9 us
  transfers between devices with their start and end apart: 22, of which 12 were waited for; matrix products, arithmetic and copies ran while one was open for 2% of the time, Pallas kernels for 32%

profile of v8, /device:TPU:0, one launch (start us, length us, event | category | flops | bytes accessed | tf_op | source)
XLA Modules:
  0.0 82.4 jit_solution(17847825588552024869)
XLA Ops:
  1.6 3.0 %collective-permute-start = (bf16[1,272,128]{2,1,0:T(8,128)(2,1)S(1)}, bf16[1,272,128]{2,1,0:T(8,128)(2,1)S(1)}, u32[]{:S(2)}, u32[]{:S(2)}) collective-permute-start(bf16[1,272,128]{2,1,0:T(8,128)(2,1)S(1)} %bitcast.34), channel_id=1, source_target_pairs={{0,2},{1,3},{2,0},{3,1},{4,6},{5,7},{6,4},{7,5},{8,10},{9,11},{10,... | collective-permute-start | bytes 208904 | tf_op jit(solution)/shard_map/ppermute | solution.py:718
  4.8 2.8 %shard_map.322 = (f32[2592,128]{1,0:T(8,128)S(1)}, bf16[2592,128]{1,0:T(8,128)(2,1)S(1)}, bf16[2592,128]{1,0:T(8,128)(2,1)S(1)}, bf16[864,320]{1,0:T(8,128)(2,1)...) custom-call(s32[2,2]{1,0:T(2,128)S(1)} %copy-done.6, s32[1]{0:T(128)} %bitcast.refs_1_.refs_0_.refs_7_, ...), custom_call_target="tpu_custom_call" | custom-call | flops 3449999872 | tf_op jit(solution)/shard_map/pallas_call | solution.py:115
  7.7 1.6 %collective-permute-start.1 = (bf16[2,272,128]{2,1,0:T(8,128)(2,1)S(1)}, bf16[2,272,128]{2,1,0:T(8,128)(2,1)S(1)}, u32[]{:S(2)}, u32[]{:S(2)}) collective-permute-start(bf16[2,272,128]{2,1,0:T(8,128)(2,1)S(1)} %pad_maximum_fusion.7.refs_14_), channel_id=1, source_target_pairs={{0,4},{1,5},{2,6},{3,7},{4,0},{5,1},{6,2},{7,3},{8,12},{9,13},{10,... | collective-permute-start | bytes 417800 | tf_op jit(solution)/shard_map/ppermute | solution.py:718
  9.4 4.3 %shard_map.324 = (f32[2592,128]{1,0:T(8,128)S(1)}, bf16[384,384]{1,0:T(8,128)(2,1)S(1)}, f32[2,32,384]{2,1,0:T(8,128)S(1)}, f32[2,384]{1,0:T(2,128)S(1)}, bf16[2...) custom-call(bf16[2592,128]{1,0:T(8,128)(2,1)S(1)} %bitcast.52, ...), custom_call_target="tpu_custom_call" | custom-call | flops 5750000128 | tf_op jit(solution)/shard_map/pallas_call | solution.py:115
  13.8 1.5 %shard_map.325 = (f32[2592,128]{1,0:T(8,128)S(1)}, bf16[2592,256]{1,0:T(8,128)(2,1)S(1)}, bf16[2592,256]{1,0:T(8,128)(2,1)S(1)}, f32[1,128]{1,0:T(1,128)S(1)}) custom-call(bf16[4,272,128]{2,1,0:T(8,128)(2,1)S(1)} %pad_maximum_fusion.2.refs_0_, bf16[2592,128]{1,0:T(8,128)(2,1)S(1)} %get-tuple-element.120.refs_1_.refs_4_.refs_8_, f32[2,128]{1,0:T(2,128)S(1)} %copy-done.13), custom_call_target="tpu_custom_call" | custom-call | flops 2300000000 | tf_op jit(solution)/shard_map/pallas_call | solution.py:115
  15.5 11.3 %shard_map.326 = (bf16[864,1152]{1,0:T(8,128)(2,1)S(1)}, bf16[4,368,128]{2,1,0:T(8,128)(2,1)S(1)}, bf16[4,368,128]{2,1,0:T(8,128)(2,1)S(1)}, bf16[2,512,128]{2,1...) custom-call(s32[2,2]{1,0:T(2,128)S(1)} %copy-done.6, ...), custom_call_target="tpu_custom_call" | custom-call | flops 18400000000 | tf_op jit(solution)/shard_map/pallas_call | solution.py:115
  27.4 2.8 %shard_map.327 = (f32[2592,128]{1,0:T(8,128)S(1)}, f32[8,128]{1,0:T(8,128)S(1)}, bf16[4,128,128]{2,1,0:T(8,128)(2,1)S(1)}, bf16[4,128,128]{2,1,0:T(8,128)(2,1)S(1)}, f32[1,128]{1,0:T(1,128)S(1)}) custom-call(s32[1]{0:T(128)} %bitcast.refs_1_.refs_0_.refs_7_, f32[2592,128]{1,0:T(8,128)S(1)} %get-tuple-element.116.refs_2_.refs_1_.refs_0_, ...), custom_call_target="tpu_custom_call" | custom-call | flops 2300000000 | tf_op jit(solution)/shard_map/pallas_call | solution.py:115
  31.2 3.2 %shard_map.328 = (bf16[2592,256]{1,0:T(8,128)(2,1)S(1)}, bf16[384,256]{1,0:T(8,128)(2,1)S(1)}, f32[3,8,128]{2,1,0:T(8,128)S(1)}, bf16[4,96,128]{2,1,0:T(8,128)(2...) custom-call(s32[2,2]{1,0:T(2,128)S(1)} %copy-done.6, s32[1]{0:T(128)} %bitcast.refs_1_.refs_0_.refs_7_, ...), custom_call_target="tpu_custom_call" | custom-call | flops 1150000000 | tf_op jit(solution)/shard_map/pallas_call | solution.py:115
  34.5 1.7 %shard_map.329 = (f32[2592,128]{1,0:T(8,128)S(1)}, f32[2,128]{1,0:T(2,128)S(1)}, f32[1,128]{1,0:T(1,128)S(1)}) custom-call(f32[2592,128]{1,0:T(8,128)S(1)} %get-tuple-element.116.refs_2_.refs_1_.refs_0_, bf16[2592,128]{1,0:T(8,128)(2,1)S(1)} %get-tuple-element.129.refs_1_, f32[2,2,128]{2,1,0:T(2,128)S(1)} %copy-done.3, ...), custom_call_target="tpu_custom_call" | custom-call | flops 57500000 | tf_op jit(solution)/shard_map/pallas_call | solution.py:115
  37.2 1.3 %collective-permute-start.10 = (bf16[1,368,128]{2,1,0:T(8,128)(2,1)S(1)}, bf16[1,368,128]{2,1,0:T(8,128)(2,1)S(1)}, u32[]{:S(2)}, u32[]{:S(2)}) collective-permute-start(bf16[1,368,128]{2,1,0:T(8,128)(2,1)S(1)} %get-tuple-element.238), channel_id=1, source_target_pairs={{0,2},{1,3},{2,0},{3,1},{4,6},{5,7},{6,4},{7,5},{8,10},{9,11},{10,... | collective-permute-start | bytes 282632 | tf_op jit(solution)/shard_map/ppermute | solution.py:718
  39.4 3.1 %shard_map.330 = (f32[2592,128]{1,0:T(8,128)S(1)}, f32[8,128]{1,0:T(8,128)S(1)}, bf16[4,128,128]{2,1,0:T(8,128)(2,1)S(1)}, bf16[4,128,128]{2,1,0:T(8,128)(2,1)S(1)}, f32[1,128]{1,0:T(1,128)S(1)}) custom-call(s32[1]{0:T(128)} %bitcast.refs_1_.refs_0_.refs_7_, f32[2592,128]{1,0:T(8,128)S(1)} %get-tuple-element.116.refs_2_.refs_1_.refs_0_, ...), custom_call_target="tpu_custom_call" | custom-call | flops 2300000000 | tf_op jit(solution)/shard_map/pallas_call | solution.py:115
  42.5 1.1 %collective-permute-done.6 = bf16[2,224,128]{2,1,0:T(8,128)(2,1)S(1)} collective-permute-done((bf16[2,224,128]{2,1,0:T(8,128)(2,1)S(1)}, bf16[2,224,128]{2,1,0:T(8,128)(2,1)S(1)}, u32[]{:S(2)}, u32[]{:S(2)}) %collective-permute-start.6) | collective-permute-done | bytes 114720 | tf_op jit(solution)/shard_map/ppermute | solution.py:718
  44.5 2.9 %shard_map.331 = (bf16[2592,256]{1,0:T(8,128)(2,1)S(1)}, bf16[384,256]{1,0:T(8,128)(2,1)S(1)}, f32[3,8,128]{2,1,0:T(8,128)S(1)}, bf16[4,96,128]{2,1,0:T(8,128)(2...) custom-call(s32[2,2]{1,0:T(2,128)S(1)} %copy-done.6, s32[1]{0:T(128)} %bitcast.refs_1_.refs_0_.refs_7_, ...), custom_call_target="tpu_custom_call" | custom-call | flops 1150000000 | tf_op jit(solution)/shard_map/pallas_call | solution.py:115
  47.9 1.6 %collective-permute-start.14 = (bf16[592,128]{1,0:T(8,128)(2,1)S(1)}, bf16[592,128]{1,0:T(8,128)(2,1)S(1)}, u32[]{:S(2)}, u32[]{:S(2)}) collective-permute-start(bf16[592,128]{1,0:T(8,128)(2,1)S(1)} %pad_maximum_fusion.6.refs_10_), channel_id=1, source_target_pairs={{0,8},{8,0},{16,24},{24,16},{1,9},{9,1},{17,25},{25,17},{2,10},{10... | collective-permute-start | bytes 454664 | tf_op jit(solution)/shard_map/ppermute | solution.py:718
  50.7 2.9 %shard_map.332 = (f32[2592,128]{1,0:T(8,128)}, f32[2,128]{1,0:T(2,128)S(1)}, f32[1,128]{1,0:T(1,128)S(1)}) custom-call(f32[2592,128]{1,0:T(8,128)S(1)} %get-tuple-element.116.refs_2_.refs_1_.refs_0_, bf16[2592,128]{1,0:T(8,128)(2,1)S(1)} %get-tuple-element.129.refs_1_, f32[2,2,128]{2,1,0:T(2,128)S(1)} %copy-done.3, ...), custom_call_target="tpu_custom_call" | custom-call | flops 57500000 | tf_op jit(solution)/shard_map/pallas_call | solution.py:115
  53.6 1.0 %collective-permute-done.8 = bf16[2,224,128]{2,1,0:T(8,128)(2,1)S(1)} collective-permute-done((bf16[2,224,128]{2,1,0:T(8,128)(2,1)S(1)}, bf16[2,224,128]{2,1,0:T(8,128)(2,1)S(1)}, u32[]{:S(2)}, u32[]{:S(2)}) %collective-permute-start.8) | collective-permute-done | bytes 114720 | tf_op jit(solution)/shard_map/ppermute | solution.py:718
  54.7 2.7 %collective-permute-start.15 = (bf16[592,128]{1,0:T(8,128)(2,1)S(1)}, bf16[592,128]{1,0:T(8,128)(2,1)S(1)}, u32[]{:S(2)}, u32[]{:S(2)}) collective-permute-start(bf16[592,128]{1,0:T(8,128)(2,1)S(1)} %add_convert_fusion.5), channel_id=1, source_target_pairs={{0,16},{8,24},{16,0},{24,8},{1,17},{9,25},{17,1},{25,9},{2,18},{10... | collective-permute-start | bytes 454664 | tf_op jit(solution)/shard_map/ppermute | solution.py:718
  57.4 1.3 %collective-permute-start.11 = (bf16[1,224,128]{2,1,0:T(8,128)(2,1)S(1)}, bf16[1,224,128]{2,1,0:T(8,128)(2,1)S(1)}, u32[]{:S(2)}, u32[]{:S(2)}) collective-permute-start(bf16[1,224,128]{2,1,0:T(8,128)(2,1)S(1)} %get-tuple-element.240), channel_id=1, source_target_pairs={{0,2},{1,3},{2,0},{3,1},{4,6},{5,7},{6,4},{7,5},{8,10},{9,11},{10,... | collective-permute-start | bytes 172040 | tf_op jit(solution)/shard_map/ppermute | solution.py:718
  58.7 1.4 %shard_map.333 = (bf16[2,18,5760]{2,1,0:T(8,128)(2,1)S(1)}, f32[1,128]{1,0:T(1,128)S(1)}) custom-call(bf16[864,1152]{1,0:T(8,128)(2,1)S(1)} %get-tuple-element.128.refs_0_, bf16[320,1152]{1,0:T(8,128)(2,1)S(1)} %bitcast.51, f32[1,320]{1,0:T(1,128)S(1)} %reshape.66.refs_2_, bf16[1,224,128]{2,1,0:T(8,128)(2,1)S(1)} %get-tuple-element.241.refs_3_), custom_call_target="tpu_custom_call" | custom-call | flops 2300000000 | tf_op jit(solution)/shard_map/pallas_call | solution.py:115
  60.1 1.5 %collective-permute-done.11 = bf16[1,224,128]{2,1,0:T(8,128)(2,1)S(1)} collective-permute-done((bf16[1,224,128]{2,1,0:T(8,128)(2,1)S(1)}, bf16[1,224,128]{2,1,0:T(8,128)(2,1)S(1)}, u32[]{:S(2)}, u32[]{:S(2)}) %collective-permute-start.11) | collective-permute-done | bytes 57376 | tf_op jit(solution)/shard_map/ppermute | solution.py:718
  61.6 1.3 %collective-permute-start.12 = (bf16[240,128]{1,0:T(8,128)(2,1)S(1)}, bf16[240,128]{1,0:T(8,128)(2,1)S(1)}, u32[]{:S(2)}, u32[]{:S(2)}) collective-permute-start(bf16[240,128]{1,0:T(8,128)(2,1)S(1)} %pad_maximum_fusion.10), channel_id=1, source_target_pairs={{0,8},{8,0},{16,24},{24,16},{1,9},{9,1},{17,25},{25,17},{2,10},{10... | collective-permute-start | bytes 184328 | tf_op jit(solution)/shard_map/ppermute | solution.py:718
  63.9 1.8 %collective-permute-start.16 = (bf16[1,464,128]{2,1,0:T(8,128)(2,1)S(1)}, bf16[1,464,128]{2,1,0:T(8,128)(2,1)S(1)}, u32[]{:S(2)}, u32[]{:S(2)}) collective-permute-start(bf16[1,464,128]{2,1,0:T(8,128)(2,1)S(1)} %slice_bitcast_fusion), channel_id=1, source_target_pairs={{0,2},{1,3},{2,0},{3,1},{4,6},{5,7},{6,4},{7,5},{8,10},{9,11},{10,... | collective-permute-start | bytes 356360 | tf_op jit(solution)/shard_map/ppermute | solution.py:718
  66.3 2.5 %collective-permute-done.16 = bf16[1,464,128]{2,1,0:T(8,128)(2,1)S(1)} collective-permute-done((bf16[1,464,128]{2,1,0:T(8,128)(2,1)S(1)}, bf16[1,464,128]{2,1,0:T(8,128)(2,1)S(1)}, u32[]{:S(2)}, u32[]{:S(2)}) %collective-permute-start.16) | collective-permute-done | bytes 118816 | tf_op jit(solution)/shard_map/ppermute | solution.py:718
  68.8 1.0 %collective-permute-start.18 = (bf16[2,464,128]{2,1,0:T(8,128)(2,1)S(1)}, bf16[2,464,128]{2,1,0:T(8,128)(2,1)S(1)}, u32[]{:S(2)}, u32[]{:S(2)}) collective-permute-start(bf16[2,464,128]{2,1,0:T(8,128)(2,1)S(1)} %pad_maximum_fusion.3), channel_id=1, source_target_pairs={{0,4},{1,5},{2,6},{3,7},{4,0},{5,1},{6,2},{7,3},{8,12},{9,13},{10,... | collective-permute-start | bytes 712712 | tf_op jit(solution)/shard_map/ppermute | solution.py:718
  69.8 1.3 %collective-permute-done.13 = bf16[240,128]{1,0:T(8,128)(2,1)S(1)} collective-permute-done((bf16[240,128]{1,0:T(8,128)(2,1)S(1)}, bf16[240,128]{1,0:T(8,128)(2,1)S(1)}, u32[]{:S(2)}, u32[]{:S(2)}) %collective-permute-start.13) | collective-permute-done | bytes 61472 | tf_op jit(solution)/shard_map/ppermute | solution.py:718
  71.1 1.3 %collective-permute-start.17 = (bf16[112,128]{1,0:T(8,128)(2,1)S(1)}, bf16[112,128]{1,0:T(8,128)(2,1)S(1)}, u32[]{:S(2)}, u32[]{:S(2)}) collective-permute-start(bf16[112,128]{1,0:T(8,128)(2,1)S(1)} %concatenate.71), channel_id=1, source_target_pairs={{0,2},{1,3},{2,0},{3,1},{4,6},{5,7},{6,4},{7,5},{8,10},{9,11},{10,... | collective-permute-start | bytes 86024 | tf_op jit(solution)/shard_map/ppermute | solution.py:718
  72.5 2.7 %collective-permute-done.18 = bf16[2,464,128]{2,1,0:T(8,128)(2,1)S(1)} collective-permute-done((bf16[2,464,128]{2,1,0:T(8,128)(2,1)S(1)}, bf16[2,464,128]{2,1,0:T(8,128)(2,1)S(1)}, u32[]{:S(2)}, u32[]{:S(2)}) %collective-permute-start.18) | collective-permute-done | bytes 237600 | tf_op jit(solution)/shard_map/ppermute | solution.py:718
  75.3 1.0 %collective-permute-start.19 = (bf16[208,128]{1,0:T(8,128)(2,1)S(1)}, bf16[208,128]{1,0:T(8,128)(2,1)S(1)}, u32[]{:S(2)}, u32[]{:S(2)}) collective-permute-start(bf16[208,128]{1,0:T(8,128)(2,1)S(1)} %pad_maximum_fusion.11), channel_id=1, source_target_pairs={{0,4},{1,5},{2,6},{3,7},{4,0},{5,1},{6,2},{7,3},{8,12},{9,13},{10,... | collective-permute-start | bytes 159752 | tf_op jit(solution)/shard_map/ppermute | solution.py:718
  76.3 1.1 %copy.38 = bf16[2,18,5760]{2,0,1:T(2,128)(2,1)} copy(bf16[2,18,5760]{2,1,0:T(8,128)(2,1)S(1)} %get-tuple-element.214) | data formatting | bytes 829440
  77.3 2.1 %collective-permute-done.19 = bf16[208,128]{1,0:T(8,128)(2,1)S(1)} collective-permute-done((bf16[208,128]{1,0:T(8,128)(2,1)S(1)}, bf16[208,128]{1,0:T(8,128)(2,1)S(1)}, u32[]{:S(2)}, u32[]{:S(2)}) %collective-permute-start.19) | collective-permute-done | bytes 53280 | tf_op jit(solution)/shard_map/ppermute | solution.py:718
  79.6 1.3 %collective-permute-done.20.refs_2_ = bf16[400,128]{1,0:T(8,128)(2,1)S(1)} collective-permute-done((bf16[400,128]{1,0:T(8,128)(2,1)S(1)}, bf16[400,128]{1,0:T(8,128)(2,1)S(1)}, u32[]{:S(2)}, u32[]{:S(2)}) %collective-permute-start.20) | collective-permute-done | bytes 102432 | tf_op jit(solution)/shard_map/ppermute | solution.py:718
  80.9 1.5 %shard_map.334 = (f32[2,3,128,128]{3,2,1,0:T(8,128)}, f32[2,2,128]{2,1,0:T(2,128)}, f32[2,32,128]{2,1,0:T(8,128)}, f32[2,32]{1,0:T(2,128)}, f32[2,32,384]{2,1,0:...) custom-call(s32[1]{0:T(128)} %bitcast.refs_1_.refs_0_.refs_7_, ...), custom_call_target="tpu_custom_call" | custom-call | flops 2300000000 | tf_op jit(solution)/shard_map/pallas_call | solution.py:115
  (111 shorter events, 9.1 us)
Async XLA Ops:
  1.6 6.0 %collective-permute-start = (bf16[1,272,128]{2,1,0:T(8,128)(2,1)S(1)}, bf16[1,272,128]{2,1,0:T(8,128)(2,1)S(1)}, u32[]{:S(2)}, u32[]{:S(2)}) collective-permute-start(bf16[1,272,128]{2,1,0:T(8,128)(2,1)S(1)} %bitcast.34), channel_id=1, source_target_pairs={{0,2},{1,3},{2,0},{3,1},{4,6},{5,7},{6,4},{7,5},{8,10},{9,11},{10,... | collective-permute-start | bytes 208904 | tf_op jit(solution)/shard_map/ppermute | solution.py:718
  4.7 4.6 %copy-start = (bf16[2,3,128,128]{3,2,1,0:T(8,128)(2,1)S(1)}, bf16[2,3,128,128]{3,2,1,0:T(8,128)(2,1)}, u32[]{:S(2)}) copy-start(bf16[2,3,128,128]{3,2,1,0:T(8,128)(2,1)} %refs_14_.5) | copy-start | bytes 589828
  4.7 4.6 %copy-start.1 = (bf16[2,128,128]{2,1,0:T(8,128)(2,1)S(1)}, bf16[2,128,128]{2,1,0:T(8,128)(2,1)}, u32[]{:S(2)}) copy-start(bf16[2,128,128]{2,1,0:T(8,128)(2,1)} %refs_18_.5) | copy-start | bytes 196612
  4.7 4.6 %copy-start.2 = (f32[2,128,32]{1,2,0:T(8,128)S(1)}, f32[2,128,32]{1,2,0:T(8,128)}, u32[]{:S(2)}) copy-start(f32[2,128,32]{1,2,0:T(8,128)} %param.24) | copy-start | bytes 98308
  4.7 4.5 %copy-start.3 = (f32[2,2,128]{2,1,0:T(2,128)S(1)}, f32[2,2,128]{2,1,0:T(2,128)}, u32[]{:S(2)}) copy-start(f32[2,2,128]{2,1,0:T(2,128)} %refs_2_.8) | copy-start | bytes 6148
  4.8 4.5 %copy-start.4 = (f32[2,2,128]{2,1,0:T(2,128)S(1)}, f32[2,2,128]{2,1,0:T(2,128)}, u32[]{:S(2)}) copy-start(f32[2,2,128]{2,1,0:T(2,128)} %refs_15_.3) | copy-start | bytes 6148
  4.8 4.5 %copy-start.5 = (f32[2,2,128]{2,1,0:T(2,128)S(1)}, f32[2,2,128]{2,1,0:T(2,128)}, u32[]{:S(2)}) copy-start(f32[2,2,128]{2,1,0:T(2,128)} %refs_21_.3) | copy-start | bytes 6148
  4.8 4.5 %copy-start.7 = (f32[2,32]{1,0:T(2,128)S(1)}, f32[2,32]{1,0:T(2,128)}, u32[]{:S(2)}) copy-start(f32[2,32]{1,0:T(2,128)} %refs_17_.5) | copy-start | bytes 772
  4.8 4.5 %copy-start.8 = (f32[2,128]{1,0:T(2,128)S(1)}, f32[2,128]{1,0:T(2,128)}, u32[]{:S(2)}) copy-start(f32[2,128]{1,0:T(2,128)} %refs_19_.5) | copy-start | bytes 3076
  4.8 4.5 %copy-start.10 = (bf16[2,36,36,128]{3,0,2,1:T(2,128)(2,1)S(1)}, bf16[2,36,36,128]{3,0,2,1:T(2,128)(2,1)}, u32[]{:S(2)}) copy-start(bf16[2,36,36,128]{3,0,2,1:T(2,128)(2,1)} %param.19) | copy-start | bytes 1990660
  7.7 6.0 %collective-permute-start.1 = (bf16[2,272,128]{2,1,0:T(8,128)(2,1)S(1)}, bf16[2,272,128]{2,1,0:T(8,128)(2,1)S(1)}, u32[]{:S(2)}, u32[]{:S(2)}) collective-permute-start(bf16[2,272,128]{2,1,0:T(8,128)(2,1)S(1)} %pad_maximum_fusion.7.refs_14_), channel_id=1, source_target_pairs={{0,4},{1,5},{2,6},{3,7},{4,0},{5,1},{6,2},{7,3},{8,12},{9,13},{10,... | collective-permute-start | bytes 417800 | tf_op jit(solution)/shard_map/ppermute | solution.py:718
  13.8 1.6 %collective-permute-start.2 = (bf16[4,272,128]{2,1,0:T(8,128)(2,1)S(1)}, bf16[4,272,128]{2,1,0:T(8,128)(2,1)S(1)}, u32[]{:S(2)}, u32[]{:S(2)}) collective-permute-start(bf16[4,272,128]{2,1,0:T(8,128)(2,1)S(1)} %pad_maximum_fusion.2.refs_0_), channel_id=1, source_target_pairs={{0,1},{1,0},{2,3},{3,2},{4,5},{5,4},{6,7},{7,6},{8,9},{9,8},{10,11... | collective-permute-start | bytes 835592 | tf_op jit(solution)/shard_map/ppermute | solution.py:718
  15.5 11.9 %copy-start.15 = (f32[320]{0:T(512)S(1)}, f32[320]{0:T(512)}, u32[]{:S(2)}) copy-start(f32[320]{0:T(512)} %param.37) | copy-start | bytes 3844
  26.9 3.4 %collective-permute-start.3 = (bf16[4,368,128]{2,1,0:T(8,128)(2,1)S(1)}, bf16[4,368,128]{2,1,0:T(8,128)(2,1)S(1)}, u32[]{:S(2)}, u32[]{:S(2)}) collective-permute-start(bf16[4,368,128]{2,1,0:T(8,128)(2,1)S(1)} %get-tuple-element.149), channel_id=1, source_target_pairs={{0,1},{1,0},{2,3},{3,2},{4,5},{5,4},{6,7},{7,6},{8,9},{9,8},{10,11... | collective-permute-start | bytes 1130504 | tf_op jit(solution)/shard_map/ppermute | solution.py:718
  30.4 6.7 %collective-permute-start.4 = (bf16[2,368,128]{2,1,0:T(8,128)(2,1)S(1)}, bf16[2,368,128]{2,1,0:T(8,128)(2,1)S(1)}, u32[]{:S(2)}, u32[]{:S(2)}) collective-permute-start(bf16[2,368,128]{2,1,0:T(8,128)(2,1)S(1)} %get-tuple-element.232), channel_id=1, source_target_pairs={{0,4},{1,5},{2,6},{3,7},{4,0},{5,1},{6,2},{7,3},{8,12},{9,13},{10,... | collective-permute-start | bytes 565256 | tf_op jit(solution)/shard_map/ppermute | solution.py:718
  34.4 4.2 %collective-permute-start.5 = (bf16[4,224,128]{2,1,0:T(8,128)(2,1)S(1)}, bf16[4,224,128]{2,1,0:T(8,128)(2,1)S(1)}, u32[]{:S(2)}, u32[]{:S(2)}) collective-permute-start(bf16[4,224,128]{2,1,0:T(8,128)(2,1)S(1)} %pad_maximum_fusion.4), channel_id=1, source_target_pairs={{0,1},{1,0},{2,3},{3,2},{4,5},{5,4},{6,7},{7,6},{8,9},{9,8},{10,11... | collective-permute-start | bytes 688136 | tf_op jit(solution)/shard_map/ppermute | solution.py:718
  37.2 10.2 %collective-permute-start.10 = (bf16[1,368,128]{2,1,0:T(8,128)(2,1)S(1)}, bf16[1,368,128]{2,1,0:T(8,128)(2,1)S(1)}, u32[]{:S(2)}, u32[]{:S(2)}) collective-permute-start(bf16[1,368,128]{2,1,0:T(8,128)(2,1)S(1)} %get-tuple-element.238), channel_id=1, source_target_pairs={{0,2},{1,3},{2,0},{3,1},{4,6},{5,7},{6,4},{7,5},{8,10},{9,11},{10,... | collective-permute-start | bytes 282632 | tf_op jit(solution)/shard_map/ppermute | solution.py:718
  38.7 4.9 %collective-permute-start.6 = (bf16[2,224,128]{2,1,0:T(8,128)(2,1)S(1)}, bf16[2,224,128]{2,1,0:T(8,128)(2,1)S(1)}, u32[]{:S(2)}, u32[]{:S(2)}) collective-permute-start(bf16[2,224,128]{2,1,0:T(8,128)(2,1)S(1)} %get-tuple-element.236), channel_id=1, source_target_pairs={{0,4},{1,5},{2,6},{3,7},{4,0},{5,1},{6,2},{7,3},{8,12},{9,13},{10,... | collective-permute-start | bytes 344072 | tf_op jit(solution)/shard_map/ppermute | solution.py:718
  43.6 4.2 %collective-permute-start.9 = (bf16[1,224,128]{2,1,0:T(8,128)(2,1)S(1)}, bf16[1,224,128]{2,1,0:T(8,128)(2,1)S(1)}, u32[]{:S(2)}, u32[]{:S(2)}) collective-permute-start(bf16[1,224,128]{2,1,0:T(8,128)(2,1)S(1)} %get-tuple-element.242), channel_id=1, source_target_pairs={{0,2},{1,3},{2,0},{3,1},{4,6},{5,7},{6,4},{7,5},{8,10},{9,11},{10,... | collective-permute-start | bytes 172040 | tf_op jit(solution)/shard_map/ppermute | solution.py:718
  47.3 2.2 %collective-permute-start.7 = (bf16[4,224,128]{2,1,0:T(8,128)(2,1)S(1)}, bf16[4,224,128]{2,1,0:T(8,128)(2,1)S(1)}, u32[]{:S(2)}, u32[]{:S(2)}) collective-permute-start(bf16[4,224,128]{2,1,0:T(8,128)(2,1)S(1)} %pad_maximum_fusion.5), channel_id=1, source_target_pairs={{0,1},{1,0},{2,3},{3,2},{4,5},{5,4},{6,7},{7,6},{8,9},{9,8},{10,11... | collective-permute-start | bytes 688136 | tf_op jit(solution)/shard_map/ppermute | solution.py:718
  47.9 6.7 %collective-permute-start.14 = (bf16[592,128]{1,0:T(8,128)(2,1)S(1)}, bf16[592,128]{1,0:T(8,128)(2,1)S(1)}, u32[]{:S(2)}, u32[]{:S(2)}) collective-permute-start(bf16[592,128]{1,0:T(8,128)(2,1)S(1)} %pad_maximum_fusion.6.refs_10_), channel_id=1, source_target_pairs={{0,8},{8,0},{16,24},{24,16},{1,9},{9,1},{17,25},{25,17},{2,10},{10... | collective-permute-start | bytes 454664 | tf_op jit(solution)/shard_map/ppermute | solution.py:718
  49.7 4.9 %collective-permute-start.8 = (bf16[2,224,128]{2,1,0:T(8,128)(2,1)S(1)}, bf16[2,224,128]{2,1,0:T(8,128)(2,1)S(1)}, u32[]{:S(2)}, u32[]{:S(2)}) collective-permute-start(bf16[2,224,128]{2,1,0:T(8,128)(2,1)S(1)} %get-tuple-element.235), channel_id=1, source_target_pairs={{0,4},{1,5},{2,6},{3,7},{4,0},{5,1},{6,2},{7,3},{8,12},{9,13},{10,... | collective-permute-start | bytes 344072 | tf_op jit(solution)/shard_map/ppermute | solution.py:718
  54.7 9.1 %collective-permute-start.15 = (bf16[592,128]{1,0:T(8,128)(2,1)S(1)}, bf16[592,128]{1,0:T(8,128)(2,1)S(1)}, u32[]{:S(2)}, u32[]{:S(2)}) collective-permute-start(bf16[592,128]{1,0:T(8,128)(2,1)S(1)} %add_convert_fusion.5), channel_id=1, source_target_pairs={{0,16},{8,24},{16,0},{24,8},{1,17},{9,25},{17,1},{25,9},{2,18},{10... | collective-permute-start | bytes 454664 | tf_op jit(solution)/shard_map/ppermute | solution.py:718
  57.4 4.2 %collective-permute-start.11 = (bf16[1,224,128]{2,1,0:T(8,128)(2,1)S(1)}, bf16[1,224,128]{2,1,0:T(8,128)(2,1)S(1)}, u32[]{:S(2)}, u32[]{:S(2)}) collective-permute-start(bf16[1,224,128]{2,1,0:T(8,128)(2,1)S(1)} %get-tuple-element.240), channel_id=1, source_target_pairs={{0,2},{1,3},{2,0},{3,1},{4,6},{5,7},{6,4},{7,5},{8,10},{9,11},{10,... | collective-permute-start | bytes 172040 | tf_op jit(solution)/shard_map/ppermute | solution.py:718
  61.6 4.3 %collective-permute-start.12 = (bf16[240,128]{1,0:T(8,128)(2,1)S(1)}, bf16[240,128]{1,0:T(8,128)(2,1)S(1)}, u32[]{:S(2)}, u32[]{:S(2)}) collective-permute-start(bf16[240,128]{1,0:T(8,128)(2,1)S(1)} %pad_maximum_fusion.10), channel_id=1, source_target_pairs={{0,8},{8,0},{16,24},{24,16},{1,9},{9,1},{17,25},{25,17},{2,10},{10... | collective-permute-start | bytes 184328 | tf_op jit(solution)/shard_map/ppermute | solution.py:718
  63.9 4.9 %collective-permute-start.16 = (bf16[1,464,128]{2,1,0:T(8,128)(2,1)S(1)}, bf16[1,464,128]{2,1,0:T(8,128)(2,1)S(1)}, u32[]{:S(2)}, u32[]{:S(2)}) collective-permute-start(bf16[1,464,128]{2,1,0:T(8,128)(2,1)S(1)} %slice_bitcast_fusion), channel_id=1, source_target_pairs={{0,2},{1,3},{2,0},{3,1},{4,6},{5,7},{6,4},{7,5},{8,10},{9,11},{10,... | collective-permute-start | bytes 356360 | tf_op jit(solution)/shard_map/ppermute | solution.py:718
  65.9 5.2 %collective-permute-start.13 = (bf16[240,128]{1,0:T(8,128)(2,1)S(1)}, bf16[240,128]{1,0:T(8,128)(2,1)S(1)}, u32[]{:S(2)}, u32[]{:S(2)}) collective-permute-start(bf16[240,128]{1,0:T(8,128)(2,1)S(1)} %add_convert_fusion.10), channel_id=1, source_target_pairs={{0,16},{8,24},{16,0},{24,8},{1,17},{9,25},{17,1},{25,9},{2,18},{10... | collective-permute-start | bytes 184328 | tf_op jit(solution)/shard_map/ppermute | solution.py:718
  68.8 6.4 %collective-permute-start.18 = (bf16[2,464,128]{2,1,0:T(8,128)(2,1)S(1)}, bf16[2,464,128]{2,1,0:T(8,128)(2,1)S(1)}, u32[]{:S(2)}, u32[]{:S(2)}) collective-permute-start(bf16[2,464,128]{2,1,0:T(8,128)(2,1)S(1)} %pad_maximum_fusion.3), channel_id=1, source_target_pairs={{0,4},{1,5},{2,6},{3,7},{4,0},{5,1},{6,2},{7,3},{8,12},{9,13},{10,... | collective-permute-start | bytes 712712 | tf_op jit(solution)/shard_map/ppermute | solution.py:718
  71.1 4.1 %collective-permute-start.17 = (bf16[112,128]{1,0:T(8,128)(2,1)S(1)}, bf16[112,128]{1,0:T(8,128)(2,1)S(1)}, u32[]{:S(2)}, u32[]{:S(2)}) collective-permute-start(bf16[112,128]{1,0:T(8,128)(2,1)S(1)} %concatenate.71), channel_id=1, source_target_pairs={{0,2},{1,3},{2,0},{3,1},{4,6},{5,7},{6,4},{7,5},{8,10},{9,11},{10,... | collective-permute-start | bytes 86024 | tf_op jit(solution)/shard_map/ppermute | solution.py:718
  75.3 4.2 %collective-permute-start.19 = (bf16[208,128]{1,0:T(8,128)(2,1)S(1)}, bf16[208,128]{1,0:T(8,128)(2,1)S(1)}, u32[]{:S(2)}, u32[]{:S(2)}) collective-permute-start(bf16[208,128]{1,0:T(8,128)(2,1)S(1)} %pad_maximum_fusion.11), channel_id=1, source_target_pairs={{0,4},{1,5},{2,6},{3,7},{4,0},{5,1},{6,2},{7,3},{8,12},{9,13},{10,... | collective-permute-start | bytes 159752 | tf_op jit(solution)/shard_map/ppermute | solution.py:718
  76.3 4.6 %collective-permute-start.21 = (bf16[4,464,128]{2,1,0:T(8,128)(2,1)S(1)}, bf16[4,464,128]{2,1,0:T(8,128)(2,1)S(1)}, u32[]{:S(2)}, u32[]{:S(2)}) collective-permute-start(bf16[4,464,128]{2,1,0:T(8,128)(2,1)S(1)} %pad_maximum_fusion.1.refs_3_), channel_id=1, source_target_pairs={{0,1},{1,0},{2,3},{3,2},{4,5},{5,4},{6,7},{7,6},{8,9},{9,8},{10,11... | collective-permute-start | bytes 1425416 | tf_op jit(solution)/shard_map/ppermute | solution.py:718
  79.5 1.4 %collective-permute-start.20 = (bf16[400,128]{1,0:T(8,128)(2,1)S(1)}, bf16[400,128]{1,0:T(8,128)(2,1)S(1)}, u32[]{:S(2)}, u32[]{:S(2)}) collective-permute-start(bf16[400,128]{1,0:T(8,128)(2,1)S(1)} %pad_maximum_fusion.8.refs_1_), channel_id=1, source_target_pairs={{0,1},{1,0},{2,3},{3,2},{4,5},{5,4},{6,7},{7,6},{8,9},{9,8},{10,11... | collective-permute-start | bytes 307208 | tf_op jit(solution)/shard_map/ppermute | solution.py:718
  (6 other events, 25.5 us)
